TPU v7x, 128 devices: a whole 4x4x4 slice. The times are simulated.
128 devices in a mesh: dp: 8 (over x, core), ctx: 4 (over y), tp: 4 (over z).
Axes of the slice: x: 4, y: 4, z: 4, core: 2. Of those that a mesh axis runs over, the one named last changes fastest.
Arguments:
- tokens: float32 [8192, 2048], P(('dp', 'ctx')), may hold values from -6 to 6
- cotangent: float32 [8192, 2048], P(('dp', 'ctx')), may hold values from -6 to 6
- gain_first: float32 [2048], replicated, may hold values from 0.25 to 1.75
- gain_second: float32 [2048], replicated, may hold values from 0.25 to 1.75
- w_query: bfloat16 [2048, 2048], P(('dp', 'ctx'), 'tp'), may hold values from -0.125 to 0.125
- w_key: bfloat16 [2048, 2048], P(('dp', 'ctx'), 'tp'), may hold values from -0.125 to 0.125
- w_value: bfloat16 [2048, 4096], P(('dp', 'ctx'), 'tp'), may hold values from -0.125 to 0.125
- w_gate: bfloat16 [2048, 4096], P(('dp', 'ctx'), 'tp'), may hold values from -0.125 to 0.125
- w_output: bfloat16 [4096, 2048], P('tp', ('dp', 'ctx')), may hold values from -0.125 to 0.125
- w_hidden: bfloat16 [2048, 4096], P(('dp', 'ctx'), 'tp'), may hold values from -0.125 to 0.125
- w_linear: bfloat16 [2048, 4096], P(('dp', 'ctx'), 'tp'), may hold values from -0.125 to 0.125
- w_down: bfloat16 [4096, 2048], P('tp', ('dp', 'ctx')), may hold values from -0.125 to 0.125
- decay_scale: float32 [8], P('tp'), may hold values from 0.3 to 40
- first_length: int32 [8], P('dp'), may hold values from 769 to 1024, as said below
Outputs:
- layer_out: float32 [8192, 2048], P(('dp', 'ctx'))
- input_grad: float32 [8192, 2048], P(('dp', 'ctx'))
- gain_first_grad: float32 [2048], P(('dp', 'ctx'))
- gain_second_grad: float32 [2048], P(('dp', 'ctx'))
- query_grad: float32 [2048, 2048], P(('dp', 'ctx'), 'tp')
- key_grad: float32 [2048, 2048], P(('dp', 'ctx'), 'tp')
- value_grad: float32 [2048, 4096], P(('dp', 'ctx'), 'tp')
- gate_grad: float32 [2048, 4096], P(('dp', 'ctx'), 'tp')
- output_grad: float32 [4096, 2048], P('tp', ('dp', 'ctx'))
- hidden_grad: float32 [2048, 4096], P(('dp', 'ctx'), 'tp')
- linear_grad: float32 [2048, 4096], P(('dp', 'ctx'), 'tp')
- down_grad: float32 [4096, 2048], P('tp', ('dp', 'ctx'))
Inputs may be any that keep to these rules, and one draw needn't show every extreme that they name: Rows of group g after the first first_length[g] form a second sequence; in some group it is empty.
All inputs are finite; a program needn't handle non-finite values.
Results may differ from a plain program's by a relative error of at most 0.03.
Values may be sent and summed in bfloat16 or wider, within the bound.
No kernel may reach another device: no remote copies, remote signals or barrier semaphores. Data moves between devices by JAX's collectives and lax.ppermute only.
A program may use at most 128 MiB of HBM per device.

v0:
```python
import math

import jax
import jax.numpy as jnp
import numpy as np
from jax import lax
from jax.experimental import pallas as pl
from jax.experimental.pallas import tpu as pltpu
from jax.sharding import Mesh, PartitionSpec as P

D = 2048
DK = 256
DV = 512
SLAB = 512
BF = jnp.bfloat16
F32 = jnp.float32
XY = ("x", "ctx")
MIB = 1 << 20


def shift(value, axis, offset):
    n = lax.axis_size(axis)
    return lax.ppermute(value, axis, [(i, (i + offset) % n) for i in range(n)])


def shift_open(value, axis, offset):
    n = lax.axis_size(axis)
    return lax.ppermute(
        value, axis, [(i, i + offset) for i in range(n) if 0 <= i + offset < n]
    )


def swap(value):
    return lax.ppermute(value, "core", [(0, 1), (1, 0)])


def after(value, *earlier):
    return lax.optimization_barrier((value, *earlier))[0]


def call(
    body,
    grid,
    ins,
    outs,
    shapes,
    scalars,
    operands,
    name,
    scratch=(),
    deps=(),
    stream=False,
    aliases=None,
):
    count = len(operands)

    def kernel(s_ref, *refs):
        body(s_ref, *refs[:count], *refs[count + len(deps) :])

    ins = [*ins, *[pl.BlockSpec(memory_space=pl.ANY)] * len(deps)]
    return pl.pallas_call(
        kernel,
        out_shape=shapes,
        grid_spec=pltpu.PrefetchScalarGridSpec(
            num_scalar_prefetch=1, grid=grid, in_specs=ins, out_specs=outs, scratch_shapes=scratch
        ),
        compiler_params=pltpu.CompilerParams(
            vmem_limit_bytes=(60 if stream else 32) * MIB, dimension_semantics=("arbitrary",) * len(grid)
        ),
        cost_estimate=pl.CostEstimate(flops=1, bytes_accessed=1, transcendentals=0),
        input_output_aliases=aliases or {},
        name=name,
    )(scalars, *operands, *deps)


def tie(values, deps):
    count = len(values)
    anywhere = pl.BlockSpec(memory_space=pl.ANY)
    return pl.pallas_call(
        lambda *refs: None,
        out_shape=tuple(sds(v.shape, v.dtype) for v in values),
        in_specs=[anywhere] * (count + len(deps)),
        out_specs=(anywhere,) * count,
        input_output_aliases={i: i for i in range(count)},
        name="tie",
    )(*values, *deps)


def whole(array):
    return pl.BlockSpec(array.shape, lambda *_: (0,) * array.ndim)


def sds(shape, dtype):
    return jax.ShapeDtypeStruct(shape, dtype)


def weight_operands(weight, start, width):
    if not isinstance(weight, tuple):
        spec = pl.BlockSpec((1, 4, 2, 64, width), lambda i, s: (i, 0, 0, 0, start // width))
        return [weight], [spec]
    piece = math.gcd(start, width) if start else width
    operands, specs = [], []
    for at in range(start, start + width, piece):
        for stack in weight:
            operands.append(stack)
            specs.append(pl.BlockSpec((4, 2, 64, piece), lambda i, s, at=at: (0, 0, 0, at // piece)))
    return operands, specs


def load_slab(s_ref, refs, held):
    core = s_ref[0]
    if len(refs) == 1:
        return jnp.concatenate(
            [refs[0][0, y, jnp.bitwise_xor(c, core)] for c in (0, 1) for y in range(4)], axis=0
        )
    x_far = lax.rem(s_ref[2] + 4 - pl.program_id(0), 4)
    at = 0
    for first in range(0, len(refs), 4):
        stacks = refs[first : first + 4]
        width = stacks[0].shape[-1]
        for j in range(4):

            @pl.when((core == 0) & (x_far == j))
            def _(j=j, at=at, width=width, stacks=stacks):
                for i in range(4):
                    y = lax.rem(s_ref[3] + 4 - i, 4)
                    for c in (0, 1):
                        held[c * 4 + y, :, at : at + width] = stacks[j][i, c]

        @pl.when(core == 1)
        def _(at=at, width=width, stacks=stacks):
            for j in range(4):
                y = lax.rem(s_ref[3] + 4 - j, 4)
                for c in (0, 1):
                    held[c * 4 + y, :, at : at + width] = stacks[j][x_far, 1 - c]

        at += width
    return held[...].reshape(SLAB, at)


def hop(value, first, offset):
    pairs = []
    for x in range(4):
        for core in (0, 1):
            for y in range(4):
                to = ((x + offset) % 4, y) if (core == 0) == first else (x, (y + offset) % 4)
                pairs.append(((x * 2 + core) * 4 + y, (to[0] * 2 + core) * 4 + to[1]))
    return lax.ppermute(value, ("x", "core", "ctx"), pairs)


def spread_near(block):
    near, far, mid = [hop(block, False, o) for o in (1, 3, 2)]
    return block, near, mid, far


def stack_blocks(blocks, start, width, scalars, name, deps=()):
    at = start // width if start % width == 0 else None
    span = width if at is not None else blocks[0].shape[1]
    first = 0 if at is not None else start
    height = blocks[0].shape[0]

    def body(s_ref, *refs):
        for k, ref in enumerate(refs[:-1]):
            refs[-1][k * height : (k + 1) * height, :] = ref[:, first : first + width]

    total = sds((height * len(blocks), width), BF)
    return call(
        body,
        (1,),
        [pl.BlockSpec((height, span), lambda i, s: (0, at or 0))] * len(blocks),
        whole(total),
        total,
        scalars,
        tuple(blocks),
        name,
        deps=deps,
    )


def stack_attn(mine, came, scalars):
    height, total = mine.shape

    def body(s_ref, mine_ref, came_ref, first_ref, other_ref):
        for k, ref in enumerate((mine_ref, came_ref)):
            span = slice(k * height, (k + 1) * height)
            first_ref[span, :] = ref[:, :768]
            other_ref[span, :] = ref[:, 768:]

    shapes = (sds((2 * height, 768), BF), sds((2 * height, total - 768), BF))
    return call(
        body,
        (1,),
        [whole(mine), whole(came)],
        tuple(whole(s) for s in shapes),
        shapes,
        scalars,
        (mine, came),
        "stack_attn",
        stream=True,
    )


def spread_far(stack, gate=False):
    stack = stack.reshape(4, 2, 64, -1)
    near, far = hop(stack, True, 1), hop(stack, True, -1)
    mid = hop(tie((stack,), (near, far))[0] if gate else stack, True, 2)
    return stack, near, mid, far


def mm_in(left, right, columns, scalars, name, deps=(), stream=False):
    operands, specs, counts = [], [], []
    for weight, start, width in columns:
        ops, sp = weight_operands(weight, start, width)
        operands += ops
        specs += sp
        counts.append(len(ops))
    total = sum(width for _, _, width in columns)

    def body(s_ref, a_ref, b_ref, *refs):
        out_ref = refs[len(operands)]
        step = pl.program_id(0)
        rows = jnp.concatenate((a_ref[...], b_ref[...]), axis=0)
        at, first = 0, 0
        for k, count in enumerate(counts):
            width = columns[k][2]
            slab = load_slab(s_ref, refs[first : first + count], refs[len(operands) + 1 + k])
            part = jnp.dot(rows, slab, preferred_element_type=F32)
            span = slice(at, at + width)

            @pl.when(step == 0)
            def _(part=part, span=span):
                out_ref[:, span] = part

            @pl.when(step > 0)
            def _(part=part, span=span):
                out_ref[:, span] += part

            at += width
            first += count

    rows = left.shape[0]
    cols = pl.BlockSpec((rows, SLAB), lambda i, s: (0, i))
    return call(
        body,
        (4,),
        [cols, cols, *specs],
        pl.BlockSpec((2 * rows, total), lambda i, s: (0, 0)),
        sds((2 * rows, total), F32),
        scalars,
        (left, right, *operands),
        name,
        scratch=[pltpu.VMEM((8, 64, width), BF) for _, _, width in columns],
        deps=deps,
        stream=stream,
    )


def mm_back(terms, scalars, name, normed=None, deps=()):
    rows = terms[0][0].shape[0]
    half = rows // 2
    operands, specs, counts, scratch = [], [], [], []
    for grad, weight, start in terms:
        ops, sp = weight_operands(weight, start, grad.shape[1])
        operands += [grad, *ops]
        specs += [whole(grad), *sp]
        counts.append(len(ops))
        scratch.append(pltpu.VMEM((8, 64, grad.shape[1]), BF))
    held = len(operands)
    cols = pl.BlockSpec((half, SLAB), lambda i, s: (0, i))
    outs = [cols, cols]
    shapes = [sds((half, D), F32), sds((half, D), BF)]
    if normed is not None:
        operands += normed
        specs += [cols, cols]
        outs.append(pl.BlockSpec((8, SLAB), lambda i, s: (0, i)))
        shapes.append(sds((8, D), F32))
    total = len(operands)

    def body(s_ref, *refs):
        at, out = 0, 0.0
        for k, count in enumerate(counts):
            slab = load_slab(s_ref, refs[at + 1 : at + 1 + count], refs[total + len(outs) + k])
            out += lax.dot_general(
                refs[at][...], slab, (((1,), (1,)), ((), ())), preferred_element_type=F32
            )
            at += count + 1
        refs[total][...] = out[:half]
        refs[total + 1][...] = out[half:].astype(BF)
        if normed is not None:
            part = out[:half] * refs[held][...].astype(F32) + out[half:] * refs[held + 1][
                ...
            ].astype(F32)
            part = jnp.sum(part, axis=0, keepdims=True)
            refs[total + 2][...] = jnp.broadcast_to(part, (8, SLAB))

    return call(
        body,
        (4,),
        specs,
        tuple(outs),
        tuple(shapes),
        scalars,
        tuple(operands),
        name,
        scratch=scratch,
        deps=deps,
    )


def split_out(out, own_ref, other_ref):
    half = out.shape[0] // 2
    own_ref[...] = out[:half]
    other_ref[...] = out[half:].astype(BF)


def retain(x_pair, weight, key, value, came, fade, mask, enter, cosine, sine, scalars):
    rows = x_pair[0].shape[0]

    def body(
        s_ref, a_ref, b_ref, w_ref, k_ref, v_ref, near_ref, mid_ref, far_ref, f_ref, m_ref, e_ref,
        cos_ref, sin_ref, own_ref, other_ref, query_ref, state_ref, weighted_ref, gate_ref,
        retained_ref, mixed_ref, sums, turned
    ):
        step = pl.program_id(0)

        @pl.when(step < 4)
        def _():
            slab = load_slab(s_ref, (w_ref,), None)
            turned[step] = slab[:, DV : 2 * DV]
            left = jnp.concatenate((a_ref[...], b_ref[...]), axis=0)
            gate = jnp.dot(left, slab[:, :DV], preferred_element_type=F32)
            query = jnp.dot(left, slab[:, 2 * DV :], preferred_element_type=F32)

            @pl.when(step == 0)
            def _():
                gate_ref[...] = gate
                sums[...] = query

            @pl.when(step > 0)
            def _():
                gate_ref[...] += gate
                sums[...] += query

        @pl.when(step == 3)
        def _():
            fade = f_ref[...]
            for g in (0, 1):
                span = slice(g * rows, (g + 1) * rows)
                state = near_ref[g].astype(F32) + fade * (
                    mid_ref[g].astype(F32) + fade * far_ref[g].astype(F32)
                )
                state_ref[g] = state.astype(BF)
                query = rotate(sums[span], cos_ref[span], sin_ref[span]).astype(BF)
                query_ref[span] = query
                scores = lax.dot_general(
                    query, k_ref[g], (((1,), (1,)), ((), ())), preferred_element_type=F32
                )
                weighted = (scores * m_ref[g]).astype(BF)
                weighted_ref[g] = weighted
                retained = jnp.dot(weighted, v_ref[g], preferred_element_type=F32)
                retained += e_ref[span] * jnp.dot(
                    query, state_ref[g], preferred_element_type=F32
                )
                retained_ref[span] = retained
                mixed_ref[span] = gate_norm(gate_ref[span], retained).astype(BF)

        @pl.when(step >= 4)
        def _():
            out = lax.dot_general(
                mixed_ref[...],
                turned[step - 4],
                (((1,), (1,)), ((), ())),
                preferred_element_type=F32,
            )
            split_out(out, own_ref, other_ref)

    cols = pl.BlockSpec((rows, SLAB), lambda i, s: (0, jnp.minimum(i, 3)))
    later = pl.BlockSpec((rows, SLAB), lambda i, s: (0, jnp.maximum(i - 4, 0)))
    operands = (*x_pair, weight, key, value, *came, fade, mask, enter, cosine, sine)
    shapes = (
        sds((rows, D), F32),
        sds((rows, D), BF),
        sds((2 * rows, DK), BF),
        sds((2, DK, DV), BF),
        sds((2, rows, rows), BF),
        sds((2 * rows, DV), F32),
        sds((2 * rows, DV), F32),
        sds((2 * rows, DV), BF),
    )
    block = pl.BlockSpec((1, 4, 2, 64, 1280), lambda i, s: (jnp.minimum(i, 3), 0, 0, 0, 0))
    return call(
        body,
        (8,),
        [cols, cols, block] + [whole(o) for o in operands[3:]],
        (later, later) + tuple(whole(s) for s in shapes[2:]),
        shapes,
        scalars,
        operands,
        "retain",
        scratch=[pltpu.VMEM((2 * rows, DK), F32), pltpu.VMEM((4, SLAB, DV), BF)],
        stream=True,
    )


def mlp(x_pair, g_pair, weight, scalars):
    rows = x_pair[0].shape[0]

    def body(
        s_ref, a_ref, b_ref, c_ref, d_ref, w_ref, own_ref, other_ref, gain_ref, pair_ref, act_ref,
        both, back, kept
    ):
        step = pl.program_id(0)

        @pl.when(step < 4)
        def _():
            slab = load_slab(s_ref, (w_ref,), None)
            kept[step] = slab[:, : 2 * DV]
            left = jnp.concatenate((a_ref[...], b_ref[...]), axis=0)
            grad = jnp.concatenate((c_ref[...], d_ref[...]), axis=0)
            up = jnp.dot(left, slab[:, : 2 * DV], preferred_element_type=F32)
            down = jnp.dot(grad, slab[:, 2 * DV :], preferred_element_type=F32)

            @pl.when(step == 0)
            def _():
                both[...] = up
                back[...] = down

            @pl.when(step > 0)
            def _():
                both[...] += up
                back[...] += down

        @pl.when(step == 3)
        def _():
            def chunk(k, carry):
                span = pl.ds(pl.multiple_of(k * 64, 64), 64)
                hidden, linear, grad = both[span, :DV], both[span, DV:], back[span, :]
                cube = 0.044715 * hidden * hidden
                bent = jnp.tanh(0.7978845608 * hidden * (1.0 + cube))
                half = 0.5 * (1.0 + bent)
                gelu = hidden * half
                slope = half + 0.5 * hidden * (1.0 - bent * bent) * (
                    0.7978845608 * (1.0 + 3.0 * cube)
                )
                act_ref[span, :] = (gelu * linear).astype(BF)
                pair_ref[span, :DV] = (grad * linear * slope).astype(BF)
                pair_ref[span, DV:] = (grad * gelu).astype(BF)
                return carry

            lax.fori_loop(0, 2 * rows // 64, chunk, 0)

        @pl.when(step >= 4)
        def _():
            out = lax.dot_general(
                pair_ref[...], kept[step - 4], (((1,), (1,)), ((), ())), preferred_element_type=F32
            )
            split_out(out, own_ref, other_ref)
            part = out[:rows] * a_ref[...].astype(F32) + out[rows:] * b_ref[...].astype(F32)
            gain_ref[...] = jnp.broadcast_to(jnp.sum(part, axis=0, keepdims=True), (8, SLAB))

    cols = pl.BlockSpec((rows, SLAB), lambda i, s: (0, lax.rem(i, 4)))
    once = pl.BlockSpec((rows, SLAB), lambda i, s: (0, jnp.minimum(i, 3)))
    block = pl.BlockSpec((1, 4, 2, 64, 3 * DV), lambda i, s: (jnp.minimum(i, 3), 0, 0, 0, 0))
    later = pl.BlockSpec((rows, SLAB), lambda i, s: (0, jnp.maximum(i - 4, 0)))
    shapes = (
        sds((rows, D), F32),
        sds((rows, D), BF),
        sds((8, D), F32),
        sds((2 * rows, 2 * DV), BF),
        sds((2 * rows, DV), BF),
    )
    return call(
        body,
        (8,),
        [cols, cols, once, once, block],
        (
            later,
            later,
            pl.BlockSpec((8, SLAB), lambda i, s: (0, jnp.maximum(i - 4, 0))),
            whole(shapes[3]),
            whole(shapes[4]),
        ),
        shapes,
        scalars,
        (*x_pair, *g_pair, weight),
        "mlp",
        scratch=[
            pltpu.VMEM((2 * rows, 2 * DV), F32),
            pltpu.VMEM((2 * rows, DV), F32),
            pltpu.VMEM((4, SLAB, 2 * DV), BF),
        ],
        stream=True,
    )


def mm_weight_into(into, pairs, start, total, scalars, name, deps=()):
    widths = [grad.shape[1] for _, grad in pairs]
    rows = pairs[0][0][0].shape[0]
    span = sum(widths)

    def body(s_ref, *refs):
        out_ref, mark_ref = refs[-2:]
        at = 0
        for k, width in enumerate(widths):
            a_ref, b_ref, g_ref = refs[3 * k : 3 * k + 3]
            out = lax.dot_general(
                jnp.concatenate((a_ref[...], b_ref[...]), axis=0),
                g_ref[...],
                (((0,), (0,)), ((), ())),
                preferred_element_type=F32,
            ).astype(BF)
            for c in (0, 1):
                for y in range(4):
                    first = (c * 4 + y) * 64
                    out_ref[0, y, jnp.bitwise_xor(c, s_ref[0]), :, at : at + width] = out[
                        first : first + 64
                    ]
            at += width
        mark_ref[...] = jnp.zeros_like(mark_ref)

    cols = pl.BlockSpec((rows, SLAB), lambda i, s: (0, i))
    specs, operands = [], []
    for (a, b), grad in pairs:
        specs += [cols, cols, whole(grad)]
        operands += [a, b, grad]
    aliases = None
    if into is not None:
        aliases = {1 + len(operands): 0}
        specs.append(pl.BlockSpec(memory_space=pl.ANY))
        operands.append(into)
    return call(
        body,
        (4,),
        specs,
        (
            pl.BlockSpec((1, 4, 2, 64, span), lambda i, s: (i, 0, 0, 0, start // span)),
            pl.BlockSpec((8, 128), lambda i, s: (0, 0)),
        ),
        (sds((4, 4, 2, 64, total), BF), sds((8, 128), F32)),
        scalars,
        tuple(operands),
        name,
        deps=deps,
        stream=True,
        aliases=aliases,
    )


def split_heads(weights, scalars, name, deps=()):
    widths = [w.shape[1] // 2 for w in weights]

    def body(s_ref, *refs):
        mine_ref, theirs_ref = refs[-2:]
        core = s_ref[0]
        for out_ref, head in ((mine_ref, core), (theirs_ref, 1 - core)):
            at = 0
            for ref, width in zip(refs, widths):
                out_ref[:, at : at + width] = ref[:, pl.ds(pl.multiple_of(head * width, width), width)]
                at += width

    total = sum(widths)
    spec = pl.BlockSpec((64, total), lambda i, s: (0, 0))
    return call(
        body,
        (1,),
        [whole(w) for w in weights],
        (spec, spec),
        (sds((64, total), BF),) * 2,
        scalars,
        tuple(weights),
        name,
        deps=deps,
        stream=True,
    )


def join_heads(mine, theirs, widths, scalars, name):
    def body(s_ref, mine_ref, theirs_ref, *outs):
        core = s_ref[0]
        for in_ref, head in ((mine_ref, core), (theirs_ref, 1 - core)):
            at = 0
            for ref, width in zip(outs, widths):
                span = pl.ds(pl.multiple_of(head * width, width), width)
                ref[:, span] = in_ref[:, at : at + width].astype(F32)
                at += width

    shapes = tuple(sds((64, 2 * w), F32) for w in widths)
    return call(
        body,
        (1,),
        [whole(mine), whole(theirs)],
        tuple(whole(s) for s in shapes),
        shapes,
        scalars,
        (mine, theirs),
        name,
    )


def scale_of(values):
    return lax.rsqrt(jnp.mean(values * values, axis=-1, keepdims=True) + 1e-06)


def turned_spec(rows):
    return pl.BlockSpec((rows, D), lambda i, s: (lax.rem(i + s[1], 4), 0))


def plain_spec(rows):
    return pl.BlockSpec((rows, D), lambda i, s: (i, 0))


def enter_rows(tokens, gain, scalars, deps=()):
    rows = tokens.shape[0]
    block = rows // 4

    def body(s_ref, t_ref, g_ref, n_out):
        values = t_ref[...]
        n_out[...] = (values * scale_of(values) * g_ref[...]).astype(BF)

    return call(
        body,
        (4,),
        [turned_spec(block), whole(gain)],
        plain_spec(block),
        sds((rows, D), BF),
        scalars,
        (tokens, gain),
        "enter_rows",
        deps=deps,
    )


def low_rows(cotangent, scalars, deps=()):
    rows = cotangent.shape[0]
    block = rows // 4

    def body(s_ref, c_ref, l_out):
        l_out[...] = c_ref[...].astype(BF)

    return call(
        body,
        (4,),
        [turned_spec(block)],
        plain_spec(block),
        sds((rows, D), BF),
        scalars,
        (cotangent,),
        "low_rows",
        deps=deps,
    )


def each_part(refs, work):
    step = pl.program_id(0)
    for k, ref in enumerate(refs):

        @pl.when(step == k)
        def _(ref=ref):
            work(ref[...].astype(F32))


def second_norm(tokens, parts, gain, scalars, deps=()):
    rows = tokens.shape[0]
    block = rows // 4

    def body(s_ref, t_ref, g_ref, *refs):
        h_out, n_out = refs[4:]

        def work(part):
            values = t_ref[...] + part
            h_out[...] = values
            n_out[...] = (values * scale_of(values) * g_ref[...]).astype(BF)

        each_part(refs[:4], work)

    plain = plain_spec(block)
    return call(
        body,
        (4,),
        [turned_spec(block), whole(gain)] + [whole(p) for p in parts],
        (plain, plain),
        (sds((rows, D), F32), sds((rows, D), BF)),
        scalars,
        (tokens, gain, *parts),
        "second_norm",
        deps=deps,
    )


def third_blocks(own, came, down_own, down_came, scalars, deps=()):
    rows = own.shape[0]
    block = rows // 4

    def body(s_ref, own_ref, came_ref, d_ref, e_ref, *refs):
        total = own_ref[...] + came_ref[...].astype(F32)
        down = d_ref[...] + e_ref[...].astype(F32)
        step = pl.program_id(0)
        for k in range(4):

            @pl.when(step == k)
            def _(k=k):
                refs[k][:block] = total.astype(BF)
                refs[k][block:] = down.astype(BF)

    plain = plain_spec(block)
    shapes = (sds((2 * block, D), BF),) * 4
    return call(
        body,
        (4,),
        [plain] * 4,
        tuple(whole(s) for s in shapes),
        shapes,
        scalars,
        (own, came, down_own, down_came),
        "third_blocks",
        deps=deps,
        stream=True,
    )


def leave_rows(hidden, tokens, grad_state, parts, gain, scalars, deps=()):
    rows = hidden.shape[0]
    block = rows // 4

    def body(s_ref, h_ref, t_ref, u_ref, g_ref, *refs):
        def work(part):
            refs[4][...] = h_ref[...] + part[block : 2 * block]
            refs[5][...] = u_ref[...] + norm_grad(t_ref[...], part[:block], g_ref[...])

        each_part(refs[:4], work)

    plain, turn = plain_spec(block), turned_spec(block)
    return call(
        body,
        (4,),
        [plain, turn, plain, whole(gain)] + [whole(p) for p in parts],
        (turn, turn),
        (sds((rows, D), F32),) * 2,
        scalars,
        (hidden, tokens, grad_state, gain, *parts),
        "leave_rows",
        deps=deps,
        stream=True,
    )


def norm_grad(values, grad, gain):
    factor = scale_of(values)
    unit = values * factor
    scaled = grad * gain
    return factor * (scaled - unit * jnp.mean(scaled * unit, axis=-1, keepdims=True))


def norm_back(values, upstream, parts, gain, scalars, name, deps=()):
    rows = values.shape[0]
    block = rows // 4

    def body(s_ref, v_ref, u_ref, g_ref, *refs):
        def work(part):
            out = u_ref[...] + norm_grad(v_ref[...], part, g_ref[...])
            refs[4][...] = out
            refs[5][...] = out.astype(BF)

        each_part(refs[:4], work)

    plain = plain_spec(block)
    return call(
        body,
        (4,),
        [plain, turned_spec(block), whole(gain)] + [whole(p) for p in parts],
        (plain, plain),
        (sds((rows, D), F32), sds((rows, D), BF)),
        scalars,
        (values, upstream, gain, *parts),
        name,
        deps=deps,
        stream=True,
    )


def tp_first(blocks):
    got = [shift(blocks[o], "tp", o) for o in (1, 3, 2)]
    near, far, mid = [part.astype(F32) for part in got]
    return (blocks[0].astype(F32) + mid) + (near + far), got


def tp_second(mine):
    near, far, mid = [shift(mine, "tp", -o) for o in (1, 3, 2)]
    return mine, near, mid, far


def tp_total(blocks):
    return tp_second(tp_first(blocks)[0].astype(BF))


def chip_blocks(own, came):
    block = own.shape[0] // 4
    return [
        (own[o * block : (o + 1) * block] + came[o * block : (o + 1) * block].astype(F32)).astype(BF)
        for o in range(4)
    ]


def gate_norm(gate_pre, retained):
    centred = retained - jnp.mean(retained, axis=-1, keepdims=True)
    normed = centred * lax.rsqrt(jnp.mean(centred * centred, axis=-1, keepdims=True) + 1.0 * DK)
    return gate_pre * jax.nn.sigmoid(gate_pre) * normed


def gelu_gate(hidden, linear):
    return jax.nn.gelu(hidden, approximate=True) * linear


def rotate(values, cosine, sine):
    half = DK // 2
    first = values[:, :half]
    second = values[:, half:]
    return jnp.concatenate((first * cosine - second * sine, first * sine + second * cosine), axis=1)


def ein(spec, left, right):
    return jnp.einsum(spec, left, right, preferred_element_type=F32)


def per_device(
    tokens,
    cotangent,
    gain_first,
    gain_second,
    w_query,
    w_key,
    w_value,
    w_gate,
    w_output,
    w_hidden,
    w_linear,
    w_down,
    decay_scale,
    first_length,
):
    rows = tokens.shape[0]
    core = lax.axis_index("core")
    place = lax.axis_index("ctx")
    plane = lax.axis_index("tp")
    scalars = jnp.stack((core, plane, lax.axis_index("x"), place)).astype(jnp.int32)

    w_output = w_output.T
    w_down = w_down.T
    mine, theirs = split_heads((w_value, w_key, w_gate, w_output, w_query), scalars, "split_attn")
    came = swap(theirs)
    block, gathered = stack_attn(mine, came, scalars)
    lengths = jnp.concatenate((first_length, swap(first_length)))
    blocks = spread_near(block)
    w_kv = stack_blocks(blocks, 0, 768, scalars, "stack_kv", deps=(lengths,))
    normed_first = enter_rows(tokens, gain_first.reshape(1, D), scalars, deps=blocks[1:])
    w_goq = lax.all_gather(gathered, XY, axis=0, tiled=True).reshape(4, 4, 2, 64, -1)
    mine, theirs = split_heads(
        (w_hidden, w_linear, w_down), scalars, "split_mlp", deps=(gathered,)
    )
    came_mlp = swap(theirs)
    gain_first = gain_first.reshape(1, D)
    gain_second = gain_second.reshape(1, D)
    x_first = (normed_first, swap(normed_first))
    cot_low = low_rows(cotangent, scalars, deps=(x_first[1],))
    g_out = (cot_low, swap(cot_low))
    w_kv = spread_far(w_kv)

    rate = lax.dynamic_index_in_dim(decay_scale, core, 0, False) / 1024.0
    local = (jnp.arange(rows, dtype=jnp.int32) + plane * (rows // 4)) % rows
    index = place * rows + local
    document = (index[None, :] >= lengths[:, None]).astype(jnp.int32)
    carried = (document == 0).astype(F32)
    steps = local.astype(F32)
    offsets = local[:, None] - local[None, :]
    linked = (offsets >= 0)[None] & (document[:, :, None] == document[:, None, :])
    mask = jnp.where(
        linked, jnp.exp(-rate * jnp.maximum(offsets, 0).astype(F32))[None], 0.0
    )
    enter = (carried * jnp.exp(-rate * (steps + 1.0))[None])[:, :, None]
    leave = jnp.exp(-rate * (rows - 1.0 - steps))[None, :, None]
    fade = jnp.exp(-rate * rows)
    half = DK // 2
    frequency = 10000.0 ** (-(jnp.arange(half).astype(F32) / half))
    angles = index.astype(F32)[:, None] * frequency[None, :]
    cosine = jnp.tile(jnp.cos(angles), (2, 1))
    sine = jnp.tile(jnp.sin(angles), (2, 1))

    def carry(came):
        near, mid, far = [part.astype(F32) for part in came]
        return near + fade * (mid + fade * far)

    def spread_state(low, way):
        return [shift_open(low, "ctx", way * o) for o in (1, 2, 3)]

    projected = mm_in(*x_first, [(w_kv, 0, 768)], scalars, "project_kv")
    key = rotate(projected[:, DV:], cosine, sine).astype(BF).reshape(2, rows, DK)
    value = projected[:, :DV].astype(BF).reshape(2, rows, DV)
    key_out = (key.astype(F32) * leave).astype(BF)
    state_out = ein("gjd,gje->gde", key_out, value).astype(BF)
    came = spread_state(state_out, 1)
    w_mlp = lax.all_gather(
        stack_blocks((mine, came_mlp), 0, 1536, scalars, "stack_mlp", deps=came),
        XY,
        axis=0,
        tiled=True,
    ).reshape(4, 4, 2, 64, -1)
    own, other, query, state_in, weighted, gate_pre, retained, mixed = retain(
        x_first,
        w_goq,
        key,
        value,
        came,
        fade.reshape(1, 1),
        mask,
        enter.reshape(2 * rows, 1),
        cosine,
        sine,
        scalars,
    )
    query = query.reshape(2, rows, DK)
    _, gate_back = jax.vjp(gate_norm, gate_pre, retained)
    parts = tp_total(chip_blocks(own, swap(other)))
    hidden_state, normed_second = second_norm(tokens, parts, gain_second, scalars)
    x_second = (normed_second, swap(normed_second))
    own, other, gain_second_part, grad_pair, activated = mlp(x_second, g_out, w_mlp, scalars)
    grads, mark = mm_weight_into(
        None, ((x_second, grad_pair),), 1024, 3584, scalars, "weight_mlp"
    )
    mine, _ = tp_first(chip_blocks(own, swap(other)))
    (mine,) = tie((mine.astype(BF),), (mark,))
    parts = tp_second(mine)
    down = mm_back([(activated, w_mlp, 2 * DV)], scalars, "project_down", deps=(mine,))
    grad_state, grad_state_low = norm_back(
        hidden_state,
        cotangent,
        parts,
        gain_second,
        scalars,
        "second_back",
        deps=(down[1],),
    )
    g_state = (grad_state_low, swap(grad_state_low))
    grad_mixed = mm_in(*g_state, [(w_goq, DV, DV)], scalars, "back_out", stream=True)
    grad_gate, grad_retained = gate_back(grad_mixed)
    grad_low = grad_retained.reshape(2, rows, DV).astype(BF)
    query_in = (query.astype(F32) * enter).astype(BF)
    back_out = ein("gid,gie->gde", query_in, grad_low).astype(BF)
    came = spread_state(back_out, -1)
    grad_scores = (ein("gie,gje->gij", grad_low, value) * mask).astype(BF)
    grad_query = ein("gij,gjd->gid", grad_scores, key) + enter * ein("gie,gde->gid", grad_low, state_in)
    grad_key = ein("gij,gid->gjd", grad_scores, query)
    grad_value = ein("gij,gie->gje", weighted, grad_low)
    grad_gate = grad_gate.astype(BF)
    grad_query = rotate(grad_query.reshape(2 * rows, DK), cosine, -sine).astype(BF)
    grads, mark = mm_weight_into(
        grads,
        ((g_state, mixed), (x_first, grad_gate)),
        2048,
        3584,
        scalars,
        "weight_og",
        deps=(back_out,),
    )
    grads, mark = mm_weight_into(
        grads, ((g_out, activated),), 3072, 3584, scalars, "weight_down"
    )
    grads, mark = mm_weight_into(
        grads, ((x_first, grad_query),), 768, 3584, scalars, "weight_query"
    )
    came[0] = tie((came[0],), (mark, grad_key, grad_value))[0]
    state_back = carry(came).astype(BF)
    grad_key += leave * ein("gje,gde->gjd", value, state_back)
    grad_value += ein("gjd,gde->gje", key_out, state_back)
    grad_key = rotate(grad_key.reshape(2 * rows, DK), cosine, -sine)
    grad_vk = jnp.concatenate(
        (grad_value.reshape(2 * rows, DV).astype(BF), grad_key.astype(BF)), axis=1
    )
    grads, mark = mm_weight_into(grads, ((x_first, grad_vk),), 0, 3584, scalars, "weight_vk")
    block = lax.psum_scatter(grads.reshape(2048, -1), XY, scatter_dimension=0, tiled=True)
    own, other, gain_first_part = mm_back(
        [(grad_vk, w_kv, 0), (grad_gate, w_goq, 0), (grad_query, w_goq, 1024)],
        scalars,
        "back_attn",
        normed=x_first,
        deps=(mark,),
    )
    down = (down[0], swap(tie((down[1],), (mark,))[0]))
    blocks = third_blocks(own, swap(other), *down, scalars)
    mine, _ = tp_first(blocks)
    gains = jnp.concatenate((gain_first_part[:1], gain_second_part[:1]))
    for axis, swapped in (
        ("core", (1, 0)),
        ("ctx", (1, 0, 3, 2)),
        ("ctx", (3, 2, 1, 0)),
        ("x", (1, 0, 3, 2)),
        ("x", (3, 2, 1, 0)),
    ):
        gains = gains + lax.ppermute(gains, axis, list(enumerate(swapped)))
    mine = jnp.concatenate((mine, gains, jnp.zeros((14, D), F32))).astype(BF)
    parts = tp_second(mine)
    gains = [part[128:130].astype(F32) for part in parts]
    gains = (gains[0] + gains[2]) + (gains[1] + gains[3])
    spot = (lax.axis_index("x") * 2 + core) * 4 + place
    gain_first_grad, gain_second_grad = [
        lax.dynamic_slice_in_dim(gains[k] / gain[0], spot * 64, 64, 0)
        for k, gain in ((0, gain_first), (1, gain_second))
    ]
    layer_out, input_grad = leave_rows(
        hidden_state, tokens, grad_state, parts, gain_first, scalars
    )
    block = tie((block,), (gain_first_grad, gain_second_grad, input_grad))[0].reshape(2, 64, -1)
    d_value, d_key, d_query, d_hidden, d_linear, d_output, d_gate, d_down = join_heads(
        block[0], swap(block[1]), (DV, DK, DK) + (DV,) * 5, scalars, "join_heads"
    )
    return (
        layer_out,
        input_grad,
        gain_first_grad,
        gain_second_grad,
        d_query,
        d_key,
        d_value,
        d_gate,
        d_output.T,
        d_hidden,
        d_linear,
        d_down.T,
    )


def solution(mesh):
    fine = Mesh(np.asarray(mesh.devices).reshape(4, 2, 4, 4), ("x", "core", "ctx", "tp"))
    split = ("x", "core", "ctx")
    row = P(split, None)
    win = P(split, "tp")
    wout = P("tp", split)
    in_specs = (row, row, P(), P(), win, win, win, win, wout, win, win, wout, P("tp"), P(("x", "core")))
    out_specs = (row, row, P(split), P(split), win, win, win, win, wout, win, win, wout)
    return jax.shard_map(
        per_device, mesh=fine, in_specs=in_specs, out_specs=out_specs, check_vma=False
    )
```

profile of v0, /device:TPU:1, one launch (start us, length us, event | category | flops | bytes accessed | tf_op | source)
XLA Modules:
  0.0 394.2 jit_solution(7758457467538822202)
XLA Ops:
  7.9 2.6 split_attn.1
  13.9 2.5 stack_attn.1
  16.5 2.6 collective-permute-start.3
  20.3 3.9 %collective-permute-done.3.refs_4_.refs_3_ = bf16[128,768]{1,0:T(8,128)(2,1)S(1)} collective-permute-done((bf16[128,768]{1,0:T(8,128)(2,1)}, bf16[128,768]{1,0:T(8,128)(2,1)S(1)}, u32[]{:S(2)}, u32[]{:S(2)}) %collective-permute-start.3) | collective-permute-done | bytes 196640 | tf_op jit(solution)/shard_map/ppermute | solution.py:148
  25.7 2.1 collective-permute-done.1.refs_2_.refs_1_
  27.8 1.7 copy-done.7
  32.1 1.8 collective-permute-start.4
  41.3 8.7 %collective-permute-done.8.refs_5_.refs_4_ = bf16[4,2,64,768]{3,2,1,0:T(8,128)(2,1)} collective-permute-done((bf16[4,2,64,768]{3,2,1,0:T(8,128)(2,1)S(1)}, bf16[4,2,64,768]{3,2,1,0:T(8,128)(2,1)}, u32[]{:S(2)}, u32[]{:S(2)}) %collective-permute-start.8) | collective-permute-done | bytes 786464 | tf_op jit(solution)/shard_map/ppermute | solution.py:148
  50.0 1.5 collective-permute-done.7.refs_4_.refs_3_
  51.6 10.1 %collective-permute-done.6.refs_3_.refs_2_ = bf16[4,2,64,768]{3,2,1,0:T(8,128)(2,1)} collective-permute-done((bf16[4,2,64,768]{3,2,1,0:T(8,128)(2,1)S(1)}, bf16[4,2,64,768]{3,2,1,0:T(8,128)(2,1)}, u32[]{:S(2)}, u32[]{:S(2)}) %collective-permute-start.6) | collective-permute-done | bytes 786464 | tf_op jit(solution)/shard_map/ppermute | solution.py:148
  61.7 5.7 %project_kv.1 = f32[512,768]{1,0:T(8,128)S(1)} custom-call(s32[4]{0:T(128)S(1)} %copy-done.27, bf16[256,2048]{1,0:T(8,128)(2,1)S(1)} %enter_rows.1.refs_0_.refs_3_.refs_9_, bf16[256,2048]{1,0:T(8,128)(2,1)S(1)} %collective-permute-done.4.refs_1_.refs_4_.refs_10_, bf16[4,2,64,768]{3,2,1,0:T(8,128)(2,1)S(1)} %bitcast.109, ...), custom_call_target="tpu_custom_call" | custom-call | flops 1 | bytes 1 | tf_op jit(solution)/shard_map/project_kv/pallas_call | solution.py:61
  68.0 2.6 collective-permute-start.11
  71.9 2.5 collective-permute-start.9
  74.4 2.5 split_mlp.1
  76.9 5.2 %collective-permute-start.21 = (bf16[64,1536]{1,0:T(8,128)(2,1)}, bf16[64,1536]{1,0:T(8,128)(2,1)S(1)}, u32[]{:S(2)}, u32[]{:S(2)}) collective-permute-start(bf16[64,1536]{1,0:T(8,128)(2,1)} %get-tuple-element.71), channel_id=1, source_target_pairs={{0,16},{16,0},{1,17},{17,1},{2,18},{18,2},{3,19},{19,3},{4,20},{20... | collective-permute-start | bytes 589832 | tf_op jit(solution)/shard_map/ppermute | solution.py:34
  83.4 16.0 %collective-permute-done.11.refs_7_.refs_4_ = bf16[2,256,512]{2,1,0:T(8,128)(2,1)S(1)} collective-permute-done((bf16[2,256,512]{2,1,0:T(8,128)(2,1)S(1)}, bf16[2,256,512]{2,1,0:T(8,128)(2,1)S(1)}, u32[]{:S(2)}, u32[]{:S(2)}) %collective-permute-start.11) | collective-permute-done | bytes 524320 | tf_op jit(solution)/shard_map/ppermute | solution.py:28
  106.7 12.9 %retain.1 = (f32[256,2048]{1,0:T(8,128)}, bf16[256,2048]{1,0:T(8,128)(2,1)}, bf16[512,256]{1,0:T(8,128)(2,1)}, bf16[2,256,512]{2,1,0:T(8,128)(2,1)}, bf16[2,256,...) custom-call(s32[4]{0:T(128)} %pad_add_fusion.s_ref, ...), custom_call_target="tpu_custom_call" | custom-call | flops 1 | bytes 1 | tf_op jit(solution)/shard_map/retain/pallas_call | solution.py:61
  119.5 2.2 collective-permute-start.12
  121.7 2.5 collective-permute-done.12
  124.2 1.7 add_convert_fusion.11
  126.0 3.4 collective-permute-start.13
  130.8 5.0 %collective-permute-done.13 = bf16[64,2048]{1,0:T(8,128)(2,1)S(1)} collective-permute-done((bf16[64,2048]{1,0:T(8,128)(2,1)S(1)}, bf16[64,2048]{1,0:T(8,128)(2,1)S(1)}, u32[]{:S(2)}, u32[]{:S(2)}) %collective-permute-start.13) | collective-permute-done | bytes 262176 | tf_op jit(solution)/shard_map/ppermute | solution.py:23
  135.8 5.8 %collective-permute-done.15 = bf16[64,2048]{1,0:T(8,128)(2,1)S(1)} collective-permute-done((bf16[64,2048]{1,0:T(8,128)(2,1)S(1)}, bf16[64,2048]{1,0:T(8,128)(2,1)S(1)}, u32[]{:S(2)}, u32[]{:S(2)}) %collective-permute-start.15) | collective-permute-done | bytes 262176 | tf_op jit(solution)/shard_map/ppermute | solution.py:23
  144.3 2.8 collective-permute-start.17
  151.7 7.1 %collective-permute-done.17.refs_4_ = bf16[64,2048]{1,0:T(8,128)(2,1)S(1)} collective-permute-done((bf16[64,2048]{1,0:T(8,128)(2,1)S(1)}, bf16[64,2048]{1,0:T(8,128)(2,1)S(1)}, u32[]{:S(2)}, u32[]{:S(2)}) %collective-permute-start.17) | collective-permute-done | bytes 262176 | tf_op jit(solution)/shard_map/ppermute | solution.py:23
  162.8 2.4 collective-permute-done.19.refs_1_
  166.1 14.4 %mlp.1 = (f32[256,2048]{1,0:T(8,128)}, bf16[256,2048]{1,0:T(8,128)(2,1)}, f32[8,2048]{1,0:T(8,128)}, bf16[512,1024]{1,0:T(8,128)(2,1)}, bf16[512,512]{1,0:T(8,128)(2,1)}) custom-call(s32[4]{0:T(128)} %pad_add_fusion.s_ref, bf16[256,2048]{1,0:T(8,128)(2,1)} %copy-done.18, bf16[256,2048]{1,0:T(8,128)(2,1)} %collective-permute-done.19.refs_1_, ...), custom_call_target="tpu_custom_call" | custom-call | flops 1 | bytes 1 | tf_op jit(solution)/shard_map/mlp/pallas_call | solution.py:61
  181.3 2.5 collective-permute-done.22
  183.8 1.6 add_convert_fusion.6
  185.3 2.9 collective-permute-start.23
  189.8 6.9 %weight_mlp.1 = (bf16[4,4,2,64,3584]{4,3,2,1,0:T(8,128)(2,1)}, f32[8,128]{1,0:T(8,128)}) custom-call(s32[4]{0:T(128)} %pad_add_fusion.s_ref, bf16[256,2048]{1,0:T(8,128)(2,1)} %copy-done.18, bf16[256,2048]{1,0:T(8,128)(2,1)} %collective-permute-done.19.refs_1_, bf16[512,1024]{1,0:T(8,128)(2,1)} %get-tuple-element.74.refs_2_), custom_call_target="tpu_custom_call" | custom-call | flops 1 | bytes 1 | tf_op jit(solution)/shard_map/weight_mlp/pallas_call | solution.py:61
  196.7 3.7 collective-permute-done.25
  200.8 1.9 add_convert_fusion.3.refs_0_
  204.0 2.6 collective-permute-start.27
  207.6 2.8 copy-done.6
  211.4 2.8 project_down.1
  216.5 1.8 collective-permute-done.27.refs_5_
  219.1 6.1 %second_back.1 = (f32[256,2048]{1,0:T(8,128)}, bf16[256,2048]{1,0:T(8,128)(2,1)}) custom-call(s32[4]{0:T(128)} %pad_add_fusion.s_ref, f32[256,2048]{1,0:T(8,128)} %copy-done.10, f32[256,2048]{1,0:T(8,128)} %refs_1_.6, f32[1,2048]{1,0:T(1,128)} %bitcast.111, bf16[64,2048]{1,0:T(8,128)(2,1)} %tie.4.refs_2_.refs_3_, bf16[64,2048]{1,0:T(8,128)(2,1)} %copy-done.67, ...), custom_call_target="tpu_custom_call" | custom-call | flops 1 | bytes 1 | tf_op jit(solution)/shard_map/second_back/pallas_call | solution.py:61
  226.7 2.2 collective-permute-done.29.refs_1_
  230.0 5.7 %back_out.1 = f32[512,512]{1,0:T(8,128)} custom-call(s32[4]{0:T(128)} %pad_add_fusion.s_ref, bf16[256,2048]{1,0:T(8,128)(2,1)} %get-tuple-element.81.refs_0_, bf16[256,2048]{1,0:T(8,128)(2,1)} %copy-done.44, bf16[4,4,2,64,1280]{4,3,2,1,0:T(8,128)(2,1)} %bitcast.101), custom_call_target="tpu_custom_call" | custom-call | flops 1 | bytes 1 | tf_op jit(solution)/shard_map/back_out/pallas_call | solution.py:61
  235.7 1.9 multiply_reduce_fusion.1
  237.7 1.6 fusion.32
  246.3 7.2 %weight_og.1 = (bf16[4,4,2,64,3584]{4,3,2,1,0:T(8,128)(2,1)}, f32[8,128]{1,0:T(8,128)}) custom-call(s32[4]{0:T(128)} %pad_add_fusion.s_ref, bf16[256,2048]{1,0:T(8,128)(2,1)} %get-tuple-element.81.refs_0_, bf16[256,2048]{1,0:T(8,128)(2,1)} %copy-done.44, bf16[512,512]{1,0:T(8,128)(2,1)} %get-tuple-element.85.refs_2_, ...), custom_call_target="tpu_custom_call", output_to_operand_aliasing={{0}: (7, {})} | custom-call | flops 1 | bytes 1 | tf_op jit(solution)/shard_map/weight_og/pallas_call | solution.py:61
  253.5 5.5 %weight_down.1 = (bf16[4,4,2,64,3584]{4,3,2,1,0:T(8,128)(2,1)}, f32[8,128]{1,0:T(8,128)}) custom-call(s32[4]{0:T(128)} %pad_add_fusion.s_ref, bf16[256,2048]{1,0:T(8,128)(2,1)} %copy-done.9, bf16[256,2048]{1,0:T(8,128)(2,1)} %copy-done.47, bf16[512,512]{1,0:T(8,128)(2,1)} %get-tuple-element.76.refs_0_.refs_2_, ...), custom_call_target="tpu_custom_call", output_to_operand_aliasing={{0}: (4, {})} | custom-call | flops 1 | bytes 1 | tf_op jit(solution)/shard_map/weight_down/pallas_call | solution.py:61
  259.0 5.1 %weight_query.1 = (bf16[4,4,2,64,3584]{4,3,2,1,0:T(8,128)(2,1)}, f32[8,128]{1,0:T(8,128)}) custom-call(s32[4]{0:T(128)} %pad_add_fusion.s_ref, bf16[256,2048]{1,0:T(8,128)(2,1)} %copy-done.4, bf16[256,2048]{1,0:T(8,128)(2,1)} %copy-done.1, bf16[512,256]{1,0:T(8,128)(2,1)} %pad_maximum_fusion.2.refs_2_.refs_7_, ...), custom_call_target="tpu_custom_call", output_to_operand_aliasing={{0}: (4, {})} | custom-call | flops 1 | bytes 1 | tf_op jit(solution)/shard_map/weight_query/pallas_call | solution.py:61
  268.3 1.6 add_convert_fusion.1
  271.7 6.2 %weight_vk.1 = (bf16[4,4,2,64,3584]{4,3,2,1,0:T(8,128)(2,1)}, f32[8,128]{1,0:T(8,128)}) custom-call(s32[4]{0:T(128)} %pad_add_fusion.s_ref, bf16[256,2048]{1,0:T(8,128)(2,1)} %copy-done.4, bf16[256,2048]{1,0:T(8,128)(2,1)} %copy-done.1, bf16[512,768]{1,0:T(8,128)(2,1)} %pad_maximum_fusion.refs_2_.refs_0_, ...), custom_call_target="tpu_custom_call", output_to_operand_aliasing={{0}: (4, {})} | custom-call | flops 1 | bytes 1 | tf_op jit(solution)/shard_map/weight_vk/pallas_call | solution.py:61
  279.8 2.5 copy-done
  284.4 7.5 %back_attn.1 = (f32[256,2048]{1,0:T(8,128)S(1)}, bf16[256,2048]{1,0:T(8,128)(2,1)S(1)}, f32[8,2048]{1,0:T(8,128)S(1)}) custom-call(s32[4]{0:T(128)S(1)} %copy-done.31, bf16[512,768]{1,0:T(8,128)(2,1)S(1)} %copy-done.12, bf16[4,2,64,768]{3,2,1,0:T(8,128)(2,1)S(1)} %bitcast.110, bf16[4,2,64,768]{3,2,1,0:T(8,128)(2,1)} %collective-permute-done.6.refs_3_.refs_2_, ...), custom_call_target="tpu_custom_call" | custom-call | flops 1 | bytes 1 | tf_op jit(solution)/shard_map/back_attn/pallas_call | solution.py:61
  296.8 3.8 collective-permute-start.39
  302.6 5.9 %third_blocks.1 = (bf16[128,2048]{1,0:T(8,128)(2,1)}, bf16[128,2048]{1,0:T(8,128)(2,1)}, bf16[128,2048]{1,0:T(8,128)(2,1)}, bf16[128,2048]{1,0:T(8,128)(2,1)}) custom-call(s32[4]{0:T(128)} %pad_add_fusion.s_ref, f32[256,2048]{1,0:T(8,128)} %copy-done.22, bf16[256,2048]{1,0:T(8,128)(2,1)} %copy-done.54, f32[256,2048]{1,0:T(8,128)} %copy-done.21, ...), custom_call_target="tpu_custom_call" | custom-call | flops 1 | bytes 1 | tf_op jit(solution)/shard_map/third_blocks/pallas_call | solution.py:61
  308.5 2.1 collective-permute-start.35
  310.6 2.7 collective-permute-start.37
  314.3 3.5 collective-permute-done.40
  319.2 2.2 collective-permute-done.41
  321.4 2.2 collective-permute-start.42
  323.7 2.0 collective-permute-done.42
  325.7 9.7 %collective-permute-done.36 = bf16[128,2048]{1,0:T(8,128)(2,1)S(1)} collective-permute-done((bf16[128,2048]{1,0:T(8,128)(2,1)}, bf16[128,2048]{1,0:T(8,128)(2,1)S(1)}, u32[]{:S(2)}, u32[]{:S(2)}) %collective-permute-start.36) | collective-permute-done | bytes 524320 | tf_op jit(solution)/shard_map/ppermute | solution.py:23
  337.7 2.0 collective-permute-start.44
  340.2 12.9 %collective-permute-done.45.refs_7_ = bf16[144,2048]{1,0:T(8,128)(2,1)S(1)} collective-permute-done((bf16[144,2048]{1,0:T(8,128)(2,1)S(1)}, bf16[144,2048]{1,0:T(8,128)(2,1)S(1)}, u32[]{:S(2)}, u32[]{:S(2)}) %collective-permute-start.45) | collective-permute-done | bytes 589856 | tf_op jit(solution)/shard_map/ppermute | solution.py:23
  353.1 12.3 %collective-permute-done.44.refs_6_ = bf16[144,2048]{1,0:T(8,128)(2,1)S(1)} collective-permute-done((bf16[144,2048]{1,0:T(8,128)(2,1)S(1)}, bf16[144,2048]{1,0:T(8,128)(2,1)S(1)}, u32[]{:S(2)}, u32[]{:S(2)}) %collective-permute-start.44) | collective-permute-done | bytes 589856 | tf_op jit(solution)/shard_map/ppermute | solution.py:23
  366.8 7.5 %leave_rows.1 = (f32[256,2048]{1,0:T(8,128)}, f32[256,2048]{1,0:T(8,128)}) custom-call(s32[4]{0:T(128)} %pad_add_fusion.s_ref, f32[256,2048]{1,0:T(8,128)} %copy-done.10, f32[256,2048]{1,0:T(8,128)} %refs_1_.7, f32[256,2048]{1,0:T(8,128)} %get-tuple-element.78.refs_2_, f32[1,2048]{1,0:T(1,128)} %bitcast.113, bf16[144,2048]{1,0:T(8,128)(2,1)} %copy-done.50, ...), custom_call_target="tpu_custom_call" | custom-call | flops 1 | bytes 1 | tf_op jit(solution)/shard_map/leave_rows/pallas_call | solution.py:61
  377.6 4.5 %reduce-scatter.2.cloned.1.call-done.refs_0_ = bf16[128,3584]{1,0:T(8,128)(2,1)} async-done(((bf16[2048,3584]{1,0:T(8,128)(2,1)}), bf16[128,3584]{1,0:T(8,128)(2,1)}) %reduce-scatter.2.cloned.1.call-update) | async-done | bytes 917520 | tf_op jit(solution)/shard_map/reduce_scatter | solution.py:979
  385.9 1.8 join_heads.1
  (278 shorter events, 88.2 us)
Async XLA Ops:
  7.2 98.0 %all-gather.3.cloned.1.call-start = ((), (), s32[]{:S(2)}) async-start(), calls=%async_computation.1 | async-start | bytes 5570560 | tf_op jit(solution)/shard_map/all_gather | solution.py:856
  10.4 2.8 collective-permute-start
  16.4 20.4 %copy-start.34 = (bf16[128,768]{1,0:T(8,128)(2,1)S(1)}, bf16[128,768]{1,0:T(8,128)(2,1)}, u32[]{:S(2)}) copy-start(bf16[128,768]{1,0:T(8,128)(2,1)} %get-tuple-element.64.refs_0_) | copy-start | bytes 589828
  16.5 149.6 %all-gather.5.cloned.1.call-start = ((), (), s32[]{:S(2)}) async-start(), calls=%async_computation.2 | async-start | bytes 6684672 | tf_op jit(solution)/shard_map/all_gather | solution.py:901
  16.5 7.7 %collective-permute-start.3 = (bf16[128,768]{1,0:T(8,128)(2,1)}, bf16[128,768]{1,0:T(8,128)(2,1)S(1)}, u32[]{:S(2)}, u32[]{:S(2)}) collective-permute-start(bf16[128,768]{1,0:T(8,128)(2,1)} %get-tuple-element.64.refs_0_), channel_id=1, source_target_pairs={{0,12},{4,0},{8,4},{12,8},{16,112},{20,116},{24,120},{28,124},{32,... | collective-permute-start | bytes 589832 | tf_op jit(solution)/shard_map/ppermute | solution.py:148
  19.2 6.6 %collective-permute-start.2 = (bf16[128,768]{1,0:T(8,128)(2,1)}, bf16[128,768]{1,0:T(8,128)(2,1)S(1)}, u32[]{:S(2)}, u32[]{:S(2)}) collective-permute-start(bf16[128,768]{1,0:T(8,128)(2,1)} %get-tuple-element.64.refs_0_), channel_id=1, source_target_pairs={{0,8},{4,12},{8,0},{12,4},{16,80},{20,84},{24,88},{28,92},{32,40},... | collective-permute-start | bytes 589832 | tf_op jit(solution)/shard_map/ppermute | solution.py:148
  19.7 8.1 %collective-permute-start.1 = (bf16[128,768]{1,0:T(8,128)(2,1)}, bf16[128,768]{1,0:T(8,128)(2,1)S(1)}, u32[]{:S(2)}, u32[]{:S(2)}) collective-permute-start(bf16[128,768]{1,0:T(8,128)(2,1)} %get-tuple-element.64.refs_0_), channel_id=1, source_target_pairs={{0,4},{4,8},{8,12},{12,0},{16,48},{20,52},{24,56},{28,60},{32,36},... | collective-permute-start | bytes 589832 | tf_op jit(solution)/shard_map/ppermute | solution.py:148
  30.9 30.8 %copy-start.27 = (s32[4]{0:T(128)S(1)}, s32[4]{0:T(128)}, u32[]{:S(2)}) copy-start(s32[4]{0:T(128)} %pad_add_fusion.s_ref) | copy-start | bytes 52
  32.1 35.3 %copy-start.4 = (bf16[256,2048]{1,0:T(8,128)(2,1)}, bf16[256,2048]{1,0:T(8,128)(2,1)S(1)}, u32[]{:S(2)}) copy-start(bf16[256,2048]{1,0:T(8,128)(2,1)S(1)} %enter_rows.1.refs_0_.refs_3_.refs_9_) | copy-start | bytes 3145732
  32.1 29.6 %collective-permute-start.4 = (bf16[256,2048]{1,0:T(8,128)(2,1)S(1)}, bf16[256,2048]{1,0:T(8,128)(2,1)S(1)}, u32[]{:S(2)}, u32[]{:S(2)}) collective-permute-start(bf16[256,2048]{1,0:T(8,128)(2,1)S(1)} %enter_rows.1.refs_0_.refs_3_.refs_9_), channel_id=1, source_target_pairs={{0,16},{16,0},{1,17},{17,1},{2,18},{18,2},{3,19},{19,3},{4,20},{20... | collective-permute-start | bytes 3145736 | tf_op jit(solution)/shard_map/ppermute | solution.py:34
  34.0 2.2 collective-permute-start.5
  37.5 29.9 %copy-start.13 = (bf16[512,768]{1,0:T(8,128)(2,1)}, bf16[512,768]{1,0:T(8,128)(2,1)S(1)}, u32[]{:S(2)}) copy-start(bf16[512,768]{1,0:T(8,128)(2,1)S(1)} %stack_kv.1) | copy-start | bytes 2359300
  37.5 12.5 %collective-permute-start.8 = (bf16[4,2,64,768]{3,2,1,0:T(8,128)(2,1)S(1)}, bf16[4,2,64,768]{3,2,1,0:T(8,128)(2,1)}, u32[]{:S(2)}, u32[]{:S(2)}) collective-permute-start(bf16[4,2,64,768]{3,2,1,0:T(8,128)(2,1)S(1)} %bitcast.106), channel_id=1, source_target_pairs={{0,96},{4,100},{8,104},{12,108},{16,28},{20,16},{24,20},{28,24},{3... | collective-permute-start | bytes 2359304 | tf_op jit(solution)/shard_map/ppermute | solution.py:148
  38.4 13.2 %collective-permute-start.7 = (bf16[4,2,64,768]{3,2,1,0:T(8,128)(2,1)S(1)}, bf16[4,2,64,768]{3,2,1,0:T(8,128)(2,1)}, u32[]{:S(2)}, u32[]{:S(2)}) collective-permute-start(bf16[4,2,64,768]{3,2,1,0:T(8,128)(2,1)S(1)} %bitcast.107), channel_id=1, source_target_pairs={{0,64},{4,68},{8,72},{12,76},{16,24},{20,28},{24,16},{28,20},{32,9... | collective-permute-start | bytes 2359304 | tf_op jit(solution)/shard_map/ppermute | solution.py:148
  38.8 22.9 %collective-permute-start.6 = (bf16[4,2,64,768]{3,2,1,0:T(8,128)(2,1)S(1)}, bf16[4,2,64,768]{3,2,1,0:T(8,128)(2,1)}, u32[]{:S(2)}, u32[]{:S(2)}) collective-permute-start(bf16[4,2,64,768]{3,2,1,0:T(8,128)(2,1)S(1)} %bitcast.108), channel_id=1, source_target_pairs={{0,32},{4,36},{8,40},{12,44},{16,20},{20,24},{24,28},{28,16},{32,6... | collective-permute-start | bytes 2359304 | tf_op jit(solution)/shard_map/ppermute | solution.py:148
  41.3 64.7 %copy-start.48 = (f32[256,128]{1,0:T(8,128)}, f32[256,128]{1,0:T(8,128)S(1)}, u32[]{:S(2)}) copy-start(f32[256,128]{1,0:T(8,128)S(1)} %get-tuple-element.136) | copy-start | bytes 393220
  67.4 32.0 %copy-start.28 = (s32[4]{0:T(128)S(1)}, s32[4]{0:T(128)}, u32[]{:S(2)}) copy-start(s32[4]{0:T(128)} %pad_add_fusion.s_ref) | copy-start | bytes 52
  68.0 31.3 %collective-permute-start.11 = (bf16[2,256,512]{2,1,0:T(8,128)(2,1)S(1)}, bf16[2,256,512]{2,1,0:T(8,128)(2,1)S(1)}, u32[]{:S(2)}, u32[]{:S(2)}) collective-permute-start(bf16[2,256,512]{2,1,0:T(8,128)(2,1)S(1)} %convolution_convert_fusion.1), channel_id=1, source_target_pairs={{0,12},{1,13},{2,14},{3,15},{16,28},{17,29},{18,30},{19,31},{32,44... | collective-permute-start | bytes 1572872 | tf_op jit(solution)/shard_map/ppermute | solution.py:28
  70.6 28.7 %collective-permute-start.10 = (bf16[2,256,512]{2,1,0:T(8,128)(2,1)S(1)}, bf16[2,256,512]{2,1,0:T(8,128)(2,1)S(1)}, u32[]{:S(2)}, u32[]{:S(2)}) collective-permute-start(bf16[2,256,512]{2,1,0:T(8,128)(2,1)S(1)} %convolution_convert_fusion.1), channel_id=1, source_target_pairs={{0,8},{4,12},{1,9},{5,13},{2,10},{6,14},{3,11},{7,15},{16,24},{20,... | collective-permute-start | bytes 1572872 | tf_op jit(solution)/shard_map/ppermute | solution.py:28
  71.9 27.4 %collective-permute-start.9 = (bf16[2,256,512]{2,1,0:T(8,128)(2,1)S(1)}, bf16[2,256,512]{2,1,0:T(8,128)(2,1)S(1)}, u32[]{:S(2)}, u32[]{:S(2)}) collective-permute-start(bf16[2,256,512]{2,1,0:T(8,128)(2,1)S(1)} %convolution_convert_fusion.1), channel_id=1, source_target_pairs={{0,4},{4,8},{8,12},{1,5},{5,9},{9,13},{2,6},{6,10},{10,14},{3,7},{... | collective-permute-start | bytes 1572872 | tf_op jit(solution)/shard_map/ppermute | solution.py:28
  76.9 6.5 %collective-permute-start.21 = (bf16[64,1536]{1,0:T(8,128)(2,1)}, bf16[64,1536]{1,0:T(8,128)(2,1)S(1)}, u32[]{:S(2)}, u32[]{:S(2)}) collective-permute-start(bf16[64,1536]{1,0:T(8,128)(2,1)} %get-tuple-element.71), channel_id=1, source_target_pairs={{0,16},{16,0},{1,17},{17,1},{2,18},{18,2},{3,19},{19,3},{4,20},{20... | collective-permute-start | bytes 589832 | tf_op jit(solution)/shard_map/ppermute | solution.py:34
  101.9 280.3 %reduce-scatter.2.cloned.1.call-start = ((), (), s32[]{:S(2)}) async-start(), calls=%async_computation.3 | async-start | bytes 15597568 | tf_op jit(solution)/shard_map/reduce_scatter | solution.py:979
  102.1 17.4 %copy-start.69 = (pred[256,256]{1,0:T(8,128)(4,1)}, pred[256,256]{1,0:T(8,128)(4,1)S(1)}, u32[]{:S(2)}) copy-start(pred[256,256]{1,0:T(8,128)(4,1)S(1)} %subtract_compare_fusion) | copy-start | bytes 196612
  102.3 17.2 %copy-start.56 = (f32[256,256]{1,0:T(8,128)}, f32[256,256]{1,0:T(8,128)S(1)}, u32[]{:S(2)}) copy-start(f32[256,256]{1,0:T(8,128)S(1)} %fusion.13) | copy-start | bytes 786436
  119.5 4.7 %collective-permute-start.12 = (bf16[256,2048]{1,0:T(8,128)(2,1)}, bf16[256,2048]{1,0:T(8,128)(2,1)S(1)}, u32[]{:S(2)}, u32[]{:S(2)}) collective-permute-start(bf16[256,2048]{1,0:T(8,128)(2,1)} %get-tuple-element.67), channel_id=1, source_target_pairs={{0,16},{16,0},{1,17},{17,1},{2,18},{18,2},{3,19},{19,3},{4,20},{20... | collective-permute-start | bytes 3145736 | tf_op jit(solution)/shard_map/ppermute | solution.py:34
  124.2 24.0 %copy-start.2 = (bf16[256,2048]{1,0:T(8,128)(2,1)S(1)}, bf16[256,2048]{1,0:T(8,128)(2,1)}, u32[]{:S(2)}) copy-start(bf16[256,2048]{1,0:T(8,128)(2,1)} %copy-done.1) | copy-start | bytes 3145732
  124.2 24.0 %copy-start.11 = (f32[256,2048]{1,0:T(8,128)S(1)}, f32[256,2048]{1,0:T(8,128)}, u32[]{:S(2)}) copy-start(f32[256,2048]{1,0:T(8,128)} %refs_1_.6) | copy-start | bytes 6291460
  124.2 24.0 %copy-start.29 = (s32[4]{0:T(128)S(1)}, s32[4]{0:T(128)}, u32[]{:S(2)}) copy-start(s32[4]{0:T(128)} %pad_add_fusion.s_ref) | copy-start | bytes 52
  126.0 9.8 %collective-permute-start.13 = (bf16[64,2048]{1,0:T(8,128)(2,1)S(1)}, bf16[64,2048]{1,0:T(8,128)(2,1)S(1)}, u32[]{:S(2)}, u32[]{:S(2)}) collective-permute-start(bf16[64,2048]{1,0:T(8,128)(2,1)S(1)} %get-tuple-element.120), channel_id=1, source_target_pairs={{0,2},{1,3},{2,0},{3,1},{4,6},{5,7},{6,4},{7,5},{8,10},{9,11},{10,... | collective-permute-start | bytes 786440 | tf_op jit(solution)/shard_map/ppermute | solution.py:23
  129.4 12.2 %collective-permute-start.15 = (bf16[64,2048]{1,0:T(8,128)(2,1)S(1)}, bf16[64,2048]{1,0:T(8,128)(2,1)S(1)}, u32[]{:S(2)}, u32[]{:S(2)}) collective-permute-start(bf16[64,2048]{1,0:T(8,128)(2,1)S(1)} %get-tuple-element.121), channel_id=1, source_target_pairs={{0,3},{1,0},{2,1},{3,2},{4,7},{5,4},{6,5},{7,6},{8,11},{9,8},{10,9... | collective-permute-start | bytes 786440 | tf_op jit(solution)/shard_map/ppermute | solution.py:23
  129.9 11.9 %collective-permute-start.14 = (bf16[64,2048]{1,0:T(8,128)(2,1)S(1)}, bf16[64,2048]{1,0:T(8,128)(2,1)S(1)}, u32[]{:S(2)}, u32[]{:S(2)}) collective-permute-start(bf16[64,2048]{1,0:T(8,128)(2,1)S(1)} %get-tuple-element.122), channel_id=1, source_target_pairs={{0,1},{1,2},{2,3},{3,0},{4,5},{5,6},{6,7},{7,4},{8,9},{9,10},{10,1... | collective-permute-start | bytes 786440 | tf_op jit(solution)/shard_map/ppermute | solution.py:23
  143.1 8.6 %collective-permute-start.18 = (bf16[64,2048]{1,0:T(8,128)(2,1)S(1)}, bf16[64,2048]{1,0:T(8,128)(2,1)S(1)}, u32[]{:S(2)}, u32[]{:S(2)}) collective-permute-start(bf16[64,2048]{1,0:T(8,128)(2,1)S(1)} %add_convert_fusion.8.refs_2_), channel_id=1, source_target_pairs={{0,1},{1,2},{2,3},{3,0},{4,5},{5,6},{6,7},{7,4},{8,9},{9,10},{10,1... | collective-permute-start | bytes 786440 | tf_op jit(solution)/shard_map/ppermute | solution.py:23
  144.3 14.5 %collective-permute-start.17 = (bf16[64,2048]{1,0:T(8,128)(2,1)S(1)}, bf16[64,2048]{1,0:T(8,128)(2,1)S(1)}, u32[]{:S(2)}, u32[]{:S(2)}) collective-permute-start(bf16[64,2048]{1,0:T(8,128)(2,1)S(1)} %add_convert_fusion.8.refs_2_), channel_id=1, source_target_pairs={{0,2},{1,3},{2,0},{3,1},{4,6},{5,7},{6,4},{7,5},{8,10},{9,11},{10,... | collective-permute-start | bytes 786440 | tf_op jit(solution)/shard_map/ppermute | solution.py:23
  147.1 11.7 %collective-permute-start.16 = (bf16[64,2048]{1,0:T(8,128)(2,1)S(1)}, bf16[64,2048]{1,0:T(8,128)(2,1)S(1)}, u32[]{:S(2)}, u32[]{:S(2)}) collective-permute-start(bf16[64,2048]{1,0:T(8,128)(2,1)S(1)} %add_convert_fusion.8.refs_2_), channel_id=1, source_target_pairs={{0,3},{1,0},{2,1},{3,2},{4,7},{5,4},{6,5},{7,6},{8,11},{9,8},{10,9... | collective-permute-start | bytes 786440 | tf_op jit(solution)/shard_map/ppermute | solution.py:23
  149.0 13.9 %collective-permute-start.20 = (bf16[256,2048]{1,0:T(8,128)(2,1)S(1)}, bf16[256,2048]{1,0:T(8,128)(2,1)S(1)}, u32[]{:S(2)}, u32[]{:S(2)}) collective-permute-start(bf16[256,2048]{1,0:T(8,128)(2,1)S(1)} %low_rows.1.refs_2_.refs_0_), channel_id=1, source_target_pairs={{0,16},{16,0},{1,17},{17,1},{2,18},{18,2},{3,19},{19,3},{4,20},{20... | collective-permute-start | bytes 3145736 | tf_op jit(solution)/shard_map/ppermute | solution.py:34
  161.6 3.6 collective-permute-start.19
  180.5 3.3 collective-permute-start.22
  185.3 11.3 %collective-permute-start.23 = (bf16[64,2048]{1,0:T(8,128)(2,1)S(1)}, bf16[64,2048]{1,0:T(8,128)(2,1)S(1)}, u32[]{:S(2)}, u32[]{:S(2)}) collective-permute-start(bf16[64,2048]{1,0:T(8,128)(2,1)S(1)} %get-tuple-element.117), channel_id=1, source_target_pairs={{0,2},{1,3},{2,0},{3,1},{4,6},{5,7},{6,4},{7,5},{8,10},{9,11},{10,... | collective-permute-start | bytes 786440 | tf_op jit(solution)/shard_map/ppermute | solution.py:23
  188.3 12.1 %collective-permute-start.25 = (bf16[64,2048]{1,0:T(8,128)(2,1)S(1)}, bf16[64,2048]{1,0:T(8,128)(2,1)S(1)}, u32[]{:S(2)}, u32[]{:S(2)}) collective-permute-start(bf16[64,2048]{1,0:T(8,128)(2,1)S(1)} %get-tuple-element.118), channel_id=1, source_target_pairs={{0,3},{1,0},{2,1},{3,2},{4,7},{5,4},{6,5},{7,6},{8,11},{9,8},{10,9... | collective-permute-start | bytes 786440 | tf_op jit(solution)/shard_map/ppermute | solution.py:23
  189.1 11.7 %collective-permute-start.24 = (bf16[64,2048]{1,0:T(8,128)(2,1)S(1)}, bf16[64,2048]{1,0:T(8,128)(2,1)S(1)}, u32[]{:S(2)}, u32[]{:S(2)}) collective-permute-start(bf16[64,2048]{1,0:T(8,128)(2,1)S(1)} %get-tuple-element.119), channel_id=1, source_target_pairs={{0,1},{1,2},{2,3},{3,0},{4,5},{5,6},{6,7},{7,4},{8,9},{9,10},{10,1... | collective-permute-start | bytes 786440 | tf_op jit(solution)/shard_map/ppermute | solution.py:23
  189.7 17.9 %copy-start.20 = (bf16[512,512]{1,0:T(8,128)(2,1)S(1)}, bf16[512,512]{1,0:T(8,128)(2,1)}, u32[]{:S(2)}) copy-start(bf16[512,512]{1,0:T(8,128)(2,1)} %get-tuple-element.76.refs_0_.refs_2_) | copy-start | bytes 1572868
  189.7 17.9 %copy-start.30 = (s32[4]{0:T(128)S(1)}, s32[4]{0:T(128)}, u32[]{:S(2)}) copy-start(s32[4]{0:T(128)} %pad_add_fusion.s_ref) | copy-start | bytes 52
  202.7 13.8 %collective-permute-start.28 = (bf16[64,2048]{1,0:T(8,128)(2,1)}, bf16[64,2048]{1,0:T(8,128)(2,1)S(1)}, u32[]{:S(2)}, u32[]{:S(2)}) collective-permute-start(bf16[64,2048]{1,0:T(8,128)(2,1)} %tie.4.refs_2_.refs_3_), channel_id=1, source_target_pairs={{0,1},{1,2},{2,3},{3,0},{4,5},{5,6},{6,7},{7,4},{8,9},{9,10},{10,1... | collective-permute-start | bytes 786440 | tf_op jit(solution)/shard_map/ppermute | solution.py:23
  204.0 14.3 %collective-permute-start.27 = (bf16[64,2048]{1,0:T(8,128)(2,1)}, bf16[64,2048]{1,0:T(8,128)(2,1)S(1)}, u32[]{:S(2)}, u32[]{:S(2)}) collective-permute-start(bf16[64,2048]{1,0:T(8,128)(2,1)} %tie.4.refs_2_.refs_3_), channel_id=1, source_target_pairs={{0,2},{1,3},{2,0},{3,1},{4,6},{5,7},{6,4},{7,5},{8,10},{9,11},{10,... | collective-permute-start | bytes 786440 | tf_op jit(solution)/shard_map/ppermute | solution.py:23
  206.5 11.7 %collective-permute-start.26 = (bf16[64,2048]{1,0:T(8,128)(2,1)}, bf16[64,2048]{1,0:T(8,128)(2,1)S(1)}, u32[]{:S(2)}, u32[]{:S(2)}) collective-permute-start(bf16[64,2048]{1,0:T(8,128)(2,1)} %tie.4.refs_2_.refs_3_), channel_id=1, source_target_pairs={{0,3},{1,0},{2,1},{3,2},{4,7},{5,4},{6,5},{7,6},{8,11},{9,8},{10,9... | collective-permute-start | bytes 786440 | tf_op jit(solution)/shard_map/ppermute | solution.py:23
  225.1 3.8 collective-permute-start.29
  240.7 27.6 %collective-permute-start.32 = (bf16[2,256,512]{2,1,0:T(8,128)(2,1)S(1)}, bf16[2,256,512]{2,1,0:T(8,128)(2,1)}, u32[]{:S(2)}, u32[]{:S(2)}) collective-permute-start(bf16[2,256,512]{2,1,0:T(8,128)(2,1)S(1)} %convolution_convert_fusion.refs_7_), channel_id=1, source_target_pairs={{12,0},{13,1},{14,2},{15,3},{28,16},{29,17},{30,18},{31,19},{44,32... | collective-permute-start | bytes 1572872 | tf_op jit(solution)/shard_map/ppermute | solution.py:28
  242.0 26.3 %collective-permute-start.31 = (bf16[2,256,512]{2,1,0:T(8,128)(2,1)S(1)}, bf16[2,256,512]{2,1,0:T(8,128)(2,1)}, u32[]{:S(2)}, u32[]{:S(2)}) collective-permute-start(bf16[2,256,512]{2,1,0:T(8,128)(2,1)S(1)} %convolution_convert_fusion.refs_7_), channel_id=1, source_target_pairs={{8,0},{12,4},{9,1},{13,5},{10,2},{14,6},{11,3},{15,7},{24,16},{28,... | collective-permute-start | bytes 1572872 | tf_op jit(solution)/shard_map/ppermute | solution.py:28
  243.3 23.2 %collective-permute-start.30 = (bf16[2,256,512]{2,1,0:T(8,128)(2,1)S(1)}, bf16[2,256,512]{2,1,0:T(8,128)(2,1)S(1)}, u32[]{:S(2)}, u32[]{:S(2)}) collective-permute-start(bf16[2,256,512]{2,1,0:T(8,128)(2,1)S(1)} %convolution_convert_fusion.refs_7_), channel_id=1, source_target_pairs={{4,0},{8,4},{12,8},{5,1},{9,5},{13,9},{6,2},{10,6},{14,10},{7,3},{... | collective-permute-start | bytes 1572872 | tf_op jit(solution)/shard_map/ppermute | solution.py:28
  278.0 22.7 %collective-permute-start.34 = (bf16[256,2048]{1,0:T(8,128)(2,1)}, bf16[256,2048]{1,0:T(8,128)(2,1)S(1)}, u32[]{:S(2)}, u32[]{:S(2)}) collective-permute-start(bf16[256,2048]{1,0:T(8,128)(2,1)} %tie.6), channel_id=1, source_target_pairs={{0,16},{16,0},{1,17},{17,1},{2,18},{18,2},{3,19},{19,3},{4,20},{20... | collective-permute-start | bytes 3145736 | tf_op jit(solution)/shard_map/ppermute | solution.py:34
  293.2 7.4 %collective-permute-start.33 = (bf16[256,2048]{1,0:T(8,128)(2,1)S(1)}, bf16[256,2048]{1,0:T(8,128)(2,1)S(1)}, u32[]{:S(2)}, u32[]{:S(2)}) collective-permute-start(bf16[256,2048]{1,0:T(8,128)(2,1)S(1)} %get-tuple-element.93), channel_id=1, source_target_pairs={{0,16},{16,0},{1,17},{17,1},{2,18},{18,2},{3,19},{19,3},{4,20},{20... | collective-permute-start | bytes 3145736 | tf_op jit(solution)/shard_map/ppermute | solution.py:34
  295.3 1.4 collective-permute-start.38
  296.8 16.5 %collective-permute-start.39 = (f32[2,2048]{1,0:T(2,128)S(1)}, f32[2,2048]{1,0:T(2,128)S(1)}, u32[]{:S(2)}, u32[]{:S(2)}) collective-permute-start(f32[2,2048]{1,0:T(2,128)S(1)} %fusion.30), channel_id=1, source_target_pairs={{0,4},{4,0},{8,12},{12,8},{1,5},{5,1},{9,13},{13,9},{2,6},{6,2},{1... | collective-permute-start | bytes 49160 | tf_op jit(solution)/shard_map/ppermute | solution.py:998
  308.5 17.2 %collective-permute-start.35 = (bf16[128,2048]{1,0:T(8,128)(2,1)}, bf16[128,2048]{1,0:T(8,128)(2,1)S(1)}, u32[]{:S(2)}, u32[]{:S(2)}) collective-permute-start(bf16[128,2048]{1,0:T(8,128)(2,1)} %get-tuple-element.96), channel_id=1, source_target_pairs={{0,2},{1,3},{2,0},{3,1},{4,6},{5,7},{6,4},{7,5},{8,10},{9,11},{10,... | collective-permute-start | bytes 1572872 | tf_op jit(solution)/shard_map/ppermute | solution.py:23
  310.6 24.8 %collective-permute-start.36 = (bf16[128,2048]{1,0:T(8,128)(2,1)}, bf16[128,2048]{1,0:T(8,128)(2,1)S(1)}, u32[]{:S(2)}, u32[]{:S(2)}) collective-permute-start(bf16[128,2048]{1,0:T(8,128)(2,1)} %get-tuple-element.97), channel_id=1, source_target_pairs={{0,1},{1,2},{2,3},{3,0},{4,5},{5,6},{6,7},{7,4},{8,9},{9,10},{10,1... | collective-permute-start | bytes 1572872 | tf_op jit(solution)/shard_map/ppermute | solution.py:23
  310.6 24.8 %collective-permute-start.37 = (bf16[128,2048]{1,0:T(8,128)(2,1)}, bf16[128,2048]{1,0:T(8,128)(2,1)S(1)}, u32[]{:S(2)}, u32[]{:S(2)}) collective-permute-start(bf16[128,2048]{1,0:T(8,128)(2,1)} %get-tuple-element.98), channel_id=1, source_target_pairs={{0,3},{1,0},{2,1},{3,2},{4,7},{5,4},{6,5},{7,6},{8,11},{9,8},{10,9... | collective-permute-start | bytes 1572872 | tf_op jit(solution)/shard_map/ppermute | solution.py:23
  313.3 4.4 %collective-permute-start.40 = (f32[2,2048]{1,0:T(2,128)S(1)}, f32[2,2048]{1,0:T(2,128)S(1)}, u32[]{:S(2)}, u32[]{:S(2)}) collective-permute-start(f32[2,2048]{1,0:T(2,128)S(1)} %fusion.51), channel_id=1, source_target_pairs={{0,12},{4,8},{8,4},{12,0},{1,13},{5,9},{9,5},{13,1},{2,14},{6,10},... | collective-permute-start | bytes 49160 | tf_op jit(solution)/shard_map/ppermute | solution.py:998
  317.8 3.6 collective-permute-start.41
  321.4 4.3 %collective-permute-start.42 = (f32[2,2048]{1,0:T(2,128)S(1)}, f32[2,2048]{1,0:T(2,128)S(1)}, u32[]{:S(2)}, u32[]{:S(2)}) collective-permute-start(f32[2,2048]{1,0:T(2,128)S(1)} %add.248), channel_id=1, source_target_pairs={{0,96},{32,64},{64,32},{96,0},{1,97},{33,65},{65,33},{97,1},{2,98}... | collective-permute-start | bytes 49160 | tf_op jit(solution)/shard_map/ppermute | solution.py:998
  337.0 28.9 %copy-start.50 = (bf16[144,2048]{1,0:T(8,128)(2,1)}, bf16[144,2048]{1,0:T(8,128)(2,1)S(1)}, u32[]{:S(2)}) copy-start(bf16[144,2048]{1,0:T(8,128)(2,1)S(1)} %maximum_maximum_fusion.refs_4_) | copy-start | bytes 1769476
  337.0 16.1 %collective-permute-start.45 = (bf16[144,2048]{1,0:T(8,128)(2,1)S(1)}, bf16[144,2048]{1,0:T(8,128)(2,1)S(1)}, u32[]{:S(2)}, u32[]{:S(2)}) collective-permute-start(bf16[144,2048]{1,0:T(8,128)(2,1)S(1)} %maximum_maximum_fusion.refs_4_), channel_id=1, source_target_pairs={{0,1},{1,2},{2,3},{3,0},{4,5},{5,6},{6,7},{7,4},{8,9},{9,10},{10,1... | collective-permute-start | bytes 1769480 | tf_op jit(solution)/shard_map/ppermute | solution.py:23
  337.7 27.7 %collective-permute-start.44 = (bf16[144,2048]{1,0:T(8,128)(2,1)S(1)}, bf16[144,2048]{1,0:T(8,128)(2,1)S(1)}, u32[]{:S(2)}, u32[]{:S(2)}) collective-permute-start(bf16[144,2048]{1,0:T(8,128)(2,1)S(1)} %maximum_maximum_fusion.refs_4_), channel_id=1, source_target_pairs={{0,2},{1,3},{2,0},{3,1},{4,6},{5,7},{6,4},{7,5},{8,10},{9,11},{10,... | collective-permute-start | bytes 1769480 | tf_op jit(solution)/shard_map/ppermute | solution.py:23
  339.8 26.2 %collective-permute-start.43 = (bf16[144,2048]{1,0:T(8,128)(2,1)S(1)}, bf16[144,2048]{1,0:T(8,128)(2,1)S(1)}, u32[]{:S(2)}, u32[]{:S(2)}) collective-permute-start(bf16[144,2048]{1,0:T(8,128)(2,1)S(1)} %maximum_maximum_fusion.refs_4_), channel_id=1, source_target_pairs={{0,3},{1,0},{2,1},{3,2},{4,7},{5,4},{6,5},{7,6},{8,11},{9,8},{10,9... | collective-permute-start | bytes 1769480 | tf_op jit(solution)/shard_map/ppermute | solution.py:23
  383.4 2.5 collective-permute-start.46
  (60 other events, 215.2 us)
Sparse Core Ops, SparseCore 0:
  16.6 78.9 all-gather.2
  102.0 64.0 all-gather.4
  278.0 104.0 reduce-scatter.1
where the time goes:
time: 396 us; the launch traced here: 394 us
  waiting for transfers between devices  135 us (34%)
  Pallas kernels  114 us (29%)
  starting transfers between devices  71 us (18%)
  local copies, waits for them, and re-layouts  30.1 us (8%)
  other arithmetic  23 us (6%)
  between operations  15.9 us (4%)
  matrix products  4.85 us (1%)
    pallas_call x23, Pallas kernels, call(): pl.pallas_call(kernel, out_shape=shapes, grid_spec=pltpu.PrefetchScalarGr...  114 us
    ppermute x18, waiting for transfers between devices, shift(): return lax.ppermute(value, axis, [(i, (i + offset) % n) for i in range(n)])  60.9 us
    ppermute x6, waiting for transfers between devices, hop(): return lax.ppermute(value, ('x', 'core', 'ctx'), pairs)  27.9 us
    ppermute x18, starting transfers between devices, shift(): return lax.ppermute(value, axis, [(i, (i + offset) % n) for i in range(n)])  27.3 us
    unnamed x150, local copies, waits for them, and re-layouts  25.9 us
    ppermute x12, starting transfers between devices, swap(): return lax.ppermute(value, 'core', [(0, 1), (1, 0)])  18.9 us
    ppermute x6, waiting for transfers between devices, shift_open(): lax.ppermute(value, axis, [(i, i + offset) for i in range(n) if 0 <= i +...  16.9 us
    ppermute x12, waiting for transfers between devices, swap(): return lax.ppermute(value, 'core', [(0, 1), (1, 0)])  15.2 us
  transfers between devices with their start and end apart: 50, of which 34 were waited for; matrix products, arithmetic and copies ran while one was open for 5% of the time, Pallas kernels for 19%

commit v1 on v0

--- a/solution.py
+++ b/solution.py
@@ -493,6 +493,140 @@
     )
 
 
+def back_gate(g_pair, weight, gate_pre, retained, query, enter, scalars):
+    rows = g_pair[0].shape[0]
+
+    def body(
+        s_ref, a_ref, b_ref, w_ref, gate_ref, kept_ref, q_ref, e_ref, dgate_ref, low_ref, state_ref,
+        sums
+    ):
+        step = pl.program_id(0)
+        left = jnp.concatenate((a_ref[...], b_ref[...]), axis=0)
+        part = jnp.dot(left, load_slab(s_ref, (w_ref,), None), preferred_element_type=F32)
+
+        @pl.when(step == 0)
+        def _():
+            sums[...] = part
+
+        @pl.when(step > 0)
+        def _():
+            sums[...] += part
+
+        @pl.when(step == 3)
+        def _():
+            def chunk(k, carry):
+                span = pl.ds(pl.multiple_of(k * 64, 64), 64)
+                gate, value, grad = gate_ref[span, :], kept_ref[span, :], sums[span, :]
+                value = value - jnp.mean(value, axis=-1, keepdims=True)
+                scale = lax.rsqrt(jnp.mean(value * value, axis=-1, keepdims=True) + 1.0 * DK)
+                normed = value * scale
+                open_part = jax.nn.sigmoid(gate)
+                slope = open_part * (1.0 + gate * (1.0 - open_part))
+                dgate_ref[span, :] = (grad * normed * slope).astype(BF)
+                grad = grad * gate * open_part
+                grad = grad - jnp.mean(grad, axis=-1, keepdims=True) - normed * jnp.mean(
+                    grad * normed, axis=-1, keepdims=True
+                )
+                low_ref[span, :] = (grad * scale).astype(BF)
+                return carry
+
+            lax.fori_loop(0, 2 * rows // 64, chunk, 0)
+            for g in (0, 1):
+                span = slice(g * rows, (g + 1) * rows)
+                entered = (q_ref[span].astype(F32) * e_ref[span]).astype(BF)
+                state_ref[g] = lax.dot_general(
+                    entered,
+                    low_ref[span],
+                    (((0,), (0,)), ((), ())),
+                    preferred_element_type=F32,
+                ).astype(BF)
+
+    cols = pl.BlockSpec((rows, SLAB), lambda i, s: (0, i))
+    operands = (*g_pair, weight, gate_pre, retained, query, enter)
+    shapes = (
+        sds((2 * rows, DV), BF),
+        sds((2 * rows, DV), BF),
+        sds((2, DK, DV), BF),
+    )
+    return call(
+        body,
+        (4,),
+        [cols, cols, pl.BlockSpec((1, 4, 2, 64, DV), lambda i, s: (i, 0, 0, 0, 1))]
+        + [whole(o) for o in operands[3:]],
+        tuple(whole(s) for s in shapes),
+        shapes,
+        scalars,
+        operands,
+        "back_gate",
+        scratch=[pltpu.VMEM((2 * rows, DV), F32)],
+        stream=True,
+    )
+
+
+def weight_last(into, pair, came, fade, value, key_out, leave, grad_value, grad_key, cosine, sine,
+                scalars):
+    rows = pair[0].shape[0]
+
+    def body(
+        s_ref, a_ref, b_ref, near_ref, mid_ref, far_ref, f_ref, v_ref, k_ref, l_ref, gv_ref, gk_ref,
+        cos_ref, sin_ref, into_ref, out_ref, mark_ref, grad_ref
+    ):
+        @pl.when(pl.program_id(0) == 0)
+        def _():
+            fade = f_ref[...]
+            for g in (0, 1):
+                span = slice(g * rows, (g + 1) * rows)
+                state = near_ref[g].astype(F32) + fade * (
+                    mid_ref[g].astype(F32) + fade * far_ref[g].astype(F32)
+                )
+                state = state.astype(BF)
+                grad_ref[span, :DV] = (
+                    gv_ref[g] + jnp.dot(k_ref[g], state, preferred_element_type=F32)
+                ).astype(BF)
+                grad_key = gk_ref[g] + l_ref[span] * lax.dot_general(
+                    v_ref[g], state, (((1,), (1,)), ((), ())), preferred_element_type=F32
+                )
+                grad_ref[span, DV:] = rotate(grad_key, cos_ref[span], -sin_ref[span]).astype(BF)
+
+        out = lax.dot_general(
+            jnp.concatenate((a_ref[...], b_ref[...]), axis=0),
+            grad_ref[...],
+            (((0,), (0,)), ((), ())),
+            preferred_element_type=F32,
+        ).astype(BF)
+        for c in (0, 1):
+            for y in range(4):
+                first = (c * 4 + y) * 64
+                out_ref[0, y, jnp.bitwise_xor(c, s_ref[0])] = out[first : first + 64]
+        mark_ref[...] = jnp.zeros_like(mark_ref)
+
+    cols = pl.BlockSpec((rows, SLAB), lambda i, s: (0, i))
+    operands = (*pair, *came, fade, value, key_out, leave, grad_value, grad_key, cosine, sine)
+    shapes = (
+        sds(into.shape, BF),
+        sds((8, 128), F32),
+        sds((2 * rows, DV + DK), BF),
+    )
+    return call(
+        body,
+        (4,),
+        [cols, cols]
+        + [whole(o) for o in operands[2:]]
+        + [pl.BlockSpec(memory_space=pl.ANY)],
+        (
+            pl.BlockSpec((1, 4, 2, 64, DV + DK), lambda i, s: (i, 0, 0, 0, 0)),
+            whole(shapes[1]),
+            whole(shapes[2]),
+        ),
+        shapes,
+        scalars,
+        (*operands, into),
+        "weight_last",
+        stream=True,
+        aliases={1 + len(operands): 0},
+    )
+
+
 def mm_weight_into(into, pairs, start, total, scalars, name, deps=()):
     widths = [grad.shape[1] for _, grad in pairs]
     rows = pairs[0][0][0].shape[0]
@@ -885,14 +1019,19 @@
     cosine = jnp.tile(jnp.cos(angles), (2, 1))
     sine = jnp.tile(jnp.sin(angles), (2, 1))
 
-    def carry(came):
-        near, mid, far = [part.astype(F32) for part in came]
-        return near + fade * (mid + fade * far)
-
     def spread_state(low, way):
         return [shift_open(low, "ctx", way * o) for o in (1, 2, 3)]
 
-    projected = mm_in(*x_first, [(w_kv, 0, 768)], scalars, "project_kv")
+    enter_rows_in = enter.reshape(2 * rows, 1)
+    leave_rows_out = jnp.tile(leave.reshape(rows, 1), (2, 1))
+    fade_in = fade.reshape(1, 1)
+    projected = mm_in(
+        *x_first,
+        [(w_kv, 0, 768)],
+        scalars,
+        "project_kv",
+        deps=(mask, enter_rows_in, leave_rows_out, fade_in, cosine, sine),
+    )
     key = rotate(projected[:, DV:], cosine, sine).astype(BF).reshape(2, rows, DK)
     value = projected[:, :DV].astype(BF).reshape(2, rows, DV)
     key_out = (key.astype(F32) * leave).astype(BF)
@@ -910,15 +1049,14 @@
         key,
         value,
         came,
-        fade.reshape(1, 1),
+        fade_in,
         mask,
-        enter.reshape(2 * rows, 1),
+        enter_rows_in,
         cosine,
         sine,
         scalars,
     )
     query = query.reshape(2, rows, DK)
-    _, gate_back = jax.vjp(gate_norm, gate_pre, retained)
     parts = tp_total(chip_blocks(own, swap(other)))
     hidden_state, normed_second = second_norm(tokens, parts, gain_second, scalars)
     x_second = (normed_second, swap(normed_second))
@@ -940,17 +1078,15 @@
         deps=(down[1],),
     )
     g_state = (grad_state_low, swap(grad_state_low))
-    grad_mixed = mm_in(*g_state, [(w_goq, DV, DV)], scalars, "back_out", stream=True)
-    grad_gate, grad_retained = gate_back(grad_mixed)
-    grad_low = grad_retained.reshape(2, rows, DV).astype(BF)
-    query_in = (query.astype(F32) * enter).astype(BF)
-    back_out = ein("gid,gie->gde", query_in, grad_low).astype(BF)
+    grad_gate, grad_low, back_out = back_gate(
+        g_state, w_goq, gate_pre, retained, query.reshape(2 * rows, DK), enter_rows_in, scalars
+    )
+    grad_low = grad_low.reshape(2, rows, DV)
     came = spread_state(back_out, -1)
     grad_scores = (ein("gie,gje->gij", grad_low, value) * mask).astype(BF)
     grad_query = ein("gij,gjd->gid", grad_scores, key) + enter * ein("gie,gde->gid", grad_low, state_in)
     grad_key = ein("gij,gid->gjd", grad_scores, query)
     grad_value = ein("gij,gie->gje", weighted, grad_low)
-    grad_gate = grad_gate.astype(BF)
     grad_query = rotate(grad_query.reshape(2 * rows, DK), cosine, -sine).astype(BF)
     grads, mark = mm_weight_into(
         grads,
@@ -968,14 +1104,20 @@
         grads, ((x_first, grad_query),), 768, 3584, scalars, "weight_query"
     )
     came[0] = tie((came[0],), (mark, grad_key, grad_value))[0]
-    state_back = carry(came).astype(BF)
-    grad_key += leave * ein("gje,gde->gjd", value, state_back)
-    grad_value += ein("gjd,gde->gje", key_out, state_back)
-    grad_key = rotate(grad_key.reshape(2 * rows, DK), cosine, -sine)
-    grad_vk = jnp.concatenate(
-        (grad_value.reshape(2 * rows, DV).astype(BF), grad_key.astype(BF)), axis=1
-    )
-    grads, mark = mm_weight_into(grads, ((x_first, grad_vk),), 0, 3584, scalars, "weight_vk")
+    grads, mark, grad_vk = weight_last(
+        grads,
+        x_first,
+        came,
+        fade_in,
+        value,
+        key_out,
+        leave_rows_out,
+        grad_value,
+        grad_key,
+        cosine,
+        sine,
+        scalars,
+    )
     block = lax.psum_scatter(grads.reshape(2048, -1), XY, scatter_dimension=0, tiled=True)
     own, other, gain_first_part = mm_back(
         [(grad_vk, w_kv, 0), (grad_gate, w_goq, 0), (grad_query, w_goq, 1024)],

time: 396 us -> 413 us (1.043)
  waiting for transfers between devices: 135 us -> 153 us
  starting transfers between devices: 71 us -> 63.7 us
  Pallas kernels: 114 us -> 120 us
  local copies, waits for them, and re-layouts: 30.1 us -> 34.3 us
    ppermute x18, waiting for transfers between devices: 60.9 us -> 71.2 us  [shift(): return lax.ppermute(value, axis, [(i, (i + offset) % n) for i in range(n)])]
    ppermute x18, starting transfers between devices: 27.3 us -> 18.9 us  [shift(): return lax.ppermute(value, axis, [(i, (i + offset) % n) for i in range(n)])]
    ppermute x12, starting transfers between devices: 18.9 us -> 11.4 us  [swap(): return lax.ppermute(value, 'core', [(0, 1), (1, 0)])]
    ppermute x6, waiting for transfers between devices: 27.9 us -> 33.7 us  [hop(): return lax.ppermute(value, ('x', 'core', 'ctx'), pairs)]
    pallas_call x23, Pallas kernels: 114 us -> 120 us  [call(): pl.pallas_call(kernel, out_shape=shapes, grid_spec=pltpu.PrefetchScalarGr...]
    all_gather x1, waiting for transfers between devices: 0.83 us -> 5.19 us  [per_device(): lax.all_gather(stack_blocks((mine, came_mlp), 0, 1536, scalars, 'stack_ml...]
    unnamed x150 -> x157, local copies, waits for them, and re-layouts: 25.9 us -> 29.8 us
  transfers between devices with their start and end apart: 50 -> 50, of which waited for: 34 -> 34; matrix products, arithmetic and copies ran while one was open for 5% -> 6% of each run, Pallas kernels for 19% -> 18%
where the time goes in v1:
time: 413 us; the launch traced here: 411 us
  waiting for transfers between devices  153 us (37%)
  Pallas kernels  120 us (29%)
  starting transfers between devices  63.7 us (15%)
  local copies, waits for them, and re-layouts  34.3 us (8%)
  other arithmetic  19.4 us (5%)
  between operations  15.9 us (4%)
  matrix products  5.53 us (1%)
    pallas_call x23, Pallas kernels, call(): pl.pallas_call(kernel, out_shape=shapes, grid_spec=pltpu.PrefetchScalarGr...  120 us
    ppermute x18, waiting for transfers between devices, shift(): return lax.ppermute(value, axis, [(i, (i + offset) % n) for i in range(n)])  71.2 us
    ppermute x6, waiting for transfers between devices, hop(): return lax.ppermute(value, ('x', 'core', 'ctx'), pairs)  33.7 us
    unnamed x157, local copies, waits for them, and re-layouts  29.8 us
    ppermute x18, starting transfers between devices, shift(): return lax.ppermute(value, axis, [(i, (i + offset) % n) for i in range(n)])  18.9 us
    ppermute x6, waiting for transfers between devices, shift_open(): lax.ppermute(value, axis, [(i, i + offset) for i in range(n) if 0 <= i +...  16.1 us
    ppermute x12, waiting for transfers between devices, swap(): return lax.ppermute(value, 'core', [(0, 1), (1, 0)])  14.2 us
    ppermute x6, starting transfers between devices, shift_open(): lax.ppermute(value, axis, [(i, i + offset) for i in range(n) if 0 <= i +...  13.5 us
  transfers between devices with their start and end apart: 50, of which 34 were waited for; matrix products, arithmetic and copies ran while one was open for 6% of the time, Pallas kernels for 18%

profile of v1, /device:TPU:1, one launch (start us, length us, event | category | flops | bytes accessed | tf_op | source)
XLA Modules:
  0.0 411.2 jit_solution(16768654455103709807)
XLA Ops:
  7.9 2.7 split_attn.1
  14.0 2.5 stack_attn.1
  22.0 2.5 collective-permute-start.2
  27.0 3.2 collective-permute-done.2.refs_3_.refs_2_
  30.2 1.7 copy-done.7
  40.6 2.1 collective-permute-start.7
  46.7 5.1 %collective-permute-done.6.refs_3_.refs_2_ = bf16[4,2,64,768]{3,2,1,0:T(8,128)(2,1)} collective-permute-done((bf16[4,2,64,768]{3,2,1,0:T(8,128)(2,1)S(1)}, bf16[4,2,64,768]{3,2,1,0:T(8,128)(2,1)}, u32[]{:S(2)}, u32[]{:S(2)}) %collective-permute-start.6) | collective-permute-done | bytes 786464 | tf_op jit(solution)/shard_map/ppermute | solution.py:148
  51.8 22.2 %collective-permute-done.7.refs_4_.refs_3_ = bf16[4,2,64,768]{3,2,1,0:T(8,128)(2,1)} collective-permute-done((bf16[4,2,64,768]{3,2,1,0:T(8,128)(2,1)S(1)}, bf16[4,2,64,768]{3,2,1,0:T(8,128)(2,1)}, u32[]{:S(2)}, u32[]{:S(2)}) %collective-permute-start.7) | collective-permute-done | bytes 786464 | tf_op jit(solution)/shard_map/ppermute | solution.py:148
  74.0 3.0 collective-permute-done.8.refs_5_.refs_4_
  78.2 5.6 %project_kv.1 = f32[512,768]{1,0:T(8,128)S(1)} custom-call(s32[4]{0:T(128)S(1)} %copy-done.33, bf16[256,2048]{1,0:T(8,128)(2,1)S(1)} %enter_rows.1.refs_0_.refs_3_.refs_9_, bf16[256,2048]{1,0:T(8,128)(2,1)S(1)} %collective-permute-done.4.refs_1_.refs_4_.refs_10_, bf16[4,2,64,768]{3,2,1,0:T(8,128)(2,1)S(1)} %bitcast.91, ...), custom_call_target="tpu_custom_call" | custom-call | flops 1 | bytes 1 | tf_op jit(solution)/shard_map/project_kv/pallas_call | solution.py:61
  85.8 3.0 collective-permute-start.9
  88.8 5.0 %collective-permute-start.10 = (bf16[2,256,512]{2,1,0:T(8,128)(2,1)}, bf16[2,256,512]{2,1,0:T(8,128)(2,1)S(1)}, u32[]{:S(2)}, u32[]{:S(2)}) collective-permute-start(bf16[2,256,512]{2,1,0:T(8,128)(2,1)} %convolution_convert_fusion), channel_id=1, source_target_pairs={{0,8},{4,12},{1,9},{5,13},{2,10},{6,14},{3,11},{7,15},{16,24},{20,... | collective-permute-start | bytes 1572872 | tf_op jit(solution)/shard_map/ppermute | solution.py:28
  95.2 2.5 split_mlp.1
  97.6 2.3 collective-permute-start.21
  101.3 6.9 %collective-permute-done.10.refs_6_.refs_3_ = bf16[2,256,512]{2,1,0:T(8,128)(2,1)S(1)} collective-permute-done((bf16[2,256,512]{2,1,0:T(8,128)(2,1)}, bf16[2,256,512]{2,1,0:T(8,128)(2,1)S(1)}, u32[]{:S(2)}, u32[]{:S(2)}) %collective-permute-start.10) | collective-permute-done | bytes 524320 | tf_op jit(solution)/shard_map/ppermute | solution.py:28
  108.2 7.3 %collective-permute-done.11.refs_7_.refs_4_ = bf16[2,256,512]{2,1,0:T(8,128)(2,1)S(1)} collective-permute-done((bf16[2,256,512]{2,1,0:T(8,128)(2,1)}, bf16[2,256,512]{2,1,0:T(8,128)(2,1)S(1)}, u32[]{:S(2)}, u32[]{:S(2)}) %collective-permute-start.11) | collective-permute-done | bytes 524320 | tf_op jit(solution)/shard_map/ppermute | solution.py:28
  118.7 12.8 %retain.1 = (f32[256,2048]{1,0:T(8,128)}, bf16[256,2048]{1,0:T(8,128)(2,1)}, bf16[512,256]{1,0:T(8,128)(2,1)}, bf16[2,256,512]{2,1,0:T(8,128)(2,1)}, bf16[2,256,...) custom-call(s32[4]{0:T(128)} %pad_add_fusion.s_ref, ...), custom_call_target="tpu_custom_call" | custom-call | flops 1 | bytes 1 | tf_op jit(solution)/shard_map/retain/pallas_call | solution.py:61
  132.1 2.5 collective-permute-done.12
  134.6 1.7 add_convert_fusion.9
  136.3 5.2 %collective-permute-start.15 = (bf16[64,2048]{1,0:T(8,128)(2,1)S(1)}, bf16[64,2048]{1,0:T(8,128)(2,1)S(1)}, u32[]{:S(2)}, u32[]{:S(2)}) collective-permute-start(bf16[64,2048]{1,0:T(8,128)(2,1)S(1)} %get-tuple-element.124), channel_id=1, source_target_pairs={{0,3},{1,0},{2,1},{3,2},{4,7},{5,4},{6,5},{7,6},{8,11},{9,8},{10,9... | collective-permute-start | bytes 786440 | tf_op jit(solution)/shard_map/ppermute | solution.py:23
  142.8 9.7 %collective-permute-done.15 = bf16[64,2048]{1,0:T(8,128)(2,1)S(1)} collective-permute-done((bf16[64,2048]{1,0:T(8,128)(2,1)S(1)}, bf16[64,2048]{1,0:T(8,128)(2,1)S(1)}, u32[]{:S(2)}, u32[]{:S(2)}) %collective-permute-start.15) | collective-permute-done | bytes 262176 | tf_op jit(solution)/shard_map/ppermute | solution.py:23
  152.5 3.1 collective-permute-done.14
  159.1 2.2 collective-permute-start.20
  161.3 2.0 collective-permute-done.16.refs_3_
  163.3 1.8 collective-permute-done.17.refs_4_
  165.1 7.6 %collective-permute-done.18.refs_5_ = bf16[64,2048]{1,0:T(8,128)(2,1)S(1)} collective-permute-done((bf16[64,2048]{1,0:T(8,128)(2,1)S(1)}, bf16[64,2048]{1,0:T(8,128)(2,1)S(1)}, u32[]{:S(2)}, u32[]{:S(2)}) %collective-permute-start.18) | collective-permute-done | bytes 262176 | tf_op jit(solution)/shard_map/ppermute | solution.py:23
  178.3 5.2 %all-gather.5.cloned.1.call-done = bf16[2048,1536]{1,0:T(8,128)(2,1)} async-done(((bf16[128,1536]{1,0:T(8,128)(2,1)}), bf16[2048,1536]{1,0:T(8,128)(2,1)}) %all-gather.5.cloned.1.call-update) | async-done | bytes 6291472 | tf_op jit(solution)/shard_map/all_gather | solution.py:1040
  183.5 14.4 %mlp.1 = (f32[256,2048]{1,0:T(8,128)}, bf16[256,2048]{1,0:T(8,128)(2,1)}, f32[8,2048]{1,0:T(8,128)}, bf16[512,1024]{1,0:T(8,128)(2,1)}, bf16[512,512]{1,0:T(8,128)(2,1)}) custom-call(s32[4]{0:T(128)} %pad_add_fusion.s_ref, bf16[256,2048]{1,0:T(8,128)(2,1)} %copy-done.18, bf16[256,2048]{1,0:T(8,128)(2,1)} %collective-permute-done.19.refs_1_, ...), custom_call_target="tpu_custom_call" | custom-call | flops 1 | bytes 1 | tf_op jit(solution)/shard_map/mlp/pallas_call | solution.py:61
  198.7 2.5 collective-permute-done.22
  201.2 2.3 add_convert_fusion.4
  203.4 2.7 collective-permute-start.25
  206.1 1.7 collective-permute-start.23
  207.8 7.0 %weight_mlp.1 = (bf16[4,4,2,64,3584]{4,3,2,1,0:T(8,128)(2,1)}, f32[8,128]{1,0:T(8,128)}) custom-call(s32[4]{0:T(128)} %pad_add_fusion.s_ref, bf16[256,2048]{1,0:T(8,128)(2,1)} %copy-done.18, bf16[256,2048]{1,0:T(8,128)(2,1)} %collective-permute-done.19.refs_1_, bf16[512,1024]{1,0:T(8,128)(2,1)} %get-tuple-element.78.refs_2_), custom_call_target="tpu_custom_call" | custom-call | flops 1 | bytes 1 | tf_op jit(solution)/shard_map/weight_mlp/pallas_call | solution.py:61
  214.7 2.5 collective-permute-done.25
  217.2 2.1 collective-permute-done.23
  219.3 2.0 add_convert_fusion.1.refs_0_
  223.7 2.8 copy-done.6
  227.5 2.8 project_down.1
  232.6 5.6 %collective-permute-done.28.refs_6_ = bf16[64,2048]{1,0:T(8,128)(2,1)S(1)} collective-permute-done((bf16[64,2048]{1,0:T(8,128)(2,1)}, bf16[64,2048]{1,0:T(8,128)(2,1)S(1)}, u32[]{:S(2)}, u32[]{:S(2)}) %collective-permute-start.28) | collective-permute-done | bytes 262176 | tf_op jit(solution)/shard_map/ppermute | solution.py:23
  238.9 6.1 %second_back.1 = (f32[256,2048]{1,0:T(8,128)}, bf16[256,2048]{1,0:T(8,128)(2,1)}) custom-call(s32[4]{0:T(128)} %pad_add_fusion.s_ref, f32[256,2048]{1,0:T(8,128)} %copy-done.10, f32[256,2048]{1,0:T(8,128)} %refs_1_.6, f32[1,2048]{1,0:T(1,128)} %bitcast.106, bf16[64,2048]{1,0:T(8,128)(2,1)} %tie.4.refs_2_.refs_3_, bf16[64,2048]{1,0:T(8,128)(2,1)} %copy-done.68, ...), custom_call_target="tpu_custom_call" | custom-call | flops 1 | bytes 1 | tf_op jit(solution)/shard_map/second_back/pallas_call | solution.py:61
  245.6 2.4 collective-permute-done.29.refs_1_
  249.0 9.6 %back_gate.1 = (bf16[512,512]{1,0:T(8,128)(2,1)}, bf16[512,512]{1,0:T(8,128)(2,1)}, bf16[2,256,512]{2,1,0:T(8,128)(2,1)}) custom-call(s32[4]{0:T(128)} %pad_add_fusion.s_ref, bf16[256,2048]{1,0:T(8,128)(2,1)} %get-tuple-element.83.refs_0_, bf16[256,2048]{1,0:T(8,128)(2,1)} %copy-done.47, bf16[4,4,2,64,1280]{4,3,2,1,0:T(8,128)(2,1)} %bitcast.83, ...), custom_call_target="tpu_custom_call" | custom-call | flops 1 | bytes 1 | tf_op jit(solution)/shard_map/back_gate/pallas_call | solution.py:61
  261.3 1.5 collective-permute-start.32
  265.7 7.2 %weight_og.1 = (bf16[4,4,2,64,3584]{4,3,2,1,0:T(8,128)(2,1)}, f32[8,128]{1,0:T(8,128)}) custom-call(s32[4]{0:T(128)} %pad_add_fusion.s_ref, bf16[256,2048]{1,0:T(8,128)(2,1)} %get-tuple-element.83.refs_0_, bf16[256,2048]{1,0:T(8,128)(2,1)} %copy-done.47, bf16[512,512]{1,0:T(8,128)(2,1)} %get-tuple-element.90.refs_2_, ...), custom_call_target="tpu_custom_call", output_to_operand_aliasing={{0}: (7, {})} | custom-call | flops 1 | bytes 1 | tf_op jit(solution)/shard_map/weight_og/pallas_call | solution.py:61
  273.0 5.6 %weight_down.1 = (bf16[4,4,2,64,3584]{4,3,2,1,0:T(8,128)(2,1)}, f32[8,128]{1,0:T(8,128)}) custom-call(s32[4]{0:T(128)} %pad_add_fusion.s_ref, bf16[256,2048]{1,0:T(8,128)(2,1)} %copy-done.9, bf16[256,2048]{1,0:T(8,128)(2,1)} %copy-done.48, bf16[512,512]{1,0:T(8,128)(2,1)} %get-tuple-element.80.refs_0_.refs_2_, ...), custom_call_target="tpu_custom_call", output_to_operand_aliasing={{0}: (4, {})} | custom-call | flops 1 | bytes 1 | tf_op jit(solution)/shard_map/weight_down/pallas_call | solution.py:61
  278.6 5.2 %weight_query.1 = (bf16[4,4,2,64,3584]{4,3,2,1,0:T(8,128)(2,1)}, f32[8,128]{1,0:T(8,128)}) custom-call(s32[4]{0:T(128)} %pad_add_fusion.s_ref, bf16[256,2048]{1,0:T(8,128)(2,1)} %copy-done.4, bf16[256,2048]{1,0:T(8,128)(2,1)} %copy-done.1, bf16[512,256]{1,0:T(8,128)(2,1)} %pad_maximum_fusion.1.refs_2_.refs_7_, ...), custom_call_target="tpu_custom_call", output_to_operand_aliasing={{0}: (4, {})} | custom-call | flops 1 | bytes 1 | tf_op jit(solution)/shard_map/weight_query/pallas_call | solution.py:61
  287.0 1.8 collective-permute-done.32.refs_4_
  288.8 8.0 %weight_last.1 = (bf16[4,4,2,64,3584]{4,3,2,1,0:T(8,128)(2,1)}, f32[8,128]{1,0:T(8,128)}, bf16[512,768]{1,0:T(8,128)(2,1)}) custom-call(s32[4]{0:T(128)} %pad_add_fusion.s_ref, bf16[256,2048]{1,0:T(8,128)(2,1)} %copy-done.4, bf16[256,2048]{1,0:T(8,128)(2,1)} %copy-done.1, bf16[2,256,512]{2,1,0:T(8,128)(2,1)} %tie.5.refs_2_, ...), custom_call_target="tpu_custom_call", output_to_operand_aliasing={{0}: (14, {})} | custom-call | flops 1 | bytes 1 | tf_op jit(solution)/shard_map/weight_last/pallas_call | solution.py:61
  298.4 2.5 copy-done
  303.1 7.5 %back_attn.1 = (f32[256,2048]{1,0:T(8,128)S(1)}, bf16[256,2048]{1,0:T(8,128)(2,1)S(1)}, f32[8,2048]{1,0:T(8,128)S(1)}) custom-call(s32[4]{0:T(128)S(1)} %copy-done.37, bf16[512,768]{1,0:T(8,128)(2,1)S(1)} %copy-done.28, bf16[4,2,64,768]{3,2,1,0:T(8,128)(2,1)S(1)} %bitcast.92, bf16[4,2,64,768]{3,2,1,0:T(8,128)(2,1)} %collective-permute-done.6.refs_3_.refs_2_, ...), custom_call_target="tpu_custom_call" | custom-call | flops 1 | bytes 1 | tf_op jit(solution)/shard_map/back_attn/pallas_call | solution.py:61
  318.4 5.7 %third_blocks.1 = (bf16[128,2048]{1,0:T(8,128)(2,1)}, bf16[128,2048]{1,0:T(8,128)(2,1)}, bf16[128,2048]{1,0:T(8,128)(2,1)}, bf16[128,2048]{1,0:T(8,128)(2,1)}) custom-call(s32[4]{0:T(128)} %pad_add_fusion.s_ref, f32[256,2048]{1,0:T(8,128)} %copy-done.23, bf16[256,2048]{1,0:T(8,128)(2,1)} %copy-done.59, f32[256,2048]{1,0:T(8,128)} %copy-done.22, ...), custom_call_target="tpu_custom_call" | custom-call | flops 1 | bytes 1 | tf_op jit(solution)/shard_map/third_blocks/pallas_call | solution.py:61
  326.0 5.5 %collective-permute-start.40 = (f32[2,2048]{1,0:T(2,128)S(1)}, f32[2,2048]{1,0:T(2,128)S(1)}, u32[]{:S(2)}, u32[]{:S(2)}) collective-permute-start(f32[2,2048]{1,0:T(2,128)S(1)} %fusion.34), channel_id=1, source_target_pairs={{0,12},{4,8},{8,4},{12,0},{1,13},{5,9},{9,5},{13,1},{2,14},{6,10},... | collective-permute-start | bytes 49160 | tf_op jit(solution)/shard_map/ppermute | solution.py:1140
  331.5 1.9 collective-permute-done.40
  334.9 2.2 collective-permute-done.41
  337.0 2.3 collective-permute-start.42
  339.4 1.9 collective-permute-done.42
  341.3 8.8 %collective-permute-done.36 = bf16[128,2048]{1,0:T(8,128)(2,1)S(1)} collective-permute-done((bf16[128,2048]{1,0:T(8,128)(2,1)}, bf16[128,2048]{1,0:T(8,128)(2,1)S(1)}, u32[]{:S(2)}, u32[]{:S(2)}) %collective-permute-start.36) | collective-permute-done | bytes 524320 | tf_op jit(solution)/shard_map/ppermute | solution.py:23
  353.9 11.4 %collective-permute-done.43.refs_5_ = bf16[144,2048]{1,0:T(8,128)(2,1)S(1)} collective-permute-done((bf16[144,2048]{1,0:T(8,128)(2,1)S(1)}, bf16[144,2048]{1,0:T(8,128)(2,1)S(1)}, u32[]{:S(2)}, u32[]{:S(2)}) %collective-permute-start.43) | collective-permute-done | bytes 589856 | tf_op jit(solution)/shard_map/ppermute | solution.py:23
  365.3 2.2 collective-permute-done.44.refs_6_
  367.5 14.5 %collective-permute-done.45.refs_7_ = bf16[144,2048]{1,0:T(8,128)(2,1)S(1)} collective-permute-done((bf16[144,2048]{1,0:T(8,128)(2,1)S(1)}, bf16[144,2048]{1,0:T(8,128)(2,1)S(1)}, u32[]{:S(2)}, u32[]{:S(2)}) %collective-permute-start.45) | collective-permute-done | bytes 589856 | tf_op jit(solution)/shard_map/ppermute | solution.py:23
  382.9 7.4 %leave_rows.1 = (f32[256,2048]{1,0:T(8,128)}, f32[256,2048]{1,0:T(8,128)}) custom-call(s32[4]{0:T(128)} %pad_add_fusion.s_ref, f32[256,2048]{1,0:T(8,128)} %copy-done.10, f32[256,2048]{1,0:T(8,128)} %refs_1_.7, f32[256,2048]{1,0:T(8,128)} %get-tuple-element.82.refs_2_, f32[1,2048]{1,0:T(1,128)} %bitcast.104, bf16[144,2048]{1,0:T(8,128)(2,1)} %copy-done.50, ...), custom_call_target="tpu_custom_call" | custom-call | flops 1 | bytes 1 | tf_op jit(solution)/shard_map/leave_rows/pallas_call | solution.py:61
  393.7 5.5 %reduce-scatter.2.cloned.1.call-done.refs_0_ = bf16[128,3584]{1,0:T(8,128)(2,1)} async-done(((bf16[2048,3584]{1,0:T(8,128)(2,1)}), bf16[128,3584]{1,0:T(8,128)(2,1)}) %reduce-scatter.2.cloned.1.call-update) | async-done | bytes 917520 | tf_op jit(solution)/shard_map/reduce_scatter | solution.py:1121
  401.4 1.4 collective-permute-done.46.refs_1_
  402.9 1.8 join_heads.1
  (273 shorter events, 85.7 us)
Async XLA Ops:
  7.2 111.5 %all-gather.3.cloned.1.call-start = ((), (), s32[]{:S(2)}) async-start(), calls=%async_computation.1 | async-start | bytes 5570560 | tf_op jit(solution)/shard_map/all_gather | solution.py:990
  10.5 2.8 collective-permute-start
  16.6 166.9 %all-gather.5.cloned.1.call-start = ((), (), s32[]{:S(2)}) async-start(), calls=%async_computation.2 | async-start | bytes 6684672 | tf_op jit(solution)/shard_map/all_gather | solution.py:1040
  16.6 18.6 %collective-permute-start.5 = (s32[1]{0:T(128)}, s32[1]{0:T(128)}, u32[]{:S(2)}, u32[]{:S(2)}) collective-permute-start(s32[1]{0:T(128)} %param.27), channel_id=1, source_target_pairs={{0,16},{16,0},{1,17},{17,1},{2,18},{18,2},{3,19},{19,3},{4,20},{20... | collective-permute-start | bytes 20 | tf_op jit(solution)/shard_map/ppermute | solution.py:34
  19.8 58.3 %copy-start.20 = (f32[1,512]{0,1:T(8,128)}, f32[1,512]{0,1:T(8,128)S(1)}, u32[]{:S(2)}) copy-start(f32[1,512]{0,1:T(8,128)S(1)} %copy.51) | copy-start | bytes 6148
  20.7 6.2 %collective-permute-start.1 = (bf16[128,768]{1,0:T(8,128)(2,1)}, bf16[128,768]{1,0:T(8,128)(2,1)S(1)}, u32[]{:S(2)}, u32[]{:S(2)}) collective-permute-start(bf16[128,768]{1,0:T(8,128)(2,1)} %get-tuple-element.68.refs_0_), channel_id=1, source_target_pairs={{0,4},{4,8},{8,12},{12,0},{16,48},{20,52},{24,56},{28,60},{32,36},... | collective-permute-start | bytes 589832 | tf_op jit(solution)/shard_map/ppermute | solution.py:148
  22.0 8.1 %collective-permute-start.2 = (bf16[128,768]{1,0:T(8,128)(2,1)}, bf16[128,768]{1,0:T(8,128)(2,1)S(1)}, u32[]{:S(2)}, u32[]{:S(2)}) collective-permute-start(bf16[128,768]{1,0:T(8,128)(2,1)} %get-tuple-element.68.refs_0_), channel_id=1, source_target_pairs={{0,8},{4,12},{8,0},{12,4},{16,80},{20,84},{24,88},{28,92},{32,40},... | collective-permute-start | bytes 589832 | tf_op jit(solution)/shard_map/ppermute | solution.py:148
  24.5 5.7 %collective-permute-start.3 = (bf16[128,768]{1,0:T(8,128)(2,1)}, bf16[128,768]{1,0:T(8,128)(2,1)S(1)}, u32[]{:S(2)}, u32[]{:S(2)}) collective-permute-start(bf16[128,768]{1,0:T(8,128)(2,1)} %get-tuple-element.68.refs_0_), channel_id=1, source_target_pairs={{0,12},{4,0},{8,4},{12,8},{16,112},{20,116},{24,120},{28,124},{32,... | collective-permute-start | bytes 589832 | tf_op jit(solution)/shard_map/ppermute | solution.py:148
  33.1 50.7 %copy-start.4 = (bf16[256,2048]{1,0:T(8,128)(2,1)}, bf16[256,2048]{1,0:T(8,128)(2,1)S(1)}, u32[]{:S(2)}) copy-start(bf16[256,2048]{1,0:T(8,128)(2,1)S(1)} %enter_rows.1.refs_0_.refs_3_.refs_9_) | copy-start | bytes 3145732
  33.1 43.9 %collective-permute-start.4 = (bf16[256,2048]{1,0:T(8,128)(2,1)S(1)}, bf16[256,2048]{1,0:T(8,128)(2,1)S(1)}, u32[]{:S(2)}, u32[]{:S(2)}) collective-permute-start(bf16[256,2048]{1,0:T(8,128)(2,1)S(1)} %enter_rows.1.refs_0_.refs_3_.refs_9_), channel_id=1, source_target_pairs={{0,16},{16,0},{1,17},{17,1},{2,18},{18,2},{3,19},{19,3},{4,20},{20... | collective-permute-start | bytes 3145736 | tf_op jit(solution)/shard_map/ppermute | solution.py:34
  39.3 12.5 %collective-permute-start.6 = (bf16[4,2,64,768]{3,2,1,0:T(8,128)(2,1)S(1)}, bf16[4,2,64,768]{3,2,1,0:T(8,128)(2,1)}, u32[]{:S(2)}, u32[]{:S(2)}) collective-permute-start(bf16[4,2,64,768]{3,2,1,0:T(8,128)(2,1)S(1)} %bitcast.88), channel_id=1, source_target_pairs={{0,32},{4,36},{8,40},{12,44},{16,20},{20,24},{24,28},{28,16},{32,6... | collective-permute-start | bytes 2359304 | tf_op jit(solution)/shard_map/ppermute | solution.py:148
  40.6 33.5 %collective-permute-start.7 = (bf16[4,2,64,768]{3,2,1,0:T(8,128)(2,1)S(1)}, bf16[4,2,64,768]{3,2,1,0:T(8,128)(2,1)}, u32[]{:S(2)}, u32[]{:S(2)}) collective-permute-start(bf16[4,2,64,768]{3,2,1,0:T(8,128)(2,1)S(1)} %bitcast.89), channel_id=1, source_target_pairs={{0,64},{4,68},{8,72},{12,76},{16,24},{20,28},{24,16},{28,20},{32,9... | collective-permute-start | bytes 2359304 | tf_op jit(solution)/shard_map/ppermute | solution.py:148
  42.7 34.4 %collective-permute-start.8 = (bf16[4,2,64,768]{3,2,1,0:T(8,128)(2,1)S(1)}, bf16[4,2,64,768]{3,2,1,0:T(8,128)(2,1)}, u32[]{:S(2)}, u32[]{:S(2)}) collective-permute-start(bf16[4,2,64,768]{3,2,1,0:T(8,128)(2,1)S(1)} %bitcast.90), channel_id=1, source_target_pairs={{0,96},{4,100},{8,104},{12,108},{16,28},{20,16},{24,20},{28,24},{3... | collective-permute-start | bytes 2359304 | tf_op jit(solution)/shard_map/ppermute | solution.py:148
  45.4 38.4 %copy-start.16 = (f32[1,512]{0,1:T(8,128)}, f32[1,512]{0,1:T(8,128)S(1)}, u32[]{:S(2)}) copy-start(f32[1,512]{0,1:T(8,128)S(1)} %copy.49) | copy-start | bytes 6148
  46.7 37.1 %copy-start.12 = (f32[2,256,256]{2,1,0:T(8,128)}, f32[2,256,256]{2,1,0:T(8,128)S(1)}, u32[]{:S(2)}) copy-start(f32[2,256,256]{2,1,0:T(8,128)S(1)} %and_select_fusion.refs_6_.refs_9_) | copy-start | bytes 1572868
  83.9 31.6 %copy-start.34 = (s32[4]{0:T(128)S(1)}, s32[4]{0:T(128)}, u32[]{:S(2)}) copy-start(s32[4]{0:T(128)} %pad_add_fusion.s_ref) | copy-start | bytes 52
  84.0 33.9 %copy-start.45 = (bf16[512,512]{1,0:T(8,128)(2,1)}, bf16[512,512]{1,0:T(8,128)(2,1)S(1)}, u32[]{:S(2)}) copy-start(bf16[512,512]{1,0:T(8,128)(2,1)S(1)} %slice.183) | copy-start | bytes 1572868
  84.7 33.2 %copy-start.49 = (bf16[2,256,256]{2,1,0:T(8,128)(2,1)}, bf16[2,256,256]{2,1,0:T(8,128)(2,1)S(1)}, u32[]{:S(2)}) copy-start(bf16[2,256,256]{2,1,0:T(8,128)(2,1)S(1)} %multiply_convert_fusion.refs_7_) | copy-start | bytes 786436
  85.8 32.1 %copy-start.56 = (bf16[512,128]{1,0:T(8,128)(2,1)S(1)}, bf16[512,128]{1,0:T(8,128)(2,1)}, u32[]{:S(2)}) copy-start(bf16[512,128]{1,0:T(8,128)(2,1)} %copy-done.55) | copy-start | bytes 393220
  85.8 32.2 %copy-start.58 = (bf16[512,128]{1,0:T(8,128)(2,1)S(1)}, bf16[512,128]{1,0:T(8,128)(2,1)}, u32[]{:S(2)}) copy-start(bf16[512,128]{1,0:T(8,128)(2,1)} %copy-done.57) | copy-start | bytes 393220
  85.8 15.4 %collective-permute-start.9 = (bf16[2,256,512]{2,1,0:T(8,128)(2,1)}, bf16[2,256,512]{2,1,0:T(8,128)(2,1)S(1)}, u32[]{:S(2)}, u32[]{:S(2)}) collective-permute-start(bf16[2,256,512]{2,1,0:T(8,128)(2,1)} %convolution_convert_fusion), channel_id=1, source_target_pairs={{0,4},{4,8},{8,12},{1,5},{5,9},{9,13},{2,6},{6,10},{10,14},{3,7},{... | collective-permute-start | bytes 1572872 | tf_op jit(solution)/shard_map/ppermute | solution.py:28
  88.8 19.4 %collective-permute-start.10 = (bf16[2,256,512]{2,1,0:T(8,128)(2,1)}, bf16[2,256,512]{2,1,0:T(8,128)(2,1)S(1)}, u32[]{:S(2)}, u32[]{:S(2)}) collective-permute-start(bf16[2,256,512]{2,1,0:T(8,128)(2,1)} %convolution_convert_fusion), channel_id=1, source_target_pairs={{0,8},{4,12},{1,9},{5,13},{2,10},{6,14},{3,11},{7,15},{16,24},{20,... | collective-permute-start | bytes 1572872 | tf_op jit(solution)/shard_map/ppermute | solution.py:28
  93.8 21.6 %collective-permute-start.11 = (bf16[2,256,512]{2,1,0:T(8,128)(2,1)}, bf16[2,256,512]{2,1,0:T(8,128)(2,1)S(1)}, u32[]{:S(2)}, u32[]{:S(2)}) collective-permute-start(bf16[2,256,512]{2,1,0:T(8,128)(2,1)} %convolution_convert_fusion), channel_id=1, source_target_pairs={{0,12},{1,13},{2,14},{3,15},{16,28},{17,29},{18,30},{19,31},{32,44... | collective-permute-start | bytes 1572872 | tf_op jit(solution)/shard_map/ppermute | solution.py:28
  97.6 3.6 collective-permute-start.21
  117.9 281.3 %reduce-scatter.2.cloned.1.call-start = ((), (), s32[]{:S(2)}) async-start(), calls=%async_computation.3 | async-start | bytes 15597568 | tf_op jit(solution)/shard_map/reduce_scatter | solution.py:1121
  131.6 3.1 collective-permute-start.12
  134.6 23.7 %copy-start.2 = (bf16[256,2048]{1,0:T(8,128)(2,1)S(1)}, bf16[256,2048]{1,0:T(8,128)(2,1)}, u32[]{:S(2)}) copy-start(bf16[256,2048]{1,0:T(8,128)(2,1)} %copy-done.1) | copy-start | bytes 3145732
  134.6 23.7 %copy-start.11 = (f32[256,2048]{1,0:T(8,128)S(1)}, f32[256,2048]{1,0:T(8,128)}, u32[]{:S(2)}) copy-start(f32[256,2048]{1,0:T(8,128)} %refs_1_.6) | copy-start | bytes 6291460
  134.6 23.8 %copy-start.35 = (s32[4]{0:T(128)S(1)}, s32[4]{0:T(128)}, u32[]{:S(2)}) copy-start(s32[4]{0:T(128)} %pad_add_fusion.s_ref) | copy-start | bytes 52
  136.3 16.2 %collective-permute-start.15 = (bf16[64,2048]{1,0:T(8,128)(2,1)S(1)}, bf16[64,2048]{1,0:T(8,128)(2,1)S(1)}, u32[]{:S(2)}, u32[]{:S(2)}) collective-permute-start(bf16[64,2048]{1,0:T(8,128)(2,1)S(1)} %get-tuple-element.124), channel_id=1, source_target_pairs={{0,3},{1,0},{2,1},{3,2},{4,7},{5,4},{6,5},{7,6},{8,11},{9,8},{10,9... | collective-permute-start | bytes 786440 | tf_op jit(solution)/shard_map/ppermute | solution.py:23
  141.5 14.0 %collective-permute-start.14 = (bf16[64,2048]{1,0:T(8,128)(2,1)S(1)}, bf16[64,2048]{1,0:T(8,128)(2,1)S(1)}, u32[]{:S(2)}, u32[]{:S(2)}) collective-permute-start(bf16[64,2048]{1,0:T(8,128)(2,1)S(1)} %get-tuple-element.125), channel_id=1, source_target_pairs={{0,1},{1,2},{2,3},{3,0},{4,5},{5,6},{6,7},{7,4},{8,9},{9,10},{10,1... | collective-permute-start | bytes 786440 | tf_op jit(solution)/shard_map/ppermute | solution.py:23
  141.6 14.0 %collective-permute-start.13 = (bf16[64,2048]{1,0:T(8,128)(2,1)S(1)}, bf16[64,2048]{1,0:T(8,128)(2,1)S(1)}, u32[]{:S(2)}, u32[]{:S(2)}) collective-permute-start(bf16[64,2048]{1,0:T(8,128)(2,1)S(1)} %get-tuple-element.123), channel_id=1, source_target_pairs={{0,2},{1,3},{2,0},{3,1},{4,6},{5,7},{6,4},{7,5},{8,10},{9,11},{10,... | collective-permute-start | bytes 786440 | tf_op jit(solution)/shard_map/ppermute | solution.py:23
  156.8 6.5 %collective-permute-start.16 = (bf16[64,2048]{1,0:T(8,128)(2,1)S(1)}, bf16[64,2048]{1,0:T(8,128)(2,1)S(1)}, u32[]{:S(2)}, u32[]{:S(2)}) collective-permute-start(bf16[64,2048]{1,0:T(8,128)(2,1)S(1)} %add_convert_fusion.6.refs_2_), channel_id=1, source_target_pairs={{0,3},{1,0},{2,1},{3,2},{4,7},{5,4},{6,5},{7,6},{8,11},{9,8},{10,9... | collective-permute-start | bytes 786440 | tf_op jit(solution)/shard_map/ppermute | solution.py:23
  157.2 7.9 %collective-permute-start.17 = (bf16[64,2048]{1,0:T(8,128)(2,1)S(1)}, bf16[64,2048]{1,0:T(8,128)(2,1)S(1)}, u32[]{:S(2)}, u32[]{:S(2)}) collective-permute-start(bf16[64,2048]{1,0:T(8,128)(2,1)S(1)} %add_convert_fusion.6.refs_2_), channel_id=1, source_target_pairs={{0,2},{1,3},{2,0},{3,1},{4,6},{5,7},{6,4},{7,5},{8,10},{9,11},{10,... | collective-permute-start | bytes 786440 | tf_op jit(solution)/shard_map/ppermute | solution.py:23
  157.6 15.1 %collective-permute-start.18 = (bf16[64,2048]{1,0:T(8,128)(2,1)S(1)}, bf16[64,2048]{1,0:T(8,128)(2,1)S(1)}, u32[]{:S(2)}, u32[]{:S(2)}) collective-permute-start(bf16[64,2048]{1,0:T(8,128)(2,1)S(1)} %add_convert_fusion.6.refs_2_), channel_id=1, source_target_pairs={{0,1},{1,2},{2,3},{3,0},{4,5},{5,6},{6,7},{7,4},{8,9},{9,10},{10,1... | collective-permute-start | bytes 786440 | tf_op jit(solution)/shard_map/ppermute | solution.py:23
  159.1 24.4 %copy-start.9 = (bf16[256,2048]{1,0:T(8,128)(2,1)}, bf16[256,2048]{1,0:T(8,128)(2,1)S(1)}, u32[]{:S(2)}) copy-start(bf16[256,2048]{1,0:T(8,128)(2,1)S(1)} %low_rows.1.refs_2_.refs_0_) | copy-start | bytes 3145732
  159.1 16.7 %collective-permute-start.20 = (bf16[256,2048]{1,0:T(8,128)(2,1)S(1)}, bf16[256,2048]{1,0:T(8,128)(2,1)S(1)}, u32[]{:S(2)}, u32[]{:S(2)}) collective-permute-start(bf16[256,2048]{1,0:T(8,128)(2,1)S(1)} %low_rows.1.refs_2_.refs_0_), channel_id=1, source_target_pairs={{0,16},{16,0},{1,17},{17,1},{2,18},{18,2},{3,19},{19,3},{4,20},{20... | collective-permute-start | bytes 3145736 | tf_op jit(solution)/shard_map/ppermute | solution.py:34
  175.5 2.8 collective-permute-start.19
  197.9 3.3 collective-permute-start.22
  203.4 13.8 %collective-permute-start.25 = (bf16[64,2048]{1,0:T(8,128)(2,1)}, bf16[64,2048]{1,0:T(8,128)(2,1)S(1)}, u32[]{:S(2)}, u32[]{:S(2)}) collective-permute-start(bf16[64,2048]{1,0:T(8,128)(2,1)} %get-tuple-element.121), channel_id=1, source_target_pairs={{0,3},{1,0},{2,1},{3,2},{4,7},{5,4},{6,5},{7,6},{8,11},{9,8},{10,9... | collective-permute-start | bytes 786440 | tf_op jit(solution)/shard_map/ppermute | solution.py:23
  206.1 11.1 %collective-permute-start.24 = (bf16[64,2048]{1,0:T(8,128)(2,1)S(1)}, bf16[64,2048]{1,0:T(8,128)(2,1)S(1)}, u32[]{:S(2)}, u32[]{:S(2)}) collective-permute-start(bf16[64,2048]{1,0:T(8,128)(2,1)S(1)} %get-tuple-element.122), channel_id=1, source_target_pairs={{0,1},{1,2},{2,3},{3,0},{4,5},{5,6},{6,7},{7,4},{8,9},{9,10},{10,1... | collective-permute-start | bytes 786440 | tf_op jit(solution)/shard_map/ppermute | solution.py:23
  206.1 13.2 %collective-permute-start.23 = (bf16[64,2048]{1,0:T(8,128)(2,1)S(1)}, bf16[64,2048]{1,0:T(8,128)(2,1)}, u32[]{:S(2)}, u32[]{:S(2)}) collective-permute-start(bf16[64,2048]{1,0:T(8,128)(2,1)S(1)} %get-tuple-element.120), channel_id=1, source_target_pairs={{0,2},{1,3},{2,0},{3,1},{4,6},{5,7},{6,4},{7,5},{8,10},{9,11},{10,... | collective-permute-start | bytes 786440 | tf_op jit(solution)/shard_map/ppermute | solution.py:23
  221.3 11.3 %collective-permute-start.26 = (bf16[64,2048]{1,0:T(8,128)(2,1)}, bf16[64,2048]{1,0:T(8,128)(2,1)S(1)}, u32[]{:S(2)}, u32[]{:S(2)}) collective-permute-start(bf16[64,2048]{1,0:T(8,128)(2,1)} %tie.4.refs_2_.refs_3_), channel_id=1, source_target_pairs={{0,3},{1,0},{2,1},{3,2},{4,7},{5,4},{6,5},{7,6},{8,11},{9,8},{10,9... | collective-permute-start | bytes 786440 | tf_op jit(solution)/shard_map/ppermute | solution.py:23
  222.7 9.9 %collective-permute-start.27 = (bf16[64,2048]{1,0:T(8,128)(2,1)}, bf16[64,2048]{1,0:T(8,128)(2,1)S(1)}, u32[]{:S(2)}, u32[]{:S(2)}) collective-permute-start(bf16[64,2048]{1,0:T(8,128)(2,1)} %tie.4.refs_2_.refs_3_), channel_id=1, source_target_pairs={{0,2},{1,3},{2,0},{3,1},{4,6},{5,7},{6,4},{7,5},{8,10},{9,11},{10,... | collective-permute-start | bytes 786440 | tf_op jit(solution)/shard_map/ppermute | solution.py:23
  222.9 15.2 %collective-permute-start.28 = (bf16[64,2048]{1,0:T(8,128)(2,1)}, bf16[64,2048]{1,0:T(8,128)(2,1)S(1)}, u32[]{:S(2)}, u32[]{:S(2)}) collective-permute-start(bf16[64,2048]{1,0:T(8,128)(2,1)} %tie.4.refs_2_.refs_3_), channel_id=1, source_target_pairs={{0,1},{1,2},{2,3},{3,0},{4,5},{5,6},{6,7},{7,4},{8,9},{9,10},{10,1... | collective-permute-start | bytes 786440 | tf_op jit(solution)/shard_map/ppermute | solution.py:23
  245.0 3.0 collective-permute-start.29
  258.6 27.6 %collective-permute-start.30 = (bf16[2,256,512]{2,1,0:T(8,128)(2,1)}, bf16[2,256,512]{2,1,0:T(8,128)(2,1)S(1)}, u32[]{:S(2)}, u32[]{:S(2)}) collective-permute-start(bf16[2,256,512]{2,1,0:T(8,128)(2,1)} %get-tuple-element.87.refs_7_), channel_id=1, source_target_pairs={{4,0},{8,4},{12,8},{5,1},{9,5},{13,9},{6,2},{10,6},{14,10},{7,3},{... | collective-permute-start | bytes 1572872 | tf_op jit(solution)/shard_map/ppermute | solution.py:28
  260.0 27.0 %collective-permute-start.31 = (bf16[2,256,512]{2,1,0:T(8,128)(2,1)}, bf16[2,256,512]{2,1,0:T(8,128)(2,1)}, u32[]{:S(2)}, u32[]{:S(2)}) collective-permute-start(bf16[2,256,512]{2,1,0:T(8,128)(2,1)} %get-tuple-element.87.refs_7_), channel_id=1, source_target_pairs={{8,0},{12,4},{9,1},{13,5},{10,2},{14,6},{11,3},{15,7},{24,16},{28,... | collective-permute-start | bytes 1572872 | tf_op jit(solution)/shard_map/ppermute | solution.py:28
  261.3 27.5 %collective-permute-start.32 = (bf16[2,256,512]{2,1,0:T(8,128)(2,1)}, bf16[2,256,512]{2,1,0:T(8,128)(2,1)}, u32[]{:S(2)}, u32[]{:S(2)}) collective-permute-start(bf16[2,256,512]{2,1,0:T(8,128)(2,1)} %get-tuple-element.87.refs_7_), channel_id=1, source_target_pairs={{12,0},{13,1},{14,2},{15,3},{28,16},{29,17},{30,18},{31,19},{44,32... | collective-permute-start | bytes 1572872 | tf_op jit(solution)/shard_map/ppermute | solution.py:28
  312.8 3.3 collective-permute-start.33
  313.3 4.0 collective-permute-start.34
  314.2 1.4 collective-permute-start.38
  315.7 10.3 %collective-permute-start.39 = (f32[2,2048]{1,0:T(2,128)S(1)}, f32[2,2048]{1,0:T(2,128)S(1)}, u32[]{:S(2)}, u32[]{:S(2)}) collective-permute-start(f32[2,2048]{1,0:T(2,128)S(1)} %fusion.17), channel_id=1, source_target_pairs={{0,4},{4,0},{8,12},{12,8},{1,5},{5,1},{9,13},{13,9},{2,6},{6,2},{1... | collective-permute-start | bytes 49160 | tf_op jit(solution)/shard_map/ppermute | solution.py:1140
  324.1 17.3 %collective-permute-start.37 = (bf16[128,2048]{1,0:T(8,128)(2,1)}, bf16[128,2048]{1,0:T(8,128)(2,1)S(1)}, u32[]{:S(2)}, u32[]{:S(2)}) collective-permute-start(bf16[128,2048]{1,0:T(8,128)(2,1)} %get-tuple-element.106), channel_id=1, source_target_pairs={{0,3},{1,0},{2,1},{3,2},{4,7},{5,4},{6,5},{7,6},{8,11},{9,8},{10,9... | collective-permute-start | bytes 1572872 | tf_op jit(solution)/shard_map/ppermute | solution.py:23
  324.5 25.6 %collective-permute-start.36 = (bf16[128,2048]{1,0:T(8,128)(2,1)}, bf16[128,2048]{1,0:T(8,128)(2,1)S(1)}, u32[]{:S(2)}, u32[]{:S(2)}) collective-permute-start(bf16[128,2048]{1,0:T(8,128)(2,1)} %get-tuple-element.105), channel_id=1, source_target_pairs={{0,1},{1,2},{2,3},{3,0},{4,5},{5,6},{6,7},{7,4},{8,9},{9,10},{10,1... | collective-permute-start | bytes 1572872 | tf_op jit(solution)/shard_map/ppermute | solution.py:23
  325.5 24.6 %collective-permute-start.35 = (bf16[128,2048]{1,0:T(8,128)(2,1)}, bf16[128,2048]{1,0:T(8,128)(2,1)S(1)}, u32[]{:S(2)}, u32[]{:S(2)}) collective-permute-start(bf16[128,2048]{1,0:T(8,128)(2,1)} %get-tuple-element.104), channel_id=1, source_target_pairs={{0,2},{1,3},{2,0},{3,1},{4,6},{5,7},{6,4},{7,5},{8,10},{9,11},{10,... | collective-permute-start | bytes 1572872 | tf_op jit(solution)/shard_map/ppermute | solution.py:23
  326.0 7.4 %collective-permute-start.40 = (f32[2,2048]{1,0:T(2,128)S(1)}, f32[2,2048]{1,0:T(2,128)S(1)}, u32[]{:S(2)}, u32[]{:S(2)}) collective-permute-start(f32[2,2048]{1,0:T(2,128)S(1)} %fusion.34), channel_id=1, source_target_pairs={{0,12},{4,8},{8,4},{12,0},{1,13},{5,9},{9,5},{13,1},{2,14},{6,10},... | collective-permute-start | bytes 49160 | tf_op jit(solution)/shard_map/ppermute | solution.py:1140
  333.4 3.6 collective-permute-start.41
  337.0 4.3 %collective-permute-start.42 = (f32[2,2048]{1,0:T(2,128)S(1)}, f32[2,2048]{1,0:T(2,128)S(1)}, u32[]{:S(2)}, u32[]{:S(2)}) collective-permute-start(f32[2,2048]{1,0:T(2,128)S(1)} %add.217), channel_id=1, source_target_pairs={{0,96},{32,64},{64,32},{96,0},{1,97},{33,65},{65,33},{97,1},{2,98}... | collective-permute-start | bytes 49160 | tf_op jit(solution)/shard_map/ppermute | solution.py:1140
  351.7 30.4 %copy-start.50 = (bf16[144,2048]{1,0:T(8,128)(2,1)}, bf16[144,2048]{1,0:T(8,128)(2,1)S(1)}, u32[]{:S(2)}) copy-start(bf16[144,2048]{1,0:T(8,128)(2,1)S(1)} %maximum_maximum_fusion.refs_4_) | copy-start | bytes 1769476
  351.7 13.6 %collective-permute-start.43 = (bf16[144,2048]{1,0:T(8,128)(2,1)S(1)}, bf16[144,2048]{1,0:T(8,128)(2,1)S(1)}, u32[]{:S(2)}, u32[]{:S(2)}) collective-permute-start(bf16[144,2048]{1,0:T(8,128)(2,1)S(1)} %maximum_maximum_fusion.refs_4_), channel_id=1, source_target_pairs={{0,3},{1,0},{2,1},{3,2},{4,7},{5,4},{6,5},{7,6},{8,11},{9,8},{10,9... | collective-permute-start | bytes 1769480 | tf_op jit(solution)/shard_map/ppermute | solution.py:23
  352.6 14.9 %collective-permute-start.44 = (bf16[144,2048]{1,0:T(8,128)(2,1)S(1)}, bf16[144,2048]{1,0:T(8,128)(2,1)S(1)}, u32[]{:S(2)}, u32[]{:S(2)}) collective-permute-start(bf16[144,2048]{1,0:T(8,128)(2,1)S(1)} %maximum_maximum_fusion.refs_4_), channel_id=1, source_target_pairs={{0,2},{1,3},{2,0},{3,1},{4,6},{5,7},{6,4},{7,5},{8,10},{9,11},{10,... | collective-permute-start | bytes 1769480 | tf_op jit(solution)/shard_map/ppermute | solution.py:23
  353.1 28.9 %collective-permute-start.45 = (bf16[144,2048]{1,0:T(8,128)(2,1)S(1)}, bf16[144,2048]{1,0:T(8,128)(2,1)S(1)}, u32[]{:S(2)}, u32[]{:S(2)}) collective-permute-start(bf16[144,2048]{1,0:T(8,128)(2,1)S(1)} %maximum_maximum_fusion.refs_4_), channel_id=1, source_target_pairs={{0,1},{1,2},{2,3},{3,0},{4,5},{5,6},{6,7},{7,4},{8,9},{9,10},{10,1... | collective-permute-start | bytes 1769480 | tf_op jit(solution)/shard_map/ppermute | solution.py:23
  400.4 2.4 collective-permute-start.46
  (62 other events, 328.1 us)
Sparse Core Ops, SparseCore 0:
  16.7 66.5 all-gather.2
  118.1 65.3 all-gather.4
  297.0 102.1 reduce-scatter.1

commit v2 on v1

--- a/solution.py
+++ b/solution.py
@@ -985,11 +985,12 @@
     block, gathered = stack_attn(mine, came, scalars)
     lengths = jnp.concatenate((first_length, swap(first_length)))
     blocks = spread_near(block)
-    w_kv = stack_blocks(blocks, 0, 768, scalars, "stack_kv", deps=(lengths,))
-    normed_first = enter_rows(tokens, gain_first.reshape(1, D), scalars, deps=blocks[1:])
+    w_kv = stack_blocks(blocks, 0, 768, scalars, "stack_kv")
+    normed_first = enter_rows(tokens, gain_first.reshape(1, D), scalars, deps=(w_kv,))
+    (gathered,) = tie((gathered,), blocks[1:])
     w_goq = lax.all_gather(gathered, XY, axis=0, tiled=True).reshape(4, 4, 2, 64, -1)
     mine, theirs = split_heads(
-        (w_hidden, w_linear, w_down), scalars, "split_mlp", deps=(gathered,)
+        (w_hidden, w_linear, w_down), scalars, "split_mlp", deps=(normed_first,)
     )
     came_mlp = swap(theirs)
     gain_first = gain_first.reshape(1, D)
@@ -1030,7 +1031,7 @@
         [(w_kv, 0, 768)],
         scalars,
         "project_kv",
-        deps=(mask, enter_rows_in, leave_rows_out, fade_in, cosine, sine),
+        deps=(mask, enter_rows_in, leave_rows_out, fade_in, cosine, sine, came_mlp),
     )
     key = rotate(projected[:, DV:], cosine, sine).astype(BF).reshape(2, rows, DK)
     value = projected[:, :DV].astype(BF).reshape(2, rows, DV)
@@ -1038,7 +1039,7 @@
     state_out = ein("gjd,gje->gde", key_out, value).astype(BF)
     came = spread_state(state_out, 1)
     w_mlp = lax.all_gather(
-        stack_blocks((mine, came_mlp), 0, 1536, scalars, "stack_mlp", deps=came),
+        stack_blocks((mine, came_mlp), 0, 1536, scalars, "stack_mlp", deps=(state_out,)),
         XY,
         axis=0,
         tiled=True,

time: 413 us -> 401 us (0.971)
  waiting for transfers between devices: 153 us -> 140 us
    ppermute x6, waiting for transfers between devices: 33.7 us -> 16.9 us  [hop(): return lax.ppermute(value, ('x', 'core', 'ctx'), pairs)]
    ppermute x6, waiting for transfers between devices: 16.1 us -> 25.9 us  [shift_open(): lax.ppermute(value, axis, [(i, i + offset) for i in range(n) if 0 <= i +...]
    unnamed x157 -> x167, local copies, waits for them, and re-layouts: 29.8 us -> 29.8 us
  transfers between devices with their start and end apart: 50 -> 50, of which waited for: 34 -> 33; matrix products, arithmetic and copies ran while one was open for 6% -> 6% of each run, Pallas kernels for 18% -> 19%
where the time goes in v2:
time: 401 us; the launch traced here: 399 us
  waiting for transfers between devices  140 us (35%)
  Pallas kernels  121 us (30%)
  starting transfers between devices  63.7 us (16%)
  local copies, waits for them, and re-layouts  33.7 us (8%)
  other arithmetic  20.2 us (5%)
  between operations  15.9 us (4%)
  matrix products  4.71 us (1%)
    pallas_call x23, Pallas kernels, call(): pl.pallas_call(kernel, out_shape=shapes, grid_spec=pltpu.PrefetchScalarGr...  121 us
    ppermute x18, waiting for transfers between devices, shift(): return lax.ppermute(value, axis, [(i, (i + offset) % n) for i in range(n)])  68.9 us
    unnamed x167, local copies, waits for them, and re-layouts  29.8 us
    ppermute x6, waiting for transfers between devices, shift_open(): lax.ppermute(value, axis, [(i, i + offset) for i in range(n) if 0 <= i +...  25.9 us
    ppermute x18, starting transfers between devices, shift(): return lax.ppermute(value, axis, [(i, (i + offset) % n) for i in range(n)])  19.4 us
    ppermute x6, waiting for transfers between devices, hop(): return lax.ppermute(value, ('x', 'core', 'ctx'), pairs)  16.9 us
    ppermute x6, starting transfers between devices, shift_open(): lax.ppermute(value, axis, [(i, i + offset) for i in range(n) if 0 <= i +...  13.7 us
    ppermute x12, waiting for transfers between devices, swap(): return lax.ppermute(value, 'core', [(0, 1), (1, 0)])  11.7 us
  transfers between devices with their start and end apart: 50, of which 33 were waited for; matrix products, arithmetic and copies ran while one was open for 6% of the time, Pallas kernels for 19%

profile of v2, /device:TPU:1, one launch (start us, length us, event | category | flops | bytes accessed | tf_op | source)
XLA Modules:
  0.0 399.3 jit_solution(17559007853051558866)
XLA Ops:
  7.9 2.7 split_attn.1
  14.1 2.5 stack_attn.1
  17.9 2.5 collective-permute-start.2
  22.8 3.2 collective-permute-done.2.refs_2_
  26.8 1.6 collective-permute-start.8
  36.0 2.5 enter_rows.1.refs_3_.refs_0_.refs_9_
  43.1 2.1 collective-permute-start.6
  49.4 2.5 split_mlp.1
  51.8 1.6 collective-permute-start.9
  54.7 3.3 collective-permute-done.5.refs_3_.refs_2_
  58.0 9.1 %collective-permute-done.6.refs_4_.refs_3_ = bf16[4,2,64,768]{3,2,1,0:T(8,128)(2,1)} collective-permute-done((bf16[4,2,64,768]{3,2,1,0:T(8,128)(2,1)}, bf16[4,2,64,768]{3,2,1,0:T(8,128)(2,1)}, u32[]{:S(2)}, u32[]{:S(2)}) %collective-permute-start.6) | collective-permute-done | bytes 786464 | tf_op jit(solution)/shard_map/ppermute | solution.py:148
  68.2 5.9 %project_kv.1 = f32[512,768]{1,0:T(8,128)S(1)} custom-call(s32[4]{0:T(128)S(1)} %copy-done.33, bf16[256,2048]{1,0:T(8,128)(2,1)} %enter_rows.1.refs_3_.refs_0_.refs_9_, bf16[256,2048]{1,0:T(8,128)(2,1)S(1)} %collective-permute-done.4.refs_1_.refs_4_.refs_10_, bf16[4,2,64,768]{3,2,1,0:T(8,128)(2,1)S(1)} %bitcast.91, ...), custom_call_target="tpu_custom_call" | custom-call | flops 1 | bytes 1 | tf_op jit(solution)/shard_map/project_kv/pallas_call | solution.py:61
  76.8 3.2 collective-permute-start.10
  80.0 4.2 %collective-permute-start.11 = (bf16[2,256,512]{2,1,0:T(8,128)(2,1)S(1)}, bf16[2,256,512]{2,1,0:T(8,128)(2,1)S(1)}, u32[]{:S(2)}, u32[]{:S(2)}) collective-permute-start(bf16[2,256,512]{2,1,0:T(8,128)(2,1)S(1)} %convolution_convert_fusion.refs_2_), channel_id=1, source_target_pairs={{0,8},{4,12},{1,9},{5,13},{2,10},{6,14},{3,11},{7,15},{16,24},{20,... | collective-permute-start | bytes 1572872 | tf_op jit(solution)/shard_map/ppermute | solution.py:28
  84.2 2.1 collective-permute-start.12
  86.3 1.7 pad_maximum_fusion.refs_3_
  88.0 12.7 %collective-permute-done.10.refs_5_ = bf16[2,256,512]{2,1,0:T(8,128)(2,1)S(1)} collective-permute-done((bf16[2,256,512]{2,1,0:T(8,128)(2,1)S(1)}, bf16[2,256,512]{2,1,0:T(8,128)(2,1)S(1)}, u32[]{:S(2)}, u32[]{:S(2)}) %collective-permute-start.10) | collective-permute-done | bytes 524320 | tf_op jit(solution)/shard_map/ppermute | solution.py:28
  100.7 11.3 %collective-permute-done.11.refs_6_ = bf16[2,256,512]{2,1,0:T(8,128)(2,1)S(1)} collective-permute-done((bf16[2,256,512]{2,1,0:T(8,128)(2,1)S(1)}, bf16[2,256,512]{2,1,0:T(8,128)(2,1)S(1)}, u32[]{:S(2)}, u32[]{:S(2)}) %collective-permute-start.11) | collective-permute-done | bytes 524320 | tf_op jit(solution)/shard_map/ppermute | solution.py:28
  112.8 12.8 %retain.1 = (f32[256,2048]{1,0:T(8,128)}, bf16[256,2048]{1,0:T(8,128)(2,1)}, bf16[512,256]{1,0:T(8,128)(2,1)}, bf16[2,256,512]{2,1,0:T(8,128)(2,1)}, bf16[2,256,...) custom-call(s32[4]{0:T(128)} %pad_add_fusion.s_ref, ...), custom_call_target="tpu_custom_call" | custom-call | flops 1 | bytes 1 | tf_op jit(solution)/shard_map/retain/pallas_call | solution.py:61
  126.5 2.5 collective-permute-done.13
  129.0 1.7 add_convert_fusion.9
  130.7 2.9 collective-permute-start.16
  133.6 1.7 collective-permute-start.14
  135.3 9.1 %collective-permute-done.16 = bf16[64,2048]{1,0:T(8,128)(2,1)S(1)} collective-permute-done((bf16[64,2048]{1,0:T(8,128)(2,1)S(1)}, bf16[64,2048]{1,0:T(8,128)(2,1)S(1)}, u32[]{:S(2)}, u32[]{:S(2)}) %collective-permute-start.16) | collective-permute-done | bytes 262176 | tf_op jit(solution)/shard_map/ppermute | solution.py:23
  144.4 2.3 collective-permute-done.14
  151.2 2.2 collective-permute-start.21
  154.5 2.6 collective-permute-done.18.refs_4_
  157.1 7.6 %collective-permute-done.19.refs_5_ = bf16[64,2048]{1,0:T(8,128)(2,1)S(1)} collective-permute-done((bf16[64,2048]{1,0:T(8,128)(2,1)S(1)}, bf16[64,2048]{1,0:T(8,128)(2,1)S(1)}, u32[]{:S(2)}, u32[]{:S(2)}) %collective-permute-start.19) | collective-permute-done | bytes 262176 | tf_op jit(solution)/shard_map/ppermute | solution.py:23
  170.2 2.3 all-gather.5.cloned.1.call-done
  172.5 14.4 %mlp.1 = (f32[256,2048]{1,0:T(8,128)}, bf16[256,2048]{1,0:T(8,128)(2,1)}, f32[8,2048]{1,0:T(8,128)}, bf16[512,1024]{1,0:T(8,128)(2,1)}, bf16[512,512]{1,0:T(8,128)(2,1)}) custom-call(s32[4]{0:T(128)} %pad_add_fusion.s_ref, bf16[256,2048]{1,0:T(8,128)(2,1)} %copy-done.18, bf16[256,2048]{1,0:T(8,128)(2,1)} %copy-done.48, bf16[256,2048]{1,0:T(8,128)(2,1)} %copy-done.9, ...), custom_call_target="tpu_custom_call" | custom-call | flops 1 | bytes 1 | tf_op jit(solution)/shard_map/mlp/pallas_call | solution.py:61
  187.6 2.5 collective-permute-done.22
  190.1 1.6 add_convert_fusion.4
  191.7 2.7 collective-permute-start.25
  194.4 1.7 collective-permute-start.23
  196.1 6.9 %weight_mlp.1 = (bf16[4,4,2,64,3584]{4,3,2,1,0:T(8,128)(2,1)}, f32[8,128]{1,0:T(8,128)}) custom-call(s32[4]{0:T(128)} %pad_add_fusion.s_ref, bf16[256,2048]{1,0:T(8,128)(2,1)} %copy-done.18, bf16[256,2048]{1,0:T(8,128)(2,1)} %copy-done.48, bf16[512,1024]{1,0:T(8,128)(2,1)} %get-tuple-element.78.refs_2_), custom_call_target="tpu_custom_call" | custom-call | flops 1 | bytes 1 | tf_op jit(solution)/shard_map/weight_mlp/pallas_call | solution.py:61
  203.0 2.2 collective-permute-done.25
  205.2 2.3 collective-permute-done.23
  207.5 1.9 add_convert_fusion.1.refs_0_
  211.8 2.8 copy-done.4
  215.6 2.8 project_down.1
  220.7 5.5 %collective-permute-done.28.refs_6_ = bf16[64,2048]{1,0:T(8,128)(2,1)S(1)} collective-permute-done((bf16[64,2048]{1,0:T(8,128)(2,1)}, bf16[64,2048]{1,0:T(8,128)(2,1)S(1)}, u32[]{:S(2)}, u32[]{:S(2)}) %collective-permute-start.28) | collective-permute-done | bytes 262176 | tf_op jit(solution)/shard_map/ppermute | solution.py:23
  227.0 6.1 %second_back.1 = (f32[256,2048]{1,0:T(8,128)}, bf16[256,2048]{1,0:T(8,128)(2,1)}) custom-call(s32[4]{0:T(128)} %pad_add_fusion.s_ref, f32[256,2048]{1,0:T(8,128)} %copy-done.10, f32[256,2048]{1,0:T(8,128)} %refs_1_.6, f32[1,2048]{1,0:T(1,128)} %bitcast.106, bf16[64,2048]{1,0:T(8,128)(2,1)} %tie.6.refs_2_.refs_3_, bf16[64,2048]{1,0:T(8,128)(2,1)} %copy-done.71, ...), custom_call_target="tpu_custom_call" | custom-call | flops 1 | bytes 1 | tf_op jit(solution)/shard_map/second_back/pallas_call | solution.py:61
  233.6 2.4 collective-permute-done.29.refs_1_
  237.0 9.7 %back_gate.1 = (bf16[512,512]{1,0:T(8,128)(2,1)}, bf16[512,512]{1,0:T(8,128)(2,1)}, bf16[2,256,512]{2,1,0:T(8,128)(2,1)}) custom-call(s32[4]{0:T(128)} %pad_add_fusion.s_ref, bf16[256,2048]{1,0:T(8,128)(2,1)} %get-tuple-element.83.refs_0_, bf16[256,2048]{1,0:T(8,128)(2,1)} %copy-done.46, bf16[4,4,2,64,1280]{4,3,2,1,0:T(8,128)(2,1)} %bitcast.83, ...), custom_call_target="tpu_custom_call" | custom-call | flops 1 | bytes 1 | tf_op jit(solution)/shard_map/back_gate/pallas_call | solution.py:61
  253.8 7.2 %weight_og.1 = (bf16[4,4,2,64,3584]{4,3,2,1,0:T(8,128)(2,1)}, f32[8,128]{1,0:T(8,128)}) custom-call(s32[4]{0:T(128)} %pad_add_fusion.s_ref, bf16[256,2048]{1,0:T(8,128)(2,1)} %get-tuple-element.83.refs_0_, bf16[256,2048]{1,0:T(8,128)(2,1)} %copy-done.46, bf16[512,512]{1,0:T(8,128)(2,1)} %get-tuple-element.90.refs_2_, ...), custom_call_target="tpu_custom_call", output_to_operand_aliasing={{0}: (7, {})} | custom-call | flops 1 | bytes 1 | tf_op jit(solution)/shard_map/weight_og/pallas_call | solution.py:61
  261.1 5.5 %weight_down.1 = (bf16[4,4,2,64,3584]{4,3,2,1,0:T(8,128)(2,1)}, f32[8,128]{1,0:T(8,128)}) custom-call(s32[4]{0:T(128)} %pad_add_fusion.s_ref, bf16[256,2048]{1,0:T(8,128)(2,1)} %copy-done.9, bf16[256,2048]{1,0:T(8,128)(2,1)} %copy-done.47, bf16[512,512]{1,0:T(8,128)(2,1)} %get-tuple-element.80.refs_0_.refs_2_, ...), custom_call_target="tpu_custom_call", output_to_operand_aliasing={{0}: (4, {})} | custom-call | flops 1 | bytes 1 | tf_op jit(solution)/shard_map/weight_down/pallas_call | solution.py:61
  266.6 5.1 %weight_query.1 = (bf16[4,4,2,64,3584]{4,3,2,1,0:T(8,128)(2,1)}, f32[8,128]{1,0:T(8,128)}) custom-call(s32[4]{0:T(128)} %pad_add_fusion.s_ref, bf16[256,2048]{1,0:T(8,128)(2,1)} %enter_rows.1.refs_3_.refs_0_.refs_9_, bf16[256,2048]{1,0:T(8,128)(2,1)} %copy-done.1, ...), custom_call_target="tpu_custom_call", output_to_operand_aliasing={{0}: (4, {})} | custom-call | flops 1 | bytes 1 | tf_op jit(solution)/shard_map/weight_query/pallas_call | solution.py:61
  275.0 1.9 collective-permute-done.32.refs_4_
  276.9 8.0 %weight_last.1 = (bf16[4,4,2,64,3584]{4,3,2,1,0:T(8,128)(2,1)}, f32[8,128]{1,0:T(8,128)}, bf16[512,768]{1,0:T(8,128)(2,1)}) custom-call(s32[4]{0:T(128)} %pad_add_fusion.s_ref, bf16[256,2048]{1,0:T(8,128)(2,1)} %enter_rows.1.refs_3_.refs_0_.refs_9_, bf16[256,2048]{1,0:T(8,128)(2,1)} %copy-done.1, ...), custom_call_target="tpu_custom_call", output_to_operand_aliasing={{0}: (14, {})} | custom-call | flops 1 | bytes 1 | tf_op jit(solution)/shard_map/weight_last/pallas_call | solution.py:61
  286.8 2.5 copy-done
  289.3 7.5 %back_attn.1 = (f32[256,2048]{1,0:T(8,128)S(1)}, bf16[256,2048]{1,0:T(8,128)(2,1)S(1)}, f32[8,2048]{1,0:T(8,128)S(1)}) custom-call(s32[4]{0:T(128)S(1)} %copy-done.36, bf16[512,768]{1,0:T(8,128)(2,1)S(1)} %copy-done.25, bf16[4,2,64,768]{3,2,1,0:T(8,128)(2,1)S(1)} %bitcast.92, bf16[4,2,64,768]{3,2,1,0:T(8,128)(2,1)} %collective-permute-done.5.refs_3_.refs_2_, ...), custom_call_target="tpu_custom_call" | custom-call | flops 1 | bytes 1 | tf_op jit(solution)/shard_map/back_attn/pallas_call | solution.py:61
  304.6 5.7 %third_blocks.1 = (bf16[128,2048]{1,0:T(8,128)(2,1)}, bf16[128,2048]{1,0:T(8,128)(2,1)}, bf16[128,2048]{1,0:T(8,128)(2,1)}, bf16[128,2048]{1,0:T(8,128)(2,1)}) custom-call(s32[4]{0:T(128)} %pad_add_fusion.s_ref, f32[256,2048]{1,0:T(8,128)} %copy-done.23, bf16[256,2048]{1,0:T(8,128)(2,1)} %copy-done.59, f32[256,2048]{1,0:T(8,128)} %copy-done.22, ...), custom_call_target="tpu_custom_call" | custom-call | flops 1 | bytes 1 | tf_op jit(solution)/shard_map/third_blocks/pallas_call | solution.py:61
  312.2 5.0 %collective-permute-start.40 = (f32[2,2048]{1,0:T(2,128)S(1)}, f32[2,2048]{1,0:T(2,128)S(1)}, u32[]{:S(2)}, u32[]{:S(2)}) collective-permute-start(f32[2,2048]{1,0:T(2,128)S(1)} %fusion.34), channel_id=1, source_target_pairs={{0,12},{4,8},{8,4},{12,0},{1,13},{5,9},{9,5},{13,1},{2,14},{6,10},... | collective-permute-start | bytes 49160 | tf_op jit(solution)/shard_map/ppermute | solution.py:1141
  317.2 1.9 collective-permute-done.40
  320.3 2.1 collective-permute-done.41
  322.5 2.3 collective-permute-start.42
  324.9 2.0 collective-permute-done.42
  326.9 8.0 %collective-permute-done.35 = bf16[128,2048]{1,0:T(8,128)(2,1)S(1)} collective-permute-done((bf16[128,2048]{1,0:T(8,128)(2,1)}, bf16[128,2048]{1,0:T(8,128)(2,1)S(1)}, u32[]{:S(2)}, u32[]{:S(2)}) %collective-permute-start.35) | collective-permute-done | bytes 524320 | tf_op jit(solution)/shard_map/ppermute | solution.py:23
  336.5 2.3 collective-permute-start.43
  340.1 12.2 %collective-permute-done.43.refs_5_ = bf16[144,2048]{1,0:T(8,128)(2,1)S(1)} collective-permute-done((bf16[144,2048]{1,0:T(8,128)(2,1)S(1)}, bf16[144,2048]{1,0:T(8,128)(2,1)S(1)}, u32[]{:S(2)}, u32[]{:S(2)}) %collective-permute-start.43) | collective-permute-done | bytes 589856 | tf_op jit(solution)/shard_map/ppermute | solution.py:23
  353.7 14.5 %collective-permute-done.45.refs_7_ = bf16[144,2048]{1,0:T(8,128)(2,1)S(1)} collective-permute-done((bf16[144,2048]{1,0:T(8,128)(2,1)S(1)}, bf16[144,2048]{1,0:T(8,128)(2,1)S(1)}, u32[]{:S(2)}, u32[]{:S(2)}) %collective-permute-start.45) | collective-permute-done | bytes 589856 | tf_op jit(solution)/shard_map/ppermute | solution.py:23
  369.1 7.3 %leave_rows.1 = (f32[256,2048]{1,0:T(8,128)}, f32[256,2048]{1,0:T(8,128)}) custom-call(s32[4]{0:T(128)} %pad_add_fusion.s_ref, f32[256,2048]{1,0:T(8,128)} %copy-done.10, f32[256,2048]{1,0:T(8,128)} %refs_1_.7, f32[256,2048]{1,0:T(8,128)} %get-tuple-element.82.refs_2_, f32[1,2048]{1,0:T(1,128)} %bitcast.104, bf16[144,2048]{1,0:T(8,128)(2,1)} %copy-done.50, ...), custom_call_target="tpu_custom_call" | custom-call | flops 1 | bytes 1 | tf_op jit(solution)/shard_map/leave_rows/pallas_call | solution.py:61
  379.8 7.4 %reduce-scatter.2.cloned.1.call-done.refs_0_ = bf16[128,3584]{1,0:T(8,128)(2,1)} async-done(((bf16[2048,3584]{1,0:T(8,128)(2,1)}), bf16[128,3584]{1,0:T(8,128)(2,1)}) %reduce-scatter.2.cloned.1.call-update) | async-done | bytes 917520 | tf_op jit(solution)/shard_map/reduce_scatter | solution.py:1122
  390.9 1.8 join_heads.1
  (284 shorter events, 85.3 us)
Async XLA Ops:
  7.2 21.2 %copy-start.80 = (f32[2]{0:T(128)S(1)}, f32[2]{0:T(128)}, u32[]{:S(2)}) copy-start(f32[2]{0:T(128)} %param.26) | copy-start | bytes 28
  7.2 105.6 %all-gather.3.cloned.1.call-start = ((), (), s32[]{:S(2)}) async-start(), calls=%async_computation.1 | async-start | bytes 5570560 | tf_op jit(solution)/shard_map/all_gather | solution.py:991
  7.9 23.7 %copy-start.32 = (s32[4]{0:T(128)S(1)}, s32[4]{0:T(128)}, u32[]{:S(2)}) copy-start(s32[4]{0:T(128)} %pad_add_fusion.s_ref) | copy-start | bytes 52
  10.6 25.4 %copy-start.5 = (f32[256,2048]{1,0:T(8,128)S(1)}, f32[256,2048]{1,0:T(8,128)}, u32[]{:S(2)}) copy-start(f32[256,2048]{1,0:T(8,128)} %refs_1_.7) | copy-start | bytes 6291460
  10.6 25.4 %copy-start.40 = (f32[2048]{0:T(1024)S(1)}, f32[2048]{0:T(1024)}, u32[]{:S(2)}) copy-start(f32[2048]{0:T(1024)} %param.16) | copy-start | bytes 24580
  10.6 2.8 collective-permute-start
  16.6 6.2 %collective-permute-start.1 = (bf16[128,768]{1,0:T(8,128)(2,1)}, bf16[128,768]{1,0:T(8,128)(2,1)S(1)}, u32[]{:S(2)}, u32[]{:S(2)}) collective-permute-start(bf16[128,768]{1,0:T(8,128)(2,1)} %get-tuple-element.68.refs_0_), channel_id=1, source_target_pairs={{0,4},{4,8},{8,12},{12,0},{16,48},{20,52},{24,56},{28,60},{32,36},... | collective-permute-start | bytes 589832 | tf_op jit(solution)/shard_map/ppermute | solution.py:148
  17.9 8.1 %collective-permute-start.2 = (bf16[128,768]{1,0:T(8,128)(2,1)}, bf16[128,768]{1,0:T(8,128)(2,1)S(1)}, u32[]{:S(2)}, u32[]{:S(2)}) collective-permute-start(bf16[128,768]{1,0:T(8,128)(2,1)} %get-tuple-element.68.refs_0_), channel_id=1, source_target_pairs={{0,8},{4,12},{8,0},{12,4},{16,80},{20,84},{24,88},{28,92},{32,40},... | collective-permute-start | bytes 589832 | tf_op jit(solution)/shard_map/ppermute | solution.py:148
  20.3 5.7 %collective-permute-start.3 = (bf16[128,768]{1,0:T(8,128)(2,1)}, bf16[128,768]{1,0:T(8,128)(2,1)S(1)}, u32[]{:S(2)}, u32[]{:S(2)}) collective-permute-start(bf16[128,768]{1,0:T(8,128)(2,1)} %get-tuple-element.68.refs_0_), channel_id=1, source_target_pairs={{0,12},{4,0},{8,4},{12,8},{16,112},{20,116},{24,120},{28,124},{32,... | collective-permute-start | bytes 589832 | tf_op jit(solution)/shard_map/ppermute | solution.py:148
  26.8 145.7 %all-gather.5.cloned.1.call-start = ((), (), s32[]{:S(2)}) async-start(), calls=%async_computation.2 | async-start | bytes 6684672 | tf_op jit(solution)/shard_map/all_gather | solution.py:1041
  26.8 19.6 %collective-permute-start.8 = (s32[1]{0:T(128)}, s32[1]{0:T(128)}, u32[]{:S(2)}, u32[]{:S(2)}) collective-permute-start(s32[1]{0:T(128)} %param.27), channel_id=1, source_target_pairs={{0,16},{16,0},{1,17},{17,1},{2,18},{18,2},{3,19},{19,3},{4,20},{20... | collective-permute-start | bytes 20 | tf_op jit(solution)/shard_map/ppermute | solution.py:34
  39.4 28.8 %copy-start.33 = (s32[4]{0:T(128)S(1)}, s32[4]{0:T(128)}, u32[]{:S(2)}) copy-start(s32[4]{0:T(128)} %pad_add_fusion.s_ref) | copy-start | bytes 52
  39.4 27.7 %collective-permute-start.4 = (bf16[256,2048]{1,0:T(8,128)(2,1)}, bf16[256,2048]{1,0:T(8,128)(2,1)S(1)}, u32[]{:S(2)}, u32[]{:S(2)}) collective-permute-start(bf16[256,2048]{1,0:T(8,128)(2,1)} %enter_rows.1.refs_3_.refs_0_.refs_9_), channel_id=1, source_target_pairs={{0,16},{16,0},{1,17},{17,1},{2,18},{18,2},{3,19},{19,3},{4,20},{20... | collective-permute-start | bytes 3145736 | tf_op jit(solution)/shard_map/ppermute | solution.py:34
  41.8 16.2 %collective-permute-start.5 = (bf16[4,2,64,768]{3,2,1,0:T(8,128)(2,1)}, bf16[4,2,64,768]{3,2,1,0:T(8,128)(2,1)}, u32[]{:S(2)}, u32[]{:S(2)}) collective-permute-start(bf16[4,2,64,768]{3,2,1,0:T(8,128)(2,1)} %bitcast.88), channel_id=1, source_target_pairs={{0,32},{4,36},{8,40},{12,44},{16,20},{20,24},{24,28},{28,16},{32,6... | collective-permute-start | bytes 2359304 | tf_op jit(solution)/shard_map/ppermute | solution.py:148
  43.1 24.0 %collective-permute-start.6 = (bf16[4,2,64,768]{3,2,1,0:T(8,128)(2,1)}, bf16[4,2,64,768]{3,2,1,0:T(8,128)(2,1)}, u32[]{:S(2)}, u32[]{:S(2)}) collective-permute-start(bf16[4,2,64,768]{3,2,1,0:T(8,128)(2,1)} %bitcast.89), channel_id=1, source_target_pairs={{0,64},{4,68},{8,72},{12,76},{16,24},{20,28},{24,16},{28,20},{32,9... | collective-permute-start | bytes 2359304 | tf_op jit(solution)/shard_map/ppermute | solution.py:148
  45.2 21.9 %collective-permute-start.7 = (bf16[4,2,64,768]{3,2,1,0:T(8,128)(2,1)}, bf16[4,2,64,768]{3,2,1,0:T(8,128)(2,1)}, u32[]{:S(2)}, u32[]{:S(2)}) collective-permute-start(bf16[4,2,64,768]{3,2,1,0:T(8,128)(2,1)} %bitcast.90), channel_id=1, source_target_pairs={{0,96},{4,100},{8,104},{12,108},{16,28},{20,16},{24,20},{28,24},{3... | collective-permute-start | bytes 2359304 | tf_op jit(solution)/shard_map/ppermute | solution.py:148
  48.6 25.6 %copy-start.16 = (f32[1,512]{0,1:T(8,128)}, f32[1,512]{0,1:T(8,128)S(1)}, u32[]{:S(2)}) copy-start(f32[1,512]{0,1:T(8,128)S(1)} %copy.50) | copy-start | bytes 6148
  51.8 2.8 collective-permute-start.9
  54.5 19.7 %copy-start.12 = (f32[2,256,256]{2,1,0:T(8,128)}, f32[2,256,256]{2,1,0:T(8,128)S(1)}, u32[]{:S(2)}) copy-start(f32[2,256,256]{2,1,0:T(8,128)S(1)} %and_select_fusion.refs_6_.refs_9_) | copy-start | bytes 1572868
  74.4 38.4 %copy-start.44 = (bf16[512,512]{1,0:T(8,128)(2,1)}, bf16[512,512]{1,0:T(8,128)(2,1)S(1)}, u32[]{:S(2)}) copy-start(bf16[512,512]{1,0:T(8,128)(2,1)S(1)} %slice.183) | copy-start | bytes 1572868
  75.0 50.6 %copy-start.49 = (bf16[2,256,256]{2,1,0:T(8,128)(2,1)}, bf16[2,256,256]{2,1,0:T(8,128)(2,1)S(1)}, u32[]{:S(2)}) copy-start(bf16[2,256,256]{2,1,0:T(8,128)(2,1)S(1)} %multiply_convert_fusion.refs_7_) | copy-start | bytes 786436
  76.7 310.5 %reduce-scatter.2.cloned.1.call-start = ((), (), s32[]{:S(2)}) async-start(), calls=%async_computation.3 | async-start | bytes 15597568 | tf_op jit(solution)/shard_map/reduce_scatter | solution.py:1122
  76.8 23.9 %collective-permute-start.10 = (bf16[2,256,512]{2,1,0:T(8,128)(2,1)S(1)}, bf16[2,256,512]{2,1,0:T(8,128)(2,1)S(1)}, u32[]{:S(2)}, u32[]{:S(2)}) collective-permute-start(bf16[2,256,512]{2,1,0:T(8,128)(2,1)S(1)} %convolution_convert_fusion.refs_2_), channel_id=1, source_target_pairs={{0,4},{4,8},{8,12},{1,5},{5,9},{9,13},{2,6},{6,10},{10,14},{3,7},{... | collective-permute-start | bytes 1572872 | tf_op jit(solution)/shard_map/ppermute | solution.py:28
  80.0 32.0 %collective-permute-start.11 = (bf16[2,256,512]{2,1,0:T(8,128)(2,1)S(1)}, bf16[2,256,512]{2,1,0:T(8,128)(2,1)S(1)}, u32[]{:S(2)}, u32[]{:S(2)}) collective-permute-start(bf16[2,256,512]{2,1,0:T(8,128)(2,1)S(1)} %convolution_convert_fusion.refs_2_), channel_id=1, source_target_pairs={{0,8},{4,12},{1,9},{5,13},{2,10},{6,14},{3,11},{7,15},{16,24},{20,... | collective-permute-start | bytes 1572872 | tf_op jit(solution)/shard_map/ppermute | solution.py:28
  84.2 28.6 %collective-permute-start.12 = (bf16[2,256,512]{2,1,0:T(8,128)(2,1)S(1)}, bf16[2,256,512]{2,1,0:T(8,128)(2,1)}, u32[]{:S(2)}, u32[]{:S(2)}) collective-permute-start(bf16[2,256,512]{2,1,0:T(8,128)(2,1)S(1)} %convolution_convert_fusion.refs_2_), channel_id=1, source_target_pairs={{0,12},{1,13},{2,14},{3,15},{16,28},{17,29},{18,30},{19,31},{32,44... | collective-permute-start | bytes 1572872 | tf_op jit(solution)/shard_map/ppermute | solution.py:28
  125.7 3.4 collective-permute-start.13
  129.0 21.4 %copy-start.2 = (bf16[256,2048]{1,0:T(8,128)(2,1)S(1)}, bf16[256,2048]{1,0:T(8,128)(2,1)}, u32[]{:S(2)}) copy-start(bf16[256,2048]{1,0:T(8,128)(2,1)} %copy-done.1) | copy-start | bytes 3145732
  129.0 21.4 %copy-start.11 = (f32[256,2048]{1,0:T(8,128)S(1)}, f32[256,2048]{1,0:T(8,128)}, u32[]{:S(2)}) copy-start(f32[256,2048]{1,0:T(8,128)} %refs_1_.6) | copy-start | bytes 6291460
  129.0 21.4 %copy-start.34 = (s32[4]{0:T(128)S(1)}, s32[4]{0:T(128)}, u32[]{:S(2)}) copy-start(s32[4]{0:T(128)} %pad_add_fusion.s_ref) | copy-start | bytes 52
  130.7 13.7 %collective-permute-start.16 = (bf16[64,2048]{1,0:T(8,128)(2,1)S(1)}, bf16[64,2048]{1,0:T(8,128)(2,1)S(1)}, u32[]{:S(2)}, u32[]{:S(2)}) collective-permute-start(bf16[64,2048]{1,0:T(8,128)(2,1)S(1)} %get-tuple-element.124), channel_id=1, source_target_pairs={{0,3},{1,0},{2,1},{3,2},{4,7},{5,4},{6,5},{7,6},{8,11},{9,8},{10,9... | collective-permute-start | bytes 786440 | tf_op jit(solution)/shard_map/ppermute | solution.py:23
  133.6 10.8 %collective-permute-start.15 = (bf16[64,2048]{1,0:T(8,128)(2,1)S(1)}, bf16[64,2048]{1,0:T(8,128)(2,1)S(1)}, u32[]{:S(2)}, u32[]{:S(2)}) collective-permute-start(bf16[64,2048]{1,0:T(8,128)(2,1)S(1)} %get-tuple-element.125), channel_id=1, source_target_pairs={{0,1},{1,2},{2,3},{3,0},{4,5},{5,6},{6,7},{7,4},{8,9},{9,10},{10,1... | collective-permute-start | bytes 786440 | tf_op jit(solution)/shard_map/ppermute | solution.py:23
  133.6 13.0 %collective-permute-start.14 = (bf16[64,2048]{1,0:T(8,128)(2,1)S(1)}, bf16[64,2048]{1,0:T(8,128)(2,1)S(1)}, u32[]{:S(2)}, u32[]{:S(2)}) collective-permute-start(bf16[64,2048]{1,0:T(8,128)(2,1)S(1)} %get-tuple-element.123), channel_id=1, source_target_pairs={{0,2},{1,3},{2,0},{3,1},{4,6},{5,7},{6,4},{7,5},{8,10},{9,11},{10,... | collective-permute-start | bytes 786440 | tf_op jit(solution)/shard_map/ppermute | solution.py:23
  147.9 6.6 %collective-permute-start.17 = (bf16[64,2048]{1,0:T(8,128)(2,1)S(1)}, bf16[64,2048]{1,0:T(8,128)(2,1)S(1)}, u32[]{:S(2)}, u32[]{:S(2)}) collective-permute-start(bf16[64,2048]{1,0:T(8,128)(2,1)S(1)} %add_convert_fusion.6.refs_2_), channel_id=1, source_target_pairs={{0,3},{1,0},{2,1},{3,2},{4,7},{5,4},{6,5},{7,6},{8,11},{9,8},{10,9... | collective-permute-start | bytes 786440 | tf_op jit(solution)/shard_map/ppermute | solution.py:23
  149.3 7.9 %collective-permute-start.18 = (bf16[64,2048]{1,0:T(8,128)(2,1)S(1)}, bf16[64,2048]{1,0:T(8,128)(2,1)S(1)}, u32[]{:S(2)}, u32[]{:S(2)}) collective-permute-start(bf16[64,2048]{1,0:T(8,128)(2,1)S(1)} %add_convert_fusion.6.refs_2_), channel_id=1, source_target_pairs={{0,2},{1,3},{2,0},{3,1},{4,6},{5,7},{6,4},{7,5},{8,10},{9,11},{10,... | collective-permute-start | bytes 786440 | tf_op jit(solution)/shard_map/ppermute | solution.py:23
  149.6 15.1 %collective-permute-start.19 = (bf16[64,2048]{1,0:T(8,128)(2,1)S(1)}, bf16[64,2048]{1,0:T(8,128)(2,1)S(1)}, u32[]{:S(2)}, u32[]{:S(2)}) collective-permute-start(bf16[64,2048]{1,0:T(8,128)(2,1)S(1)} %add_convert_fusion.6.refs_2_), channel_id=1, source_target_pairs={{0,1},{1,2},{2,3},{3,0},{4,5},{5,6},{6,7},{7,4},{8,9},{9,10},{10,1... | collective-permute-start | bytes 786440 | tf_op jit(solution)/shard_map/ppermute | solution.py:23
  151.2 21.3 %copy-start.9 = (bf16[256,2048]{1,0:T(8,128)(2,1)}, bf16[256,2048]{1,0:T(8,128)(2,1)S(1)}, u32[]{:S(2)}) copy-start(bf16[256,2048]{1,0:T(8,128)(2,1)S(1)} %low_rows.1.refs_2_.refs_0_) | copy-start | bytes 3145732
  151.2 16.7 %collective-permute-start.21 = (bf16[256,2048]{1,0:T(8,128)(2,1)S(1)}, bf16[256,2048]{1,0:T(8,128)(2,1)S(1)}, u32[]{:S(2)}, u32[]{:S(2)}) collective-permute-start(bf16[256,2048]{1,0:T(8,128)(2,1)S(1)} %low_rows.1.refs_2_.refs_0_), channel_id=1, source_target_pairs={{0,16},{16,0},{1,17},{17,1},{2,18},{18,2},{3,19},{19,3},{4,20},{20... | collective-permute-start | bytes 3145736 | tf_op jit(solution)/shard_map/ppermute | solution.py:34
  167.5 2.7 collective-permute-start.20
  186.9 3.3 collective-permute-start.22
  191.7 13.5 %collective-permute-start.25 = (bf16[64,2048]{1,0:T(8,128)(2,1)S(1)}, bf16[64,2048]{1,0:T(8,128)(2,1)S(1)}, u32[]{:S(2)}, u32[]{:S(2)}) collective-permute-start(bf16[64,2048]{1,0:T(8,128)(2,1)S(1)} %get-tuple-element.121), channel_id=1, source_target_pairs={{0,3},{1,0},{2,1},{3,2},{4,7},{5,4},{6,5},{7,6},{8,11},{9,8},{10,9... | collective-permute-start | bytes 786440 | tf_op jit(solution)/shard_map/ppermute | solution.py:23
  194.4 10.8 %collective-permute-start.24 = (bf16[64,2048]{1,0:T(8,128)(2,1)S(1)}, bf16[64,2048]{1,0:T(8,128)(2,1)S(1)}, u32[]{:S(2)}, u32[]{:S(2)}) collective-permute-start(bf16[64,2048]{1,0:T(8,128)(2,1)S(1)} %get-tuple-element.122), channel_id=1, source_target_pairs={{0,1},{1,2},{2,3},{3,0},{4,5},{5,6},{6,7},{7,4},{8,9},{9,10},{10,1... | collective-permute-start | bytes 786440 | tf_op jit(solution)/shard_map/ppermute | solution.py:23
  194.4 13.1 %collective-permute-start.23 = (bf16[64,2048]{1,0:T(8,128)(2,1)S(1)}, bf16[64,2048]{1,0:T(8,128)(2,1)S(1)}, u32[]{:S(2)}, u32[]{:S(2)}) collective-permute-start(bf16[64,2048]{1,0:T(8,128)(2,1)S(1)} %get-tuple-element.120), channel_id=1, source_target_pairs={{0,2},{1,3},{2,0},{3,1},{4,6},{5,7},{6,4},{7,5},{8,10},{9,11},{10,... | collective-permute-start | bytes 786440 | tf_op jit(solution)/shard_map/ppermute | solution.py:23
  209.4 11.3 %collective-permute-start.26 = (bf16[64,2048]{1,0:T(8,128)(2,1)}, bf16[64,2048]{1,0:T(8,128)(2,1)S(1)}, u32[]{:S(2)}, u32[]{:S(2)}) collective-permute-start(bf16[64,2048]{1,0:T(8,128)(2,1)} %tie.6.refs_2_.refs_3_), channel_id=1, source_target_pairs={{0,3},{1,0},{2,1},{3,2},{4,7},{5,4},{6,5},{7,6},{8,11},{9,8},{10,9... | collective-permute-start | bytes 786440 | tf_op jit(solution)/shard_map/ppermute | solution.py:23
  210.7 10.0 %collective-permute-start.27 = (bf16[64,2048]{1,0:T(8,128)(2,1)}, bf16[64,2048]{1,0:T(8,128)(2,1)S(1)}, u32[]{:S(2)}, u32[]{:S(2)}) collective-permute-start(bf16[64,2048]{1,0:T(8,128)(2,1)} %tie.6.refs_2_.refs_3_), channel_id=1, source_target_pairs={{0,2},{1,3},{2,0},{3,1},{4,6},{5,7},{6,4},{7,5},{8,10},{9,11},{10,... | collective-permute-start | bytes 786440 | tf_op jit(solution)/shard_map/ppermute | solution.py:23
  211.0 15.3 %collective-permute-start.28 = (bf16[64,2048]{1,0:T(8,128)(2,1)}, bf16[64,2048]{1,0:T(8,128)(2,1)S(1)}, u32[]{:S(2)}, u32[]{:S(2)}) collective-permute-start(bf16[64,2048]{1,0:T(8,128)(2,1)} %tie.6.refs_2_.refs_3_), channel_id=1, source_target_pairs={{0,1},{1,2},{2,3},{3,0},{4,5},{5,6},{6,7},{7,4},{8,9},{9,10},{10,1... | collective-permute-start | bytes 786440 | tf_op jit(solution)/shard_map/ppermute | solution.py:23
  233.0 3.0 collective-permute-start.29
  246.7 27.5 %collective-permute-start.30 = (bf16[2,256,512]{2,1,0:T(8,128)(2,1)}, bf16[2,256,512]{2,1,0:T(8,128)(2,1)S(1)}, u32[]{:S(2)}, u32[]{:S(2)}) collective-permute-start(bf16[2,256,512]{2,1,0:T(8,128)(2,1)} %get-tuple-element.87.refs_7_), channel_id=1, source_target_pairs={{4,0},{8,4},{12,8},{5,1},{9,5},{13,9},{6,2},{10,6},{14,10},{7,3},{... | collective-permute-start | bytes 1572872 | tf_op jit(solution)/shard_map/ppermute | solution.py:28
  248.1 26.9 %collective-permute-start.31 = (bf16[2,256,512]{2,1,0:T(8,128)(2,1)}, bf16[2,256,512]{2,1,0:T(8,128)(2,1)S(1)}, u32[]{:S(2)}, u32[]{:S(2)}) collective-permute-start(bf16[2,256,512]{2,1,0:T(8,128)(2,1)} %get-tuple-element.87.refs_7_), channel_id=1, source_target_pairs={{8,0},{12,4},{9,1},{13,5},{10,2},{14,6},{11,3},{15,7},{24,16},{28,... | collective-permute-start | bytes 1572872 | tf_op jit(solution)/shard_map/ppermute | solution.py:28
  249.4 27.5 %collective-permute-start.32 = (bf16[2,256,512]{2,1,0:T(8,128)(2,1)}, bf16[2,256,512]{2,1,0:T(8,128)(2,1)}, u32[]{:S(2)}, u32[]{:S(2)}) collective-permute-start(bf16[2,256,512]{2,1,0:T(8,128)(2,1)} %get-tuple-element.87.refs_7_), channel_id=1, source_target_pairs={{12,0},{13,1},{14,2},{15,3},{28,16},{29,17},{30,18},{31,19},{44,32... | collective-permute-start | bytes 1572872 | tf_op jit(solution)/shard_map/ppermute | solution.py:28
  299.1 4.0 collective-permute-start.33
  299.6 4.0 %collective-permute-start.34 = (bf16[256,2048]{1,0:T(8,128)(2,1)}, bf16[256,2048]{1,0:T(8,128)(2,1)S(1)}, u32[]{:S(2)}, u32[]{:S(2)}) collective-permute-start(bf16[256,2048]{1,0:T(8,128)(2,1)} %tie.8), channel_id=1, source_target_pairs={{0,16},{16,0},{1,17},{17,1},{2,18},{18,2},{3,19},{19,3},{4,20},{20... | collective-permute-start | bytes 3145736 | tf_op jit(solution)/shard_map/ppermute | solution.py:34
  300.5 1.4 collective-permute-start.38
  302.0 10.2 %collective-permute-start.39 = (f32[2,2048]{1,0:T(2,128)S(1)}, f32[2,2048]{1,0:T(2,128)S(1)}, u32[]{:S(2)}, u32[]{:S(2)}) collective-permute-start(f32[2,2048]{1,0:T(2,128)S(1)} %fusion.17), channel_id=1, source_target_pairs={{0,4},{4,0},{8,12},{12,8},{1,5},{5,1},{9,13},{13,9},{2,6},{6,2},{1... | collective-permute-start | bytes 49160 | tf_op jit(solution)/shard_map/ppermute | solution.py:1141
  310.3 16.6 %collective-permute-start.37 = (bf16[128,2048]{1,0:T(8,128)(2,1)}, bf16[128,2048]{1,0:T(8,128)(2,1)S(1)}, u32[]{:S(2)}, u32[]{:S(2)}) collective-permute-start(bf16[128,2048]{1,0:T(8,128)(2,1)} %get-tuple-element.106), channel_id=1, source_target_pairs={{0,3},{1,0},{2,1},{3,2},{4,7},{5,4},{6,5},{7,6},{8,11},{9,8},{10,9... | collective-permute-start | bytes 1572872 | tf_op jit(solution)/shard_map/ppermute | solution.py:23
  310.8 16.2 %collective-permute-start.36 = (bf16[128,2048]{1,0:T(8,128)(2,1)}, bf16[128,2048]{1,0:T(8,128)(2,1)S(1)}, u32[]{:S(2)}, u32[]{:S(2)}) collective-permute-start(bf16[128,2048]{1,0:T(8,128)(2,1)} %get-tuple-element.105), channel_id=1, source_target_pairs={{0,1},{1,2},{2,3},{3,0},{4,5},{5,6},{6,7},{7,4},{8,9},{9,10},{10,1... | collective-permute-start | bytes 1572872 | tf_op jit(solution)/shard_map/ppermute | solution.py:23
  311.8 23.2 %collective-permute-start.35 = (bf16[128,2048]{1,0:T(8,128)(2,1)}, bf16[128,2048]{1,0:T(8,128)(2,1)S(1)}, u32[]{:S(2)}, u32[]{:S(2)}) collective-permute-start(bf16[128,2048]{1,0:T(8,128)(2,1)} %get-tuple-element.104), channel_id=1, source_target_pairs={{0,2},{1,3},{2,0},{3,1},{4,6},{5,7},{6,4},{7,5},{8,10},{9,11},{10,... | collective-permute-start | bytes 1572872 | tf_op jit(solution)/shard_map/ppermute | solution.py:23
  312.2 6.9 %collective-permute-start.40 = (f32[2,2048]{1,0:T(2,128)S(1)}, f32[2,2048]{1,0:T(2,128)S(1)}, u32[]{:S(2)}, u32[]{:S(2)}) collective-permute-start(f32[2,2048]{1,0:T(2,128)S(1)} %fusion.34), channel_id=1, source_target_pairs={{0,12},{4,8},{8,4},{12,0},{1,13},{5,9},{9,5},{13,1},{2,14},{6,10},... | collective-permute-start | bytes 49160 | tf_op jit(solution)/shard_map/ppermute | solution.py:1141
  319.1 3.4 collective-permute-start.41
  322.5 4.4 %collective-permute-start.42 = (f32[2,2048]{1,0:T(2,128)S(1)}, f32[2,2048]{1,0:T(2,128)S(1)}, u32[]{:S(2)}, u32[]{:S(2)}) collective-permute-start(f32[2,2048]{1,0:T(2,128)S(1)} %add.217), channel_id=1, source_target_pairs={{0,96},{32,64},{64,32},{96,0},{1,97},{33,65},{65,33},{97,1},{2,98}... | collective-permute-start | bytes 49160 | tf_op jit(solution)/shard_map/ppermute | solution.py:1141
  336.5 31.8 %copy-start.50 = (bf16[144,2048]{1,0:T(8,128)(2,1)}, bf16[144,2048]{1,0:T(8,128)(2,1)S(1)}, u32[]{:S(2)}) copy-start(bf16[144,2048]{1,0:T(8,128)(2,1)S(1)} %maximum_maximum_fusion.refs_4_) | copy-start | bytes 1769476
  336.5 15.8 %collective-permute-start.43 = (bf16[144,2048]{1,0:T(8,128)(2,1)S(1)}, bf16[144,2048]{1,0:T(8,128)(2,1)S(1)}, u32[]{:S(2)}, u32[]{:S(2)}) collective-permute-start(bf16[144,2048]{1,0:T(8,128)(2,1)S(1)} %maximum_maximum_fusion.refs_4_), channel_id=1, source_target_pairs={{0,3},{1,0},{2,1},{3,2},{4,7},{5,4},{6,5},{7,6},{8,11},{9,8},{10,9... | collective-permute-start | bytes 1769480 | tf_op jit(solution)/shard_map/ppermute | solution.py:23
  338.9 14.8 %collective-permute-start.44 = (bf16[144,2048]{1,0:T(8,128)(2,1)S(1)}, bf16[144,2048]{1,0:T(8,128)(2,1)S(1)}, u32[]{:S(2)}, u32[]{:S(2)}) collective-permute-start(bf16[144,2048]{1,0:T(8,128)(2,1)S(1)} %maximum_maximum_fusion.refs_4_), channel_id=1, source_target_pairs={{0,2},{1,3},{2,0},{3,1},{4,6},{5,7},{6,4},{7,5},{8,10},{9,11},{10,... | collective-permute-start | bytes 1769480 | tf_op jit(solution)/shard_map/ppermute | solution.py:23
  339.3 28.9 %collective-permute-start.45 = (bf16[144,2048]{1,0:T(8,128)(2,1)S(1)}, bf16[144,2048]{1,0:T(8,128)(2,1)S(1)}, u32[]{:S(2)}, u32[]{:S(2)}) collective-permute-start(bf16[144,2048]{1,0:T(8,128)(2,1)S(1)} %maximum_maximum_fusion.refs_4_), channel_id=1, source_target_pairs={{0,1},{1,2},{2,3},{3,0},{4,5},{5,6},{6,7},{7,4},{8,9},{9,10},{10,1... | collective-permute-start | bytes 1769480 | tf_op jit(solution)/shard_map/ppermute | solution.py:23
  388.5 2.4 collective-permute-start.46
  (67 other events, 334.6 us)
Sparse Core Ops, SparseCore 0:
  26.9 78.4 all-gather.2
  107.6 64.8 all-gather.4
  285.1 102.1 reduce-scatter.1

commit v3 on v2

--- a/solution.py
+++ b/solution.py
@@ -985,7 +985,7 @@
     block, gathered = stack_attn(mine, came, scalars)
     lengths = jnp.concatenate((first_length, swap(first_length)))
     blocks = spread_near(block)
-    w_kv = stack_blocks(blocks, 0, 768, scalars, "stack_kv")
+    w_kv = stack_blocks(blocks, 0, 768, scalars, "stack_kv", deps=(lengths,))
     normed_first = enter_rows(tokens, gain_first.reshape(1, D), scalars, deps=(w_kv,))
     (gathered,) = tie((gathered,), blocks[1:])
     w_goq = lax.all_gather(gathered, XY, axis=0, tiled=True).reshape(4, 4, 2, 64, -1)
@@ -1031,7 +1031,7 @@
         [(w_kv, 0, 768)],
         scalars,
         "project_kv",
-        deps=(mask, enter_rows_in, leave_rows_out, fade_in, cosine, sine, came_mlp),
+        deps=(came_mlp,),
     )
     key = rotate(projected[:, DV:], cosine, sine).astype(BF).reshape(2, rows, DK)
     value = projected[:, :DV].astype(BF).reshape(2, rows, DV)

time: 401 us -> 411 us (1.025)
  waiting for transfers between devices: 140 us -> 157 us
  other arithmetic: 20.2 us -> 15.2 us
    ppermute x6, waiting for transfers between devices: 25.9 us -> 33 us  [shift_open(): lax.ppermute(value, axis, [(i, i + offset) for i in range(n) if 0 <= i +...]
    all_gather x1, waiting for transfers between devices: 2.28 us -> 7.05 us  [per_device(): lax.all_gather(stack_blocks((mine, came_mlp), 0, 1536, scalars, 'stack_ml...]
    unnamed x167 -> x153, local copies, waits for them, and re-layouts: 29.8 us -> 29.8 us
  transfers between devices with their start and end apart: 50 -> 50, of which waited for: 33 -> 35; matrix products, arithmetic and copies ran while one was open for 6% -> 5% of each run, Pallas kernels for 19% -> 18%
where the time goes in v3:
time: 411 us; the launch traced here: 409 us
  waiting for transfers between devices  157 us (38%)
  Pallas kernels  120 us (29%)
  starting transfers between devices  61.3 us (15%)
  local copies, waits for them, and re-layouts  34.2 us (8%)
  between operations  15.8 us (4%)
  other arithmetic  15.2 us (4%)
  matrix products  4.71 us (1%)
    pallas_call x23, Pallas kernels, call(): pl.pallas_call(kernel, out_shape=shapes, grid_spec=pltpu.PrefetchScalarGr...  120 us
    ppermute x18, waiting for transfers between devices, shift(): return lax.ppermute(value, axis, [(i, (i + offset) % n) for i in range(n)])  70.7 us
    ppermute x6, waiting for transfers between devices, shift_open(): lax.ppermute(value, axis, [(i, i + offset) for i in range(n) if 0 <= i +...  33 us
    unnamed x153, local copies, waits for them, and re-layouts  29.8 us
    ppermute x6, waiting for transfers between devices, hop(): return lax.ppermute(value, ('x', 'core', 'ctx'), pairs)  20.6 us
    ppermute x18, starting transfers between devices, shift(): return lax.ppermute(value, axis, [(i, (i + offset) % n) for i in range(n)])  18.1 us
    ppermute x12, waiting for transfers between devices, swap(): return lax.ppermute(value, 'core', [(0, 1), (1, 0)])  14.4 us
    ppermute x6, starting transfers between devices, shift_open(): lax.ppermute(value, axis, [(i, i + offset) for i in range(n) if 0 <= i +...  12.9 us
  transfers between devices with their start and end apart: 50, of which 35 were waited for; matrix products, arithmetic and copies ran while one was open for 5% of the time, Pallas kernels for 18%

profile of v3, /device:TPU:1, one launch (start us, length us, event | category | flops | bytes accessed | tf_op | source)
XLA Modules:
  0.0 408.7 jit_solution(6234790638960824050)
XLA Ops:
  7.8 2.7 split_attn.1
  14.0 2.5 stack_attn.1
  17.8 2.5 collective-permute-start.2
  22.7 3.2 collective-permute-done.2.refs_2_
  26.7 1.6 collective-permute-start.4
  38.0 2.1 collective-permute-start.7
  42.7 2.5 split_mlp.1
  47.7 5.1 %collective-permute-done.6.refs_3_.refs_2_ = bf16[4,2,64,768]{3,2,1,0:T(8,128)(2,1)S(1)} collective-permute-done((bf16[4,2,64,768]{3,2,1,0:T(8,128)(2,1)}, bf16[4,2,64,768]{3,2,1,0:T(8,128)(2,1)S(1)}, u32[]{:S(2)}, u32[]{:S(2)}) %collective-permute-start.6) | collective-permute-done | bytes 786464 | tf_op jit(solution)/shard_map/ppermute | solution.py:148
  52.9 11.0 %collective-permute-done.7.refs_4_.refs_3_ = bf16[4,2,64,768]{3,2,1,0:T(8,128)(2,1)} collective-permute-done((bf16[4,2,64,768]{3,2,1,0:T(8,128)(2,1)}, bf16[4,2,64,768]{3,2,1,0:T(8,128)(2,1)}, u32[]{:S(2)}, u32[]{:S(2)}) %collective-permute-start.7) | collective-permute-done | bytes 786464 | tf_op jit(solution)/shard_map/ppermute | solution.py:148
  65.1 5.6 %project_kv.1 = f32[512,768]{1,0:T(8,128)S(1)} custom-call(s32[4]{0:T(128)S(1)} %copy-done.31, bf16[256,2048]{1,0:T(8,128)(2,1)S(1)} %copy-done.2, bf16[256,2048]{1,0:T(8,128)(2,1)S(1)} %collective-permute-done.5.refs_1_.refs_4_.refs_10_, bf16[4,2,64,768]{3,2,1,0:T(8,128)(2,1)} %bitcast.8.refs_2_.refs_1_, ...), custom_call_target="tpu_custom_call" | custom-call | flops 1 | bytes 1 | tf_op jit(solution)/shard_map/project_kv/pallas_call | solution.py:61
  74.4 3.3 collective-permute-start.10
  77.7 4.0 collective-permute-start.11
  84.8 15.1 %collective-permute-done.10.refs_5_ = bf16[2,256,512]{2,1,0:T(8,128)(2,1)S(1)} collective-permute-done((bf16[2,256,512]{2,1,0:T(8,128)(2,1)S(1)}, bf16[2,256,512]{2,1,0:T(8,128)(2,1)S(1)}, u32[]{:S(2)}, u32[]{:S(2)}) %collective-permute-start.10) | collective-permute-done | bytes 524320 | tf_op jit(solution)/shard_map/ppermute | solution.py:28
  99.9 16.0 %collective-permute-done.11.refs_6_ = bf16[2,256,512]{2,1,0:T(8,128)(2,1)S(1)} collective-permute-done((bf16[2,256,512]{2,1,0:T(8,128)(2,1)S(1)}, bf16[2,256,512]{2,1,0:T(8,128)(2,1)S(1)}, u32[]{:S(2)}, u32[]{:S(2)}) %collective-permute-start.11) | collective-permute-done | bytes 524320 | tf_op jit(solution)/shard_map/ppermute | solution.py:28
  117.6 12.8 %retain.1 = (f32[256,2048]{1,0:T(8,128)}, bf16[256,2048]{1,0:T(8,128)(2,1)}, bf16[512,256]{1,0:T(8,128)(2,1)}, bf16[2,256,512]{2,1,0:T(8,128)(2,1)}, bf16[2,256,...) custom-call(s32[4]{0:T(128)} %pad_add_fusion.s_ref, ...), custom_call_target="tpu_custom_call" | custom-call | flops 1 | bytes 1 | tf_op jit(solution)/shard_map/retain/pallas_call | solution.py:61
  131.6 2.5 collective-permute-done.13
  134.1 1.7 add_convert_fusion.9
  135.8 2.8 collective-permute-start.16
  138.6 1.7 collective-permute-start.14
  140.2 9.1 %collective-permute-done.16 = bf16[64,2048]{1,0:T(8,128)(2,1)S(1)} collective-permute-done((bf16[64,2048]{1,0:T(8,128)(2,1)S(1)}, bf16[64,2048]{1,0:T(8,128)(2,1)S(1)}, u32[]{:S(2)}, u32[]{:S(2)}) %collective-permute-start.16) | collective-permute-done | bytes 262176 | tf_op jit(solution)/shard_map/ppermute | solution.py:23
  149.3 2.3 collective-permute-done.14
  156.1 2.3 collective-permute-start.21
  159.6 2.5 collective-permute-done.18.refs_4_
  162.1 7.6 %collective-permute-done.19.refs_5_ = bf16[64,2048]{1,0:T(8,128)(2,1)S(1)} collective-permute-done((bf16[64,2048]{1,0:T(8,128)(2,1)S(1)}, bf16[64,2048]{1,0:T(8,128)(2,1)S(1)}, u32[]{:S(2)}, u32[]{:S(2)}) %collective-permute-start.19) | collective-permute-done | bytes 262176 | tf_op jit(solution)/shard_map/ppermute | solution.py:23
  172.9 2.4 collective-permute-done.20.refs_1_
  175.3 7.0 %all-gather.5.cloned.1.call-done = bf16[2048,1536]{1,0:T(8,128)(2,1)} async-done(((bf16[128,1536]{1,0:T(8,128)(2,1)}), bf16[2048,1536]{1,0:T(8,128)(2,1)}) %all-gather.5.cloned.1.call-update) | async-done | bytes 6291472 | tf_op jit(solution)/shard_map/all_gather | solution.py:1041
  182.3 14.4 %mlp.1 = (f32[256,2048]{1,0:T(8,128)}, bf16[256,2048]{1,0:T(8,128)(2,1)}, f32[8,2048]{1,0:T(8,128)}, bf16[512,1024]{1,0:T(8,128)(2,1)}, bf16[512,512]{1,0:T(8,128)(2,1)}) custom-call(s32[4]{0:T(128)} %pad_add_fusion.s_ref, bf16[256,2048]{1,0:T(8,128)(2,1)} %copy-done.15, bf16[256,2048]{1,0:T(8,128)(2,1)} %collective-permute-done.20.refs_1_, ...), custom_call_target="tpu_custom_call" | custom-call | flops 1 | bytes 1 | tf_op jit(solution)/shard_map/mlp/pallas_call | solution.py:61
  197.5 2.5 collective-permute-done.22
  200.0 1.6 add_convert_fusion.4
  201.6 2.7 collective-permute-start.25
  204.3 1.7 collective-permute-start.23
  206.0 6.9 %weight_mlp.1 = (bf16[4,4,2,64,3584]{4,3,2,1,0:T(8,128)(2,1)}, f32[8,128]{1,0:T(8,128)}) custom-call(s32[4]{0:T(128)} %pad_add_fusion.s_ref, bf16[256,2048]{1,0:T(8,128)(2,1)} %copy-done.15, bf16[256,2048]{1,0:T(8,128)(2,1)} %collective-permute-done.20.refs_1_, bf16[512,1024]{1,0:T(8,128)(2,1)} %get-tuple-element.78.refs_2_), custom_call_target="tpu_custom_call" | custom-call | flops 1 | bytes 1 | tf_op jit(solution)/shard_map/weight_mlp/pallas_call | solution.py:61
  212.9 2.2 collective-permute-done.25
  215.1 2.3 collective-permute-done.23
  217.4 1.9 add_convert_fusion.1.refs_0_
  221.7 2.8 copy-done.7
  225.5 2.8 project_down.1
  230.6 5.5 %collective-permute-done.28.refs_6_ = bf16[64,2048]{1,0:T(8,128)(2,1)S(1)} collective-permute-done((bf16[64,2048]{1,0:T(8,128)(2,1)}, bf16[64,2048]{1,0:T(8,128)(2,1)S(1)}, u32[]{:S(2)}, u32[]{:S(2)}) %collective-permute-start.28) | collective-permute-done | bytes 262176 | tf_op jit(solution)/shard_map/ppermute | solution.py:23
  236.8 5.9 %second_back.1 = (f32[256,2048]{1,0:T(8,128)}, bf16[256,2048]{1,0:T(8,128)(2,1)}) custom-call(s32[4]{0:T(128)} %pad_add_fusion.s_ref, f32[256,2048]{1,0:T(8,128)} %copy-done.11, f32[256,2048]{1,0:T(8,128)} %refs_1_.6, f32[1,2048]{1,0:T(1,128)} %bitcast.88, bf16[64,2048]{1,0:T(8,128)(2,1)} %tie.6.refs_2_.refs_3_, bf16[64,2048]{1,0:T(8,128)(2,1)} %copy-done.69, ...), custom_call_target="tpu_custom_call" | custom-call | flops 1 | bytes 1 | tf_op jit(solution)/shard_map/second_back/pallas_call | solution.py:61
  244.2 1.6 collective-permute-done.29.refs_1_
  246.8 9.7 %back_gate.1 = (bf16[512,512]{1,0:T(8,128)(2,1)}, bf16[512,512]{1,0:T(8,128)(2,1)}, bf16[2,256,512]{2,1,0:T(8,128)(2,1)}) custom-call(s32[4]{0:T(128)} %pad_add_fusion.s_ref, bf16[256,2048]{1,0:T(8,128)(2,1)} %get-tuple-element.83.refs_0_, bf16[256,2048]{1,0:T(8,128)(2,1)} %copy-done.44, bf16[4,4,2,64,1280]{4,3,2,1,0:T(8,128)(2,1)} %bitcast.83, ...), custom_call_target="tpu_custom_call" | custom-call | flops 1 | bytes 1 | tf_op jit(solution)/shard_map/back_gate/pallas_call | solution.py:61
  259.2 1.5 collective-permute-start.32
  263.5 7.2 %weight_og.1 = (bf16[4,4,2,64,3584]{4,3,2,1,0:T(8,128)(2,1)}, f32[8,128]{1,0:T(8,128)}) custom-call(s32[4]{0:T(128)} %pad_add_fusion.s_ref, bf16[256,2048]{1,0:T(8,128)(2,1)} %get-tuple-element.83.refs_0_, bf16[256,2048]{1,0:T(8,128)(2,1)} %copy-done.44, bf16[512,512]{1,0:T(8,128)(2,1)} %get-tuple-element.90.refs_2_, ...), custom_call_target="tpu_custom_call", output_to_operand_aliasing={{0}: (7, {})} | custom-call | flops 1 | bytes 1 | tf_op jit(solution)/shard_map/weight_og/pallas_call | solution.py:61
  270.7 5.5 %weight_down.1 = (bf16[4,4,2,64,3584]{4,3,2,1,0:T(8,128)(2,1)}, f32[8,128]{1,0:T(8,128)}) custom-call(s32[4]{0:T(128)} %pad_add_fusion.s_ref, bf16[256,2048]{1,0:T(8,128)(2,1)} %copy-done.10, bf16[256,2048]{1,0:T(8,128)(2,1)} %copy-done.45, bf16[512,512]{1,0:T(8,128)(2,1)} %get-tuple-element.80.refs_0_.refs_2_, ...), custom_call_target="tpu_custom_call", output_to_operand_aliasing={{0}: (4, {})} | custom-call | flops 1 | bytes 1 | tf_op jit(solution)/shard_map/weight_down/pallas_call | solution.py:61
  276.3 5.1 %weight_query.1 = (bf16[4,4,2,64,3584]{4,3,2,1,0:T(8,128)(2,1)}, f32[8,128]{1,0:T(8,128)}) custom-call(s32[4]{0:T(128)} %pad_add_fusion.s_ref, bf16[256,2048]{1,0:T(8,128)(2,1)} %copy-done.1, bf16[256,2048]{1,0:T(8,128)(2,1)} %copy-done.4, bf16[512,256]{1,0:T(8,128)(2,1)} %pad_maximum_fusion.1.refs_2_.refs_7_, ...), custom_call_target="tpu_custom_call", output_to_operand_aliasing={{0}: (4, {})} | custom-call | flops 1 | bytes 1 | tf_op jit(solution)/shard_map/weight_query/pallas_call | solution.py:61
  284.7 1.9 collective-permute-done.32.refs_4_
  287.4 8.0 %weight_last.1 = (bf16[4,4,2,64,3584]{4,3,2,1,0:T(8,128)(2,1)}, f32[8,128]{1,0:T(8,128)}, bf16[512,768]{1,0:T(8,128)(2,1)}) custom-call(s32[4]{0:T(128)} %pad_add_fusion.s_ref, bf16[256,2048]{1,0:T(8,128)(2,1)} %copy-done.1, bf16[256,2048]{1,0:T(8,128)(2,1)} %copy-done.4, bf16[2,256,512]{2,1,0:T(8,128)(2,1)} %tie.7.refs_2_, ...), custom_call_target="tpu_custom_call", output_to_operand_aliasing={{0}: (14, {})} | custom-call | flops 1 | bytes 1 | tf_op jit(solution)/shard_map/weight_last/pallas_call | solution.py:61
  297.2 2.5 copy-done
  301.8 7.5 %back_attn.1 = (f32[256,2048]{1,0:T(8,128)S(1)}, bf16[256,2048]{1,0:T(8,128)(2,1)S(1)}, f32[8,2048]{1,0:T(8,128)S(1)}) custom-call(s32[4]{0:T(128)S(1)} %copy-done.34, bf16[512,768]{1,0:T(8,128)(2,1)S(1)} %copy-done.23, bf16[4,2,64,768]{3,2,1,0:T(8,128)(2,1)} %bitcast.8.refs_2_.refs_1_, bf16[4,2,64,768]{3,2,1,0:T(8,128)(2,1)S(1)} %copy-done.17, ...), custom_call_target="tpu_custom_call" | custom-call | flops 1 | bytes 1 | tf_op jit(solution)/shard_map/back_attn/pallas_call | solution.py:61
  314.6 1.5 collective-permute-done.34.refs_3_
  317.2 5.9 %third_blocks.1 = (bf16[128,2048]{1,0:T(8,128)(2,1)}, bf16[128,2048]{1,0:T(8,128)(2,1)}, bf16[128,2048]{1,0:T(8,128)(2,1)}, bf16[128,2048]{1,0:T(8,128)(2,1)}) custom-call(s32[4]{0:T(128)} %pad_add_fusion.s_ref, f32[256,2048]{1,0:T(8,128)} %copy-done.21, bf16[256,2048]{1,0:T(8,128)(2,1)} %copy-done.54, f32[256,2048]{1,0:T(8,128)} %copy-done.20, ...), custom_call_target="tpu_custom_call" | custom-call | flops 1 | bytes 1 | tf_op jit(solution)/shard_map/third_blocks/pallas_call | solution.py:61
  324.7 4.5 %collective-permute-start.40 = (f32[2,2048]{1,0:T(2,128)S(1)}, f32[2,2048]{1,0:T(2,128)S(1)}, u32[]{:S(2)}, u32[]{:S(2)}) collective-permute-start(f32[2,2048]{1,0:T(2,128)S(1)} %fusion.34), channel_id=1, source_target_pairs={{0,12},{4,8},{8,4},{12,0},{1,13},{5,9},{9,5},{13,1},{2,14},{6,10},... | collective-permute-start | bytes 49160 | tf_op jit(solution)/shard_map/ppermute | solution.py:1141
  329.2 1.6 collective-permute-done.40
  330.9 1.8 collective-permute-start.41
  332.6 2.0 collective-permute-done.41
  334.7 2.5 collective-permute-start.42
  337.2 1.8 collective-permute-done.42
  339.1 9.8 %collective-permute-done.36 = bf16[128,2048]{1,0:T(8,128)(2,1)S(1)} collective-permute-done((bf16[128,2048]{1,0:T(8,128)(2,1)}, bf16[128,2048]{1,0:T(8,128)(2,1)S(1)}, u32[]{:S(2)}, u32[]{:S(2)}) %collective-permute-start.36) | collective-permute-done | bytes 524320 | tf_op jit(solution)/shard_map/ppermute | solution.py:23
  353.1 10.8 %collective-permute-done.43.refs_5_ = bf16[144,2048]{1,0:T(8,128)(2,1)S(1)} collective-permute-done((bf16[144,2048]{1,0:T(8,128)(2,1)S(1)}, bf16[144,2048]{1,0:T(8,128)(2,1)S(1)}, u32[]{:S(2)}, u32[]{:S(2)}) %collective-permute-start.43) | collective-permute-done | bytes 589856 | tf_op jit(solution)/shard_map/ppermute | solution.py:23
  364.0 3.0 collective-permute-done.44.refs_6_
  367.0 14.4 %collective-permute-done.45.refs_7_ = bf16[144,2048]{1,0:T(8,128)(2,1)S(1)} collective-permute-done((bf16[144,2048]{1,0:T(8,128)(2,1)S(1)}, bf16[144,2048]{1,0:T(8,128)(2,1)S(1)}, u32[]{:S(2)}, u32[]{:S(2)}) %collective-permute-start.45) | collective-permute-done | bytes 589856 | tf_op jit(solution)/shard_map/ppermute | solution.py:23
  382.3 7.5 %leave_rows.1 = (f32[256,2048]{1,0:T(8,128)}, f32[256,2048]{1,0:T(8,128)}) custom-call(s32[4]{0:T(128)} %pad_add_fusion.s_ref, f32[256,2048]{1,0:T(8,128)} %copy-done.11, f32[256,2048]{1,0:T(8,128)} %refs_1_.7, f32[256,2048]{1,0:T(8,128)} %get-tuple-element.82.refs_2_, f32[1,2048]{1,0:T(1,128)} %bitcast.90, bf16[144,2048]{1,0:T(8,128)(2,1)} %copy-done.47, ...), custom_call_target="tpu_custom_call" | custom-call | flops 1 | bytes 1 | tf_op jit(solution)/shard_map/leave_rows/pallas_call | solution.py:61
  391.9 4.7 %reduce-scatter.2.cloned.1.call-done.refs_0_ = bf16[128,3584]{1,0:T(8,128)(2,1)} async-done(((bf16[2048,3584]{1,0:T(8,128)(2,1)}), bf16[128,3584]{1,0:T(8,128)(2,1)}) %reduce-scatter.2.cloned.1.call-update) | async-done | bytes 917520 | tf_op jit(solution)/shard_map/reduce_scatter | solution.py:1122
  400.3 1.8 join_heads.1
  (270 shorter events, 83.8 us)
Async XLA Ops:
  7.2 108.8 %all-gather.3.cloned.1.call-start = ((), (), s32[]{:S(2)}) async-start(), calls=%async_computation.1 | async-start | bytes 5570560 | tf_op jit(solution)/shard_map/all_gather | solution.py:991
  7.8 22.2 %copy-start.30 = (s32[4]{0:T(128)S(1)}, s32[4]{0:T(128)}, u32[]{:S(2)}) copy-start(s32[4]{0:T(128)} %pad_add_fusion.s_ref) | copy-start | bytes 52
  7.8 27.4 %copy-start.8 = (f32[256,2048]{1,0:T(8,128)S(1)}, f32[256,2048]{1,0:T(8,128)}, u32[]{:S(2)}) copy-start(f32[256,2048]{1,0:T(8,128)} %refs_1_.7) | copy-start | bytes 6291460
  7.8 27.4 %copy-start.39 = (f32[2048]{0:T(1024)S(1)}, f32[2048]{0:T(1024)}, u32[]{:S(2)}) copy-start(f32[2048]{0:T(1024)} %param.16) | copy-start | bytes 24580
  10.5 2.8 collective-permute-start
  16.5 6.2 %collective-permute-start.1 = (bf16[128,768]{1,0:T(8,128)(2,1)}, bf16[128,768]{1,0:T(8,128)(2,1)S(1)}, u32[]{:S(2)}, u32[]{:S(2)}) collective-permute-start(bf16[128,768]{1,0:T(8,128)(2,1)} %get-tuple-element.68.refs_0_), channel_id=1, source_target_pairs={{0,4},{4,8},{8,12},{12,0},{16,48},{20,52},{24,56},{28,60},{32,36},... | collective-permute-start | bytes 589832 | tf_op jit(solution)/shard_map/ppermute | solution.py:148
  17.8 8.1 %collective-permute-start.2 = (bf16[128,768]{1,0:T(8,128)(2,1)}, bf16[128,768]{1,0:T(8,128)(2,1)S(1)}, u32[]{:S(2)}, u32[]{:S(2)}) collective-permute-start(bf16[128,768]{1,0:T(8,128)(2,1)} %get-tuple-element.68.refs_0_), channel_id=1, source_target_pairs={{0,8},{4,12},{8,0},{12,4},{16,80},{20,84},{24,88},{28,92},{32,40},... | collective-permute-start | bytes 589832 | tf_op jit(solution)/shard_map/ppermute | solution.py:148
  20.2 5.7 %collective-permute-start.3 = (bf16[128,768]{1,0:T(8,128)(2,1)}, bf16[128,768]{1,0:T(8,128)(2,1)S(1)}, u32[]{:S(2)}, u32[]{:S(2)}) collective-permute-start(bf16[128,768]{1,0:T(8,128)(2,1)} %get-tuple-element.68.refs_0_), channel_id=1, source_target_pairs={{0,12},{4,0},{8,4},{12,8},{16,112},{20,116},{24,120},{28,124},{32,... | collective-permute-start | bytes 589832 | tf_op jit(solution)/shard_map/ppermute | solution.py:148
  26.7 155.7 %all-gather.5.cloned.1.call-start = ((), (), s32[]{:S(2)}) async-start(), calls=%async_computation.2 | async-start | bytes 6684672 | tf_op jit(solution)/shard_map/all_gather | solution.py:1041
  26.7 2.5 collective-permute-start.4
  35.2 28.7 %copy-start.31 = (s32[4]{0:T(128)S(1)}, s32[4]{0:T(128)}, u32[]{:S(2)}) copy-start(s32[4]{0:T(128)} %pad_add_fusion.s_ref) | copy-start | bytes 52
  36.4 27.4 %collective-permute-start.5 = (bf16[256,2048]{1,0:T(8,128)(2,1)S(1)}, bf16[256,2048]{1,0:T(8,128)(2,1)S(1)}, u32[]{:S(2)}, u32[]{:S(2)}) collective-permute-start(bf16[256,2048]{1,0:T(8,128)(2,1)S(1)} %enter_rows.1.refs_3_.refs_0_.refs_9_), channel_id=1, source_target_pairs={{0,16},{16,0},{1,17},{17,1},{2,18},{18,2},{3,19},{19,3},{4,20},{20... | collective-permute-start | bytes 3145736 | tf_op jit(solution)/shard_map/ppermute | solution.py:34
  36.8 16.1 %collective-permute-start.6 = (bf16[4,2,64,768]{3,2,1,0:T(8,128)(2,1)}, bf16[4,2,64,768]{3,2,1,0:T(8,128)(2,1)S(1)}, u32[]{:S(2)}, u32[]{:S(2)}) collective-permute-start(bf16[4,2,64,768]{3,2,1,0:T(8,128)(2,1)} %bitcast.8.refs_2_.refs_1_), channel_id=1, source_target_pairs={{0,32},{4,36},{8,40},{12,44},{16,20},{20,24},{24,28},{28,16},{32,6... | collective-permute-start | bytes 2359304 | tf_op jit(solution)/shard_map/ppermute | solution.py:148
  38.0 25.8 %collective-permute-start.7 = (bf16[4,2,64,768]{3,2,1,0:T(8,128)(2,1)}, bf16[4,2,64,768]{3,2,1,0:T(8,128)(2,1)}, u32[]{:S(2)}, u32[]{:S(2)}) collective-permute-start(bf16[4,2,64,768]{3,2,1,0:T(8,128)(2,1)} %bitcast.8.refs_2_.refs_1_), channel_id=1, source_target_pairs={{0,64},{4,68},{8,72},{12,76},{16,24},{20,28},{24,16},{28,20},{32,9... | collective-permute-start | bytes 2359304 | tf_op jit(solution)/shard_map/ppermute | solution.py:148
  40.1 23.7 %collective-permute-start.8 = (bf16[4,2,64,768]{3,2,1,0:T(8,128)(2,1)}, bf16[4,2,64,768]{3,2,1,0:T(8,128)(2,1)}, u32[]{:S(2)}, u32[]{:S(2)}) collective-permute-start(bf16[4,2,64,768]{3,2,1,0:T(8,128)(2,1)} %bitcast.8.refs_2_.refs_1_), channel_id=1, source_target_pairs={{0,96},{4,100},{8,104},{12,108},{16,28},{20,16},{24,20},{28,24},{3... | collective-permute-start | bytes 2359304 | tf_op jit(solution)/shard_map/ppermute | solution.py:148
  45.1 2.6 collective-permute-start.9
  52.8 17.8 %copy-start.16 = (bf16[4,2,64,768]{3,2,1,0:T(8,128)(2,1)}, bf16[4,2,64,768]{3,2,1,0:T(8,128)(2,1)S(1)}, u32[]{:S(2)}) copy-start(bf16[4,2,64,768]{3,2,1,0:T(8,128)(2,1)S(1)} %collective-permute-done.6.refs_3_.refs_2_) | copy-start | bytes 2359300
  73.0 323.6 %reduce-scatter.2.cloned.1.call-start = ((), (), s32[]{:S(2)}) async-start(), calls=%async_computation.3 | async-start | bytes 15597568 | tf_op jit(solution)/shard_map/reduce_scatter | solution.py:1122
  73.4 57.0 %copy-start.56 = (f32[256,256]{1,0:T(8,128)}, f32[256,256]{1,0:T(8,128)S(1)}, u32[]{:S(2)}) copy-start(f32[256,256]{1,0:T(8,128)S(1)} %fusion.6) | copy-start | bytes 786436
  74.4 25.6 %collective-permute-start.10 = (bf16[2,256,512]{2,1,0:T(8,128)(2,1)S(1)}, bf16[2,256,512]{2,1,0:T(8,128)(2,1)S(1)}, u32[]{:S(2)}, u32[]{:S(2)}) collective-permute-start(bf16[2,256,512]{2,1,0:T(8,128)(2,1)S(1)} %convolution_convert_fusion.refs_2_), channel_id=1, source_target_pairs={{0,4},{4,8},{8,12},{1,5},{5,9},{9,13},{2,6},{6,10},{10,14},{3,7},{... | collective-permute-start | bytes 1572872 | tf_op jit(solution)/shard_map/ppermute | solution.py:28
  77.7 38.3 %collective-permute-start.11 = (bf16[2,256,512]{2,1,0:T(8,128)(2,1)S(1)}, bf16[2,256,512]{2,1,0:T(8,128)(2,1)S(1)}, u32[]{:S(2)}, u32[]{:S(2)}) collective-permute-start(bf16[2,256,512]{2,1,0:T(8,128)(2,1)S(1)} %convolution_convert_fusion.refs_2_), channel_id=1, source_target_pairs={{0,8},{4,12},{1,9},{5,13},{2,10},{6,14},{3,11},{7,15},{16,24},{20,... | collective-permute-start | bytes 1572872 | tf_op jit(solution)/shard_map/ppermute | solution.py:28
  81.7 34.2 %collective-permute-start.12 = (bf16[2,256,512]{2,1,0:T(8,128)(2,1)S(1)}, bf16[2,256,512]{2,1,0:T(8,128)(2,1)S(1)}, u32[]{:S(2)}, u32[]{:S(2)}) collective-permute-start(bf16[2,256,512]{2,1,0:T(8,128)(2,1)S(1)} %convolution_convert_fusion.refs_2_), channel_id=1, source_target_pairs={{0,12},{1,13},{2,14},{3,15},{16,28},{17,29},{18,30},{19,31},{32,44... | collective-permute-start | bytes 1572872 | tf_op jit(solution)/shard_map/ppermute | solution.py:28
  99.9 17.7 %copy-start.65 = (bf16[2,256,512]{2,1,0:T(8,128)(2,1)}, bf16[2,256,512]{2,1,0:T(8,128)(2,1)S(1)}, u32[]{:S(2)}) copy-start(bf16[2,256,512]{2,1,0:T(8,128)(2,1)S(1)} %collective-permute-done.10.refs_5_) | copy-start | bytes 1572868
  130.4 3.6 collective-permute-start.13
  134.1 21.3 %copy-start.5 = (bf16[256,2048]{1,0:T(8,128)(2,1)S(1)}, bf16[256,2048]{1,0:T(8,128)(2,1)}, u32[]{:S(2)}) copy-start(bf16[256,2048]{1,0:T(8,128)(2,1)} %copy-done.4) | copy-start | bytes 3145732
  134.1 21.3 %copy-start.12 = (f32[256,2048]{1,0:T(8,128)S(1)}, f32[256,2048]{1,0:T(8,128)}, u32[]{:S(2)}) copy-start(f32[256,2048]{1,0:T(8,128)} %refs_1_.6) | copy-start | bytes 6291460
  134.1 21.3 %copy-start.32 = (s32[4]{0:T(128)S(1)}, s32[4]{0:T(128)}, u32[]{:S(2)}) copy-start(s32[4]{0:T(128)} %pad_add_fusion.s_ref) | copy-start | bytes 52
  135.8 13.6 %collective-permute-start.16 = (bf16[64,2048]{1,0:T(8,128)(2,1)S(1)}, bf16[64,2048]{1,0:T(8,128)(2,1)S(1)}, u32[]{:S(2)}, u32[]{:S(2)}) collective-permute-start(bf16[64,2048]{1,0:T(8,128)(2,1)S(1)} %get-tuple-element.124), channel_id=1, source_target_pairs={{0,3},{1,0},{2,1},{3,2},{4,7},{5,4},{6,5},{7,6},{8,11},{9,8},{10,9... | collective-permute-start | bytes 786440 | tf_op jit(solution)/shard_map/ppermute | solution.py:23
  138.6 10.8 %collective-permute-start.15 = (bf16[64,2048]{1,0:T(8,128)(2,1)S(1)}, bf16[64,2048]{1,0:T(8,128)(2,1)S(1)}, u32[]{:S(2)}, u32[]{:S(2)}) collective-permute-start(bf16[64,2048]{1,0:T(8,128)(2,1)S(1)} %get-tuple-element.125), channel_id=1, source_target_pairs={{0,1},{1,2},{2,3},{3,0},{4,5},{5,6},{6,7},{7,4},{8,9},{9,10},{10,1... | collective-permute-start | bytes 786440 | tf_op jit(solution)/shard_map/ppermute | solution.py:23
  138.6 13.1 %collective-permute-start.14 = (bf16[64,2048]{1,0:T(8,128)(2,1)S(1)}, bf16[64,2048]{1,0:T(8,128)(2,1)S(1)}, u32[]{:S(2)}, u32[]{:S(2)}) collective-permute-start(bf16[64,2048]{1,0:T(8,128)(2,1)S(1)} %get-tuple-element.123), channel_id=1, source_target_pairs={{0,2},{1,3},{2,0},{3,1},{4,6},{5,7},{6,4},{7,5},{8,10},{9,11},{10,... | collective-permute-start | bytes 786440 | tf_op jit(solution)/shard_map/ppermute | solution.py:23
  152.8 16.8 %copy-start.9 = (f32[256,2048]{1,0:T(8,128)S(1)}, f32[256,2048]{1,0:T(8,128)}, u32[]{:S(2)}) copy-start(f32[256,2048]{1,0:T(8,128)} %refs_1_.7) | copy-start | bytes 6291460
  152.9 6.8 %collective-permute-start.17 = (bf16[64,2048]{1,0:T(8,128)(2,1)S(1)}, bf16[64,2048]{1,0:T(8,128)(2,1)S(1)}, u32[]{:S(2)}, u32[]{:S(2)}) collective-permute-start(bf16[64,2048]{1,0:T(8,128)(2,1)S(1)} %add_convert_fusion.6.refs_2_), channel_id=1, source_target_pairs={{0,3},{1,0},{2,1},{3,2},{4,7},{5,4},{6,5},{7,6},{8,11},{9,8},{10,9... | collective-permute-start | bytes 786440 | tf_op jit(solution)/shard_map/ppermute | solution.py:23
  154.2 7.9 %collective-permute-start.18 = (bf16[64,2048]{1,0:T(8,128)(2,1)S(1)}, bf16[64,2048]{1,0:T(8,128)(2,1)S(1)}, u32[]{:S(2)}, u32[]{:S(2)}) collective-permute-start(bf16[64,2048]{1,0:T(8,128)(2,1)S(1)} %add_convert_fusion.6.refs_2_), channel_id=1, source_target_pairs={{0,2},{1,3},{2,0},{3,1},{4,6},{5,7},{6,4},{7,5},{8,10},{9,11},{10,... | collective-permute-start | bytes 786440 | tf_op jit(solution)/shard_map/ppermute | solution.py:23
  154.6 15.1 %collective-permute-start.19 = (bf16[64,2048]{1,0:T(8,128)(2,1)S(1)}, bf16[64,2048]{1,0:T(8,128)(2,1)S(1)}, u32[]{:S(2)}, u32[]{:S(2)}) collective-permute-start(bf16[64,2048]{1,0:T(8,128)(2,1)S(1)} %add_convert_fusion.6.refs_2_), channel_id=1, source_target_pairs={{0,1},{1,2},{2,3},{3,0},{4,5},{5,6},{6,7},{7,4},{8,9},{9,10},{10,1... | collective-permute-start | bytes 786440 | tf_op jit(solution)/shard_map/ppermute | solution.py:23
  156.1 26.2 %copy-start.10 = (bf16[256,2048]{1,0:T(8,128)(2,1)}, bf16[256,2048]{1,0:T(8,128)(2,1)S(1)}, u32[]{:S(2)}) copy-start(bf16[256,2048]{1,0:T(8,128)(2,1)S(1)} %low_rows.1.refs_2_.refs_0_) | copy-start | bytes 3145732
  156.1 16.7 %collective-permute-start.21 = (bf16[256,2048]{1,0:T(8,128)(2,1)S(1)}, bf16[256,2048]{1,0:T(8,128)(2,1)S(1)}, u32[]{:S(2)}, u32[]{:S(2)}) collective-permute-start(bf16[256,2048]{1,0:T(8,128)(2,1)S(1)} %low_rows.1.refs_2_.refs_0_), channel_id=1, source_target_pairs={{0,16},{16,0},{1,17},{17,1},{2,18},{18,2},{3,19},{19,3},{4,20},{20... | collective-permute-start | bytes 3145736 | tf_op jit(solution)/shard_map/ppermute | solution.py:34
  172.5 2.8 collective-permute-start.20
  196.7 3.3 collective-permute-start.22
  201.6 13.5 %collective-permute-start.25 = (bf16[64,2048]{1,0:T(8,128)(2,1)S(1)}, bf16[64,2048]{1,0:T(8,128)(2,1)S(1)}, u32[]{:S(2)}, u32[]{:S(2)}) collective-permute-start(bf16[64,2048]{1,0:T(8,128)(2,1)S(1)} %get-tuple-element.121), channel_id=1, source_target_pairs={{0,3},{1,0},{2,1},{3,2},{4,7},{5,4},{6,5},{7,6},{8,11},{9,8},{10,9... | collective-permute-start | bytes 786440 | tf_op jit(solution)/shard_map/ppermute | solution.py:23
  204.3 10.8 %collective-permute-start.24 = (bf16[64,2048]{1,0:T(8,128)(2,1)S(1)}, bf16[64,2048]{1,0:T(8,128)(2,1)S(1)}, u32[]{:S(2)}, u32[]{:S(2)}) collective-permute-start(bf16[64,2048]{1,0:T(8,128)(2,1)S(1)} %get-tuple-element.122), channel_id=1, source_target_pairs={{0,1},{1,2},{2,3},{3,0},{4,5},{5,6},{6,7},{7,4},{8,9},{9,10},{10,1... | collective-permute-start | bytes 786440 | tf_op jit(solution)/shard_map/ppermute | solution.py:23
  204.3 13.1 %collective-permute-start.23 = (bf16[64,2048]{1,0:T(8,128)(2,1)S(1)}, bf16[64,2048]{1,0:T(8,128)(2,1)S(1)}, u32[]{:S(2)}, u32[]{:S(2)}) collective-permute-start(bf16[64,2048]{1,0:T(8,128)(2,1)S(1)} %get-tuple-element.120), channel_id=1, source_target_pairs={{0,2},{1,3},{2,0},{3,1},{4,6},{5,7},{6,4},{7,5},{8,10},{9,11},{10,... | collective-permute-start | bytes 786440 | tf_op jit(solution)/shard_map/ppermute | solution.py:23
  219.3 11.3 %collective-permute-start.26 = (bf16[64,2048]{1,0:T(8,128)(2,1)}, bf16[64,2048]{1,0:T(8,128)(2,1)S(1)}, u32[]{:S(2)}, u32[]{:S(2)}) collective-permute-start(bf16[64,2048]{1,0:T(8,128)(2,1)} %tie.6.refs_2_.refs_3_), channel_id=1, source_target_pairs={{0,3},{1,0},{2,1},{3,2},{4,7},{5,4},{6,5},{7,6},{8,11},{9,8},{10,9... | collective-permute-start | bytes 786440 | tf_op jit(solution)/shard_map/ppermute | solution.py:23
  220.6 10.0 %collective-permute-start.27 = (bf16[64,2048]{1,0:T(8,128)(2,1)}, bf16[64,2048]{1,0:T(8,128)(2,1)S(1)}, u32[]{:S(2)}, u32[]{:S(2)}) collective-permute-start(bf16[64,2048]{1,0:T(8,128)(2,1)} %tie.6.refs_2_.refs_3_), channel_id=1, source_target_pairs={{0,2},{1,3},{2,0},{3,1},{4,6},{5,7},{6,4},{7,5},{8,10},{9,11},{10,... | collective-permute-start | bytes 786440 | tf_op jit(solution)/shard_map/ppermute | solution.py:23
  220.9 15.3 %collective-permute-start.28 = (bf16[64,2048]{1,0:T(8,128)(2,1)}, bf16[64,2048]{1,0:T(8,128)(2,1)S(1)}, u32[]{:S(2)}, u32[]{:S(2)}) collective-permute-start(bf16[64,2048]{1,0:T(8,128)(2,1)} %tie.6.refs_2_.refs_3_), channel_id=1, source_target_pairs={{0,1},{1,2},{2,3},{3,0},{4,5},{5,6},{6,7},{7,4},{8,9},{9,10},{10,1... | collective-permute-start | bytes 786440 | tf_op jit(solution)/shard_map/ppermute | solution.py:23
  242.8 3.0 collective-permute-start.29
  256.4 27.4 %collective-permute-start.30 = (bf16[2,256,512]{2,1,0:T(8,128)(2,1)}, bf16[2,256,512]{2,1,0:T(8,128)(2,1)S(1)}, u32[]{:S(2)}, u32[]{:S(2)}) collective-permute-start(bf16[2,256,512]{2,1,0:T(8,128)(2,1)} %get-tuple-element.87.refs_7_), channel_id=1, source_target_pairs={{4,0},{8,4},{12,8},{5,1},{9,5},{13,9},{6,2},{10,6},{14,10},{7,3},{... | collective-permute-start | bytes 1572872 | tf_op jit(solution)/shard_map/ppermute | solution.py:28
  257.9 26.8 %collective-permute-start.31 = (bf16[2,256,512]{2,1,0:T(8,128)(2,1)}, bf16[2,256,512]{2,1,0:T(8,128)(2,1)S(1)}, u32[]{:S(2)}, u32[]{:S(2)}) collective-permute-start(bf16[2,256,512]{2,1,0:T(8,128)(2,1)} %get-tuple-element.87.refs_7_), channel_id=1, source_target_pairs={{8,0},{12,4},{9,1},{13,5},{10,2},{14,6},{11,3},{15,7},{24,16},{28,... | collective-permute-start | bytes 1572872 | tf_op jit(solution)/shard_map/ppermute | solution.py:28
  259.2 27.4 %collective-permute-start.32 = (bf16[2,256,512]{2,1,0:T(8,128)(2,1)}, bf16[2,256,512]{2,1,0:T(8,128)(2,1)S(1)}, u32[]{:S(2)}, u32[]{:S(2)}) collective-permute-start(bf16[2,256,512]{2,1,0:T(8,128)(2,1)} %get-tuple-element.87.refs_7_), channel_id=1, source_target_pairs={{12,0},{13,1},{14,2},{15,3},{28,16},{29,17},{30,18},{31,19},{44,32... | collective-permute-start | bytes 1572872 | tf_op jit(solution)/shard_map/ppermute | solution.py:28
  311.6 3.0 collective-permute-start.33
  312.1 4.0 collective-permute-start.34
  313.0 1.4 collective-permute-start.38
  314.5 10.2 %collective-permute-start.39 = (f32[2,2048]{1,0:T(2,128)S(1)}, f32[2,2048]{1,0:T(2,128)S(1)}, u32[]{:S(2)}, u32[]{:S(2)}) collective-permute-start(f32[2,2048]{1,0:T(2,128)S(1)} %fusion.17), channel_id=1, source_target_pairs={{0,4},{4,0},{8,12},{12,8},{1,5},{5,1},{9,13},{13,9},{2,6},{6,2},{1... | collective-permute-start | bytes 49160 | tf_op jit(solution)/shard_map/ppermute | solution.py:1141
  323.1 16.0 %collective-permute-start.37 = (bf16[128,2048]{1,0:T(8,128)(2,1)}, bf16[128,2048]{1,0:T(8,128)(2,1)S(1)}, u32[]{:S(2)}, u32[]{:S(2)}) collective-permute-start(bf16[128,2048]{1,0:T(8,128)(2,1)} %get-tuple-element.106), channel_id=1, source_target_pairs={{0,3},{1,0},{2,1},{3,2},{4,7},{5,4},{6,5},{7,6},{8,11},{9,8},{10,9... | collective-permute-start | bytes 1572872 | tf_op jit(solution)/shard_map/ppermute | solution.py:23
  323.3 25.6 %collective-permute-start.36 = (bf16[128,2048]{1,0:T(8,128)(2,1)}, bf16[128,2048]{1,0:T(8,128)(2,1)S(1)}, u32[]{:S(2)}, u32[]{:S(2)}) collective-permute-start(bf16[128,2048]{1,0:T(8,128)(2,1)} %get-tuple-element.105), channel_id=1, source_target_pairs={{0,1},{1,2},{2,3},{3,0},{4,5},{5,6},{6,7},{7,4},{8,9},{9,10},{10,1... | collective-permute-start | bytes 1572872 | tf_op jit(solution)/shard_map/ppermute | solution.py:23
  324.6 24.3 %collective-permute-start.35 = (bf16[128,2048]{1,0:T(8,128)(2,1)}, bf16[128,2048]{1,0:T(8,128)(2,1)S(1)}, u32[]{:S(2)}, u32[]{:S(2)}) collective-permute-start(bf16[128,2048]{1,0:T(8,128)(2,1)} %get-tuple-element.104), channel_id=1, source_target_pairs={{0,2},{1,3},{2,0},{3,1},{4,6},{5,7},{6,4},{7,5},{8,10},{9,11},{10,... | collective-permute-start | bytes 1572872 | tf_op jit(solution)/shard_map/ppermute | solution.py:23
  324.7 6.1 %collective-permute-start.40 = (f32[2,2048]{1,0:T(2,128)S(1)}, f32[2,2048]{1,0:T(2,128)S(1)}, u32[]{:S(2)}, u32[]{:S(2)}) collective-permute-start(f32[2,2048]{1,0:T(2,128)S(1)} %fusion.34), channel_id=1, source_target_pairs={{0,12},{4,8},{8,4},{12,0},{1,13},{5,9},{9,5},{13,1},{2,14},{6,10},... | collective-permute-start | bytes 49160 | tf_op jit(solution)/shard_map/ppermute | solution.py:1141
  330.9 3.8 collective-permute-start.41
  334.7 4.3 %collective-permute-start.42 = (f32[2,2048]{1,0:T(2,128)S(1)}, f32[2,2048]{1,0:T(2,128)S(1)}, u32[]{:S(2)}, u32[]{:S(2)}) collective-permute-start(f32[2,2048]{1,0:T(2,128)S(1)} %add.217), channel_id=1, source_target_pairs={{0,96},{32,64},{64,32},{96,0},{1,97},{33,65},{65,33},{97,1},{2,98}... | collective-permute-start | bytes 49160 | tf_op jit(solution)/shard_map/ppermute | solution.py:1141
  350.4 31.0 %copy-start.47 = (bf16[144,2048]{1,0:T(8,128)(2,1)}, bf16[144,2048]{1,0:T(8,128)(2,1)S(1)}, u32[]{:S(2)}) copy-start(bf16[144,2048]{1,0:T(8,128)(2,1)S(1)} %maximum_maximum_fusion.refs_4_) | copy-start | bytes 1769476
  350.4 13.6 %collective-permute-start.43 = (bf16[144,2048]{1,0:T(8,128)(2,1)S(1)}, bf16[144,2048]{1,0:T(8,128)(2,1)S(1)}, u32[]{:S(2)}, u32[]{:S(2)}) collective-permute-start(bf16[144,2048]{1,0:T(8,128)(2,1)S(1)} %maximum_maximum_fusion.refs_4_), channel_id=1, source_target_pairs={{0,3},{1,0},{2,1},{3,2},{4,7},{5,4},{6,5},{7,6},{8,11},{9,8},{10,9... | collective-permute-start | bytes 1769480 | tf_op jit(solution)/shard_map/ppermute | solution.py:23
  351.9 15.1 %collective-permute-start.44 = (bf16[144,2048]{1,0:T(8,128)(2,1)S(1)}, bf16[144,2048]{1,0:T(8,128)(2,1)S(1)}, u32[]{:S(2)}, u32[]{:S(2)}) collective-permute-start(bf16[144,2048]{1,0:T(8,128)(2,1)S(1)} %maximum_maximum_fusion.refs_4_), channel_id=1, source_target_pairs={{0,2},{1,3},{2,0},{3,1},{4,6},{5,7},{6,4},{7,5},{8,10},{9,11},{10,... | collective-permute-start | bytes 1769480 | tf_op jit(solution)/shard_map/ppermute | solution.py:23
  352.4 29.0 %collective-permute-start.45 = (bf16[144,2048]{1,0:T(8,128)(2,1)S(1)}, bf16[144,2048]{1,0:T(8,128)(2,1)S(1)}, u32[]{:S(2)}, u32[]{:S(2)}) collective-permute-start(bf16[144,2048]{1,0:T(8,128)(2,1)S(1)} %maximum_maximum_fusion.refs_4_), channel_id=1, source_target_pairs={{0,1},{1,2},{2,3},{3,0},{4,5},{5,6},{6,7},{7,4},{8,9},{9,10},{10,1... | collective-permute-start | bytes 1769480 | tf_op jit(solution)/shard_map/ppermute | solution.py:23
  364.0 17.4 %copy-start.59 = (bf16[144,2048]{1,0:T(8,128)(2,1)}, bf16[144,2048]{1,0:T(8,128)(2,1)S(1)}, u32[]{:S(2)}) copy-start(bf16[144,2048]{1,0:T(8,128)(2,1)S(1)} %collective-permute-done.43.refs_5_) | copy-start | bytes 1769476
  397.8 2.5 collective-permute-start.46
  (60 other events, 285.8 us)
Sparse Core Ops, SparseCore 0:
  26.8 89.1 all-gather.2
  118.2 64.0 all-gather.4
  295.5 100.9 reduce-scatter.1

commit v4 on v1

--- a/solution.py
+++ b/solution.py
@@ -313,15 +313,34 @@
     other_ref[...] = out[half:].astype(BF)
 
 
-def retain(x_pair, weight, key, value, came, fade, mask, enter, cosine, sine, scalars):
+def retain(x_pair, weight, key, value, came, rate, cosine, sine, scalars):
     rows = x_pair[0].shape[0]
 
     def body(
-        s_ref, a_ref, b_ref, w_ref, k_ref, v_ref, near_ref, mid_ref, far_ref, f_ref, m_ref, e_ref,
-        cos_ref, sin_ref, own_ref, other_ref, query_ref, state_ref, weighted_ref, gate_ref,
-        retained_ref, mixed_ref, sums, turned
+        s_ref, a_ref, b_ref, w_ref, k_ref, v_ref, near_ref, mid_ref, far_ref, r_ref, cos_ref,
+        sin_ref, own_ref, other_ref, query_ref, state_ref, weighted_ref, gate_ref, retained_ref,
+        mixed_ref, m_ref, e_ref, sums, turned
     ):
         step = pl.program_id(0)
+
+        @pl.when(step == 0)
+        def _():
+            rate = r_ref[...]
+
+            def place_of(shape, dim):
+                index = lax.broadcasted_iota(jnp.int32, shape, dim)
+                return lax.rem(index + s_ref[1] * (rows // 4), rows)
+
+            left, right = place_of((rows, rows), 0), place_of((rows, rows), 1)
+            column = place_of((rows, 1), 0)
+            decay = jnp.exp(-rate * jnp.maximum(left - right, 0).astype(F32))
+            for g in (0, 1):
+                length = s_ref[4 + g] - s_ref[3] * rows
+                linked = (left >= right) & ((left >= length) == (right >= length))
+                m_ref[g] = jnp.where(linked, decay, 0.0)
+                e_ref[g * rows : (g + 1) * rows] = jnp.where(
+                    column >= length, 0.0, jnp.exp(-rate * (column.astype(F32) + 1.0))
+                )
 
         @pl.when(step < 4)
         def _():
@@ -343,14 +362,14 @@
 
         @pl.when(step == 3)
         def _():
-            fade = f_ref[...]
+            fade = jnp.exp(-r_ref[...] * rows)
             for g in (0, 1):
                 span = slice(g * rows, (g + 1) * rows)
                 state = near_ref[g].astype(F32) + fade * (
                     mid_ref[g].astype(F32) + fade * far_ref[g].astype(F32)
                 )
                 state_ref[g] = state.astype(BF)
-                query = rotate(sums[span], cos_ref[span], sin_ref[span]).astype(BF)
+                query = rotate(sums[span], cos_ref[...], sin_ref[...]).astype(BF)
                 query_ref[span] = query
                 scores = lax.dot_general(
                     query, k_ref[g], (((1,), (1,)), ((), ())), preferred_element_type=F32
@@ -376,7 +395,7 @@
 
     cols = pl.BlockSpec((rows, SLAB), lambda i, s: (0, jnp.minimum(i, 3)))
     later = pl.BlockSpec((rows, SLAB), lambda i, s: (0, jnp.maximum(i - 4, 0)))
-    operands = (*x_pair, weight, key, value, *came, fade, mask, enter, cosine, sine)
+    operands = (*x_pair, weight, key, value, *came, rate, cosine, sine)
     shapes = (
         sds((rows, D), F32),
         sds((rows, D), BF),
@@ -386,6 +405,8 @@
         sds((2 * rows, DV), F32),
         sds((2 * rows, DV), F32),
         sds((2 * rows, DV), BF),
+        sds((2, rows, rows), F32),
+        sds((2 * rows, 1), F32),
     )
     block = pl.BlockSpec((1, 4, 2, 64, 1280), lambda i, s: (jnp.minimum(i, 3), 0, 0, 0, 0))
     return call(
@@ -583,10 +604,10 @@
                 grad_ref[span, :DV] = (
                     gv_ref[g] + jnp.dot(k_ref[g], state, preferred_element_type=F32)
                 ).astype(BF)
-                grad_key = gk_ref[g] + l_ref[span] * lax.dot_general(
+                grad_key = gk_ref[g] + l_ref[...] * lax.dot_general(
                     v_ref[g], state, (((1,), (1,)), ((), ())), preferred_element_type=F32
                 )
-                grad_ref[span, DV:] = rotate(grad_key, cos_ref[span], -sin_ref[span]).astype(BF)
+                grad_ref[span, DV:] = rotate(grad_key, cos_ref[...], -sin_ref[...]).astype(BF)
 
         out = lax.dot_general(
             jnp.concatenate((a_ref[...], b_ref[...]), axis=0),
@@ -947,9 +968,9 @@
 
 def rotate(values, cosine, sine):
     half = DK // 2
-    first = values[:, :half]
-    second = values[:, half:]
-    return jnp.concatenate((first * cosine - second * sine, first * sine + second * cosine), axis=1)
+    first = values[..., :half]
+    second = values[..., half:]
+    return jnp.concatenate((first * cosine - second * sine, first * sine + second * cosine), axis=-1)
 
 
 def ein(spec, left, right):
@@ -1002,37 +1023,22 @@
     rate = lax.dynamic_index_in_dim(decay_scale, core, 0, False) / 1024.0
     local = (jnp.arange(rows, dtype=jnp.int32) + plane * (rows // 4)) % rows
     index = place * rows + local
-    document = (index[None, :] >= lengths[:, None]).astype(jnp.int32)
-    carried = (document == 0).astype(F32)
     steps = local.astype(F32)
-    offsets = local[:, None] - local[None, :]
-    linked = (offsets >= 0)[None] & (document[:, :, None] == document[:, None, :])
-    mask = jnp.where(
-        linked, jnp.exp(-rate * jnp.maximum(offsets, 0).astype(F32))[None], 0.0
-    )
-    enter = (carried * jnp.exp(-rate * (steps + 1.0))[None])[:, :, None]
     leave = jnp.exp(-rate * (rows - 1.0 - steps))[None, :, None]
     fade = jnp.exp(-rate * rows)
     half = DK // 2
     frequency = 10000.0 ** (-(jnp.arange(half).astype(F32) / half))
     angles = index.astype(F32)[:, None] * frequency[None, :]
-    cosine = jnp.tile(jnp.cos(angles), (2, 1))
-    sine = jnp.tile(jnp.sin(angles), (2, 1))
+    cosine = jnp.cos(angles)
+    sine = jnp.sin(angles)
 
     def spread_state(low, way):
         return [shift_open(low, "ctx", way * o) for o in (1, 2, 3)]
 
-    enter_rows_in = enter.reshape(2 * rows, 1)
-    leave_rows_out = jnp.tile(leave.reshape(rows, 1), (2, 1))
+    leave_rows_out = leave.reshape(rows, 1)
     fade_in = fade.reshape(1, 1)
-    projected = mm_in(
-        *x_first,
-        [(w_kv, 0, 768)],
-        scalars,
-        "project_kv",
-        deps=(mask, enter_rows_in, leave_rows_out, fade_in, cosine, sine),
-    )
-    key = rotate(projected[:, DV:], cosine, sine).astype(BF).reshape(2, rows, DK)
+    projected = mm_in(*x_first, [(w_kv, 0, 768)], scalars, "project_kv")
+    key = rotate(projected[:, DV:].reshape(2, rows, DK), cosine, sine).astype(BF)
     value = projected[:, :DV].astype(BF).reshape(2, rows, DV)
     key_out = (key.astype(F32) * leave).astype(BF)
     state_out = ein("gjd,gje->gde", key_out, value).astype(BF)
@@ -1043,19 +1049,18 @@
         axis=0,
         tiled=True,
     ).reshape(4, 4, 2, 64, -1)
-    own, other, query, state_in, weighted, gate_pre, retained, mixed = retain(
+    own, other, query, state_in, weighted, gate_pre, retained, mixed, mask, enter_rows_in = retain(
         x_first,
         w_goq,
         key,
         value,
         came,
-        fade_in,
-        mask,
-        enter_rows_in,
+        rate.reshape(1, 1),
         cosine,
         sine,
-        scalars,
-    )
+        jnp.concatenate((scalars, lengths)),
+    )
+    enter = enter_rows_in.reshape(2, rows, 1)
     query = query.reshape(2, rows, DK)
     parts = tp_total(chip_blocks(own, swap(other)))
     hidden_state, normed_second = second_norm(tokens, parts, gain_second, scalars)
@@ -1087,7 +1092,7 @@
     grad_query = ein("gij,gjd->gid", grad_scores, key) + enter * ein("gie,gde->gid", grad_low, state_in)
     grad_key = ein("gij,gid->gjd", grad_scores, query)
     grad_value = ein("gij,gie->gje", weighted, grad_low)
-    grad_query = rotate(grad_query.reshape(2 * rows, DK), cosine, -sine).astype(BF)
+    grad_query = rotate(grad_query, cosine, -sine).astype(BF).reshape(2 * rows, DK)
     grads, mark = mm_weight_into(
         grads,
         ((g_state, mixed), (x_first, grad_gate)),

time: 413 us -> 398 us (0.964)
  waiting for transfers between devices: 153 us -> 144 us
    ppermute x6, waiting for transfers between devices: 33.7 us -> 21.1 us  [hop(): return lax.ppermute(value, ('x', 'core', 'ctx'), pairs)]
    ppermute x6, waiting for transfers between devices: 16.1 us -> 23 us  [shift_open(): lax.ppermute(value, axis, [(i, i + offset) for i in range(n) if 0 <= i +...]
    ppermute x18, waiting for transfers between devices: 71.2 us -> 66.9 us  [shift(): return lax.ppermute(value, axis, [(i, (i + offset) % n) for i in range(n)])]
    unnamed x157 -> x122, local copies, waits for them, and re-layouts: 29.8 us -> 26.3 us
  transfers between devices with their start and end apart: 50 -> 50, of which waited for: 34 -> 35; matrix products, arithmetic and copies ran while one was open for 6% -> 5% of each run, Pallas kernels for 18% -> 19%
where the time goes in v4:
time: 398 us; the launch traced here: 396 us
  waiting for transfers between devices  144 us (36%)
  Pallas kernels  119 us (30%)
  starting transfers between devices  65 us (16%)
  local copies, waits for them, and re-layouts  30.4 us (8%)
  between operations  15.7 us (4%)
  other arithmetic  15.4 us (4%)
  matrix products  5.94 us (1%)
    pallas_call x23, Pallas kernels, call(): pl.pallas_call(kernel, out_shape=shapes, grid_spec=pltpu.PrefetchScalarGr...  119 us
    ppermute x18, waiting for transfers between devices, shift(): return lax.ppermute(value, axis, [(i, (i + offset) % n) for i in range(n)])  66.9 us
    unnamed x122, local copies, waits for them, and re-layouts  26.3 us
    ppermute x6, waiting for transfers between devices, shift_open(): lax.ppermute(value, axis, [(i, i + offset) for i in range(n) if 0 <= i +...  23 us
    ppermute x6, waiting for transfers between devices, hop(): return lax.ppermute(value, ('x', 'core', 'ctx'), pairs)  21.1 us
    ppermute x18, starting transfers between devices, shift(): return lax.ppermute(value, axis, [(i, (i + offset) % n) for i in range(n)])  19.7 us
    ppermute x12, waiting for transfers between devices, swap(): return lax.ppermute(value, 'core', [(0, 1), (1, 0)])  13.9 us
    ppermute x6, starting transfers between devices, shift_open(): lax.ppermute(value, axis, [(i, i + offset) for i in range(n) if 0 <= i +...  12.8 us
  transfers between devices with their start and end apart: 50, of which 35 were waited for; matrix products, arithmetic and copies ran while one was open for 5% of the time, Pallas kernels for 19%

profile of v4, /device:TPU:1, one launch (start us, length us, event | category | flops | bytes accessed | tf_op | source)
XLA Modules:
  0.0 395.7 jit_solution(124688136372609551)
XLA Ops:
  7.9 2.6 split_attn.1
  13.9 2.5 stack_attn.1
  17.9 2.5 collective-permute-start.3
  22.8 3.2 collective-permute-done.3.refs_3_.refs_2_
  26.0 1.6 copy-done.7
  30.1 1.6 collective-permute-start.5
  32.5 1.6 collective-permute-done
  36.8 2.1 collective-permute-start.7
  42.0 7.7 %collective-permute-done.6.refs_3_.refs_2_ = bf16[4,2,64,768]{3,2,1,0:T(8,128)(2,1)} collective-permute-done((bf16[4,2,64,768]{3,2,1,0:T(8,128)(2,1)S(1)}, bf16[4,2,64,768]{3,2,1,0:T(8,128)(2,1)}, u32[]{:S(2)}, u32[]{:S(2)}) %collective-permute-start.6) | collective-permute-done | bytes 786464 | tf_op jit(solution)/shard_map/ppermute | solution.py:148
  49.7 8.9 %collective-permute-done.7.refs_4_.refs_3_ = bf16[4,2,64,768]{3,2,1,0:T(8,128)(2,1)} collective-permute-done((bf16[4,2,64,768]{3,2,1,0:T(8,128)(2,1)S(1)}, bf16[4,2,64,768]{3,2,1,0:T(8,128)(2,1)}, u32[]{:S(2)}, u32[]{:S(2)}) %collective-permute-start.7) | collective-permute-done | bytes 786464 | tf_op jit(solution)/shard_map/ppermute | solution.py:148
  58.6 5.6 %project_kv.1 = f32[512,768]{1,0:T(8,128)S(1)} custom-call(s32[4]{0:T(128)S(1)} %copy-done.25, bf16[256,2048]{1,0:T(8,128)(2,1)S(1)} %enter_rows.1.refs_0_.refs_3_.refs_9_, bf16[256,2048]{1,0:T(8,128)(2,1)S(1)} %collective-permute-done.5.refs_1_.refs_4_.refs_10_, bf16[4,2,64,768]{3,2,1,0:T(8,128)(2,1)S(1)} %bitcast.45, ...), custom_call_target="tpu_custom_call" | custom-call | flops 1 | bytes 1 | tf_op jit(solution)/shard_map/project_kv/pallas_call | solution.py:61
  65.0 2.9 collective-permute-start.9
  67.9 4.5 %collective-permute-start.10 = (bf16[2,256,512]{2,1,0:T(8,128)(2,1)S(1)}, bf16[2,256,512]{2,1,0:T(8,128)(2,1)S(1)}, u32[]{:S(2)}, u32[]{:S(2)}) collective-permute-start(bf16[2,256,512]{2,1,0:T(8,128)(2,1)S(1)} %convolution_convert_fusion), channel_id=1, source_target_pairs={{0,8},{4,12},{1,9},{5,13},{2,10},{6,14},{3,11},{7,15},{16,24},{20,... | collective-permute-start | bytes 1572872 | tf_op jit(solution)/shard_map/ppermute | solution.py:28
  73.7 2.5 split_mlp.1
  78.5 10.7 %collective-permute-done.9.refs_5_.refs_2_ = bf16[2,256,512]{2,1,0:T(8,128)(2,1)S(1)} collective-permute-done((bf16[2,256,512]{2,1,0:T(8,128)(2,1)S(1)}, bf16[2,256,512]{2,1,0:T(8,128)(2,1)S(1)}, u32[]{:S(2)}, u32[]{:S(2)}) %collective-permute-start.9) | collective-permute-done | bytes 524320 | tf_op jit(solution)/shard_map/ppermute | solution.py:28
  89.2 11.3 %collective-permute-done.10.refs_6_.refs_3_ = bf16[2,256,512]{2,1,0:T(8,128)(2,1)S(1)} collective-permute-done((bf16[2,256,512]{2,1,0:T(8,128)(2,1)S(1)}, bf16[2,256,512]{2,1,0:T(8,128)(2,1)S(1)}, u32[]{:S(2)}, u32[]{:S(2)}) %collective-permute-start.10) | collective-permute-done | bytes 524320 | tf_op jit(solution)/shard_map/ppermute | solution.py:28
  105.2 13.1 %retain.1 = (f32[256,2048]{1,0:T(8,128)}, bf16[256,2048]{1,0:T(8,128)(2,1)}, bf16[512,256]{1,0:T(8,128)(2,1)}, bf16[2,256,512]{2,1,0:T(8,128)(2,1)}, bf16[2,256,...) custom-call(s32[6]{0:T(128)} %concatenate.27.s_ref, ...), custom_call_target="tpu_custom_call" | custom-call | flops 1 | bytes 1 | tf_op jit(solution)/shard_map/retain/pallas_call | solution.py:61
  119.0 2.5 collective-permute-done.12
  121.5 1.7 add_convert_fusion.9
  123.3 3.1 collective-permute-start.15
  126.4 1.6 collective-permute-start.13
  128.0 9.2 %collective-permute-done.15 = bf16[64,2048]{1,0:T(8,128)(2,1)S(1)} collective-permute-done((bf16[64,2048]{1,0:T(8,128)(2,1)S(1)}, bf16[64,2048]{1,0:T(8,128)(2,1)S(1)}, u32[]{:S(2)}, u32[]{:S(2)}) %collective-permute-start.15) | collective-permute-done | bytes 262176 | tf_op jit(solution)/shard_map/ppermute | solution.py:23
  137.2 2.2 collective-permute-done.13
  140.6 1.6 collective-permute-start.16
  144.1 2.2 collective-permute-start.20
  146.3 1.8 collective-permute-done.16.refs_3_
  148.1 2.1 collective-permute-done.17.refs_4_
  150.3 7.4 %collective-permute-done.18.refs_5_ = bf16[64,2048]{1,0:T(8,128)(2,1)S(1)} collective-permute-done((bf16[64,2048]{1,0:T(8,128)(2,1)S(1)}, bf16[64,2048]{1,0:T(8,128)(2,1)S(1)}, u32[]{:S(2)}, u32[]{:S(2)}) %collective-permute-start.18) | collective-permute-done | bytes 262176 | tf_op jit(solution)/shard_map/ppermute | solution.py:23
  163.3 3.7 all-gather.5.cloned.1.call-done
  167.0 14.4 %mlp.1 = (f32[256,2048]{1,0:T(8,128)}, bf16[256,2048]{1,0:T(8,128)(2,1)}, f32[8,2048]{1,0:T(8,128)}, bf16[512,1024]{1,0:T(8,128)(2,1)}, bf16[512,512]{1,0:T(8,128)(2,1)}) custom-call(s32[4]{0:T(128)} %pad_add_fusion.s_ref, bf16[256,2048]{1,0:T(8,128)(2,1)} %copy-done.14, bf16[256,2048]{1,0:T(8,128)(2,1)} %collective-permute-done.19.refs_1_, ...), custom_call_target="tpu_custom_call" | custom-call | flops 1 | bytes 1 | tf_op jit(solution)/shard_map/mlp/pallas_call | solution.py:61
  182.2 2.5 collective-permute-done.22
  184.7 2.3 add_convert_fusion.4
  187.0 2.7 collective-permute-start.25
  189.6 1.7 collective-permute-start.23
  191.3 6.9 %weight_mlp.1 = (bf16[4,4,2,64,3584]{4,3,2,1,0:T(8,128)(2,1)}, f32[8,128]{1,0:T(8,128)}) custom-call(s32[4]{0:T(128)} %pad_add_fusion.s_ref, bf16[256,2048]{1,0:T(8,128)(2,1)} %copy-done.14, bf16[256,2048]{1,0:T(8,128)(2,1)} %collective-permute-done.19.refs_1_, bf16[512,1024]{1,0:T(8,128)(2,1)} %get-tuple-element.80.refs_2_), custom_call_target="tpu_custom_call" | custom-call | flops 1 | bytes 1 | tf_op jit(solution)/shard_map/weight_mlp/pallas_call | solution.py:61
  198.2 2.5 collective-permute-done.25
  200.7 1.9 collective-permute-done.23
  202.7 1.9 add_convert_fusion.1.refs_0_
  207.0 2.8 copy-done.6
  210.8 2.8 project_down.1
  215.9 5.5 %collective-permute-done.28.refs_6_ = bf16[64,2048]{1,0:T(8,128)(2,1)S(1)} collective-permute-done((bf16[64,2048]{1,0:T(8,128)(2,1)}, bf16[64,2048]{1,0:T(8,128)(2,1)S(1)}, u32[]{:S(2)}, u32[]{:S(2)}) %collective-permute-start.28) | collective-permute-done | bytes 262176 | tf_op jit(solution)/shard_map/ppermute | solution.py:23
  222.1 6.1 %second_back.1 = (f32[256,2048]{1,0:T(8,128)}, bf16[256,2048]{1,0:T(8,128)(2,1)}) custom-call(s32[4]{0:T(128)} %pad_add_fusion.s_ref, f32[256,2048]{1,0:T(8,128)} %copy-done.10, f32[256,2048]{1,0:T(8,128)} %refs_1_.6, f32[1,2048]{1,0:T(1,128)} %bitcast.47, bf16[64,2048]{1,0:T(8,128)(2,1)} %tie.4.refs_2_.refs_3_, bf16[64,2048]{1,0:T(8,128)(2,1)} %copy-done.56, ...), custom_call_target="tpu_custom_call" | custom-call | flops 1 | bytes 1 | tf_op jit(solution)/shard_map/second_back/pallas_call | solution.py:61
  229.8 1.5 collective-permute-done.29.refs_1_
  232.3 9.6 %back_gate.1 = (bf16[512,512]{1,0:T(8,128)(2,1)}, bf16[512,512]{1,0:T(8,128)(2,1)}, bf16[2,256,512]{2,1,0:T(8,128)(2,1)}) custom-call(s32[4]{0:T(128)} %pad_add_fusion.s_ref, bf16[256,2048]{1,0:T(8,128)(2,1)} %get-tuple-element.85.refs_0_, bf16[256,2048]{1,0:T(8,128)(2,1)} %copy-done.39, bf16[4,4,2,64,1280]{4,3,2,1,0:T(8,128)(2,1)} %bitcast.37, ...), custom_call_target="tpu_custom_call" | custom-call | flops 1 | bytes 1 | tf_op jit(solution)/shard_map/back_gate/pallas_call | solution.py:61
  246.1 1.5 fusion.15
  250.1 7.2 %weight_og.1 = (bf16[4,4,2,64,3584]{4,3,2,1,0:T(8,128)(2,1)}, f32[8,128]{1,0:T(8,128)}) custom-call(s32[4]{0:T(128)} %pad_add_fusion.s_ref, bf16[256,2048]{1,0:T(8,128)(2,1)} %get-tuple-element.85.refs_0_, bf16[256,2048]{1,0:T(8,128)(2,1)} %copy-done.39, bf16[512,512]{1,0:T(8,128)(2,1)} %get-tuple-element.94.refs_2_, ...), custom_call_target="tpu_custom_call", output_to_operand_aliasing={{0}: (7, {})} | custom-call | flops 1 | bytes 1 | tf_op jit(solution)/shard_map/weight_og/pallas_call | solution.py:61
  257.3 5.5 %weight_down.1 = (bf16[4,4,2,64,3584]{4,3,2,1,0:T(8,128)(2,1)}, f32[8,128]{1,0:T(8,128)}) custom-call(s32[4]{0:T(128)} %pad_add_fusion.s_ref, bf16[256,2048]{1,0:T(8,128)(2,1)} %copy-done.9, bf16[256,2048]{1,0:T(8,128)(2,1)} %copy-done.40, bf16[512,512]{1,0:T(8,128)(2,1)} %get-tuple-element.82.refs_0_.refs_2_, ...), custom_call_target="tpu_custom_call", output_to_operand_aliasing={{0}: (4, {})} | custom-call | flops 1 | bytes 1 | tf_op jit(solution)/shard_map/weight_down/pallas_call | solution.py:61
  262.9 5.2 %weight_query.1 = (bf16[4,4,2,64,3584]{4,3,2,1,0:T(8,128)(2,1)}, f32[8,128]{1,0:T(8,128)}) custom-call(s32[4]{0:T(128)} %pad_add_fusion.s_ref, bf16[256,2048]{1,0:T(8,128)(2,1)} %copy-done.4, bf16[256,2048]{1,0:T(8,128)(2,1)} %copy-done.1, bf16[512,256]{1,0:T(8,128)(2,1)} %pad_maximum_fusion.1.refs_2_.refs_7_, ...), custom_call_target="tpu_custom_call", output_to_operand_aliasing={{0}: (4, {})} | custom-call | flops 1 | bytes 1 | tf_op jit(solution)/shard_map/weight_query/pallas_call | solution.py:61
  272.0 7.9 %weight_last.1 = (bf16[4,4,2,64,3584]{4,3,2,1,0:T(8,128)(2,1)}, f32[8,128]{1,0:T(8,128)}, bf16[512,768]{1,0:T(8,128)(2,1)}) custom-call(s32[4]{0:T(128)} %pad_add_fusion.s_ref, bf16[256,2048]{1,0:T(8,128)(2,1)} %copy-done.4, bf16[256,2048]{1,0:T(8,128)(2,1)} %copy-done.1, bf16[2,256,512]{2,1,0:T(8,128)(2,1)} %tie.5.refs_2_, ...), custom_call_target="tpu_custom_call", output_to_operand_aliasing={{0}: (14, {})} | custom-call | flops 1 | bytes 1 | tf_op jit(solution)/shard_map/weight_last/pallas_call | solution.py:61
  281.5 2.5 copy-done
  286.1 7.5 %back_attn.1 = (f32[256,2048]{1,0:T(8,128)S(1)}, bf16[256,2048]{1,0:T(8,128)(2,1)S(1)}, f32[8,2048]{1,0:T(8,128)S(1)}) custom-call(s32[4]{0:T(128)S(1)} %copy-done.28, bf16[512,768]{1,0:T(8,128)(2,1)S(1)} %copy-done.23, bf16[4,2,64,768]{3,2,1,0:T(8,128)(2,1)S(1)} %bitcast.46, bf16[4,2,64,768]{3,2,1,0:T(8,128)(2,1)} %collective-permute-done.6.refs_3_.refs_2_, ...), custom_call_target="tpu_custom_call" | custom-call | flops 1 | bytes 1 | tf_op jit(solution)/shard_map/back_attn/pallas_call | solution.py:61
  301.7 5.7 %third_blocks.1 = (bf16[128,2048]{1,0:T(8,128)(2,1)}, bf16[128,2048]{1,0:T(8,128)(2,1)}, bf16[128,2048]{1,0:T(8,128)(2,1)}, bf16[128,2048]{1,0:T(8,128)(2,1)}) custom-call(s32[4]{0:T(128)} %pad_add_fusion.s_ref, f32[256,2048]{1,0:T(8,128)} %copy-done.18, bf16[256,2048]{1,0:T(8,128)(2,1)} %copy-done.47, f32[256,2048]{1,0:T(8,128)} %copy-done.17, ...), custom_call_target="tpu_custom_call" | custom-call | flops 1 | bytes 1 | tf_op jit(solution)/shard_map/third_blocks/pallas_call | solution.py:61
  309.2 6.4 %collective-permute-start.40 = (f32[2,2048]{1,0:T(2,128)S(1)}, f32[2,2048]{1,0:T(2,128)S(1)}, u32[]{:S(2)}, u32[]{:S(2)}) collective-permute-start(f32[2,2048]{1,0:T(2,128)S(1)} %fusion.29), channel_id=1, source_target_pairs={{0,12},{4,8},{8,4},{12,0},{1,13},{5,9},{9,5},{13,1},{2,14},{6,10},... | collective-permute-start | bytes 49160 | tf_op jit(solution)/shard_map/ppermute | solution.py:1145
  315.5 1.8 collective-permute-done.40
  318.9 2.1 collective-permute-done.41
  321.0 2.4 collective-permute-start.42
  323.5 2.1 collective-permute-done.42
  325.6 6.0 %collective-permute-done.35 = bf16[128,2048]{1,0:T(8,128)(2,1)S(1)} collective-permute-done((bf16[128,2048]{1,0:T(8,128)(2,1)}, bf16[128,2048]{1,0:T(8,128)(2,1)S(1)}, u32[]{:S(2)}, u32[]{:S(2)}) %collective-permute-start.35) | collective-permute-done | bytes 524320 | tf_op jit(solution)/shard_map/ppermute | solution.py:23
  333.2 2.5 collective-permute-start.43
  336.9 12.4 %collective-permute-done.43.refs_5_ = bf16[144,2048]{1,0:T(8,128)(2,1)S(1)} collective-permute-done((bf16[144,2048]{1,0:T(8,128)(2,1)S(1)}, bf16[144,2048]{1,0:T(8,128)(2,1)S(1)}, u32[]{:S(2)}, u32[]{:S(2)}) %collective-permute-start.43) | collective-permute-done | bytes 589856 | tf_op jit(solution)/shard_map/ppermute | solution.py:23
  350.3 14.8 %collective-permute-done.45.refs_7_ = bf16[144,2048]{1,0:T(8,128)(2,1)S(1)} collective-permute-done((bf16[144,2048]{1,0:T(8,128)(2,1)S(1)}, bf16[144,2048]{1,0:T(8,128)(2,1)S(1)}, u32[]{:S(2)}, u32[]{:S(2)}) %collective-permute-start.45) | collective-permute-done | bytes 589856 | tf_op jit(solution)/shard_map/ppermute | solution.py:23
  365.9 7.4 %leave_rows.1 = (f32[256,2048]{1,0:T(8,128)}, f32[256,2048]{1,0:T(8,128)}) custom-call(s32[4]{0:T(128)} %pad_add_fusion.s_ref, f32[256,2048]{1,0:T(8,128)} %copy-done.10, f32[256,2048]{1,0:T(8,128)} %refs_1_.7, f32[256,2048]{1,0:T(8,128)} %get-tuple-element.84.refs_2_, f32[1,2048]{1,0:T(1,128)} %bitcast.49, bf16[144,2048]{1,0:T(8,128)(2,1)} %copy-done.44, ...), custom_call_target="tpu_custom_call" | custom-call | flops 1 | bytes 1 | tf_op jit(solution)/shard_map/leave_rows/pallas_call | solution.py:61
  375.5 8.3 %reduce-scatter.2.cloned.1.call-done.refs_0_ = bf16[128,3584]{1,0:T(8,128)(2,1)} async-done(((bf16[2048,3584]{1,0:T(8,128)(2,1)}), bf16[128,3584]{1,0:T(8,128)(2,1)}) %reduce-scatter.2.cloned.1.call-update) | async-done | bytes 917520 | tf_op jit(solution)/shard_map/reduce_scatter | solution.py:1126
  387.3 1.8 join_heads.1
  (232 shorter events, 80.1 us)
Async XLA Ops:
  7.2 98.1 %all-gather.3.cloned.1.call-start = ((), (), s32[]{:S(2)}) async-start(), calls=%async_computation.1 | async-start | bytes 5570560 | tf_op jit(solution)/shard_map/all_gather | solution.py:1011
  10.4 2.8 collective-permute-start.1
  16.4 18.5 %copy-start.25 = (s32[4]{0:T(128)S(1)}, s32[4]{0:T(128)}, u32[]{:S(2)}) copy-start(s32[4]{0:T(128)} %pad_add_fusion.s_ref) | copy-start | bytes 52
  16.4 18.5 %copy-start.31 = (bf16[128,768]{1,0:T(8,128)(2,1)S(1)}, bf16[128,768]{1,0:T(8,128)(2,1)}, u32[]{:S(2)}) copy-start(bf16[128,768]{1,0:T(8,128)(2,1)} %get-tuple-element.70.refs_0_) | copy-start | bytes 589828
  16.4 150.6 %all-gather.5.cloned.1.call-start = ((), (), s32[]{:S(2)}) async-start(), calls=%async_computation.2 | async-start | bytes 6684672 | tf_op jit(solution)/shard_map/all_gather | solution.py:1046
  16.5 6.3 %collective-permute-start.2 = (bf16[128,768]{1,0:T(8,128)(2,1)}, bf16[128,768]{1,0:T(8,128)(2,1)S(1)}, u32[]{:S(2)}, u32[]{:S(2)}) collective-permute-start(bf16[128,768]{1,0:T(8,128)(2,1)} %get-tuple-element.70.refs_0_), channel_id=1, source_target_pairs={{0,4},{4,8},{8,12},{12,0},{16,48},{20,52},{24,56},{28,60},{32,36},... | collective-permute-start | bytes 589832 | tf_op jit(solution)/shard_map/ppermute | solution.py:148
  17.9 8.1 %collective-permute-start.3 = (bf16[128,768]{1,0:T(8,128)(2,1)}, bf16[128,768]{1,0:T(8,128)(2,1)S(1)}, u32[]{:S(2)}, u32[]{:S(2)}) collective-permute-start(bf16[128,768]{1,0:T(8,128)(2,1)} %get-tuple-element.70.refs_0_), channel_id=1, source_target_pairs={{0,8},{4,12},{8,0},{12,4},{16,80},{20,84},{24,88},{28,92},{32,40},... | collective-permute-start | bytes 589832 | tf_op jit(solution)/shard_map/ppermute | solution.py:148
  20.3 5.7 %collective-permute-start.4 = (bf16[128,768]{1,0:T(8,128)(2,1)}, bf16[128,768]{1,0:T(8,128)(2,1)S(1)}, u32[]{:S(2)}, u32[]{:S(2)}) collective-permute-start(bf16[128,768]{1,0:T(8,128)(2,1)} %get-tuple-element.70.refs_0_), channel_id=1, source_target_pairs={{0,12},{4,0},{8,4},{12,8},{16,112},{20,116},{24,120},{28,124},{32,... | collective-permute-start | bytes 589832 | tf_op jit(solution)/shard_map/ppermute | solution.py:148
  30.1 34.1 %copy-start.4 = (bf16[256,2048]{1,0:T(8,128)(2,1)}, bf16[256,2048]{1,0:T(8,128)(2,1)S(1)}, u32[]{:S(2)}) copy-start(bf16[256,2048]{1,0:T(8,128)(2,1)S(1)} %enter_rows.1.refs_0_.refs_3_.refs_9_) | copy-start | bytes 3145732
  30.1 28.5 %collective-permute-start.5 = (bf16[256,2048]{1,0:T(8,128)(2,1)S(1)}, bf16[256,2048]{1,0:T(8,128)(2,1)S(1)}, u32[]{:S(2)}, u32[]{:S(2)}) collective-permute-start(bf16[256,2048]{1,0:T(8,128)(2,1)S(1)} %enter_rows.1.refs_0_.refs_3_.refs_9_), channel_id=1, source_target_pairs={{0,16},{16,0},{1,17},{17,1},{2,18},{18,2},{3,19},{19,3},{4,20},{20... | collective-permute-start | bytes 3145736 | tf_op jit(solution)/shard_map/ppermute | solution.py:34
  31.8 2.4 collective-permute-start
  35.5 14.3 %collective-permute-start.6 = (bf16[4,2,64,768]{3,2,1,0:T(8,128)(2,1)S(1)}, bf16[4,2,64,768]{3,2,1,0:T(8,128)(2,1)}, u32[]{:S(2)}, u32[]{:S(2)}) collective-permute-start(bf16[4,2,64,768]{3,2,1,0:T(8,128)(2,1)S(1)} %bitcast.42), channel_id=1, source_target_pairs={{0,32},{4,36},{8,40},{12,44},{16,20},{20,24},{24,28},{28,16},{32,6... | collective-permute-start | bytes 2359304 | tf_op jit(solution)/shard_map/ppermute | solution.py:148
  36.8 21.8 %collective-permute-start.7 = (bf16[4,2,64,768]{3,2,1,0:T(8,128)(2,1)S(1)}, bf16[4,2,64,768]{3,2,1,0:T(8,128)(2,1)}, u32[]{:S(2)}, u32[]{:S(2)}) collective-permute-start(bf16[4,2,64,768]{3,2,1,0:T(8,128)(2,1)S(1)} %bitcast.43), channel_id=1, source_target_pairs={{0,64},{4,68},{8,72},{12,76},{16,24},{20,28},{24,16},{28,20},{32,9... | collective-permute-start | bytes 2359304 | tf_op jit(solution)/shard_map/ppermute | solution.py:148
  38.9 19.7 %collective-permute-start.8 = (bf16[4,2,64,768]{3,2,1,0:T(8,128)(2,1)S(1)}, bf16[4,2,64,768]{3,2,1,0:T(8,128)(2,1)}, u32[]{:S(2)}, u32[]{:S(2)}) collective-permute-start(bf16[4,2,64,768]{3,2,1,0:T(8,128)(2,1)S(1)} %bitcast.44), channel_id=1, source_target_pairs={{0,96},{4,100},{8,104},{12,108},{16,28},{20,16},{24,20},{28,24},{3... | collective-permute-start | bytes 2359304 | tf_op jit(solution)/shard_map/ppermute | solution.py:148
  42.0 22.4 %copy-start.41 = (f32[256,128]{1,0:T(8,128)}, f32[256,128]{1,0:T(8,128)S(1)}, u32[]{:S(2)}) copy-start(f32[256,128]{1,0:T(8,128)S(1)} %get-tuple-element.140.refs_9_.refs_11_) | copy-start | bytes 393220
  42.0 22.4 %copy-start.45 = (f32[256,128]{1,0:T(8,128)}, f32[256,128]{1,0:T(8,128)S(1)}, u32[]{:S(2)}) copy-start(f32[256,128]{1,0:T(8,128)S(1)} %get-tuple-element.139.refs_10_.refs_12_) | copy-start | bytes 393220
  64.3 36.4 %copy-start.26 = (s32[4]{0:T(128)S(1)}, s32[4]{0:T(128)}, u32[]{:S(2)}) copy-start(s32[4]{0:T(128)} %pad_add_fusion.s_ref) | copy-start | bytes 52
  64.4 38.8 %copy-start.36 = (bf16[512,512]{1,0:T(8,128)(2,1)}, bf16[512,512]{1,0:T(8,128)(2,1)S(1)}, u32[]{:S(2)}) copy-start(bf16[512,512]{1,0:T(8,128)(2,1)S(1)} %slice.185) | copy-start | bytes 1572868
  64.6 38.6 %copy-start.43 = (bf16[2,256,256]{2,1,0:T(8,128)(2,1)}, bf16[2,256,256]{2,1,0:T(8,128)(2,1)S(1)}, u32[]{:S(2)}) copy-start(bf16[2,256,256]{2,1,0:T(8,128)(2,1)S(1)} %multiply_convert_fusion.refs_7_) | copy-start | bytes 786436
  65.0 24.2 %collective-permute-start.9 = (bf16[2,256,512]{2,1,0:T(8,128)(2,1)S(1)}, bf16[2,256,512]{2,1,0:T(8,128)(2,1)S(1)}, u32[]{:S(2)}, u32[]{:S(2)}) collective-permute-start(bf16[2,256,512]{2,1,0:T(8,128)(2,1)S(1)} %convolution_convert_fusion), channel_id=1, source_target_pairs={{0,4},{4,8},{8,12},{1,5},{5,9},{9,13},{2,6},{6,10},{10,14},{3,7},{... | collective-permute-start | bytes 1572872 | tf_op jit(solution)/shard_map/ppermute | solution.py:28
  67.9 32.6 %collective-permute-start.10 = (bf16[2,256,512]{2,1,0:T(8,128)(2,1)S(1)}, bf16[2,256,512]{2,1,0:T(8,128)(2,1)S(1)}, u32[]{:S(2)}, u32[]{:S(2)}) collective-permute-start(bf16[2,256,512]{2,1,0:T(8,128)(2,1)S(1)} %convolution_convert_fusion), channel_id=1, source_target_pairs={{0,8},{4,12},{1,9},{5,13},{2,10},{6,14},{3,11},{7,15},{16,24},{20,... | collective-permute-start | bytes 1572872 | tf_op jit(solution)/shard_map/ppermute | solution.py:28
  72.3 28.4 %collective-permute-start.11 = (bf16[2,256,512]{2,1,0:T(8,128)(2,1)S(1)}, bf16[2,256,512]{2,1,0:T(8,128)(2,1)S(1)}, u32[]{:S(2)}, u32[]{:S(2)}) collective-permute-start(bf16[2,256,512]{2,1,0:T(8,128)(2,1)S(1)} %convolution_convert_fusion), channel_id=1, source_target_pairs={{0,12},{1,13},{2,14},{3,15},{16,28},{17,29},{18,30},{19,31},{32,44... | collective-permute-start | bytes 1572872 | tf_op jit(solution)/shard_map/ppermute | solution.py:28
  76.1 2.4 collective-permute-start.21
  103.2 280.5 %reduce-scatter.2.cloned.1.call-start = ((), (), s32[]{:S(2)}) async-start(), calls=%async_computation.3 | async-start | bytes 15597568 | tf_op jit(solution)/shard_map/reduce_scatter | solution.py:1126
  118.3 3.2 collective-permute-start.12
  121.5 21.8 %copy-start.2 = (bf16[256,2048]{1,0:T(8,128)(2,1)S(1)}, bf16[256,2048]{1,0:T(8,128)(2,1)}, u32[]{:S(2)}) copy-start(bf16[256,2048]{1,0:T(8,128)(2,1)} %copy-done.1) | copy-start | bytes 3145732
  121.5 21.8 %copy-start.11 = (f32[256,2048]{1,0:T(8,128)S(1)}, f32[256,2048]{1,0:T(8,128)}, u32[]{:S(2)}) copy-start(f32[256,2048]{1,0:T(8,128)} %refs_1_.6) | copy-start | bytes 6291460
  123.3 13.9 %collective-permute-start.15 = (bf16[64,2048]{1,0:T(8,128)(2,1)S(1)}, bf16[64,2048]{1,0:T(8,128)(2,1)S(1)}, u32[]{:S(2)}, u32[]{:S(2)}) collective-permute-start(bf16[64,2048]{1,0:T(8,128)(2,1)S(1)} %get-tuple-element.128), channel_id=1, source_target_pairs={{0,3},{1,0},{2,1},{3,2},{4,7},{5,4},{6,5},{7,6},{8,11},{9,8},{10,9... | collective-permute-start | bytes 786440 | tf_op jit(solution)/shard_map/ppermute | solution.py:23
  126.4 10.8 %collective-permute-start.14 = (bf16[64,2048]{1,0:T(8,128)(2,1)S(1)}, bf16[64,2048]{1,0:T(8,128)(2,1)S(1)}, u32[]{:S(2)}, u32[]{:S(2)}) collective-permute-start(bf16[64,2048]{1,0:T(8,128)(2,1)S(1)} %get-tuple-element.129), channel_id=1, source_target_pairs={{0,1},{1,2},{2,3},{3,0},{4,5},{5,6},{6,7},{7,4},{8,9},{9,10},{10,1... | collective-permute-start | bytes 786440 | tf_op jit(solution)/shard_map/ppermute | solution.py:23
  126.4 13.0 %collective-permute-start.13 = (bf16[64,2048]{1,0:T(8,128)(2,1)S(1)}, bf16[64,2048]{1,0:T(8,128)(2,1)S(1)}, u32[]{:S(2)}, u32[]{:S(2)}) collective-permute-start(bf16[64,2048]{1,0:T(8,128)(2,1)S(1)} %get-tuple-element.127), channel_id=1, source_target_pairs={{0,2},{1,3},{2,0},{3,1},{4,6},{5,7},{6,4},{7,5},{8,10},{9,11},{10,... | collective-permute-start | bytes 786440 | tf_op jit(solution)/shard_map/ppermute | solution.py:23
  140.6 17.1 %copy-start.8 = (f32[256,2048]{1,0:T(8,128)S(1)}, f32[256,2048]{1,0:T(8,128)}, u32[]{:S(2)}) copy-start(f32[256,2048]{1,0:T(8,128)} %refs_1_.7) | copy-start | bytes 6291460
  140.6 17.1 %copy-start.32 = (f32[2048]{0:T(1024)S(1)}, f32[2048]{0:T(1024)}, u32[]{:S(2)}) copy-start(f32[2048]{0:T(1024)} %param.17) | copy-start | bytes 24580
  140.6 7.5 %collective-permute-start.16 = (bf16[64,2048]{1,0:T(8,128)(2,1)S(1)}, bf16[64,2048]{1,0:T(8,128)(2,1)S(1)}, u32[]{:S(2)}, u32[]{:S(2)}) collective-permute-start(bf16[64,2048]{1,0:T(8,128)(2,1)S(1)} %add_convert_fusion.6.refs_2_), channel_id=1, source_target_pairs={{0,3},{1,0},{2,1},{3,2},{4,7},{5,4},{6,5},{7,6},{8,11},{9,8},{10,9... | collective-permute-start | bytes 786440 | tf_op jit(solution)/shard_map/ppermute | solution.py:23
  142.2 8.0 %collective-permute-start.17 = (bf16[64,2048]{1,0:T(8,128)(2,1)S(1)}, bf16[64,2048]{1,0:T(8,128)(2,1)S(1)}, u32[]{:S(2)}, u32[]{:S(2)}) collective-permute-start(bf16[64,2048]{1,0:T(8,128)(2,1)S(1)} %add_convert_fusion.6.refs_2_), channel_id=1, source_target_pairs={{0,2},{1,3},{2,0},{3,1},{4,6},{5,7},{6,4},{7,5},{8,10},{9,11},{10,... | collective-permute-start | bytes 786440 | tf_op jit(solution)/shard_map/ppermute | solution.py:23
  142.6 15.1 %collective-permute-start.18 = (bf16[64,2048]{1,0:T(8,128)(2,1)S(1)}, bf16[64,2048]{1,0:T(8,128)(2,1)S(1)}, u32[]{:S(2)}, u32[]{:S(2)}) collective-permute-start(bf16[64,2048]{1,0:T(8,128)(2,1)S(1)} %add_convert_fusion.6.refs_2_), channel_id=1, source_target_pairs={{0,1},{1,2},{2,3},{3,0},{4,5},{5,6},{6,7},{7,4},{8,9},{9,10},{10,1... | collective-permute-start | bytes 786440 | tf_op jit(solution)/shard_map/ppermute | solution.py:23
  144.1 22.9 %copy-start.9 = (bf16[256,2048]{1,0:T(8,128)(2,1)}, bf16[256,2048]{1,0:T(8,128)(2,1)S(1)}, u32[]{:S(2)}) copy-start(bf16[256,2048]{1,0:T(8,128)(2,1)S(1)} %low_rows.1.refs_2_.refs_0_) | copy-start | bytes 3145732
  144.1 16.7 %collective-permute-start.20 = (bf16[256,2048]{1,0:T(8,128)(2,1)S(1)}, bf16[256,2048]{1,0:T(8,128)(2,1)S(1)}, u32[]{:S(2)}, u32[]{:S(2)}) collective-permute-start(bf16[256,2048]{1,0:T(8,128)(2,1)S(1)} %low_rows.1.refs_2_.refs_0_), channel_id=1, source_target_pairs={{0,16},{16,0},{1,17},{17,1},{2,18},{18,2},{3,19},{19,3},{4,20},{20... | collective-permute-start | bytes 3145736 | tf_op jit(solution)/shard_map/ppermute | solution.py:34
  160.5 2.8 collective-permute-start.19
  181.4 3.3 collective-permute-start.22
  187.0 13.8 %collective-permute-start.25 = (bf16[64,2048]{1,0:T(8,128)(2,1)}, bf16[64,2048]{1,0:T(8,128)(2,1)S(1)}, u32[]{:S(2)}, u32[]{:S(2)}) collective-permute-start(bf16[64,2048]{1,0:T(8,128)(2,1)} %get-tuple-element.125), channel_id=1, source_target_pairs={{0,3},{1,0},{2,1},{3,2},{4,7},{5,4},{6,5},{7,6},{8,11},{9,8},{10,9... | collective-permute-start | bytes 786440 | tf_op jit(solution)/shard_map/ppermute | solution.py:23
  189.6 11.1 %collective-permute-start.24 = (bf16[64,2048]{1,0:T(8,128)(2,1)S(1)}, bf16[64,2048]{1,0:T(8,128)(2,1)S(1)}, u32[]{:S(2)}, u32[]{:S(2)}) collective-permute-start(bf16[64,2048]{1,0:T(8,128)(2,1)S(1)} %get-tuple-element.126), channel_id=1, source_target_pairs={{0,1},{1,2},{2,3},{3,0},{4,5},{5,6},{6,7},{7,4},{8,9},{9,10},{10,1... | collective-permute-start | bytes 786440 | tf_op jit(solution)/shard_map/ppermute | solution.py:23
  189.6 13.1 %collective-permute-start.23 = (bf16[64,2048]{1,0:T(8,128)(2,1)S(1)}, bf16[64,2048]{1,0:T(8,128)(2,1)S(1)}, u32[]{:S(2)}, u32[]{:S(2)}) collective-permute-start(bf16[64,2048]{1,0:T(8,128)(2,1)S(1)} %get-tuple-element.124), channel_id=1, source_target_pairs={{0,2},{1,3},{2,0},{3,1},{4,6},{5,7},{6,4},{7,5},{8,10},{9,11},{10,... | collective-permute-start | bytes 786440 | tf_op jit(solution)/shard_map/ppermute | solution.py:23
  204.6 11.3 %collective-permute-start.26 = (bf16[64,2048]{1,0:T(8,128)(2,1)}, bf16[64,2048]{1,0:T(8,128)(2,1)S(1)}, u32[]{:S(2)}, u32[]{:S(2)}) collective-permute-start(bf16[64,2048]{1,0:T(8,128)(2,1)} %tie.4.refs_2_.refs_3_), channel_id=1, source_target_pairs={{0,3},{1,0},{2,1},{3,2},{4,7},{5,4},{6,5},{7,6},{8,11},{9,8},{10,9... | collective-permute-start | bytes 786440 | tf_op jit(solution)/shard_map/ppermute | solution.py:23
  206.1 9.8 %collective-permute-start.27 = (bf16[64,2048]{1,0:T(8,128)(2,1)}, bf16[64,2048]{1,0:T(8,128)(2,1)S(1)}, u32[]{:S(2)}, u32[]{:S(2)}) collective-permute-start(bf16[64,2048]{1,0:T(8,128)(2,1)} %tie.4.refs_2_.refs_3_), channel_id=1, source_target_pairs={{0,2},{1,3},{2,0},{3,1},{4,6},{5,7},{6,4},{7,5},{8,10},{9,11},{10,... | collective-permute-start | bytes 786440 | tf_op jit(solution)/shard_map/ppermute | solution.py:23
  206.3 15.1 %collective-permute-start.28 = (bf16[64,2048]{1,0:T(8,128)(2,1)}, bf16[64,2048]{1,0:T(8,128)(2,1)S(1)}, u32[]{:S(2)}, u32[]{:S(2)}) collective-permute-start(bf16[64,2048]{1,0:T(8,128)(2,1)} %tie.4.refs_2_.refs_3_), channel_id=1, source_target_pairs={{0,1},{1,2},{2,3},{3,0},{4,5},{5,6},{6,7},{7,4},{8,9},{9,10},{10,1... | collective-permute-start | bytes 786440 | tf_op jit(solution)/shard_map/ppermute | solution.py:23
  228.2 3.1 collective-permute-start.29
  242.0 28.5 %collective-permute-start.30 = (bf16[2,256,512]{2,1,0:T(8,128)(2,1)}, bf16[2,256,512]{2,1,0:T(8,128)(2,1)S(1)}, u32[]{:S(2)}, u32[]{:S(2)}) collective-permute-start(bf16[2,256,512]{2,1,0:T(8,128)(2,1)} %get-tuple-element.90.refs_7_), channel_id=1, source_target_pairs={{4,0},{8,4},{12,8},{5,1},{9,5},{13,9},{6,2},{10,6},{14,10},{7,3},{... | collective-permute-start | bytes 1572872 | tf_op jit(solution)/shard_map/ppermute | solution.py:28
  243.2 28.0 %collective-permute-start.31 = (bf16[2,256,512]{2,1,0:T(8,128)(2,1)}, bf16[2,256,512]{2,1,0:T(8,128)(2,1)}, u32[]{:S(2)}, u32[]{:S(2)}) collective-permute-start(bf16[2,256,512]{2,1,0:T(8,128)(2,1)} %get-tuple-element.90.refs_7_), channel_id=1, source_target_pairs={{8,0},{12,4},{9,1},{13,5},{10,2},{14,6},{11,3},{15,7},{24,16},{28,... | collective-permute-start | bytes 1572872 | tf_op jit(solution)/shard_map/ppermute | solution.py:28
  244.5 27.5 %collective-permute-start.32 = (bf16[2,256,512]{2,1,0:T(8,128)(2,1)}, bf16[2,256,512]{2,1,0:T(8,128)(2,1)}, u32[]{:S(2)}, u32[]{:S(2)}) collective-permute-start(bf16[2,256,512]{2,1,0:T(8,128)(2,1)} %get-tuple-element.90.refs_7_), channel_id=1, source_target_pairs={{12,0},{13,1},{14,2},{15,3},{28,16},{29,17},{30,18},{31,19},{44,32... | collective-permute-start | bytes 1572872 | tf_op jit(solution)/shard_map/ppermute | solution.py:28
  296.0 4.4 %collective-permute-start.33 = (bf16[256,2048]{1,0:T(8,128)(2,1)}, bf16[256,2048]{1,0:T(8,128)(2,1)S(1)}, u32[]{:S(2)}, u32[]{:S(2)}) collective-permute-start(bf16[256,2048]{1,0:T(8,128)(2,1)} %copy-done.35), channel_id=1, source_target_pairs={{0,16},{16,0},{1,17},{17,1},{2,18},{18,2},{3,19},{19,3},{4,20},{20... | collective-permute-start | bytes 3145736 | tf_op jit(solution)/shard_map/ppermute | solution.py:34
  296.5 4.0 %collective-permute-start.34 = (bf16[256,2048]{1,0:T(8,128)(2,1)}, bf16[256,2048]{1,0:T(8,128)(2,1)S(1)}, u32[]{:S(2)}, u32[]{:S(2)}) collective-permute-start(bf16[256,2048]{1,0:T(8,128)(2,1)} %tie.6), channel_id=1, source_target_pairs={{0,16},{16,0},{1,17},{17,1},{2,18},{18,2},{3,19},{19,3},{4,20},{20... | collective-permute-start | bytes 3145736 | tf_op jit(solution)/shard_map/ppermute | solution.py:34
  297.4 1.4 collective-permute-start.38
  298.8 10.3 %collective-permute-start.39 = (f32[2,2048]{1,0:T(2,128)S(1)}, f32[2,2048]{1,0:T(2,128)S(1)}, u32[]{:S(2)}, u32[]{:S(2)}) collective-permute-start(f32[2,2048]{1,0:T(2,128)S(1)} %fusion.11), channel_id=1, source_target_pairs={{0,4},{4,0},{8,12},{12,8},{1,5},{5,1},{9,13},{13,9},{2,6},{6,2},{1... | collective-permute-start | bytes 49160 | tf_op jit(solution)/shard_map/ppermute | solution.py:1145
  307.4 18.2 %collective-permute-start.37 = (bf16[128,2048]{1,0:T(8,128)(2,1)}, bf16[128,2048]{1,0:T(8,128)(2,1)S(1)}, u32[]{:S(2)}, u32[]{:S(2)}) collective-permute-start(bf16[128,2048]{1,0:T(8,128)(2,1)} %get-tuple-element.110), channel_id=1, source_target_pairs={{0,3},{1,0},{2,1},{3,2},{4,7},{5,4},{6,5},{7,6},{8,11},{9,8},{10,9... | collective-permute-start | bytes 1572872 | tf_op jit(solution)/shard_map/ppermute | solution.py:23
  307.9 17.7 %collective-permute-start.36 = (bf16[128,2048]{1,0:T(8,128)(2,1)}, bf16[128,2048]{1,0:T(8,128)(2,1)S(1)}, u32[]{:S(2)}, u32[]{:S(2)}) collective-permute-start(bf16[128,2048]{1,0:T(8,128)(2,1)} %get-tuple-element.109), channel_id=1, source_target_pairs={{0,1},{1,2},{2,3},{3,0},{4,5},{5,6},{6,7},{7,4},{8,9},{9,10},{10,1... | collective-permute-start | bytes 1572872 | tf_op jit(solution)/shard_map/ppermute | solution.py:23
  308.9 22.7 %collective-permute-start.35 = (bf16[128,2048]{1,0:T(8,128)(2,1)}, bf16[128,2048]{1,0:T(8,128)(2,1)S(1)}, u32[]{:S(2)}, u32[]{:S(2)}) collective-permute-start(bf16[128,2048]{1,0:T(8,128)(2,1)} %get-tuple-element.108), channel_id=1, source_target_pairs={{0,2},{1,3},{2,0},{3,1},{4,6},{5,7},{6,4},{7,5},{8,10},{9,11},{10,... | collective-permute-start | bytes 1572872 | tf_op jit(solution)/shard_map/ppermute | solution.py:23
  309.2 8.2 %collective-permute-start.40 = (f32[2,2048]{1,0:T(2,128)S(1)}, f32[2,2048]{1,0:T(2,128)S(1)}, u32[]{:S(2)}, u32[]{:S(2)}) collective-permute-start(f32[2,2048]{1,0:T(2,128)S(1)} %fusion.29), channel_id=1, source_target_pairs={{0,12},{4,8},{8,4},{12,0},{1,13},{5,9},{9,5},{13,1},{2,14},{6,10},... | collective-permute-start | bytes 49160 | tf_op jit(solution)/shard_map/ppermute | solution.py:1145
  317.4 3.6 collective-permute-start.41
  321.0 4.6 %collective-permute-start.42 = (f32[2,2048]{1,0:T(2,128)S(1)}, f32[2,2048]{1,0:T(2,128)S(1)}, u32[]{:S(2)}, u32[]{:S(2)}) collective-permute-start(f32[2,2048]{1,0:T(2,128)S(1)} %add.188), channel_id=1, source_target_pairs={{0,96},{32,64},{64,32},{96,0},{1,97},{33,65},{65,33},{97,1},{2,98}... | collective-permute-start | bytes 49160 | tf_op jit(solution)/shard_map/ppermute | solution.py:1145
  333.2 31.9 %copy-start.44 = (bf16[144,2048]{1,0:T(8,128)(2,1)}, bf16[144,2048]{1,0:T(8,128)(2,1)S(1)}, u32[]{:S(2)}) copy-start(bf16[144,2048]{1,0:T(8,128)(2,1)S(1)} %maximum_maximum_fusion.refs_4_) | copy-start | bytes 1769476
  333.2 16.1 %collective-permute-start.43 = (bf16[144,2048]{1,0:T(8,128)(2,1)S(1)}, bf16[144,2048]{1,0:T(8,128)(2,1)S(1)}, u32[]{:S(2)}, u32[]{:S(2)}) collective-permute-start(bf16[144,2048]{1,0:T(8,128)(2,1)S(1)} %maximum_maximum_fusion.refs_4_), channel_id=1, source_target_pairs={{0,3},{1,0},{2,1},{3,2},{4,7},{5,4},{6,5},{7,6},{8,11},{9,8},{10,9... | collective-permute-start | bytes 1769480 | tf_op jit(solution)/shard_map/ppermute | solution.py:23
  335.7 14.6 %collective-permute-start.44 = (bf16[144,2048]{1,0:T(8,128)(2,1)S(1)}, bf16[144,2048]{1,0:T(8,128)(2,1)S(1)}, u32[]{:S(2)}, u32[]{:S(2)}) collective-permute-start(bf16[144,2048]{1,0:T(8,128)(2,1)S(1)} %maximum_maximum_fusion.refs_4_), channel_id=1, source_target_pairs={{0,2},{1,3},{2,0},{3,1},{4,6},{5,7},{6,4},{7,5},{8,10},{9,11},{10,... | collective-permute-start | bytes 1769480 | tf_op jit(solution)/shard_map/ppermute | solution.py:23
  336.2 28.9 %collective-permute-start.45 = (bf16[144,2048]{1,0:T(8,128)(2,1)S(1)}, bf16[144,2048]{1,0:T(8,128)(2,1)S(1)}, u32[]{:S(2)}, u32[]{:S(2)}) collective-permute-start(bf16[144,2048]{1,0:T(8,128)(2,1)S(1)} %maximum_maximum_fusion.refs_4_), channel_id=1, source_target_pairs={{0,1},{1,2},{2,3},{3,0},{4,5},{5,6},{6,7},{7,4},{8,9},{9,10},{10,1... | collective-permute-start | bytes 1769480 | tf_op jit(solution)/shard_map/ppermute | solution.py:23
  384.9 2.4 collective-permute-start.46
  (47 other events, 216.3 us)
Sparse Core Ops, SparseCore 0:
  16.6 78.0 all-gather.2
  103.3 63.6 all-gather.4
  280.1 103.5 reduce-scatter.1

commit v5 on v4

--- a/solution.py
+++ b/solution.py
@@ -1006,11 +1006,11 @@
     block, gathered = stack_attn(mine, came, scalars)
     lengths = jnp.concatenate((first_length, swap(first_length)))
     blocks = spread_near(block)
-    w_kv = stack_blocks(blocks, 0, 768, scalars, "stack_kv", deps=(lengths,))
+    w_kv = stack_blocks(blocks, 0, 768, scalars, "stack_kv")
     normed_first = enter_rows(tokens, gain_first.reshape(1, D), scalars, deps=blocks[1:])
     w_goq = lax.all_gather(gathered, XY, axis=0, tiled=True).reshape(4, 4, 2, 64, -1)
     mine, theirs = split_heads(
-        (w_hidden, w_linear, w_down), scalars, "split_mlp", deps=(gathered,)
+        (w_hidden, w_linear, w_down), scalars, "split_mlp", deps=(normed_first,)
     )
     came_mlp = swap(theirs)
     gain_first = gain_first.reshape(1, D)
@@ -1037,14 +1037,14 @@
 
     leave_rows_out = leave.reshape(rows, 1)
     fade_in = fade.reshape(1, 1)
-    projected = mm_in(*x_first, [(w_kv, 0, 768)], scalars, "project_kv")
+    projected = mm_in(*x_first, [(w_kv, 0, 768)], scalars, "project_kv", deps=(came_mlp,))
     key = rotate(projected[:, DV:].reshape(2, rows, DK), cosine, sine).astype(BF)
     value = projected[:, :DV].astype(BF).reshape(2, rows, DV)
     key_out = (key.astype(F32) * leave).astype(BF)
     state_out = ein("gjd,gje->gde", key_out, value).astype(BF)
     came = spread_state(state_out, 1)
     w_mlp = lax.all_gather(
-        stack_blocks((mine, came_mlp), 0, 1536, scalars, "stack_mlp", deps=came),
+        stack_blocks((mine, came_mlp), 0, 1536, scalars, "stack_mlp", deps=(state_out,)),
         XY,
         axis=0,
         tiled=True,

time: 398 us -> 392 us (0.985)
  waiting for transfers between devices: 144 us -> 138 us
    unnamed x122 -> x124, local copies, waits for them, and re-layouts: 26.3 us -> 27.8 us
where the time goes in v5:
time: 392 us; the launch traced here: 390 us
  waiting for transfers between devices  138 us (35%)
  Pallas kernels  120 us (31%)
  starting transfers between devices  64.6 us (16%)
  local copies, waits for them, and re-layouts  31.8 us (8%)
  between operations  15.7 us (4%)
  other arithmetic  14.6 us (4%)
  matrix products  5.77 us (1%)
    pallas_call x23, Pallas kernels, call(): pl.pallas_call(kernel, out_shape=shapes, grid_spec=pltpu.PrefetchScalarGr...  120 us
    ppermute x18, waiting for transfers between devices, shift(): return lax.ppermute(value, axis, [(i, (i + offset) % n) for i in range(n)])  67 us
    unnamed x124, local copies, waits for them, and re-layouts  27.8 us
    ppermute x6, waiting for transfers between devices, shift_open(): lax.ppermute(value, axis, [(i, i + offset) for i in range(n) if 0 <= i +...  23.4 us
    ppermute x18, starting transfers between devices, shift(): return lax.ppermute(value, axis, [(i, (i + offset) % n) for i in range(n)])  19.3 us
    ppermute x6, waiting for transfers between devices, hop(): return lax.ppermute(value, ('x', 'core', 'ctx'), pairs)  18.8 us
    ppermute x5, starting transfers between devices, per_device(): gains = gains + lax.ppermute(gains, axis, list(enumerate(swapped)))  12.3 us
    ppermute x12, waiting for transfers between devices, swap(): return lax.ppermute(value, 'core', [(0, 1), (1, 0)])  12.2 us
  transfers between devices with their start and end apart: 50, of which 35 were waited for; matrix products, arithmetic and copies ran while one was open for 5% of the time, Pallas kernels for 19%

profile of v5, /device:TPU:1, one launch (start us, length us, event | category | flops | bytes accessed | tf_op | source)
XLA Modules:
  0.0 390.2 jit_solution(4557744541561929646)
XLA Ops:
  7.8 2.6 split_attn.1
  13.9 2.5 stack_attn.1
  17.8 2.5 collective-permute-start.3
  22.8 3.2 collective-permute-done.3.refs_3_.refs_2_
  26.0 1.6 copy-done.8
  30.1 1.6 collective-permute-start.5
  33.7 2.1 collective-permute-start.7
  38.3 2.5 split_mlp.1
  43.1 5.2 %collective-permute-done.6.refs_3_.refs_2_ = bf16[4,2,64,768]{3,2,1,0:T(8,128)(2,1)} collective-permute-done((bf16[4,2,64,768]{3,2,1,0:T(8,128)(2,1)S(1)}, bf16[4,2,64,768]{3,2,1,0:T(8,128)(2,1)}, u32[]{:S(2)}, u32[]{:S(2)}) %collective-permute-start.6) | collective-permute-done | bytes 786464 | tf_op jit(solution)/shard_map/ppermute | solution.py:148
  48.4 9.1 %collective-permute-done.7.refs_4_.refs_3_ = bf16[4,2,64,768]{3,2,1,0:T(8,128)(2,1)} collective-permute-done((bf16[4,2,64,768]{3,2,1,0:T(8,128)(2,1)S(1)}, bf16[4,2,64,768]{3,2,1,0:T(8,128)(2,1)}, u32[]{:S(2)}, u32[]{:S(2)}) %collective-permute-start.7) | collective-permute-done | bytes 786464 | tf_op jit(solution)/shard_map/ppermute | solution.py:148
  57.5 1.5 copy-done.2
  59.0 5.6 %project_kv.1 = f32[512,768]{1,0:T(8,128)S(1)} custom-call(s32[4]{0:T(128)S(1)} %copy-done.23, bf16[256,2048]{1,0:T(8,128)(2,1)S(1)} %copy-done.2, bf16[256,2048]{1,0:T(8,128)(2,1)S(1)} %collective-permute-done.5.refs_1_.refs_4_.refs_10_, bf16[4,2,64,768]{3,2,1,0:T(8,128)(2,1)S(1)} %bitcast.45, ...), custom_call_target="tpu_custom_call" | custom-call | flops 1 | bytes 1 | tf_op jit(solution)/shard_map/project_kv/pallas_call | solution.py:61
  67.0 2.3 collective-permute-start.10
  69.4 4.1 %collective-permute-start.11 = (bf16[2,256,512]{2,1,0:T(8,128)(2,1)S(1)}, bf16[2,256,512]{2,1,0:T(8,128)(2,1)S(1)}, u32[]{:S(2)}, u32[]{:S(2)}) collective-permute-start(bf16[2,256,512]{2,1,0:T(8,128)(2,1)S(1)} %convolution_convert_fusion.refs_2_), channel_id=1, source_target_pairs={{0,8},{4,12},{1,9},{5,13},{2,10},{6,14},{3,11},{7,15},{16,24},{20,... | collective-permute-start | bytes 1572872 | tf_op jit(solution)/shard_map/ppermute | solution.py:28
  78.7 11.2 %collective-permute-done.10.refs_5_ = bf16[2,256,512]{2,1,0:T(8,128)(2,1)S(1)} collective-permute-done((bf16[2,256,512]{2,1,0:T(8,128)(2,1)S(1)}, bf16[2,256,512]{2,1,0:T(8,128)(2,1)S(1)}, u32[]{:S(2)}, u32[]{:S(2)}) %collective-permute-start.10) | collective-permute-done | bytes 524320 | tf_op jit(solution)/shard_map/ppermute | solution.py:28
  89.9 11.3 %collective-permute-done.11.refs_6_ = bf16[2,256,512]{2,1,0:T(8,128)(2,1)S(1)} collective-permute-done((bf16[2,256,512]{2,1,0:T(8,128)(2,1)S(1)}, bf16[2,256,512]{2,1,0:T(8,128)(2,1)S(1)}, u32[]{:S(2)}, u32[]{:S(2)}) %collective-permute-start.11) | collective-permute-done | bytes 524320 | tf_op jit(solution)/shard_map/ppermute | solution.py:28
  102.2 13.1 %retain.1 = (f32[256,2048]{1,0:T(8,128)}, bf16[256,2048]{1,0:T(8,128)(2,1)}, bf16[512,256]{1,0:T(8,128)(2,1)}, bf16[2,256,512]{2,1,0:T(8,128)(2,1)}, bf16[2,256,...) custom-call(s32[6]{0:T(128)} %concatenate.24.s_ref, ...), custom_call_target="tpu_custom_call" | custom-call | flops 1 | bytes 1 | tf_op jit(solution)/shard_map/retain/pallas_call | solution.py:61
  116.1 2.5 collective-permute-done.13
  118.6 1.7 add_convert_fusion.9
  120.3 2.9 collective-permute-start.16
  123.2 1.7 collective-permute-start.14
  124.9 9.1 %collective-permute-done.16 = bf16[64,2048]{1,0:T(8,128)(2,1)S(1)} collective-permute-done((bf16[64,2048]{1,0:T(8,128)(2,1)S(1)}, bf16[64,2048]{1,0:T(8,128)(2,1)S(1)}, u32[]{:S(2)}, u32[]{:S(2)}) %collective-permute-start.16) | collective-permute-done | bytes 262176 | tf_op jit(solution)/shard_map/ppermute | solution.py:23
  134.0 2.3 collective-permute-done.14
  140.8 2.3 collective-permute-start.21
  144.2 2.6 collective-permute-done.18.refs_4_
  146.8 7.5 %collective-permute-done.19.refs_5_ = bf16[64,2048]{1,0:T(8,128)(2,1)S(1)} collective-permute-done((bf16[64,2048]{1,0:T(8,128)(2,1)S(1)}, bf16[64,2048]{1,0:T(8,128)(2,1)S(1)}, u32[]{:S(2)}, u32[]{:S(2)}) %collective-permute-start.19) | collective-permute-done | bytes 262176 | tf_op jit(solution)/shard_map/ppermute | solution.py:23
  160.0 1.6 all-gather.5.cloned.1.call-done
  161.6 14.4 %mlp.1 = (f32[256,2048]{1,0:T(8,128)}, bf16[256,2048]{1,0:T(8,128)(2,1)}, f32[8,2048]{1,0:T(8,128)}, bf16[512,1024]{1,0:T(8,128)(2,1)}, bf16[512,512]{1,0:T(8,128)(2,1)}) custom-call(s32[4]{0:T(128)} %pad_add_fusion.s_ref, bf16[256,2048]{1,0:T(8,128)(2,1)} %copy-done.15, bf16[256,2048]{1,0:T(8,128)(2,1)} %collective-permute-done.20.refs_1_, ...), custom_call_target="tpu_custom_call" | custom-call | flops 1 | bytes 1 | tf_op jit(solution)/shard_map/mlp/pallas_call | solution.py:61
  176.8 2.5 collective-permute-done.22
  179.3 2.2 add_convert_fusion.4
  181.5 2.7 collective-permute-start.25
  184.2 1.7 collective-permute-start.23
  185.9 6.9 %weight_mlp.1 = (bf16[4,4,2,64,3584]{4,3,2,1,0:T(8,128)(2,1)}, f32[8,128]{1,0:T(8,128)}) custom-call(s32[4]{0:T(128)} %pad_add_fusion.s_ref, bf16[256,2048]{1,0:T(8,128)(2,1)} %copy-done.15, bf16[256,2048]{1,0:T(8,128)(2,1)} %collective-permute-done.20.refs_1_, bf16[512,1024]{1,0:T(8,128)(2,1)} %get-tuple-element.80.refs_2_), custom_call_target="tpu_custom_call" | custom-call | flops 1 | bytes 1 | tf_op jit(solution)/shard_map/weight_mlp/pallas_call | solution.py:61
  192.8 2.5 collective-permute-done.25
  195.3 1.9 collective-permute-done.23
  197.3 1.9 add_convert_fusion.1.refs_0_
  199.2 1.5 collective-permute-start.26
  201.6 2.8 copy-done.7
  205.3 2.8 project_down.1
  210.5 5.5 %collective-permute-done.28.refs_6_ = bf16[64,2048]{1,0:T(8,128)(2,1)S(1)} collective-permute-done((bf16[64,2048]{1,0:T(8,128)(2,1)}, bf16[64,2048]{1,0:T(8,128)(2,1)S(1)}, u32[]{:S(2)}, u32[]{:S(2)}) %collective-permute-start.28) | collective-permute-done | bytes 262176 | tf_op jit(solution)/shard_map/ppermute | solution.py:23
  216.7 6.1 %second_back.1 = (f32[256,2048]{1,0:T(8,128)}, bf16[256,2048]{1,0:T(8,128)(2,1)}) custom-call(s32[4]{0:T(128)} %pad_add_fusion.s_ref, f32[256,2048]{1,0:T(8,128)} %copy-done.11, f32[256,2048]{1,0:T(8,128)} %refs_1_.6, f32[1,2048]{1,0:T(1,128)} %bitcast.47, bf16[64,2048]{1,0:T(8,128)(2,1)} %tie.4.refs_2_.refs_3_, bf16[64,2048]{1,0:T(8,128)(2,1)} %copy-done.57, ...), custom_call_target="tpu_custom_call" | custom-call | flops 1 | bytes 1 | tf_op jit(solution)/shard_map/second_back/pallas_call | solution.py:61
  224.3 1.5 collective-permute-done.29.refs_1_
  226.9 9.6 %back_gate.1 = (bf16[512,512]{1,0:T(8,128)(2,1)}, bf16[512,512]{1,0:T(8,128)(2,1)}, bf16[2,256,512]{2,1,0:T(8,128)(2,1)}) custom-call(s32[4]{0:T(128)} %pad_add_fusion.s_ref, bf16[256,2048]{1,0:T(8,128)(2,1)} %get-tuple-element.85.refs_0_, bf16[256,2048]{1,0:T(8,128)(2,1)} %copy-done.36, bf16[4,4,2,64,1280]{4,3,2,1,0:T(8,128)(2,1)} %bitcast.37, ...), custom_call_target="tpu_custom_call" | custom-call | flops 1 | bytes 1 | tf_op jit(solution)/shard_map/back_gate/pallas_call | solution.py:61
  239.1 1.5 collective-permute-start.32
  244.5 7.2 %weight_og.1 = (bf16[4,4,2,64,3584]{4,3,2,1,0:T(8,128)(2,1)}, f32[8,128]{1,0:T(8,128)}) custom-call(s32[4]{0:T(128)} %pad_add_fusion.s_ref, bf16[256,2048]{1,0:T(8,128)(2,1)} %get-tuple-element.85.refs_0_, bf16[256,2048]{1,0:T(8,128)(2,1)} %copy-done.36, bf16[512,512]{1,0:T(8,128)(2,1)} %get-tuple-element.94.refs_2_, ...), custom_call_target="tpu_custom_call", output_to_operand_aliasing={{0}: (7, {})} | custom-call | flops 1 | bytes 1 | tf_op jit(solution)/shard_map/weight_og/pallas_call | solution.py:61
  251.7 5.6 %weight_down.1 = (bf16[4,4,2,64,3584]{4,3,2,1,0:T(8,128)(2,1)}, f32[8,128]{1,0:T(8,128)}) custom-call(s32[4]{0:T(128)} %pad_add_fusion.s_ref, bf16[256,2048]{1,0:T(8,128)(2,1)} %copy-done.10, bf16[256,2048]{1,0:T(8,128)(2,1)} %copy-done.37, bf16[512,512]{1,0:T(8,128)(2,1)} %get-tuple-element.82.refs_0_.refs_2_, ...), custom_call_target="tpu_custom_call", output_to_operand_aliasing={{0}: (4, {})} | custom-call | flops 1 | bytes 1 | tf_op jit(solution)/shard_map/weight_down/pallas_call | solution.py:61
  257.3 5.2 %weight_query.1 = (bf16[4,4,2,64,3584]{4,3,2,1,0:T(8,128)(2,1)}, f32[8,128]{1,0:T(8,128)}) custom-call(s32[4]{0:T(128)} %pad_add_fusion.s_ref, bf16[256,2048]{1,0:T(8,128)(2,1)} %copy-done.1, bf16[256,2048]{1,0:T(8,128)(2,1)} %copy-done.4, bf16[512,256]{1,0:T(8,128)(2,1)} %pad_maximum_fusion.1.refs_2_.refs_7_, ...), custom_call_target="tpu_custom_call", output_to_operand_aliasing={{0}: (4, {})} | custom-call | flops 1 | bytes 1 | tf_op jit(solution)/shard_map/weight_query/pallas_call | solution.py:61
  266.6 7.8 %weight_last.1 = (bf16[4,4,2,64,3584]{4,3,2,1,0:T(8,128)(2,1)}, f32[8,128]{1,0:T(8,128)}, bf16[512,768]{1,0:T(8,128)(2,1)}) custom-call(s32[4]{0:T(128)} %pad_add_fusion.s_ref, bf16[256,2048]{1,0:T(8,128)(2,1)} %copy-done.1, bf16[256,2048]{1,0:T(8,128)(2,1)} %copy-done.4, bf16[2,256,512]{2,1,0:T(8,128)(2,1)} %tie.5.refs_2_, ...), custom_call_target="tpu_custom_call", output_to_operand_aliasing={{0}: (14, {})} | custom-call | flops 1 | bytes 1 | tf_op jit(solution)/shard_map/weight_last/pallas_call | solution.py:61
  276.0 2.5 copy-done
  280.7 7.5 %back_attn.1 = (f32[256,2048]{1,0:T(8,128)S(1)}, bf16[256,2048]{1,0:T(8,128)(2,1)S(1)}, f32[8,2048]{1,0:T(8,128)S(1)}) custom-call(s32[4]{0:T(128)S(1)} %copy-done.25, bf16[512,768]{1,0:T(8,128)(2,1)S(1)} %copy-done.21, bf16[4,2,64,768]{3,2,1,0:T(8,128)(2,1)S(1)} %bitcast.46, bf16[4,2,64,768]{3,2,1,0:T(8,128)(2,1)} %collective-permute-done.6.refs_3_.refs_2_, ...), custom_call_target="tpu_custom_call" | custom-call | flops 1 | bytes 1 | tf_op jit(solution)/shard_map/back_attn/pallas_call | solution.py:61
  296.1 5.7 %third_blocks.1 = (bf16[128,2048]{1,0:T(8,128)(2,1)}, bf16[128,2048]{1,0:T(8,128)(2,1)}, bf16[128,2048]{1,0:T(8,128)(2,1)}, bf16[128,2048]{1,0:T(8,128)(2,1)}) custom-call(s32[4]{0:T(128)} %pad_add_fusion.s_ref, f32[256,2048]{1,0:T(8,128)} %copy-done.19, bf16[256,2048]{1,0:T(8,128)(2,1)} %copy-done.44, f32[256,2048]{1,0:T(8,128)} %copy-done.18, ...), custom_call_target="tpu_custom_call" | custom-call | flops 1 | bytes 1 | tf_op jit(solution)/shard_map/third_blocks/pallas_call | solution.py:61
  303.6 6.4 %collective-permute-start.40 = (f32[2,2048]{1,0:T(2,128)S(1)}, f32[2,2048]{1,0:T(2,128)S(1)}, u32[]{:S(2)}, u32[]{:S(2)}) collective-permute-start(f32[2,2048]{1,0:T(2,128)S(1)} %fusion.29), channel_id=1, source_target_pairs={{0,12},{4,8},{8,4},{12,0},{1,13},{5,9},{9,5},{13,1},{2,14},{6,10},... | collective-permute-start | bytes 49160 | tf_op jit(solution)/shard_map/ppermute | solution.py:1145
  310.0 1.9 collective-permute-done.40
  311.8 1.5 collective-permute-start.41
  313.3 2.1 collective-permute-done.41
  315.4 2.4 collective-permute-start.42
  317.9 1.9 collective-permute-done.42
  319.9 6.2 %collective-permute-done.35 = bf16[128,2048]{1,0:T(8,128)(2,1)S(1)} collective-permute-done((bf16[128,2048]{1,0:T(8,128)(2,1)}, bf16[128,2048]{1,0:T(8,128)(2,1)S(1)}, u32[]{:S(2)}, u32[]{:S(2)}) %collective-permute-start.35) | collective-permute-done | bytes 524320 | tf_op jit(solution)/shard_map/ppermute | solution.py:23
  327.6 2.5 collective-permute-start.43
  331.3 12.3 %collective-permute-done.43.refs_5_ = bf16[144,2048]{1,0:T(8,128)(2,1)S(1)} collective-permute-done((bf16[144,2048]{1,0:T(8,128)(2,1)S(1)}, bf16[144,2048]{1,0:T(8,128)(2,1)S(1)}, u32[]{:S(2)}, u32[]{:S(2)}) %collective-permute-start.43) | collective-permute-done | bytes 589856 | tf_op jit(solution)/shard_map/ppermute | solution.py:23
  344.7 14.8 %collective-permute-done.45.refs_7_ = bf16[144,2048]{1,0:T(8,128)(2,1)S(1)} collective-permute-done((bf16[144,2048]{1,0:T(8,128)(2,1)S(1)}, bf16[144,2048]{1,0:T(8,128)(2,1)S(1)}, u32[]{:S(2)}, u32[]{:S(2)}) %collective-permute-start.45) | collective-permute-done | bytes 589856 | tf_op jit(solution)/shard_map/ppermute | solution.py:23
  360.3 7.4 %leave_rows.1 = (f32[256,2048]{1,0:T(8,128)}, f32[256,2048]{1,0:T(8,128)}) custom-call(s32[4]{0:T(128)} %pad_add_fusion.s_ref, f32[256,2048]{1,0:T(8,128)} %copy-done.11, f32[256,2048]{1,0:T(8,128)} %refs_1_.7, f32[256,2048]{1,0:T(8,128)} %get-tuple-element.84.refs_2_, f32[1,2048]{1,0:T(1,128)} %bitcast.49, bf16[144,2048]{1,0:T(8,128)(2,1)} %copy-done.41, ...), custom_call_target="tpu_custom_call" | custom-call | flops 1 | bytes 1 | tf_op jit(solution)/shard_map/leave_rows/pallas_call | solution.py:61
  369.8 8.3 %reduce-scatter.2.cloned.1.call-done.refs_0_ = bf16[128,3584]{1,0:T(8,128)(2,1)} async-done(((bf16[2048,3584]{1,0:T(8,128)(2,1)}), bf16[128,3584]{1,0:T(8,128)(2,1)}) %reduce-scatter.2.cloned.1.call-update) | async-done | bytes 917520 | tf_op jit(solution)/shard_map/reduce_scatter | solution.py:1126
  381.8 1.8 join_heads.1
  (233 shorter events, 79.2 us)
Async XLA Ops:
  7.2 94.1 %all-gather.3.cloned.1.call-start = ((), (), s32[]{:S(2)}) async-start(), calls=%async_computation.1 | async-start | bytes 5570560 | tf_op jit(solution)/shard_map/all_gather | solution.py:1011
  10.4 2.8 collective-permute-start.1
  16.4 15.4 %copy-start.28 = (bf16[128,768]{1,0:T(8,128)(2,1)S(1)}, bf16[128,768]{1,0:T(8,128)(2,1)}, u32[]{:S(2)}) copy-start(bf16[128,768]{1,0:T(8,128)(2,1)} %get-tuple-element.70.refs_0_) | copy-start | bytes 589828
  16.4 145.2 %all-gather.5.cloned.1.call-start = ((), (), s32[]{:S(2)}) async-start(), calls=%async_computation.2 | async-start | bytes 6684672 | tf_op jit(solution)/shard_map/all_gather | solution.py:1046
  16.5 6.3 %collective-permute-start.2 = (bf16[128,768]{1,0:T(8,128)(2,1)}, bf16[128,768]{1,0:T(8,128)(2,1)S(1)}, u32[]{:S(2)}, u32[]{:S(2)}) collective-permute-start(bf16[128,768]{1,0:T(8,128)(2,1)} %get-tuple-element.70.refs_0_), channel_id=1, source_target_pairs={{0,4},{4,8},{8,12},{12,0},{16,48},{20,52},{24,56},{28,60},{32,36},... | collective-permute-start | bytes 589832 | tf_op jit(solution)/shard_map/ppermute | solution.py:148
  17.8 8.1 %collective-permute-start.3 = (bf16[128,768]{1,0:T(8,128)(2,1)}, bf16[128,768]{1,0:T(8,128)(2,1)S(1)}, u32[]{:S(2)}, u32[]{:S(2)}) collective-permute-start(bf16[128,768]{1,0:T(8,128)(2,1)} %get-tuple-element.70.refs_0_), channel_id=1, source_target_pairs={{0,8},{4,12},{8,0},{12,4},{16,80},{20,84},{24,88},{28,92},{32,40},... | collective-permute-start | bytes 589832 | tf_op jit(solution)/shard_map/ppermute | solution.py:148
  20.3 5.7 %collective-permute-start.4 = (bf16[128,768]{1,0:T(8,128)(2,1)}, bf16[128,768]{1,0:T(8,128)(2,1)S(1)}, u32[]{:S(2)}, u32[]{:S(2)}) collective-permute-start(bf16[128,768]{1,0:T(8,128)(2,1)} %get-tuple-element.70.refs_0_), channel_id=1, source_target_pairs={{0,12},{4,0},{8,4},{12,8},{16,112},{20,116},{24,120},{28,124},{32,... | collective-permute-start | bytes 589832 | tf_op jit(solution)/shard_map/ppermute | solution.py:148
  30.1 27.4 %copy-start.23 = (s32[4]{0:T(128)S(1)}, s32[4]{0:T(128)}, u32[]{:S(2)}) copy-start(s32[4]{0:T(128)} %pad_add_fusion.s_ref) | copy-start | bytes 52
  30.1 27.3 %collective-permute-start.5 = (bf16[256,2048]{1,0:T(8,128)(2,1)S(1)}, bf16[256,2048]{1,0:T(8,128)(2,1)S(1)}, u32[]{:S(2)}, u32[]{:S(2)}) collective-permute-start(bf16[256,2048]{1,0:T(8,128)(2,1)S(1)} %enter_rows.1.refs_3_.refs_0_.refs_9_), channel_id=1, source_target_pairs={{0,16},{16,0},{1,17},{17,1},{2,18},{18,2},{3,19},{19,3},{4,20},{20... | collective-permute-start | bytes 3145736 | tf_op jit(solution)/shard_map/ppermute | solution.py:34
  32.4 16.0 %collective-permute-start.6 = (bf16[4,2,64,768]{3,2,1,0:T(8,128)(2,1)S(1)}, bf16[4,2,64,768]{3,2,1,0:T(8,128)(2,1)}, u32[]{:S(2)}, u32[]{:S(2)}) collective-permute-start(bf16[4,2,64,768]{3,2,1,0:T(8,128)(2,1)S(1)} %bitcast.42), channel_id=1, source_target_pairs={{0,32},{4,36},{8,40},{12,44},{16,20},{20,24},{24,28},{28,16},{32,6... | collective-permute-start | bytes 2359304 | tf_op jit(solution)/shard_map/ppermute | solution.py:148
  33.7 23.8 %collective-permute-start.7 = (bf16[4,2,64,768]{3,2,1,0:T(8,128)(2,1)S(1)}, bf16[4,2,64,768]{3,2,1,0:T(8,128)(2,1)}, u32[]{:S(2)}, u32[]{:S(2)}) collective-permute-start(bf16[4,2,64,768]{3,2,1,0:T(8,128)(2,1)S(1)} %bitcast.43), channel_id=1, source_target_pairs={{0,64},{4,68},{8,72},{12,76},{16,24},{20,28},{24,16},{28,20},{32,9... | collective-permute-start | bytes 2359304 | tf_op jit(solution)/shard_map/ppermute | solution.py:148
  35.7 21.7 %collective-permute-start.8 = (bf16[4,2,64,768]{3,2,1,0:T(8,128)(2,1)S(1)}, bf16[4,2,64,768]{3,2,1,0:T(8,128)(2,1)}, u32[]{:S(2)}, u32[]{:S(2)}) collective-permute-start(bf16[4,2,64,768]{3,2,1,0:T(8,128)(2,1)S(1)} %bitcast.44), channel_id=1, source_target_pairs={{0,96},{4,100},{8,104},{12,108},{16,28},{20,16},{24,20},{28,24},{3... | collective-permute-start | bytes 2359304 | tf_op jit(solution)/shard_map/ppermute | solution.py:148
  40.8 2.4 collective-permute-start.9
  42.4 22.4 %copy-start.38 = (f32[256,128]{1,0:T(8,128)}, f32[256,128]{1,0:T(8,128)S(1)}, u32[]{:S(2)}) copy-start(f32[256,128]{1,0:T(8,128)S(1)} %get-tuple-element.140.refs_9_.refs_11_) | copy-start | bytes 393220
  42.4 22.4 %copy-start.42 = (f32[256,128]{1,0:T(8,128)}, f32[256,128]{1,0:T(8,128)S(1)}, u32[]{:S(2)}) copy-start(f32[256,128]{1,0:T(8,128)S(1)} %get-tuple-element.139.refs_10_.refs_12_) | copy-start | bytes 393220
  65.0 50.3 %copy-start.40 = (bf16[2,256,256]{2,1,0:T(8,128)(2,1)}, bf16[2,256,256]{2,1,0:T(8,128)(2,1)S(1)}, u32[]{:S(2)}) copy-start(bf16[2,256,256]{2,1,0:T(8,128)(2,1)S(1)} %multiply_convert_fusion.refs_7_) | copy-start | bytes 786436
  67.0 311.2 %reduce-scatter.2.cloned.1.call-start = ((), (), s32[]{:S(2)}) async-start(), calls=%async_computation.3 | async-start | bytes 15597568 | tf_op jit(solution)/shard_map/reduce_scatter | solution.py:1126
  67.0 22.9 %collective-permute-start.10 = (bf16[2,256,512]{2,1,0:T(8,128)(2,1)S(1)}, bf16[2,256,512]{2,1,0:T(8,128)(2,1)S(1)}, u32[]{:S(2)}, u32[]{:S(2)}) collective-permute-start(bf16[2,256,512]{2,1,0:T(8,128)(2,1)S(1)} %convolution_convert_fusion.refs_2_), channel_id=1, source_target_pairs={{0,4},{4,8},{8,12},{1,5},{5,9},{9,13},{2,6},{6,10},{10,14},{3,7},{... | collective-permute-start | bytes 1572872 | tf_op jit(solution)/shard_map/ppermute | solution.py:28
  69.4 31.8 %collective-permute-start.11 = (bf16[2,256,512]{2,1,0:T(8,128)(2,1)S(1)}, bf16[2,256,512]{2,1,0:T(8,128)(2,1)S(1)}, u32[]{:S(2)}, u32[]{:S(2)}) collective-permute-start(bf16[2,256,512]{2,1,0:T(8,128)(2,1)S(1)} %convolution_convert_fusion.refs_2_), channel_id=1, source_target_pairs={{0,8},{4,12},{1,9},{5,13},{2,10},{6,14},{3,11},{7,15},{16,24},{20,... | collective-permute-start | bytes 1572872 | tf_op jit(solution)/shard_map/ppermute | solution.py:28
  73.5 27.8 %collective-permute-start.12 = (bf16[2,256,512]{2,1,0:T(8,128)(2,1)S(1)}, bf16[2,256,512]{2,1,0:T(8,128)(2,1)S(1)}, u32[]{:S(2)}, u32[]{:S(2)}) collective-permute-start(bf16[2,256,512]{2,1,0:T(8,128)(2,1)S(1)} %convolution_convert_fusion.refs_2_), channel_id=1, source_target_pairs={{0,12},{1,13},{2,14},{3,15},{16,28},{17,29},{18,30},{19,31},{32,44... | collective-permute-start | bytes 1572872 | tf_op jit(solution)/shard_map/ppermute | solution.py:28
  74.8 2.0 collective-permute-start
  115.3 3.3 collective-permute-start.13
  118.5 21.5 %copy-start.5 = (bf16[256,2048]{1,0:T(8,128)(2,1)S(1)}, bf16[256,2048]{1,0:T(8,128)(2,1)}, u32[]{:S(2)}) copy-start(bf16[256,2048]{1,0:T(8,128)(2,1)} %copy-done.4) | copy-start | bytes 3145732
  118.6 21.5 %copy-start.12 = (f32[256,2048]{1,0:T(8,128)S(1)}, f32[256,2048]{1,0:T(8,128)}, u32[]{:S(2)}) copy-start(f32[256,2048]{1,0:T(8,128)} %refs_1_.6) | copy-start | bytes 6291460
  120.3 13.7 %collective-permute-start.16 = (bf16[64,2048]{1,0:T(8,128)(2,1)S(1)}, bf16[64,2048]{1,0:T(8,128)(2,1)S(1)}, u32[]{:S(2)}, u32[]{:S(2)}) collective-permute-start(bf16[64,2048]{1,0:T(8,128)(2,1)S(1)} %get-tuple-element.128), channel_id=1, source_target_pairs={{0,3},{1,0},{2,1},{3,2},{4,7},{5,4},{6,5},{7,6},{8,11},{9,8},{10,9... | collective-permute-start | bytes 786440 | tf_op jit(solution)/shard_map/ppermute | solution.py:23
  123.2 10.8 %collective-permute-start.15 = (bf16[64,2048]{1,0:T(8,128)(2,1)S(1)}, bf16[64,2048]{1,0:T(8,128)(2,1)S(1)}, u32[]{:S(2)}, u32[]{:S(2)}) collective-permute-start(bf16[64,2048]{1,0:T(8,128)(2,1)S(1)} %get-tuple-element.129), channel_id=1, source_target_pairs={{0,1},{1,2},{2,3},{3,0},{4,5},{5,6},{6,7},{7,4},{8,9},{9,10},{10,1... | collective-permute-start | bytes 786440 | tf_op jit(solution)/shard_map/ppermute | solution.py:23
  123.2 13.1 %collective-permute-start.14 = (bf16[64,2048]{1,0:T(8,128)(2,1)S(1)}, bf16[64,2048]{1,0:T(8,128)(2,1)S(1)}, u32[]{:S(2)}, u32[]{:S(2)}) collective-permute-start(bf16[64,2048]{1,0:T(8,128)(2,1)S(1)} %get-tuple-element.127), channel_id=1, source_target_pairs={{0,2},{1,3},{2,0},{3,1},{4,6},{5,7},{6,4},{7,5},{8,10},{9,11},{10,... | collective-permute-start | bytes 786440 | tf_op jit(solution)/shard_map/ppermute | solution.py:23
  137.5 16.8 %copy-start.9 = (f32[256,2048]{1,0:T(8,128)S(1)}, f32[256,2048]{1,0:T(8,128)}, u32[]{:S(2)}) copy-start(f32[256,2048]{1,0:T(8,128)} %refs_1_.7) | copy-start | bytes 6291460
  137.5 16.8 %copy-start.29 = (f32[2048]{0:T(1024)S(1)}, f32[2048]{0:T(1024)}, u32[]{:S(2)}) copy-start(f32[2048]{0:T(1024)} %param.17) | copy-start | bytes 24580
  137.5 6.6 %collective-permute-start.17 = (bf16[64,2048]{1,0:T(8,128)(2,1)S(1)}, bf16[64,2048]{1,0:T(8,128)(2,1)S(1)}, u32[]{:S(2)}, u32[]{:S(2)}) collective-permute-start(bf16[64,2048]{1,0:T(8,128)(2,1)S(1)} %add_convert_fusion.6.refs_2_), channel_id=1, source_target_pairs={{0,3},{1,0},{2,1},{3,2},{4,7},{5,4},{6,5},{7,6},{8,11},{9,8},{10,9... | collective-permute-start | bytes 786440 | tf_op jit(solution)/shard_map/ppermute | solution.py:23
  138.9 7.9 %collective-permute-start.18 = (bf16[64,2048]{1,0:T(8,128)(2,1)S(1)}, bf16[64,2048]{1,0:T(8,128)(2,1)S(1)}, u32[]{:S(2)}, u32[]{:S(2)}) collective-permute-start(bf16[64,2048]{1,0:T(8,128)(2,1)S(1)} %add_convert_fusion.6.refs_2_), channel_id=1, source_target_pairs={{0,2},{1,3},{2,0},{3,1},{4,6},{5,7},{6,4},{7,5},{8,10},{9,11},{10,... | collective-permute-start | bytes 786440 | tf_op jit(solution)/shard_map/ppermute | solution.py:23
  139.3 15.1 %collective-permute-start.19 = (bf16[64,2048]{1,0:T(8,128)(2,1)S(1)}, bf16[64,2048]{1,0:T(8,128)(2,1)S(1)}, u32[]{:S(2)}, u32[]{:S(2)}) collective-permute-start(bf16[64,2048]{1,0:T(8,128)(2,1)S(1)} %add_convert_fusion.6.refs_2_), channel_id=1, source_target_pairs={{0,1},{1,2},{2,3},{3,0},{4,5},{5,6},{6,7},{7,4},{8,9},{9,10},{10,1... | collective-permute-start | bytes 786440 | tf_op jit(solution)/shard_map/ppermute | solution.py:23
  140.8 20.8 %copy-start.10 = (bf16[256,2048]{1,0:T(8,128)(2,1)}, bf16[256,2048]{1,0:T(8,128)(2,1)S(1)}, u32[]{:S(2)}) copy-start(bf16[256,2048]{1,0:T(8,128)(2,1)S(1)} %low_rows.1.refs_2_.refs_0_) | copy-start | bytes 3145732
  140.8 16.8 %collective-permute-start.21 = (bf16[256,2048]{1,0:T(8,128)(2,1)S(1)}, bf16[256,2048]{1,0:T(8,128)(2,1)S(1)}, u32[]{:S(2)}, u32[]{:S(2)}) collective-permute-start(bf16[256,2048]{1,0:T(8,128)(2,1)S(1)} %low_rows.1.refs_2_.refs_0_), channel_id=1, source_target_pairs={{0,16},{16,0},{1,17},{17,1},{2,18},{18,2},{3,19},{19,3},{4,20},{20... | collective-permute-start | bytes 3145736 | tf_op jit(solution)/shard_map/ppermute | solution.py:34
  157.2 2.8 collective-permute-start.20
  176.0 3.3 collective-permute-start.22
  181.5 13.8 %collective-permute-start.25 = (bf16[64,2048]{1,0:T(8,128)(2,1)}, bf16[64,2048]{1,0:T(8,128)(2,1)S(1)}, u32[]{:S(2)}, u32[]{:S(2)}) collective-permute-start(bf16[64,2048]{1,0:T(8,128)(2,1)} %get-tuple-element.125), channel_id=1, source_target_pairs={{0,3},{1,0},{2,1},{3,2},{4,7},{5,4},{6,5},{7,6},{8,11},{9,8},{10,9... | collective-permute-start | bytes 786440 | tf_op jit(solution)/shard_map/ppermute | solution.py:23
  184.2 11.1 %collective-permute-start.24 = (bf16[64,2048]{1,0:T(8,128)(2,1)S(1)}, bf16[64,2048]{1,0:T(8,128)(2,1)S(1)}, u32[]{:S(2)}, u32[]{:S(2)}) collective-permute-start(bf16[64,2048]{1,0:T(8,128)(2,1)S(1)} %get-tuple-element.126), channel_id=1, source_target_pairs={{0,1},{1,2},{2,3},{3,0},{4,5},{5,6},{6,7},{7,4},{8,9},{9,10},{10,1... | collective-permute-start | bytes 786440 | tf_op jit(solution)/shard_map/ppermute | solution.py:23
  184.2 13.1 %collective-permute-start.23 = (bf16[64,2048]{1,0:T(8,128)(2,1)S(1)}, bf16[64,2048]{1,0:T(8,128)(2,1)S(1)}, u32[]{:S(2)}, u32[]{:S(2)}) collective-permute-start(bf16[64,2048]{1,0:T(8,128)(2,1)S(1)} %get-tuple-element.124), channel_id=1, source_target_pairs={{0,2},{1,3},{2,0},{3,1},{4,6},{5,7},{6,4},{7,5},{8,10},{9,11},{10,... | collective-permute-start | bytes 786440 | tf_op jit(solution)/shard_map/ppermute | solution.py:23
  185.9 15.7 %copy-start.17 = (bf16[512,512]{1,0:T(8,128)(2,1)S(1)}, bf16[512,512]{1,0:T(8,128)(2,1)}, u32[]{:S(2)}) copy-start(bf16[512,512]{1,0:T(8,128)(2,1)} %get-tuple-element.82.refs_0_.refs_2_) | copy-start | bytes 1572868
  185.9 15.7 %copy-start.24 = (s32[4]{0:T(128)S(1)}, s32[4]{0:T(128)}, u32[]{:S(2)}) copy-start(s32[4]{0:T(128)} %pad_add_fusion.s_ref) | copy-start | bytes 52
  199.2 11.3 %collective-permute-start.26 = (bf16[64,2048]{1,0:T(8,128)(2,1)}, bf16[64,2048]{1,0:T(8,128)(2,1)S(1)}, u32[]{:S(2)}, u32[]{:S(2)}) collective-permute-start(bf16[64,2048]{1,0:T(8,128)(2,1)} %tie.4.refs_2_.refs_3_), channel_id=1, source_target_pairs={{0,3},{1,0},{2,1},{3,2},{4,7},{5,4},{6,5},{7,6},{8,11},{9,8},{10,9... | collective-permute-start | bytes 786440 | tf_op jit(solution)/shard_map/ppermute | solution.py:23
  200.7 9.8 %collective-permute-start.27 = (bf16[64,2048]{1,0:T(8,128)(2,1)}, bf16[64,2048]{1,0:T(8,128)(2,1)S(1)}, u32[]{:S(2)}, u32[]{:S(2)}) collective-permute-start(bf16[64,2048]{1,0:T(8,128)(2,1)} %tie.4.refs_2_.refs_3_), channel_id=1, source_target_pairs={{0,2},{1,3},{2,0},{3,1},{4,6},{5,7},{6,4},{7,5},{8,10},{9,11},{10,... | collective-permute-start | bytes 786440 | tf_op jit(solution)/shard_map/ppermute | solution.py:23
  200.8 15.1 %collective-permute-start.28 = (bf16[64,2048]{1,0:T(8,128)(2,1)}, bf16[64,2048]{1,0:T(8,128)(2,1)S(1)}, u32[]{:S(2)}, u32[]{:S(2)}) collective-permute-start(bf16[64,2048]{1,0:T(8,128)(2,1)} %tie.4.refs_2_.refs_3_), channel_id=1, source_target_pairs={{0,1},{1,2},{2,3},{3,0},{4,5},{5,6},{6,7},{7,4},{8,9},{9,10},{10,1... | collective-permute-start | bytes 786440 | tf_op jit(solution)/shard_map/ppermute | solution.py:23
  222.8 3.1 collective-permute-start.29
  236.5 28.4 %collective-permute-start.30 = (bf16[2,256,512]{2,1,0:T(8,128)(2,1)}, bf16[2,256,512]{2,1,0:T(8,128)(2,1)S(1)}, u32[]{:S(2)}, u32[]{:S(2)}) collective-permute-start(bf16[2,256,512]{2,1,0:T(8,128)(2,1)} %get-tuple-element.90.refs_7_), channel_id=1, source_target_pairs={{4,0},{8,4},{12,8},{5,1},{9,5},{13,9},{6,2},{10,6},{14,10},{7,3},{... | collective-permute-start | bytes 1572872 | tf_op jit(solution)/shard_map/ppermute | solution.py:28
  237.8 27.9 %collective-permute-start.31 = (bf16[2,256,512]{2,1,0:T(8,128)(2,1)}, bf16[2,256,512]{2,1,0:T(8,128)(2,1)}, u32[]{:S(2)}, u32[]{:S(2)}) collective-permute-start(bf16[2,256,512]{2,1,0:T(8,128)(2,1)} %get-tuple-element.90.refs_7_), channel_id=1, source_target_pairs={{8,0},{12,4},{9,1},{13,5},{10,2},{14,6},{11,3},{15,7},{24,16},{28,... | collective-permute-start | bytes 1572872 | tf_op jit(solution)/shard_map/ppermute | solution.py:28
  239.1 27.5 %collective-permute-start.32 = (bf16[2,256,512]{2,1,0:T(8,128)(2,1)}, bf16[2,256,512]{2,1,0:T(8,128)(2,1)}, u32[]{:S(2)}, u32[]{:S(2)}) collective-permute-start(bf16[2,256,512]{2,1,0:T(8,128)(2,1)} %get-tuple-element.90.refs_7_), channel_id=1, source_target_pairs={{12,0},{13,1},{14,2},{15,3},{28,16},{29,17},{30,18},{31,19},{44,32... | collective-permute-start | bytes 1572872 | tf_op jit(solution)/shard_map/ppermute | solution.py:28
  290.5 4.3 %collective-permute-start.33 = (bf16[256,2048]{1,0:T(8,128)(2,1)}, bf16[256,2048]{1,0:T(8,128)(2,1)S(1)}, u32[]{:S(2)}, u32[]{:S(2)}) collective-permute-start(bf16[256,2048]{1,0:T(8,128)(2,1)} %copy-done.32), channel_id=1, source_target_pairs={{0,16},{16,0},{1,17},{17,1},{2,18},{18,2},{3,19},{19,3},{4,20},{20... | collective-permute-start | bytes 3145736 | tf_op jit(solution)/shard_map/ppermute | solution.py:34
  291.0 4.0 %collective-permute-start.34 = (bf16[256,2048]{1,0:T(8,128)(2,1)}, bf16[256,2048]{1,0:T(8,128)(2,1)S(1)}, u32[]{:S(2)}, u32[]{:S(2)}) collective-permute-start(bf16[256,2048]{1,0:T(8,128)(2,1)} %tie.6), channel_id=1, source_target_pairs={{0,16},{16,0},{1,17},{17,1},{2,18},{18,2},{3,19},{19,3},{4,20},{20... | collective-permute-start | bytes 3145736 | tf_op jit(solution)/shard_map/ppermute | solution.py:34
  291.9 1.4 collective-permute-start.38
  293.4 10.2 %collective-permute-start.39 = (f32[2,2048]{1,0:T(2,128)S(1)}, f32[2,2048]{1,0:T(2,128)S(1)}, u32[]{:S(2)}, u32[]{:S(2)}) collective-permute-start(f32[2,2048]{1,0:T(2,128)S(1)} %fusion.11), channel_id=1, source_target_pairs={{0,4},{4,0},{8,12},{12,8},{1,5},{5,1},{9,13},{13,9},{2,6},{6,2},{1... | collective-permute-start | bytes 49160 | tf_op jit(solution)/shard_map/ppermute | solution.py:1145
  301.8 18.0 %collective-permute-start.37 = (bf16[128,2048]{1,0:T(8,128)(2,1)}, bf16[128,2048]{1,0:T(8,128)(2,1)S(1)}, u32[]{:S(2)}, u32[]{:S(2)}) collective-permute-start(bf16[128,2048]{1,0:T(8,128)(2,1)} %get-tuple-element.110), channel_id=1, source_target_pairs={{0,3},{1,0},{2,1},{3,2},{4,7},{5,4},{6,5},{7,6},{8,11},{9,8},{10,9... | collective-permute-start | bytes 1572872 | tf_op jit(solution)/shard_map/ppermute | solution.py:23
  302.3 17.6 %collective-permute-start.36 = (bf16[128,2048]{1,0:T(8,128)(2,1)}, bf16[128,2048]{1,0:T(8,128)(2,1)S(1)}, u32[]{:S(2)}, u32[]{:S(2)}) collective-permute-start(bf16[128,2048]{1,0:T(8,128)(2,1)} %get-tuple-element.109), channel_id=1, source_target_pairs={{0,1},{1,2},{2,3},{3,0},{4,5},{5,6},{6,7},{7,4},{8,9},{9,10},{10,1... | collective-permute-start | bytes 1572872 | tf_op jit(solution)/shard_map/ppermute | solution.py:23
  303.3 22.8 %collective-permute-start.35 = (bf16[128,2048]{1,0:T(8,128)(2,1)}, bf16[128,2048]{1,0:T(8,128)(2,1)S(1)}, u32[]{:S(2)}, u32[]{:S(2)}) collective-permute-start(bf16[128,2048]{1,0:T(8,128)(2,1)} %get-tuple-element.108), channel_id=1, source_target_pairs={{0,2},{1,3},{2,0},{3,1},{4,6},{5,7},{6,4},{7,5},{8,10},{9,11},{10,... | collective-permute-start | bytes 1572872 | tf_op jit(solution)/shard_map/ppermute | solution.py:23
  303.6 8.2 %collective-permute-start.40 = (f32[2,2048]{1,0:T(2,128)S(1)}, f32[2,2048]{1,0:T(2,128)S(1)}, u32[]{:S(2)}, u32[]{:S(2)}) collective-permute-start(f32[2,2048]{1,0:T(2,128)S(1)} %fusion.29), channel_id=1, source_target_pairs={{0,12},{4,8},{8,4},{12,0},{1,13},{5,9},{9,5},{13,1},{2,14},{6,10},... | collective-permute-start | bytes 49160 | tf_op jit(solution)/shard_map/ppermute | solution.py:1145
  311.8 3.6 collective-permute-start.41
  315.4 4.4 %collective-permute-start.42 = (f32[2,2048]{1,0:T(2,128)S(1)}, f32[2,2048]{1,0:T(2,128)S(1)}, u32[]{:S(2)}, u32[]{:S(2)}) collective-permute-start(f32[2,2048]{1,0:T(2,128)S(1)} %add.188), channel_id=1, source_target_pairs={{0,96},{32,64},{64,32},{96,0},{1,97},{33,65},{65,33},{97,1},{2,98}... | collective-permute-start | bytes 49160 | tf_op jit(solution)/shard_map/ppermute | solution.py:1145
  327.6 31.9 %copy-start.41 = (bf16[144,2048]{1,0:T(8,128)(2,1)}, bf16[144,2048]{1,0:T(8,128)(2,1)S(1)}, u32[]{:S(2)}) copy-start(bf16[144,2048]{1,0:T(8,128)(2,1)S(1)} %maximum_maximum_fusion.refs_4_) | copy-start | bytes 1769476
  327.6 16.1 %collective-permute-start.43 = (bf16[144,2048]{1,0:T(8,128)(2,1)S(1)}, bf16[144,2048]{1,0:T(8,128)(2,1)S(1)}, u32[]{:S(2)}, u32[]{:S(2)}) collective-permute-start(bf16[144,2048]{1,0:T(8,128)(2,1)S(1)} %maximum_maximum_fusion.refs_4_), channel_id=1, source_target_pairs={{0,3},{1,0},{2,1},{3,2},{4,7},{5,4},{6,5},{7,6},{8,11},{9,8},{10,9... | collective-permute-start | bytes 1769480 | tf_op jit(solution)/shard_map/ppermute | solution.py:23
  330.1 14.6 %collective-permute-start.44 = (bf16[144,2048]{1,0:T(8,128)(2,1)S(1)}, bf16[144,2048]{1,0:T(8,128)(2,1)S(1)}, u32[]{:S(2)}, u32[]{:S(2)}) collective-permute-start(bf16[144,2048]{1,0:T(8,128)(2,1)S(1)} %maximum_maximum_fusion.refs_4_), channel_id=1, source_target_pairs={{0,2},{1,3},{2,0},{3,1},{4,6},{5,7},{6,4},{7,5},{8,10},{9,11},{10,... | collective-permute-start | bytes 1769480 | tf_op jit(solution)/shard_map/ppermute | solution.py:23
  330.6 28.9 %collective-permute-start.45 = (bf16[144,2048]{1,0:T(8,128)(2,1)S(1)}, bf16[144,2048]{1,0:T(8,128)(2,1)S(1)}, u32[]{:S(2)}, u32[]{:S(2)}) collective-permute-start(bf16[144,2048]{1,0:T(8,128)(2,1)S(1)} %maximum_maximum_fusion.refs_4_), channel_id=1, source_target_pairs={{0,1},{1,2},{2,3},{3,0},{4,5},{5,6},{6,7},{7,4},{8,9},{9,10},{10,1... | collective-permute-start | bytes 1769480 | tf_op jit(solution)/shard_map/ppermute | solution.py:23
  343.7 15.8 %copy-start.48 = (bf16[144,2048]{1,0:T(8,128)(2,1)}, bf16[144,2048]{1,0:T(8,128)(2,1)S(1)}, u32[]{:S(2)}) copy-start(bf16[144,2048]{1,0:T(8,128)(2,1)S(1)} %collective-permute-done.43.refs_5_) | copy-start | bytes 1769476
  379.4 2.4 collective-permute-start.46
  (48 other events, 176.8 us)
Sparse Core Ops, SparseCore 0:
  16.5 77.8 all-gather.2
  96.6 64.9 all-gather.4
  274.6 103.4 reduce-scatter.1

commit v6 on v5

--- a/solution.py
+++ b/solution.py
@@ -309,7 +309,7 @@
 
 def split_out(out, own_ref, other_ref):
     half = out.shape[0] // 2
-    own_ref[...] = out[:half]
+    own_ref[...] = out[:half].astype(BF)
     other_ref[...] = out[half:].astype(BF)
 
 
@@ -397,7 +397,7 @@
     later = pl.BlockSpec((rows, SLAB), lambda i, s: (0, jnp.maximum(i - 4, 0)))
     operands = (*x_pair, weight, key, value, *came, rate, cosine, sine)
     shapes = (
-        sds((rows, D), F32),
+        sds((rows, D), BF),
         sds((rows, D), BF),
         sds((2 * rows, DK), BF),
         sds((2, DK, DV), BF),
@@ -484,7 +484,7 @@
     block = pl.BlockSpec((1, 4, 2, 64, 3 * DV), lambda i, s: (jnp.minimum(i, 3), 0, 0, 0, 0))
     later = pl.BlockSpec((rows, SLAB), lambda i, s: (0, jnp.maximum(i - 4, 0)))
     shapes = (
-        sds((rows, D), F32),
+        sds((rows, D), BF),
         sds((rows, D), BF),
         sds((8, D), F32),
         sds((2 * rows, 2 * DV), BF),
@@ -950,10 +950,8 @@
 
 def chip_blocks(own, came):
     block = own.shape[0] // 4
-    return [
-        (own[o * block : (o + 1) * block] + came[o * block : (o + 1) * block].astype(F32)).astype(BF)
-        for o in range(4)
-    ]
+    spans = [slice(o * block, (o + 1) * block) for o in range(4)]
+    return [(own[span].astype(F32) + came[span].astype(F32)).astype(BF) for span in spans]
 
 
 def gate_norm(gate_pre, retained):

time: 392 us -> 391 us (level)
  no operation moved by 1% of the time
where the time goes in v6:
time: 391 us; the launch traced here: 389 us
  waiting for transfers between devices  139 us (36%)
  Pallas kernels  119 us (30%)
  starting transfers between devices  64.4 us (16%)
  local copies, waits for them, and re-layouts  31.9 us (8%)
  between operations  15.8 us (4%)
  other arithmetic  13.3 us (3%)
  matrix products  5.79 us (1%)
    pallas_call x23, Pallas kernels, call(): pl.pallas_call(kernel, out_shape=shapes, grid_spec=pltpu.PrefetchScalarGr...  119 us
    ppermute x18, waiting for transfers between devices, shift(): return lax.ppermute(value, axis, [(i, (i + offset) % n) for i in range(n)])  67.3 us
    unnamed x124, local copies, waits for them, and re-layouts  27.9 us
    ppermute x6, waiting for transfers between devices, shift_open(): lax.ppermute(value, axis, [(i, i + offset) for i in range(n) if 0 <= i +...  23.3 us
    ppermute x18, starting transfers between devices, shift(): return lax.ppermute(value, axis, [(i, (i + offset) % n) for i in range(n)])  19.4 us
    ppermute x6, waiting for transfers between devices, hop(): return lax.ppermute(value, ('x', 'core', 'ctx'), pairs)  18.8 us
    ppermute x5, starting transfers between devices, per_device(): gains = gains + lax.ppermute(gains, axis, list(enumerate(swapped)))  12.2 us
    ppermute x12, waiting for transfers between devices, swap(): return lax.ppermute(value, 'core', [(0, 1), (1, 0)])  12.1 us
  transfers between devices with their start and end apart: 50, of which 35 were waited for; matrix products, arithmetic and copies ran while one was open for 5% of the time, Pallas kernels for 19%

profile of v6, /device:TPU:1, one launch (start us, length us, event | category | flops | bytes accessed | tf_op | source)
XLA Modules:
  0.0 388.9 jit_solution(11885350068125613346)
XLA Ops:
  7.8 2.6 split_attn.1
  13.9 2.5 stack_attn.1
  17.8 2.5 collective-permute-start.3
  22.8 3.2 collective-permute-done.3.refs_3_.refs_2_
  25.9 1.6 copy-done.8
  30.1 1.6 collective-permute-start.5
  33.6 2.1 collective-permute-start.7
  38.3 2.5 split_mlp.1
  43.1 5.2 %collective-permute-done.6.refs_3_.refs_2_ = bf16[4,2,64,768]{3,2,1,0:T(8,128)(2,1)} collective-permute-done((bf16[4,2,64,768]{3,2,1,0:T(8,128)(2,1)S(1)}, bf16[4,2,64,768]{3,2,1,0:T(8,128)(2,1)}, u32[]{:S(2)}, u32[]{:S(2)}) %collective-permute-start.6) | collective-permute-done | bytes 786464 | tf_op jit(solution)/shard_map/ppermute | solution.py:148
  48.3 9.1 %collective-permute-done.7.refs_4_.refs_3_ = bf16[4,2,64,768]{3,2,1,0:T(8,128)(2,1)} collective-permute-done((bf16[4,2,64,768]{3,2,1,0:T(8,128)(2,1)S(1)}, bf16[4,2,64,768]{3,2,1,0:T(8,128)(2,1)}, u32[]{:S(2)}, u32[]{:S(2)}) %collective-permute-start.7) | collective-permute-done | bytes 786464 | tf_op jit(solution)/shard_map/ppermute | solution.py:148
  57.4 1.5 copy-done.2
  58.9 5.6 %project_kv.1 = f32[512,768]{1,0:T(8,128)S(1)} custom-call(s32[4]{0:T(128)S(1)} %copy-done.23, bf16[256,2048]{1,0:T(8,128)(2,1)S(1)} %copy-done.2, bf16[256,2048]{1,0:T(8,128)(2,1)S(1)} %collective-permute-done.5.refs_1_.refs_4_.refs_10_, bf16[4,2,64,768]{3,2,1,0:T(8,128)(2,1)S(1)} %bitcast.45, ...), custom_call_target="tpu_custom_call" | custom-call | flops 1 | bytes 1 | tf_op jit(solution)/shard_map/project_kv/pallas_call | solution.py:61
  67.0 2.4 collective-permute-start.10
  69.3 4.1 %collective-permute-start.11 = (bf16[2,256,512]{2,1,0:T(8,128)(2,1)S(1)}, bf16[2,256,512]{2,1,0:T(8,128)(2,1)S(1)}, u32[]{:S(2)}, u32[]{:S(2)}) collective-permute-start(bf16[2,256,512]{2,1,0:T(8,128)(2,1)S(1)} %convolution_convert_fusion.refs_2_), channel_id=1, source_target_pairs={{0,8},{4,12},{1,9},{5,13},{2,10},{6,14},{3,11},{7,15},{16,24},{20,... | collective-permute-start | bytes 1572872 | tf_op jit(solution)/shard_map/ppermute | solution.py:28
  78.7 11.1 %collective-permute-done.10.refs_5_ = bf16[2,256,512]{2,1,0:T(8,128)(2,1)S(1)} collective-permute-done((bf16[2,256,512]{2,1,0:T(8,128)(2,1)S(1)}, bf16[2,256,512]{2,1,0:T(8,128)(2,1)S(1)}, u32[]{:S(2)}, u32[]{:S(2)}) %collective-permute-start.10) | collective-permute-done | bytes 524320 | tf_op jit(solution)/shard_map/ppermute | solution.py:28
  89.9 11.3 %collective-permute-done.11.refs_6_ = bf16[2,256,512]{2,1,0:T(8,128)(2,1)S(1)} collective-permute-done((bf16[2,256,512]{2,1,0:T(8,128)(2,1)S(1)}, bf16[2,256,512]{2,1,0:T(8,128)(2,1)S(1)}, u32[]{:S(2)}, u32[]{:S(2)}) %collective-permute-start.11) | collective-permute-done | bytes 524320 | tf_op jit(solution)/shard_map/ppermute | solution.py:28
  102.2 12.9 %retain.1 = (bf16[256,2048]{1,0:T(8,128)(2,1)}, bf16[256,2048]{1,0:T(8,128)(2,1)}, bf16[512,256]{1,0:T(8,128)(2,1)}, bf16[2,256,512]{2,1,0:T(8,128)(2,1)}, bf16[...) custom-call(s32[6]{0:T(128)} %concatenate.24.s_ref, ...), custom_call_target="tpu_custom_call" | custom-call | flops 1 | bytes 1 | tf_op jit(solution)/shard_map/retain/pallas_call | solution.py:61
  115.9 2.5 collective-permute-done.13
  119.8 2.9 collective-permute-start.16
  122.7 1.7 collective-permute-start.14
  124.4 9.1 %collective-permute-done.16 = bf16[64,2048]{1,0:T(8,128)(2,1)S(1)} collective-permute-done((bf16[64,2048]{1,0:T(8,128)(2,1)S(1)}, bf16[64,2048]{1,0:T(8,128)(2,1)S(1)}, u32[]{:S(2)}, u32[]{:S(2)}) %collective-permute-start.16) | collective-permute-done | bytes 262176 | tf_op jit(solution)/shard_map/ppermute | solution.py:23
  133.5 2.3 collective-permute-done.14
  140.2 2.2 collective-permute-start.21
  143.6 2.6 collective-permute-done.18.refs_4_
  146.2 7.6 %collective-permute-done.19.refs_5_ = bf16[64,2048]{1,0:T(8,128)(2,1)S(1)} collective-permute-done((bf16[64,2048]{1,0:T(8,128)(2,1)S(1)}, bf16[64,2048]{1,0:T(8,128)(2,1)S(1)}, u32[]{:S(2)}, u32[]{:S(2)}) %collective-permute-start.19) | collective-permute-done | bytes 262176 | tf_op jit(solution)/shard_map/ppermute | solution.py:23
  159.3 2.2 all-gather.5.cloned.1.call-done
  161.6 14.3 %mlp.1 = (bf16[256,2048]{1,0:T(8,128)(2,1)}, bf16[256,2048]{1,0:T(8,128)(2,1)}, f32[8,2048]{1,0:T(8,128)}, bf16[512,1024]{1,0:T(8,128)(2,1)}, bf16[512,512]{1,0:T(8,128)(2,1)}) custom-call(s32[4]{0:T(128)} %pad_add_fusion.s_ref, bf16[256,2048]{1,0:T(8,128)(2,1)} %copy-done.15, bf16[256,2048]{1,0:T(8,128)(2,1)} %collective-permute-done.20.refs_1_, ...), custom_call_target="tpu_custom_call" | custom-call | flops 1 | bytes 1 | tf_op jit(solution)/shard_map/mlp/pallas_call | solution.py:61
  176.6 2.5 collective-permute-done.22
  180.5 2.7 collective-permute-start.25
  183.2 1.7 collective-permute-start.23
  184.9 6.9 %weight_mlp.1 = (bf16[4,4,2,64,3584]{4,3,2,1,0:T(8,128)(2,1)}, f32[8,128]{1,0:T(8,128)}) custom-call(s32[4]{0:T(128)} %pad_add_fusion.s_ref, bf16[256,2048]{1,0:T(8,128)(2,1)} %copy-done.15, bf16[256,2048]{1,0:T(8,128)(2,1)} %collective-permute-done.20.refs_1_, bf16[512,1024]{1,0:T(8,128)(2,1)} %get-tuple-element.80.refs_2_), custom_call_target="tpu_custom_call" | custom-call | flops 1 | bytes 1 | tf_op jit(solution)/shard_map/weight_mlp/pallas_call | solution.py:61
  191.8 2.2 collective-permute-done.25
  194.0 2.4 collective-permute-done.23
  196.4 1.9 add_convert_fusion.1.refs_0_
  200.7 2.8 copy-done.7
  204.5 2.8 project_down.1
  209.6 5.4 %collective-permute-done.28.refs_6_ = bf16[64,2048]{1,0:T(8,128)(2,1)S(1)} collective-permute-done((bf16[64,2048]{1,0:T(8,128)(2,1)}, bf16[64,2048]{1,0:T(8,128)(2,1)S(1)}, u32[]{:S(2)}, u32[]{:S(2)}) %collective-permute-start.28) | collective-permute-done | bytes 262176 | tf_op jit(solution)/shard_map/ppermute | solution.py:23
  215.7 6.1 %second_back.1 = (f32[256,2048]{1,0:T(8,128)}, bf16[256,2048]{1,0:T(8,128)(2,1)}) custom-call(s32[4]{0:T(128)} %pad_add_fusion.s_ref, f32[256,2048]{1,0:T(8,128)} %copy-done.11, f32[256,2048]{1,0:T(8,128)} %refs_1_.6, f32[1,2048]{1,0:T(1,128)} %bitcast.47, bf16[64,2048]{1,0:T(8,128)(2,1)} %tie.4.refs_2_.refs_3_, bf16[64,2048]{1,0:T(8,128)(2,1)} %copy-done.57, ...), custom_call_target="tpu_custom_call" | custom-call | flops 1 | bytes 1 | tf_op jit(solution)/shard_map/second_back/pallas_call | solution.py:61
  223.3 1.5 collective-permute-done.29.refs_1_
  225.8 9.6 %back_gate.1 = (bf16[512,512]{1,0:T(8,128)(2,1)}, bf16[512,512]{1,0:T(8,128)(2,1)}, bf16[2,256,512]{2,1,0:T(8,128)(2,1)}) custom-call(s32[4]{0:T(128)} %pad_add_fusion.s_ref, bf16[256,2048]{1,0:T(8,128)(2,1)} %get-tuple-element.85.refs_0_, bf16[256,2048]{1,0:T(8,128)(2,1)} %copy-done.36, bf16[4,4,2,64,1280]{4,3,2,1,0:T(8,128)(2,1)} %bitcast.37, ...), custom_call_target="tpu_custom_call" | custom-call | flops 1 | bytes 1 | tf_op jit(solution)/shard_map/back_gate/pallas_call | solution.py:61
  238.0 1.5 collective-permute-start.32
  243.4 7.2 %weight_og.1 = (bf16[4,4,2,64,3584]{4,3,2,1,0:T(8,128)(2,1)}, f32[8,128]{1,0:T(8,128)}) custom-call(s32[4]{0:T(128)} %pad_add_fusion.s_ref, bf16[256,2048]{1,0:T(8,128)(2,1)} %get-tuple-element.85.refs_0_, bf16[256,2048]{1,0:T(8,128)(2,1)} %copy-done.36, bf16[512,512]{1,0:T(8,128)(2,1)} %get-tuple-element.94.refs_2_, ...), custom_call_target="tpu_custom_call", output_to_operand_aliasing={{0}: (7, {})} | custom-call | flops 1 | bytes 1 | tf_op jit(solution)/shard_map/weight_og/pallas_call | solution.py:61
  250.6 5.6 %weight_down.1 = (bf16[4,4,2,64,3584]{4,3,2,1,0:T(8,128)(2,1)}, f32[8,128]{1,0:T(8,128)}) custom-call(s32[4]{0:T(128)} %pad_add_fusion.s_ref, bf16[256,2048]{1,0:T(8,128)(2,1)} %copy-done.10, bf16[256,2048]{1,0:T(8,128)(2,1)} %copy-done.37, bf16[512,512]{1,0:T(8,128)(2,1)} %get-tuple-element.82.refs_0_.refs_2_, ...), custom_call_target="tpu_custom_call", output_to_operand_aliasing={{0}: (4, {})} | custom-call | flops 1 | bytes 1 | tf_op jit(solution)/shard_map/weight_down/pallas_call | solution.py:61
  256.2 5.2 %weight_query.1 = (bf16[4,4,2,64,3584]{4,3,2,1,0:T(8,128)(2,1)}, f32[8,128]{1,0:T(8,128)}) custom-call(s32[4]{0:T(128)} %pad_add_fusion.s_ref, bf16[256,2048]{1,0:T(8,128)(2,1)} %copy-done.1, bf16[256,2048]{1,0:T(8,128)(2,1)} %copy-done.4, bf16[512,256]{1,0:T(8,128)(2,1)} %pad_maximum_fusion.1.refs_2_.refs_7_, ...), custom_call_target="tpu_custom_call", output_to_operand_aliasing={{0}: (4, {})} | custom-call | flops 1 | bytes 1 | tf_op jit(solution)/shard_map/weight_query/pallas_call | solution.py:61
  265.5 7.8 %weight_last.1 = (bf16[4,4,2,64,3584]{4,3,2,1,0:T(8,128)(2,1)}, f32[8,128]{1,0:T(8,128)}, bf16[512,768]{1,0:T(8,128)(2,1)}) custom-call(s32[4]{0:T(128)} %pad_add_fusion.s_ref, bf16[256,2048]{1,0:T(8,128)(2,1)} %copy-done.1, bf16[256,2048]{1,0:T(8,128)(2,1)} %copy-done.4, bf16[2,256,512]{2,1,0:T(8,128)(2,1)} %tie.5.refs_2_, ...), custom_call_target="tpu_custom_call", output_to_operand_aliasing={{0}: (14, {})} | custom-call | flops 1 | bytes 1 | tf_op jit(solution)/shard_map/weight_last/pallas_call | solution.py:61
  274.9 2.5 copy-done
  279.6 7.5 %back_attn.1 = (f32[256,2048]{1,0:T(8,128)S(1)}, bf16[256,2048]{1,0:T(8,128)(2,1)S(1)}, f32[8,2048]{1,0:T(8,128)S(1)}) custom-call(s32[4]{0:T(128)S(1)} %copy-done.25, bf16[512,768]{1,0:T(8,128)(2,1)S(1)} %copy-done.21, bf16[4,2,64,768]{3,2,1,0:T(8,128)(2,1)S(1)} %bitcast.46, bf16[4,2,64,768]{3,2,1,0:T(8,128)(2,1)} %collective-permute-done.6.refs_3_.refs_2_, ...), custom_call_target="tpu_custom_call" | custom-call | flops 1 | bytes 1 | tf_op jit(solution)/shard_map/back_attn/pallas_call | solution.py:61
  292.2 1.5 collective-permute-start.39
  295.1 5.7 %third_blocks.1 = (bf16[128,2048]{1,0:T(8,128)(2,1)}, bf16[128,2048]{1,0:T(8,128)(2,1)}, bf16[128,2048]{1,0:T(8,128)(2,1)}, bf16[128,2048]{1,0:T(8,128)(2,1)}) custom-call(s32[4]{0:T(128)} %pad_add_fusion.s_ref, f32[256,2048]{1,0:T(8,128)} %copy-done.19, bf16[256,2048]{1,0:T(8,128)(2,1)} %copy-done.44, f32[256,2048]{1,0:T(8,128)} %copy-done.18, ...), custom_call_target="tpu_custom_call" | custom-call | flops 1 | bytes 1 | tf_op jit(solution)/shard_map/third_blocks/pallas_call | solution.py:61
  302.7 6.3 %collective-permute-start.40 = (f32[2,2048]{1,0:T(2,128)S(1)}, f32[2,2048]{1,0:T(2,128)S(1)}, u32[]{:S(2)}, u32[]{:S(2)}) collective-permute-start(f32[2,2048]{1,0:T(2,128)S(1)} %fusion.29), channel_id=1, source_target_pairs={{0,12},{4,8},{8,4},{12,0},{1,13},{5,9},{9,5},{13,1},{2,14},{6,10},... | collective-permute-start | bytes 49160 | tf_op jit(solution)/shard_map/ppermute | solution.py:1143
  309.0 1.9 collective-permute-done.40
  310.9 1.5 collective-permute-start.41
  312.4 2.1 collective-permute-done.41
  314.5 2.4 collective-permute-start.42
  317.0 1.8 collective-permute-done.42
  318.8 6.3 %collective-permute-done.35 = bf16[128,2048]{1,0:T(8,128)(2,1)S(1)} collective-permute-done((bf16[128,2048]{1,0:T(8,128)(2,1)}, bf16[128,2048]{1,0:T(8,128)(2,1)S(1)}, u32[]{:S(2)}, u32[]{:S(2)}) %collective-permute-start.35) | collective-permute-done | bytes 524320 | tf_op jit(solution)/shard_map/ppermute | solution.py:23
  326.7 2.3 collective-permute-start.43
  330.3 11.9 %collective-permute-done.43.refs_5_ = bf16[144,2048]{1,0:T(8,128)(2,1)S(1)} collective-permute-done((bf16[144,2048]{1,0:T(8,128)(2,1)S(1)}, bf16[144,2048]{1,0:T(8,128)(2,1)S(1)}, u32[]{:S(2)}, u32[]{:S(2)}) %collective-permute-start.43) | collective-permute-done | bytes 589856 | tf_op jit(solution)/shard_map/ppermute | solution.py:23
  342.2 1.5 collective-permute-done.44.refs_6_
  343.7 14.8 %collective-permute-done.45.refs_7_ = bf16[144,2048]{1,0:T(8,128)(2,1)S(1)} collective-permute-done((bf16[144,2048]{1,0:T(8,128)(2,1)S(1)}, bf16[144,2048]{1,0:T(8,128)(2,1)S(1)}, u32[]{:S(2)}, u32[]{:S(2)}) %collective-permute-start.45) | collective-permute-done | bytes 589856 | tf_op jit(solution)/shard_map/ppermute | solution.py:23
  359.3 7.4 %leave_rows.1 = (f32[256,2048]{1,0:T(8,128)}, f32[256,2048]{1,0:T(8,128)}) custom-call(s32[4]{0:T(128)} %pad_add_fusion.s_ref, f32[256,2048]{1,0:T(8,128)} %copy-done.11, f32[256,2048]{1,0:T(8,128)} %refs_1_.7, f32[256,2048]{1,0:T(8,128)} %get-tuple-element.84.refs_2_, f32[1,2048]{1,0:T(1,128)} %bitcast.49, bf16[144,2048]{1,0:T(8,128)(2,1)} %copy-done.41, ...), custom_call_target="tpu_custom_call" | custom-call | flops 1 | bytes 1 | tf_op jit(solution)/shard_map/leave_rows/pallas_call | solution.py:61
  368.8 8.1 %reduce-scatter.2.cloned.1.call-done.refs_0_ = bf16[128,3584]{1,0:T(8,128)(2,1)} async-done(((bf16[2048,3584]{1,0:T(8,128)(2,1)}), bf16[128,3584]{1,0:T(8,128)(2,1)}) %reduce-scatter.2.cloned.1.call-update) | async-done | bytes 917520 | tf_op jit(solution)/shard_map/reduce_scatter | solution.py:1124
  379.1 1.4 collective-permute-done.46.refs_1_
  380.6 1.8 join_heads.1
  (233 shorter events, 79.5 us)
Async XLA Ops:
  7.2 94.1 %all-gather.3.cloned.1.call-start = ((), (), s32[]{:S(2)}) async-start(), calls=%async_computation.1 | async-start | bytes 5570560 | tf_op jit(solution)/shard_map/all_gather | solution.py:1009
  10.4 2.8 collective-permute-start.1
  16.4 15.3 %copy-start.28 = (bf16[128,768]{1,0:T(8,128)(2,1)S(1)}, bf16[128,768]{1,0:T(8,128)(2,1)}, u32[]{:S(2)}) copy-start(bf16[128,768]{1,0:T(8,128)(2,1)} %get-tuple-element.70.refs_0_) | copy-start | bytes 589828
  16.4 145.2 %all-gather.5.cloned.1.call-start = ((), (), s32[]{:S(2)}) async-start(), calls=%async_computation.2 | async-start | bytes 6684672 | tf_op jit(solution)/shard_map/all_gather | solution.py:1044
  16.4 6.3 %collective-permute-start.2 = (bf16[128,768]{1,0:T(8,128)(2,1)}, bf16[128,768]{1,0:T(8,128)(2,1)S(1)}, u32[]{:S(2)}, u32[]{:S(2)}) collective-permute-start(bf16[128,768]{1,0:T(8,128)(2,1)} %get-tuple-element.70.refs_0_), channel_id=1, source_target_pairs={{0,4},{4,8},{8,12},{12,0},{16,48},{20,52},{24,56},{28,60},{32,36},... | collective-permute-start | bytes 589832 | tf_op jit(solution)/shard_map/ppermute | solution.py:148
  17.8 8.1 %collective-permute-start.3 = (bf16[128,768]{1,0:T(8,128)(2,1)}, bf16[128,768]{1,0:T(8,128)(2,1)S(1)}, u32[]{:S(2)}, u32[]{:S(2)}) collective-permute-start(bf16[128,768]{1,0:T(8,128)(2,1)} %get-tuple-element.70.refs_0_), channel_id=1, source_target_pairs={{0,8},{4,12},{8,0},{12,4},{16,80},{20,84},{24,88},{28,92},{32,40},... | collective-permute-start | bytes 589832 | tf_op jit(solution)/shard_map/ppermute | solution.py:148
  20.3 5.7 %collective-permute-start.4 = (bf16[128,768]{1,0:T(8,128)(2,1)}, bf16[128,768]{1,0:T(8,128)(2,1)S(1)}, u32[]{:S(2)}, u32[]{:S(2)}) collective-permute-start(bf16[128,768]{1,0:T(8,128)(2,1)} %get-tuple-element.70.refs_0_), channel_id=1, source_target_pairs={{0,12},{4,0},{8,4},{12,8},{16,112},{20,116},{24,120},{28,124},{32,... | collective-permute-start | bytes 589832 | tf_op jit(solution)/shard_map/ppermute | solution.py:148
  30.1 27.4 %copy-start.23 = (s32[4]{0:T(128)S(1)}, s32[4]{0:T(128)}, u32[]{:S(2)}) copy-start(s32[4]{0:T(128)} %pad_add_fusion.s_ref) | copy-start | bytes 52
  30.1 27.3 %collective-permute-start.5 = (bf16[256,2048]{1,0:T(8,128)(2,1)S(1)}, bf16[256,2048]{1,0:T(8,128)(2,1)S(1)}, u32[]{:S(2)}, u32[]{:S(2)}) collective-permute-start(bf16[256,2048]{1,0:T(8,128)(2,1)S(1)} %enter_rows.1.refs_3_.refs_0_.refs_9_), channel_id=1, source_target_pairs={{0,16},{16,0},{1,17},{17,1},{2,18},{18,2},{3,19},{19,3},{4,20},{20... | collective-permute-start | bytes 3145736 | tf_op jit(solution)/shard_map/ppermute | solution.py:34
  32.3 16.0 %collective-permute-start.6 = (bf16[4,2,64,768]{3,2,1,0:T(8,128)(2,1)S(1)}, bf16[4,2,64,768]{3,2,1,0:T(8,128)(2,1)}, u32[]{:S(2)}, u32[]{:S(2)}) collective-permute-start(bf16[4,2,64,768]{3,2,1,0:T(8,128)(2,1)S(1)} %bitcast.42), channel_id=1, source_target_pairs={{0,32},{4,36},{8,40},{12,44},{16,20},{20,24},{24,28},{28,16},{32,6... | collective-permute-start | bytes 2359304 | tf_op jit(solution)/shard_map/ppermute | solution.py:148
  33.6 23.8 %collective-permute-start.7 = (bf16[4,2,64,768]{3,2,1,0:T(8,128)(2,1)S(1)}, bf16[4,2,64,768]{3,2,1,0:T(8,128)(2,1)}, u32[]{:S(2)}, u32[]{:S(2)}) collective-permute-start(bf16[4,2,64,768]{3,2,1,0:T(8,128)(2,1)S(1)} %bitcast.43), channel_id=1, source_target_pairs={{0,64},{4,68},{8,72},{12,76},{16,24},{20,28},{24,16},{28,20},{32,9... | collective-permute-start | bytes 2359304 | tf_op jit(solution)/shard_map/ppermute | solution.py:148
  35.7 21.7 %collective-permute-start.8 = (bf16[4,2,64,768]{3,2,1,0:T(8,128)(2,1)S(1)}, bf16[4,2,64,768]{3,2,1,0:T(8,128)(2,1)}, u32[]{:S(2)}, u32[]{:S(2)}) collective-permute-start(bf16[4,2,64,768]{3,2,1,0:T(8,128)(2,1)S(1)} %bitcast.44), channel_id=1, source_target_pairs={{0,96},{4,100},{8,104},{12,108},{16,28},{20,16},{24,20},{28,24},{3... | collective-permute-start | bytes 2359304 | tf_op jit(solution)/shard_map/ppermute | solution.py:148
  40.8 2.4 collective-permute-start.9
  42.4 22.4 %copy-start.38 = (f32[256,128]{1,0:T(8,128)}, f32[256,128]{1,0:T(8,128)S(1)}, u32[]{:S(2)}) copy-start(f32[256,128]{1,0:T(8,128)S(1)} %get-tuple-element.140.refs_9_.refs_11_) | copy-start | bytes 393220
  42.4 22.4 %copy-start.42 = (f32[256,128]{1,0:T(8,128)}, f32[256,128]{1,0:T(8,128)S(1)}, u32[]{:S(2)}) copy-start(f32[256,128]{1,0:T(8,128)S(1)} %get-tuple-element.139.refs_10_.refs_12_) | copy-start | bytes 393220
  64.9 50.2 %copy-start.40 = (bf16[2,256,256]{2,1,0:T(8,128)(2,1)}, bf16[2,256,256]{2,1,0:T(8,128)(2,1)S(1)}, u32[]{:S(2)}) copy-start(bf16[2,256,256]{2,1,0:T(8,128)(2,1)S(1)} %multiply_convert_fusion.refs_7_) | copy-start | bytes 786436
  66.9 310.0 %reduce-scatter.2.cloned.1.call-start = ((), (), s32[]{:S(2)}) async-start(), calls=%async_computation.3 | async-start | bytes 15597568 | tf_op jit(solution)/shard_map/reduce_scatter | solution.py:1124
  67.0 22.9 %collective-permute-start.10 = (bf16[2,256,512]{2,1,0:T(8,128)(2,1)S(1)}, bf16[2,256,512]{2,1,0:T(8,128)(2,1)S(1)}, u32[]{:S(2)}, u32[]{:S(2)}) collective-permute-start(bf16[2,256,512]{2,1,0:T(8,128)(2,1)S(1)} %convolution_convert_fusion.refs_2_), channel_id=1, source_target_pairs={{0,4},{4,8},{8,12},{1,5},{5,9},{9,13},{2,6},{6,10},{10,14},{3,7},{... | collective-permute-start | bytes 1572872 | tf_op jit(solution)/shard_map/ppermute | solution.py:28
  69.3 31.8 %collective-permute-start.11 = (bf16[2,256,512]{2,1,0:T(8,128)(2,1)S(1)}, bf16[2,256,512]{2,1,0:T(8,128)(2,1)S(1)}, u32[]{:S(2)}, u32[]{:S(2)}) collective-permute-start(bf16[2,256,512]{2,1,0:T(8,128)(2,1)S(1)} %convolution_convert_fusion.refs_2_), channel_id=1, source_target_pairs={{0,8},{4,12},{1,9},{5,13},{2,10},{6,14},{3,11},{7,15},{16,24},{20,... | collective-permute-start | bytes 1572872 | tf_op jit(solution)/shard_map/ppermute | solution.py:28
  73.5 27.8 %collective-permute-start.12 = (bf16[2,256,512]{2,1,0:T(8,128)(2,1)S(1)}, bf16[2,256,512]{2,1,0:T(8,128)(2,1)S(1)}, u32[]{:S(2)}, u32[]{:S(2)}) collective-permute-start(bf16[2,256,512]{2,1,0:T(8,128)(2,1)S(1)} %convolution_convert_fusion.refs_2_), channel_id=1, source_target_pairs={{0,12},{1,13},{2,14},{3,15},{16,28},{17,29},{18,30},{19,31},{32,44... | collective-permute-start | bytes 1572872 | tf_op jit(solution)/shard_map/ppermute | solution.py:28
  74.8 2.0 collective-permute-start
  115.1 24.3 %copy-start.5 = (bf16[256,2048]{1,0:T(8,128)(2,1)S(1)}, bf16[256,2048]{1,0:T(8,128)(2,1)}, u32[]{:S(2)}) copy-start(bf16[256,2048]{1,0:T(8,128)(2,1)} %copy-done.4) | copy-start | bytes 3145732
  115.1 24.3 %copy-start.12 = (f32[256,2048]{1,0:T(8,128)S(1)}, f32[256,2048]{1,0:T(8,128)}, u32[]{:S(2)}) copy-start(f32[256,2048]{1,0:T(8,128)} %refs_1_.6) | copy-start | bytes 6291460
  115.1 3.3 collective-permute-start.13
  119.8 13.7 %collective-permute-start.16 = (bf16[64,2048]{1,0:T(8,128)(2,1)S(1)}, bf16[64,2048]{1,0:T(8,128)(2,1)S(1)}, u32[]{:S(2)}, u32[]{:S(2)}) collective-permute-start(bf16[64,2048]{1,0:T(8,128)(2,1)S(1)} %get-tuple-element.128), channel_id=1, source_target_pairs={{0,3},{1,0},{2,1},{3,2},{4,7},{5,4},{6,5},{7,6},{8,11},{9,8},{10,9... | collective-permute-start | bytes 786440 | tf_op jit(solution)/shard_map/ppermute | solution.py:23
  122.7 10.8 %collective-permute-start.15 = (bf16[64,2048]{1,0:T(8,128)(2,1)S(1)}, bf16[64,2048]{1,0:T(8,128)(2,1)S(1)}, u32[]{:S(2)}, u32[]{:S(2)}) collective-permute-start(bf16[64,2048]{1,0:T(8,128)(2,1)S(1)} %get-tuple-element.129), channel_id=1, source_target_pairs={{0,1},{1,2},{2,3},{3,0},{4,5},{5,6},{6,7},{7,4},{8,9},{9,10},{10,1... | collective-permute-start | bytes 786440 | tf_op jit(solution)/shard_map/ppermute | solution.py:23
  122.7 13.0 %collective-permute-start.14 = (bf16[64,2048]{1,0:T(8,128)(2,1)S(1)}, bf16[64,2048]{1,0:T(8,128)(2,1)S(1)}, u32[]{:S(2)}, u32[]{:S(2)}) collective-permute-start(bf16[64,2048]{1,0:T(8,128)(2,1)S(1)} %get-tuple-element.127), channel_id=1, source_target_pairs={{0,2},{1,3},{2,0},{3,1},{4,6},{5,7},{6,4},{7,5},{8,10},{9,11},{10,... | collective-permute-start | bytes 786440 | tf_op jit(solution)/shard_map/ppermute | solution.py:23
  136.9 16.8 %copy-start.9 = (f32[256,2048]{1,0:T(8,128)S(1)}, f32[256,2048]{1,0:T(8,128)}, u32[]{:S(2)}) copy-start(f32[256,2048]{1,0:T(8,128)} %refs_1_.7) | copy-start | bytes 6291460
  136.9 16.8 %copy-start.29 = (f32[2048]{0:T(1024)S(1)}, f32[2048]{0:T(1024)}, u32[]{:S(2)}) copy-start(f32[2048]{0:T(1024)} %param.17) | copy-start | bytes 24580
  136.9 6.7 %collective-permute-start.17 = (bf16[64,2048]{1,0:T(8,128)(2,1)S(1)}, bf16[64,2048]{1,0:T(8,128)(2,1)S(1)}, u32[]{:S(2)}, u32[]{:S(2)}) collective-permute-start(bf16[64,2048]{1,0:T(8,128)(2,1)S(1)} %add_convert_fusion.6.refs_2_), channel_id=1, source_target_pairs={{0,3},{1,0},{2,1},{3,2},{4,7},{5,4},{6,5},{7,6},{8,11},{9,8},{10,9... | collective-permute-start | bytes 786440 | tf_op jit(solution)/shard_map/ppermute | solution.py:23
  138.3 7.9 %collective-permute-start.18 = (bf16[64,2048]{1,0:T(8,128)(2,1)S(1)}, bf16[64,2048]{1,0:T(8,128)(2,1)S(1)}, u32[]{:S(2)}, u32[]{:S(2)}) collective-permute-start(bf16[64,2048]{1,0:T(8,128)(2,1)S(1)} %add_convert_fusion.6.refs_2_), channel_id=1, source_target_pairs={{0,2},{1,3},{2,0},{3,1},{4,6},{5,7},{6,4},{7,5},{8,10},{9,11},{10,... | collective-permute-start | bytes 786440 | tf_op jit(solution)/shard_map/ppermute | solution.py:23
  138.7 15.1 %collective-permute-start.19 = (bf16[64,2048]{1,0:T(8,128)(2,1)S(1)}, bf16[64,2048]{1,0:T(8,128)(2,1)S(1)}, u32[]{:S(2)}, u32[]{:S(2)}) collective-permute-start(bf16[64,2048]{1,0:T(8,128)(2,1)S(1)} %add_convert_fusion.6.refs_2_), channel_id=1, source_target_pairs={{0,1},{1,2},{2,3},{3,0},{4,5},{5,6},{6,7},{7,4},{8,9},{9,10},{10,1... | collective-permute-start | bytes 786440 | tf_op jit(solution)/shard_map/ppermute | solution.py:23
  140.2 21.4 %copy-start.10 = (bf16[256,2048]{1,0:T(8,128)(2,1)}, bf16[256,2048]{1,0:T(8,128)(2,1)S(1)}, u32[]{:S(2)}) copy-start(bf16[256,2048]{1,0:T(8,128)(2,1)S(1)} %low_rows.1.refs_2_.refs_0_) | copy-start | bytes 3145732
  140.2 16.8 %collective-permute-start.21 = (bf16[256,2048]{1,0:T(8,128)(2,1)S(1)}, bf16[256,2048]{1,0:T(8,128)(2,1)S(1)}, u32[]{:S(2)}, u32[]{:S(2)}) collective-permute-start(bf16[256,2048]{1,0:T(8,128)(2,1)S(1)} %low_rows.1.refs_2_.refs_0_), channel_id=1, source_target_pairs={{0,16},{16,0},{1,17},{17,1},{2,18},{18,2},{3,19},{19,3},{4,20},{20... | collective-permute-start | bytes 3145736 | tf_op jit(solution)/shard_map/ppermute | solution.py:34
  156.5 2.8 collective-permute-start.20
  175.9 3.3 collective-permute-start.22
  180.5 13.5 %collective-permute-start.25 = (bf16[64,2048]{1,0:T(8,128)(2,1)S(1)}, bf16[64,2048]{1,0:T(8,128)(2,1)S(1)}, u32[]{:S(2)}, u32[]{:S(2)}) collective-permute-start(bf16[64,2048]{1,0:T(8,128)(2,1)S(1)} %get-tuple-element.125), channel_id=1, source_target_pairs={{0,3},{1,0},{2,1},{3,2},{4,7},{5,4},{6,5},{7,6},{8,11},{9,8},{10,9... | collective-permute-start | bytes 786440 | tf_op jit(solution)/shard_map/ppermute | solution.py:23
  183.2 10.8 %collective-permute-start.24 = (bf16[64,2048]{1,0:T(8,128)(2,1)S(1)}, bf16[64,2048]{1,0:T(8,128)(2,1)S(1)}, u32[]{:S(2)}, u32[]{:S(2)}) collective-permute-start(bf16[64,2048]{1,0:T(8,128)(2,1)S(1)} %get-tuple-element.126), channel_id=1, source_target_pairs={{0,1},{1,2},{2,3},{3,0},{4,5},{5,6},{6,7},{7,4},{8,9},{9,10},{10,1... | collective-permute-start | bytes 786440 | tf_op jit(solution)/shard_map/ppermute | solution.py:23
  183.2 13.2 %collective-permute-start.23 = (bf16[64,2048]{1,0:T(8,128)(2,1)S(1)}, bf16[64,2048]{1,0:T(8,128)(2,1)}, u32[]{:S(2)}, u32[]{:S(2)}) collective-permute-start(bf16[64,2048]{1,0:T(8,128)(2,1)S(1)} %get-tuple-element.124), channel_id=1, source_target_pairs={{0,2},{1,3},{2,0},{3,1},{4,6},{5,7},{6,4},{7,5},{8,10},{9,11},{10,... | collective-permute-start | bytes 786440 | tf_op jit(solution)/shard_map/ppermute | solution.py:23
  184.9 15.8 %copy-start.17 = (bf16[512,512]{1,0:T(8,128)(2,1)S(1)}, bf16[512,512]{1,0:T(8,128)(2,1)}, u32[]{:S(2)}) copy-start(bf16[512,512]{1,0:T(8,128)(2,1)} %get-tuple-element.82.refs_0_.refs_2_) | copy-start | bytes 1572868
  184.9 15.8 %copy-start.24 = (s32[4]{0:T(128)S(1)}, s32[4]{0:T(128)}, u32[]{:S(2)}) copy-start(s32[4]{0:T(128)} %pad_add_fusion.s_ref) | copy-start | bytes 52
  198.3 11.3 %collective-permute-start.26 = (bf16[64,2048]{1,0:T(8,128)(2,1)}, bf16[64,2048]{1,0:T(8,128)(2,1)S(1)}, u32[]{:S(2)}, u32[]{:S(2)}) collective-permute-start(bf16[64,2048]{1,0:T(8,128)(2,1)} %tie.4.refs_2_.refs_3_), channel_id=1, source_target_pairs={{0,3},{1,0},{2,1},{3,2},{4,7},{5,4},{6,5},{7,6},{8,11},{9,8},{10,9... | collective-permute-start | bytes 786440 | tf_op jit(solution)/shard_map/ppermute | solution.py:23
  199.5 10.1 %collective-permute-start.27 = (bf16[64,2048]{1,0:T(8,128)(2,1)}, bf16[64,2048]{1,0:T(8,128)(2,1)S(1)}, u32[]{:S(2)}, u32[]{:S(2)}) collective-permute-start(bf16[64,2048]{1,0:T(8,128)(2,1)} %tie.4.refs_2_.refs_3_), channel_id=1, source_target_pairs={{0,2},{1,3},{2,0},{3,1},{4,6},{5,7},{6,4},{7,5},{8,10},{9,11},{10,... | collective-permute-start | bytes 786440 | tf_op jit(solution)/shard_map/ppermute | solution.py:23
  199.9 15.2 %collective-permute-start.28 = (bf16[64,2048]{1,0:T(8,128)(2,1)}, bf16[64,2048]{1,0:T(8,128)(2,1)S(1)}, u32[]{:S(2)}, u32[]{:S(2)}) collective-permute-start(bf16[64,2048]{1,0:T(8,128)(2,1)} %tie.4.refs_2_.refs_3_), channel_id=1, source_target_pairs={{0,1},{1,2},{2,3},{3,0},{4,5},{5,6},{6,7},{7,4},{8,9},{9,10},{10,1... | collective-permute-start | bytes 786440 | tf_op jit(solution)/shard_map/ppermute | solution.py:23
  221.8 3.0 collective-permute-start.29
  235.4 28.4 %collective-permute-start.30 = (bf16[2,256,512]{2,1,0:T(8,128)(2,1)}, bf16[2,256,512]{2,1,0:T(8,128)(2,1)S(1)}, u32[]{:S(2)}, u32[]{:S(2)}) collective-permute-start(bf16[2,256,512]{2,1,0:T(8,128)(2,1)} %get-tuple-element.90.refs_7_), channel_id=1, source_target_pairs={{4,0},{8,4},{12,8},{5,1},{9,5},{13,9},{6,2},{10,6},{14,10},{7,3},{... | collective-permute-start | bytes 1572872 | tf_op jit(solution)/shard_map/ppermute | solution.py:28
  236.7 28.0 %collective-permute-start.31 = (bf16[2,256,512]{2,1,0:T(8,128)(2,1)}, bf16[2,256,512]{2,1,0:T(8,128)(2,1)}, u32[]{:S(2)}, u32[]{:S(2)}) collective-permute-start(bf16[2,256,512]{2,1,0:T(8,128)(2,1)} %get-tuple-element.90.refs_7_), channel_id=1, source_target_pairs={{8,0},{12,4},{9,1},{13,5},{10,2},{14,6},{11,3},{15,7},{24,16},{28,... | collective-permute-start | bytes 1572872 | tf_op jit(solution)/shard_map/ppermute | solution.py:28
  238.0 27.5 %collective-permute-start.32 = (bf16[2,256,512]{2,1,0:T(8,128)(2,1)}, bf16[2,256,512]{2,1,0:T(8,128)(2,1)}, u32[]{:S(2)}, u32[]{:S(2)}) collective-permute-start(bf16[2,256,512]{2,1,0:T(8,128)(2,1)} %get-tuple-element.90.refs_7_), channel_id=1, source_target_pairs={{12,0},{13,1},{14,2},{15,3},{28,16},{29,17},{30,18},{31,19},{44,32... | collective-permute-start | bytes 1572872 | tf_op jit(solution)/shard_map/ppermute | solution.py:28
  289.4 4.4 %collective-permute-start.33 = (bf16[256,2048]{1,0:T(8,128)(2,1)}, bf16[256,2048]{1,0:T(8,128)(2,1)S(1)}, u32[]{:S(2)}, u32[]{:S(2)}) collective-permute-start(bf16[256,2048]{1,0:T(8,128)(2,1)} %copy-done.32), channel_id=1, source_target_pairs={{0,16},{16,0},{1,17},{17,1},{2,18},{18,2},{3,19},{19,3},{4,20},{20... | collective-permute-start | bytes 3145736 | tf_op jit(solution)/shard_map/ppermute | solution.py:34
  289.9 4.0 %collective-permute-start.34 = (bf16[256,2048]{1,0:T(8,128)(2,1)}, bf16[256,2048]{1,0:T(8,128)(2,1)S(1)}, u32[]{:S(2)}, u32[]{:S(2)}) collective-permute-start(bf16[256,2048]{1,0:T(8,128)(2,1)} %tie.6), channel_id=1, source_target_pairs={{0,16},{16,0},{1,17},{17,1},{2,18},{18,2},{3,19},{19,3},{4,20},{20... | collective-permute-start | bytes 3145736 | tf_op jit(solution)/shard_map/ppermute | solution.py:34
  290.8 1.4 collective-permute-start.38
  292.2 10.4 %collective-permute-start.39 = (f32[2,2048]{1,0:T(2,128)S(1)}, f32[2,2048]{1,0:T(2,128)S(1)}, u32[]{:S(2)}, u32[]{:S(2)}) collective-permute-start(f32[2,2048]{1,0:T(2,128)S(1)} %fusion.11), channel_id=1, source_target_pairs={{0,4},{4,0},{8,12},{12,8},{1,5},{5,1},{9,13},{13,9},{2,6},{6,2},{1... | collective-permute-start | bytes 49160 | tf_op jit(solution)/shard_map/ppermute | solution.py:1143
  300.8 18.0 %collective-permute-start.37 = (bf16[128,2048]{1,0:T(8,128)(2,1)}, bf16[128,2048]{1,0:T(8,128)(2,1)S(1)}, u32[]{:S(2)}, u32[]{:S(2)}) collective-permute-start(bf16[128,2048]{1,0:T(8,128)(2,1)} %get-tuple-element.110), channel_id=1, source_target_pairs={{0,3},{1,0},{2,1},{3,2},{4,7},{5,4},{6,5},{7,6},{8,11},{9,8},{10,9... | collective-permute-start | bytes 1572872 | tf_op jit(solution)/shard_map/ppermute | solution.py:23
  301.2 17.7 %collective-permute-start.36 = (bf16[128,2048]{1,0:T(8,128)(2,1)}, bf16[128,2048]{1,0:T(8,128)(2,1)S(1)}, u32[]{:S(2)}, u32[]{:S(2)}) collective-permute-start(bf16[128,2048]{1,0:T(8,128)(2,1)} %get-tuple-element.109), channel_id=1, source_target_pairs={{0,1},{1,2},{2,3},{3,0},{4,5},{5,6},{6,7},{7,4},{8,9},{9,10},{10,1... | collective-permute-start | bytes 1572872 | tf_op jit(solution)/shard_map/ppermute | solution.py:23
  302.3 22.9 %collective-permute-start.35 = (bf16[128,2048]{1,0:T(8,128)(2,1)}, bf16[128,2048]{1,0:T(8,128)(2,1)S(1)}, u32[]{:S(2)}, u32[]{:S(2)}) collective-permute-start(bf16[128,2048]{1,0:T(8,128)(2,1)} %get-tuple-element.108), channel_id=1, source_target_pairs={{0,2},{1,3},{2,0},{3,1},{4,6},{5,7},{6,4},{7,5},{8,10},{9,11},{10,... | collective-permute-start | bytes 1572872 | tf_op jit(solution)/shard_map/ppermute | solution.py:23
  302.7 8.2 %collective-permute-start.40 = (f32[2,2048]{1,0:T(2,128)S(1)}, f32[2,2048]{1,0:T(2,128)S(1)}, u32[]{:S(2)}, u32[]{:S(2)}) collective-permute-start(f32[2,2048]{1,0:T(2,128)S(1)} %fusion.29), channel_id=1, source_target_pairs={{0,12},{4,8},{8,4},{12,0},{1,13},{5,9},{9,5},{13,1},{2,14},{6,10},... | collective-permute-start | bytes 49160 | tf_op jit(solution)/shard_map/ppermute | solution.py:1143
  310.9 3.6 collective-permute-start.41
  314.5 4.3 %collective-permute-start.42 = (f32[2,2048]{1,0:T(2,128)S(1)}, f32[2,2048]{1,0:T(2,128)S(1)}, u32[]{:S(2)}, u32[]{:S(2)}) collective-permute-start(f32[2,2048]{1,0:T(2,128)S(1)} %add.188), channel_id=1, source_target_pairs={{0,96},{32,64},{64,32},{96,0},{1,97},{33,65},{65,33},{97,1},{2,98}... | collective-permute-start | bytes 49160 | tf_op jit(solution)/shard_map/ppermute | solution.py:1143
  326.7 31.8 %copy-start.41 = (bf16[144,2048]{1,0:T(8,128)(2,1)}, bf16[144,2048]{1,0:T(8,128)(2,1)S(1)}, u32[]{:S(2)}) copy-start(bf16[144,2048]{1,0:T(8,128)(2,1)S(1)} %maximum_maximum_fusion.refs_4_) | copy-start | bytes 1769476
  326.7 15.4 %collective-permute-start.43 = (bf16[144,2048]{1,0:T(8,128)(2,1)S(1)}, bf16[144,2048]{1,0:T(8,128)(2,1)S(1)}, u32[]{:S(2)}, u32[]{:S(2)}) collective-permute-start(bf16[144,2048]{1,0:T(8,128)(2,1)S(1)} %maximum_maximum_fusion.refs_4_), channel_id=1, source_target_pairs={{0,3},{1,0},{2,1},{3,2},{4,7},{5,4},{6,5},{7,6},{8,11},{9,8},{10,9... | collective-permute-start | bytes 1769480 | tf_op jit(solution)/shard_map/ppermute | solution.py:23
  329.1 14.6 %collective-permute-start.44 = (bf16[144,2048]{1,0:T(8,128)(2,1)S(1)}, bf16[144,2048]{1,0:T(8,128)(2,1)S(1)}, u32[]{:S(2)}, u32[]{:S(2)}) collective-permute-start(bf16[144,2048]{1,0:T(8,128)(2,1)S(1)} %maximum_maximum_fusion.refs_4_), channel_id=1, source_target_pairs={{0,2},{1,3},{2,0},{3,1},{4,6},{5,7},{6,4},{7,5},{8,10},{9,11},{10,... | collective-permute-start | bytes 1769480 | tf_op jit(solution)/shard_map/ppermute | solution.py:23
  329.5 28.9 %collective-permute-start.45 = (bf16[144,2048]{1,0:T(8,128)(2,1)S(1)}, bf16[144,2048]{1,0:T(8,128)(2,1)S(1)}, u32[]{:S(2)}, u32[]{:S(2)}) collective-permute-start(bf16[144,2048]{1,0:T(8,128)(2,1)S(1)} %maximum_maximum_fusion.refs_4_), channel_id=1, source_target_pairs={{0,1},{1,2},{2,3},{3,0},{4,5},{5,6},{6,7},{7,4},{8,9},{9,10},{10,1... | collective-permute-start | bytes 1769480 | tf_op jit(solution)/shard_map/ppermute | solution.py:23
  342.2 16.3 %copy-start.48 = (bf16[144,2048]{1,0:T(8,128)(2,1)}, bf16[144,2048]{1,0:T(8,128)(2,1)S(1)}, u32[]{:S(2)}) copy-start(bf16[144,2048]{1,0:T(8,128)(2,1)S(1)} %collective-permute-done.43.refs_5_) | copy-start | bytes 1769476
  378.1 2.4 collective-permute-start.46
  (48 other events, 177.2 us)
Sparse Core Ops, SparseCore 0:
  16.5 77.8 all-gather.2
  96.6 64.9 all-gather.4
  273.5 103.3 reduce-scatter.1

commit v7 on v6

--- a/solution.py
+++ b/solution.py
@@ -910,23 +910,32 @@
     rows = values.shape[0]
     block = rows // 4
 
-    def body(s_ref, v_ref, u_ref, g_ref, *refs):
-        def work(part):
-            out = u_ref[...] + norm_grad(v_ref[...], part, g_ref[...])
-            refs[4][...] = out
-            refs[5][...] = out.astype(BF)
-
-        each_part(refs[:4], work)
-
-    plain = plain_spec(block)
-    return call(
-        body,
-        (4,),
-        [plain, turned_spec(block), whole(gain)] + [whole(p) for p in parts],
+    def body(s_ref, v_ref, a_ref, b_ref, g_ref, *refs):
+        def work(span, above, part):
+            out = above + norm_grad(v_ref[span], part, g_ref[...])
+            refs[4][span] = out
+            refs[5][span] = out.astype(BF)
+
+        for k in (0, 1):
+
+            @pl.when(pl.program_id(0) == k)
+            def _(k=k):
+                work(slice(0, block), a_ref[...], refs[2 * k][...].astype(F32))
+                work(slice(block, 2 * block), b_ref[...], refs[2 * k + 1][...].astype(F32))
+
+    plain = pl.BlockSpec((2 * block, D), lambda i, s: (i, 0))
+    turned = [
+        pl.BlockSpec((block, D), lambda i, s, h=h: (lax.rem(2 * i + h + s[1], 4), 0))
+        for h in (0, 1)
+    ]
+    return call(
+        body,
+        (2,),
+        [plain, *turned, whole(gain)] + [whole(p) for p in parts],
         (plain, plain),
         (sds((rows, D), F32), sds((rows, D), BF)),
         scalars,
-        (values, upstream, gain, *parts),
+        (values, upstream, upstream, gain, *parts),
         name,
         deps=deps,
         stream=True,

time: 391 us -> 390 us (level)
  no operation moved by 1% of the time
where the time goes in v7:
time: 390 us; the launch traced here: 388 us
  waiting for transfers between devices  139 us (36%)
  Pallas kernels  118 us (30%)
  starting transfers between devices  64.3 us (16%)
  local copies, waits for them, and re-layouts  31.9 us (8%)
  between operations  15.8 us (4%)
  other arithmetic  13.3 us (3%)
  matrix products  5.79 us (1%)
    pallas_call x23, Pallas kernels, call(): pl.pallas_call(kernel, out_shape=shapes, grid_spec=pltpu.PrefetchScalarGr...  118 us
    ppermute x18, waiting for transfers between devices, shift(): return lax.ppermute(value, axis, [(i, (i + offset) % n) for i in range(n)])  67.2 us
    unnamed x124, local copies, waits for them, and re-layouts  27.8 us
    ppermute x6, waiting for transfers between devices, shift_open(): lax.ppermute(value, axis, [(i, i + offset) for i in range(n) if 0 <= i +...  23.3 us
    ppermute x18, starting transfers between devices, shift(): return lax.ppermute(value, axis, [(i, (i + offset) % n) for i in range(n)])  19.4 us
    ppermute x6, waiting for transfers between devices, hop(): return lax.ppermute(value, ('x', 'core', 'ctx'), pairs)  18.8 us
    ppermute x12, waiting for transfers between devices, swap(): return lax.ppermute(value, 'core', [(0, 1), (1, 0)])  12.1 us
    ppermute x5, starting transfers between devices, per_device(): gains = gains + lax.ppermute(gains, axis, list(enumerate(swapped)))  12.1 us
  transfers between devices with their start and end apart: 50, of which 35 were waited for; matrix products, arithmetic and copies ran while one was open for 5% of the time, Pallas kernels for 19%

profile of v7, /device:TPU:1, one launch (start us, length us, event | category | flops | bytes accessed | tf_op | source)
XLA Modules:
  0.0 388.0 jit_solution(14644471693508268831)
XLA Ops:
  7.8 2.6 split_attn.1
  13.9 2.5 stack_attn.1
  17.8 2.5 collective-permute-start.3
  22.8 3.2 collective-permute-done.3.refs_3_.refs_2_
  25.9 1.6 copy-done.9
  30.1 1.6 collective-permute-start.5
  33.6 2.1 collective-permute-start.7
  38.3 2.5 split_mlp.1
  43.1 5.2 %collective-permute-done.6.refs_3_.refs_2_ = bf16[4,2,64,768]{3,2,1,0:T(8,128)(2,1)} collective-permute-done((bf16[4,2,64,768]{3,2,1,0:T(8,128)(2,1)S(1)}, bf16[4,2,64,768]{3,2,1,0:T(8,128)(2,1)}, u32[]{:S(2)}, u32[]{:S(2)}) %collective-permute-start.6) | collective-permute-done | bytes 786464 | tf_op jit(solution)/shard_map/ppermute | solution.py:148
  48.3 9.1 %collective-permute-done.7.refs_4_.refs_3_ = bf16[4,2,64,768]{3,2,1,0:T(8,128)(2,1)} collective-permute-done((bf16[4,2,64,768]{3,2,1,0:T(8,128)(2,1)S(1)}, bf16[4,2,64,768]{3,2,1,0:T(8,128)(2,1)}, u32[]{:S(2)}, u32[]{:S(2)}) %collective-permute-start.7) | collective-permute-done | bytes 786464 | tf_op jit(solution)/shard_map/ppermute | solution.py:148
  57.4 1.5 copy-done.2
  58.9 5.6 %project_kv.1 = f32[512,768]{1,0:T(8,128)S(1)} custom-call(s32[4]{0:T(128)S(1)} %copy-done.23, bf16[256,2048]{1,0:T(8,128)(2,1)S(1)} %copy-done.2, bf16[256,2048]{1,0:T(8,128)(2,1)S(1)} %collective-permute-done.5.refs_1_.refs_4_.refs_10_, bf16[4,2,64,768]{3,2,1,0:T(8,128)(2,1)S(1)} %bitcast.45, ...), custom_call_target="tpu_custom_call" | custom-call | flops 1 | bytes 1 | tf_op jit(solution)/shard_map/project_kv/pallas_call | solution.py:61
  67.0 2.4 collective-permute-start.10
  69.3 4.1 %collective-permute-start.11 = (bf16[2,256,512]{2,1,0:T(8,128)(2,1)S(1)}, bf16[2,256,512]{2,1,0:T(8,128)(2,1)S(1)}, u32[]{:S(2)}, u32[]{:S(2)}) collective-permute-start(bf16[2,256,512]{2,1,0:T(8,128)(2,1)S(1)} %convolution_convert_fusion.refs_2_), channel_id=1, source_target_pairs={{0,8},{4,12},{1,9},{5,13},{2,10},{6,14},{3,11},{7,15},{16,24},{20,... | collective-permute-start | bytes 1572872 | tf_op jit(solution)/shard_map/ppermute | solution.py:28
  78.7 11.1 %collective-permute-done.10.refs_5_ = bf16[2,256,512]{2,1,0:T(8,128)(2,1)S(1)} collective-permute-done((bf16[2,256,512]{2,1,0:T(8,128)(2,1)S(1)}, bf16[2,256,512]{2,1,0:T(8,128)(2,1)S(1)}, u32[]{:S(2)}, u32[]{:S(2)}) %collective-permute-start.10) | collective-permute-done | bytes 524320 | tf_op jit(solution)/shard_map/ppermute | solution.py:28
  89.9 11.3 %collective-permute-done.11.refs_6_ = bf16[2,256,512]{2,1,0:T(8,128)(2,1)S(1)} collective-permute-done((bf16[2,256,512]{2,1,0:T(8,128)(2,1)S(1)}, bf16[2,256,512]{2,1,0:T(8,128)(2,1)S(1)}, u32[]{:S(2)}, u32[]{:S(2)}) %collective-permute-start.11) | collective-permute-done | bytes 524320 | tf_op jit(solution)/shard_map/ppermute | solution.py:28
  102.2 12.9 %retain.1 = (bf16[256,2048]{1,0:T(8,128)(2,1)}, bf16[256,2048]{1,0:T(8,128)(2,1)}, bf16[512,256]{1,0:T(8,128)(2,1)}, bf16[2,256,512]{2,1,0:T(8,128)(2,1)}, bf16[...) custom-call(s32[6]{0:T(128)} %concatenate.24.s_ref, ...), custom_call_target="tpu_custom_call" | custom-call | flops 1 | bytes 1 | tf_op jit(solution)/shard_map/retain/pallas_call | solution.py:61
  115.9 2.5 collective-permute-done.13
  119.8 2.9 collective-permute-start.16
  122.7 1.7 collective-permute-start.14
  124.4 9.1 %collective-permute-done.16 = bf16[64,2048]{1,0:T(8,128)(2,1)S(1)} collective-permute-done((bf16[64,2048]{1,0:T(8,128)(2,1)S(1)}, bf16[64,2048]{1,0:T(8,128)(2,1)S(1)}, u32[]{:S(2)}, u32[]{:S(2)}) %collective-permute-start.16) | collective-permute-done | bytes 262176 | tf_op jit(solution)/shard_map/ppermute | solution.py:23
  133.5 2.3 collective-permute-done.14
  140.2 2.2 collective-permute-start.21
  143.6 2.6 collective-permute-done.18.refs_4_
  146.2 7.6 %collective-permute-done.19.refs_5_ = bf16[64,2048]{1,0:T(8,128)(2,1)S(1)} collective-permute-done((bf16[64,2048]{1,0:T(8,128)(2,1)S(1)}, bf16[64,2048]{1,0:T(8,128)(2,1)S(1)}, u32[]{:S(2)}, u32[]{:S(2)}) %collective-permute-start.19) | collective-permute-done | bytes 262176 | tf_op jit(solution)/shard_map/ppermute | solution.py:23
  155.1 1.4 copy-done.12
  159.3 2.2 all-gather.5.cloned.1.call-done
  161.6 14.3 %mlp.1 = (bf16[256,2048]{1,0:T(8,128)(2,1)}, bf16[256,2048]{1,0:T(8,128)(2,1)}, f32[8,2048]{1,0:T(8,128)}, bf16[512,1024]{1,0:T(8,128)(2,1)}, bf16[512,512]{1,0:T(8,128)(2,1)}) custom-call(s32[4]{0:T(128)} %pad_add_fusion.s_ref, bf16[256,2048]{1,0:T(8,128)(2,1)} %copy-done.15, bf16[256,2048]{1,0:T(8,128)(2,1)} %collective-permute-done.20.refs_1_, ...), custom_call_target="tpu_custom_call" | custom-call | flops 1 | bytes 1 | tf_op jit(solution)/shard_map/mlp/pallas_call | solution.py:61
  176.6 2.5 collective-permute-done.22
  180.5 2.7 collective-permute-start.25
  183.2 1.7 collective-permute-start.23
  184.9 6.9 %weight_mlp.1 = (bf16[4,4,2,64,3584]{4,3,2,1,0:T(8,128)(2,1)}, f32[8,128]{1,0:T(8,128)}) custom-call(s32[4]{0:T(128)} %pad_add_fusion.s_ref, bf16[256,2048]{1,0:T(8,128)(2,1)} %copy-done.15, bf16[256,2048]{1,0:T(8,128)(2,1)} %collective-permute-done.20.refs_1_, bf16[512,1024]{1,0:T(8,128)(2,1)} %get-tuple-element.80.refs_2_), custom_call_target="tpu_custom_call" | custom-call | flops 1 | bytes 1 | tf_op jit(solution)/shard_map/weight_mlp/pallas_call | solution.py:61
  191.8 2.2 collective-permute-done.25
  194.0 2.4 collective-permute-done.23
  196.4 1.9 add_convert_fusion.1.refs_0_
  200.7 2.8 copy-done.7
  204.5 2.8 project_down.1
  209.6 5.4 %collective-permute-done.28.refs_7_ = bf16[64,2048]{1,0:T(8,128)(2,1)S(1)} collective-permute-done((bf16[64,2048]{1,0:T(8,128)(2,1)}, bf16[64,2048]{1,0:T(8,128)(2,1)S(1)}, u32[]{:S(2)}, u32[]{:S(2)}) %collective-permute-start.28) | collective-permute-done | bytes 262176 | tf_op jit(solution)/shard_map/ppermute | solution.py:23
  215.7 5.3 %second_back.1 = (f32[256,2048]{1,0:T(8,128)}, bf16[256,2048]{1,0:T(8,128)(2,1)}) custom-call(s32[4]{0:T(128)} %pad_add_fusion.s_ref, f32[256,2048]{1,0:T(8,128)} %copy-done.12, f32[256,2048]{1,0:T(8,128)} %refs_2_.3, f32[256,2048]{1,0:T(8,128)} %refs_2_.3, f32[1,2048]{1,0:T(1,128)} %bitcast.47, bf16[64,2048]{1,0:T(8,128)(2,1)} %tie.4.refs_2_.refs_4_, ...), custom_call_target="tpu_custom_call" | custom-call | flops 1 | bytes 1 | tf_op jit(solution)/shard_map/second_back/pallas_call | solution.py:61
  222.5 1.5 collective-permute-done.29.refs_1_
  225.0 9.6 %back_gate.1 = (bf16[512,512]{1,0:T(8,128)(2,1)}, bf16[512,512]{1,0:T(8,128)(2,1)}, bf16[2,256,512]{2,1,0:T(8,128)(2,1)}) custom-call(s32[4]{0:T(128)} %pad_add_fusion.s_ref, bf16[256,2048]{1,0:T(8,128)(2,1)} %get-tuple-element.85.refs_0_, bf16[256,2048]{1,0:T(8,128)(2,1)} %copy-done.36, bf16[4,4,2,64,1280]{4,3,2,1,0:T(8,128)(2,1)} %bitcast.37, ...), custom_call_target="tpu_custom_call" | custom-call | flops 1 | bytes 1 | tf_op jit(solution)/shard_map/back_gate/pallas_call | solution.py:61
  237.2 1.5 collective-permute-start.32
  242.6 7.2 %weight_og.1 = (bf16[4,4,2,64,3584]{4,3,2,1,0:T(8,128)(2,1)}, f32[8,128]{1,0:T(8,128)}) custom-call(s32[4]{0:T(128)} %pad_add_fusion.s_ref, bf16[256,2048]{1,0:T(8,128)(2,1)} %get-tuple-element.85.refs_0_, bf16[256,2048]{1,0:T(8,128)(2,1)} %copy-done.36, bf16[512,512]{1,0:T(8,128)(2,1)} %get-tuple-element.94.refs_2_, ...), custom_call_target="tpu_custom_call", output_to_operand_aliasing={{0}: (7, {})} | custom-call | flops 1 | bytes 1 | tf_op jit(solution)/shard_map/weight_og/pallas_call | solution.py:61
  249.8 5.6 %weight_down.1 = (bf16[4,4,2,64,3584]{4,3,2,1,0:T(8,128)(2,1)}, f32[8,128]{1,0:T(8,128)}) custom-call(s32[4]{0:T(128)} %pad_add_fusion.s_ref, bf16[256,2048]{1,0:T(8,128)(2,1)} %copy-done.11, bf16[256,2048]{1,0:T(8,128)(2,1)} %copy-done.37, bf16[512,512]{1,0:T(8,128)(2,1)} %get-tuple-element.82.refs_0_.refs_2_, ...), custom_call_target="tpu_custom_call", output_to_operand_aliasing={{0}: (4, {})} | custom-call | flops 1 | bytes 1 | tf_op jit(solution)/shard_map/weight_down/pallas_call | solution.py:61
  255.4 5.2 %weight_query.1 = (bf16[4,4,2,64,3584]{4,3,2,1,0:T(8,128)(2,1)}, f32[8,128]{1,0:T(8,128)}) custom-call(s32[4]{0:T(128)} %pad_add_fusion.s_ref, bf16[256,2048]{1,0:T(8,128)(2,1)} %copy-done.1, bf16[256,2048]{1,0:T(8,128)(2,1)} %copy-done.4, bf16[512,256]{1,0:T(8,128)(2,1)} %pad_maximum_fusion.1.refs_2_.refs_7_, ...), custom_call_target="tpu_custom_call", output_to_operand_aliasing={{0}: (4, {})} | custom-call | flops 1 | bytes 1 | tf_op jit(solution)/shard_map/weight_query/pallas_call | solution.py:61
  264.7 7.8 %weight_last.1 = (bf16[4,4,2,64,3584]{4,3,2,1,0:T(8,128)(2,1)}, f32[8,128]{1,0:T(8,128)}, bf16[512,768]{1,0:T(8,128)(2,1)}) custom-call(s32[4]{0:T(128)} %pad_add_fusion.s_ref, bf16[256,2048]{1,0:T(8,128)(2,1)} %copy-done.1, bf16[256,2048]{1,0:T(8,128)(2,1)} %copy-done.4, bf16[2,256,512]{2,1,0:T(8,128)(2,1)} %tie.5.refs_2_, ...), custom_call_target="tpu_custom_call", output_to_operand_aliasing={{0}: (14, {})} | custom-call | flops 1 | bytes 1 | tf_op jit(solution)/shard_map/weight_last/pallas_call | solution.py:61
  274.1 2.5 copy-done
  278.8 7.5 %back_attn.1 = (f32[256,2048]{1,0:T(8,128)S(1)}, bf16[256,2048]{1,0:T(8,128)(2,1)S(1)}, f32[8,2048]{1,0:T(8,128)S(1)}) custom-call(s32[4]{0:T(128)S(1)} %copy-done.25, bf16[512,768]{1,0:T(8,128)(2,1)S(1)} %copy-done.21, bf16[4,2,64,768]{3,2,1,0:T(8,128)(2,1)S(1)} %bitcast.46, bf16[4,2,64,768]{3,2,1,0:T(8,128)(2,1)} %collective-permute-done.6.refs_3_.refs_2_, ...), custom_call_target="tpu_custom_call" | custom-call | flops 1 | bytes 1 | tf_op jit(solution)/shard_map/back_attn/pallas_call | solution.py:61
  291.4 1.5 collective-permute-start.39
  294.3 5.7 %third_blocks.1 = (bf16[128,2048]{1,0:T(8,128)(2,1)}, bf16[128,2048]{1,0:T(8,128)(2,1)}, bf16[128,2048]{1,0:T(8,128)(2,1)}, bf16[128,2048]{1,0:T(8,128)(2,1)}) custom-call(s32[4]{0:T(128)} %pad_add_fusion.s_ref, f32[256,2048]{1,0:T(8,128)} %copy-done.19, bf16[256,2048]{1,0:T(8,128)(2,1)} %copy-done.44, f32[256,2048]{1,0:T(8,128)} %copy-done.18, ...), custom_call_target="tpu_custom_call" | custom-call | flops 1 | bytes 1 | tf_op jit(solution)/shard_map/third_blocks/pallas_call | solution.py:61
  301.9 6.3 %collective-permute-start.40 = (f32[2,2048]{1,0:T(2,128)S(1)}, f32[2,2048]{1,0:T(2,128)S(1)}, u32[]{:S(2)}, u32[]{:S(2)}) collective-permute-start(f32[2,2048]{1,0:T(2,128)S(1)} %fusion.29), channel_id=1, source_target_pairs={{0,12},{4,8},{8,4},{12,0},{1,13},{5,9},{9,5},{13,1},{2,14},{6,10},... | collective-permute-start | bytes 49160 | tf_op jit(solution)/shard_map/ppermute | solution.py:1152
  308.2 2.0 collective-permute-done.40
  311.6 2.2 collective-permute-done.41
  313.8 2.4 collective-permute-start.42
  316.3 1.8 collective-permute-done.42
  318.2 6.2 %collective-permute-done.35 = bf16[128,2048]{1,0:T(8,128)(2,1)S(1)} collective-permute-done((bf16[128,2048]{1,0:T(8,128)(2,1)}, bf16[128,2048]{1,0:T(8,128)(2,1)S(1)}, u32[]{:S(2)}, u32[]{:S(2)}) %collective-permute-start.35) | collective-permute-done | bytes 524320 | tf_op jit(solution)/shard_map/ppermute | solution.py:23
  325.9 2.4 collective-permute-start.43
  329.5 12.0 %collective-permute-done.43.refs_5_ = bf16[144,2048]{1,0:T(8,128)(2,1)S(1)} collective-permute-done((bf16[144,2048]{1,0:T(8,128)(2,1)S(1)}, bf16[144,2048]{1,0:T(8,128)(2,1)S(1)}, u32[]{:S(2)}, u32[]{:S(2)}) %collective-permute-start.43) | collective-permute-done | bytes 589856 | tf_op jit(solution)/shard_map/ppermute | solution.py:23
  341.5 1.4 collective-permute-done.44.refs_6_
  342.9 14.8 %collective-permute-done.45.refs_7_ = bf16[144,2048]{1,0:T(8,128)(2,1)S(1)} collective-permute-done((bf16[144,2048]{1,0:T(8,128)(2,1)S(1)}, bf16[144,2048]{1,0:T(8,128)(2,1)S(1)}, u32[]{:S(2)}, u32[]{:S(2)}) %collective-permute-start.45) | collective-permute-done | bytes 589856 | tf_op jit(solution)/shard_map/ppermute | solution.py:23
  358.5 7.4 %leave_rows.1 = (f32[256,2048]{1,0:T(8,128)}, f32[256,2048]{1,0:T(8,128)}) custom-call(s32[4]{0:T(128)} %pad_add_fusion.s_ref, f32[256,2048]{1,0:T(8,128)} %copy-done.12, f32[256,2048]{1,0:T(8,128)} %refs_1_.7, f32[256,2048]{1,0:T(8,128)} %get-tuple-element.84.refs_2_, f32[1,2048]{1,0:T(1,128)} %bitcast.49, bf16[144,2048]{1,0:T(8,128)(2,1)} %copy-done.41, ...), custom_call_target="tpu_custom_call" | custom-call | flops 1 | bytes 1 | tf_op jit(solution)/shard_map/leave_rows/pallas_call | solution.py:61
  368.0 7.9 %reduce-scatter.2.cloned.1.call-done.refs_0_ = bf16[128,3584]{1,0:T(8,128)(2,1)} async-done(((bf16[2048,3584]{1,0:T(8,128)(2,1)}), bf16[128,3584]{1,0:T(8,128)(2,1)}) %reduce-scatter.2.cloned.1.call-update) | async-done | bytes 917520 | tf_op jit(solution)/shard_map/reduce_scatter | solution.py:1133
  378.2 1.4 collective-permute-done.46.refs_1_
  379.6 1.8 join_heads.1
  (233 shorter events, 79.4 us)
Async XLA Ops:
  7.2 94.1 %all-gather.3.cloned.1.call-start = ((), (), s32[]{:S(2)}) async-start(), calls=%async_computation.1 | async-start | bytes 5570560 | tf_op jit(solution)/shard_map/all_gather | solution.py:1018
  10.4 2.8 collective-permute-start.1
  16.4 15.3 %copy-start.28 = (bf16[128,768]{1,0:T(8,128)(2,1)S(1)}, bf16[128,768]{1,0:T(8,128)(2,1)}, u32[]{:S(2)}) copy-start(bf16[128,768]{1,0:T(8,128)(2,1)} %get-tuple-element.70.refs_0_) | copy-start | bytes 589828
  16.4 145.2 %all-gather.5.cloned.1.call-start = ((), (), s32[]{:S(2)}) async-start(), calls=%async_computation.2 | async-start | bytes 6684672 | tf_op jit(solution)/shard_map/all_gather | solution.py:1053
  16.4 6.3 %collective-permute-start.2 = (bf16[128,768]{1,0:T(8,128)(2,1)}, bf16[128,768]{1,0:T(8,128)(2,1)S(1)}, u32[]{:S(2)}, u32[]{:S(2)}) collective-permute-start(bf16[128,768]{1,0:T(8,128)(2,1)} %get-tuple-element.70.refs_0_), channel_id=1, source_target_pairs={{0,4},{4,8},{8,12},{12,0},{16,48},{20,52},{24,56},{28,60},{32,36},... | collective-permute-start | bytes 589832 | tf_op jit(solution)/shard_map/ppermute | solution.py:148
  17.8 8.1 %collective-permute-start.3 = (bf16[128,768]{1,0:T(8,128)(2,1)}, bf16[128,768]{1,0:T(8,128)(2,1)S(1)}, u32[]{:S(2)}, u32[]{:S(2)}) collective-permute-start(bf16[128,768]{1,0:T(8,128)(2,1)} %get-tuple-element.70.refs_0_), channel_id=1, source_target_pairs={{0,8},{4,12},{8,0},{12,4},{16,80},{20,84},{24,88},{28,92},{32,40},... | collective-permute-start | bytes 589832 | tf_op jit(solution)/shard_map/ppermute | solution.py:148
  20.3 5.7 %collective-permute-start.4 = (bf16[128,768]{1,0:T(8,128)(2,1)}, bf16[128,768]{1,0:T(8,128)(2,1)S(1)}, u32[]{:S(2)}, u32[]{:S(2)}) collective-permute-start(bf16[128,768]{1,0:T(8,128)(2,1)} %get-tuple-element.70.refs_0_), channel_id=1, source_target_pairs={{0,12},{4,0},{8,4},{12,8},{16,112},{20,116},{24,120},{28,124},{32,... | collective-permute-start | bytes 589832 | tf_op jit(solution)/shard_map/ppermute | solution.py:148
  30.1 27.4 %copy-start.23 = (s32[4]{0:T(128)S(1)}, s32[4]{0:T(128)}, u32[]{:S(2)}) copy-start(s32[4]{0:T(128)} %pad_add_fusion.s_ref) | copy-start | bytes 52
  30.1 27.3 %collective-permute-start.5 = (bf16[256,2048]{1,0:T(8,128)(2,1)S(1)}, bf16[256,2048]{1,0:T(8,128)(2,1)S(1)}, u32[]{:S(2)}, u32[]{:S(2)}) collective-permute-start(bf16[256,2048]{1,0:T(8,128)(2,1)S(1)} %enter_rows.1.refs_3_.refs_0_.refs_9_), channel_id=1, source_target_pairs={{0,16},{16,0},{1,17},{17,1},{2,18},{18,2},{3,19},{19,3},{4,20},{20... | collective-permute-start | bytes 3145736 | tf_op jit(solution)/shard_map/ppermute | solution.py:34
  32.3 16.0 %collective-permute-start.6 = (bf16[4,2,64,768]{3,2,1,0:T(8,128)(2,1)S(1)}, bf16[4,2,64,768]{3,2,1,0:T(8,128)(2,1)}, u32[]{:S(2)}, u32[]{:S(2)}) collective-permute-start(bf16[4,2,64,768]{3,2,1,0:T(8,128)(2,1)S(1)} %bitcast.42), channel_id=1, source_target_pairs={{0,32},{4,36},{8,40},{12,44},{16,20},{20,24},{24,28},{28,16},{32,6... | collective-permute-start | bytes 2359304 | tf_op jit(solution)/shard_map/ppermute | solution.py:148
  33.6 23.8 %collective-permute-start.7 = (bf16[4,2,64,768]{3,2,1,0:T(8,128)(2,1)S(1)}, bf16[4,2,64,768]{3,2,1,0:T(8,128)(2,1)}, u32[]{:S(2)}, u32[]{:S(2)}) collective-permute-start(bf16[4,2,64,768]{3,2,1,0:T(8,128)(2,1)S(1)} %bitcast.43), channel_id=1, source_target_pairs={{0,64},{4,68},{8,72},{12,76},{16,24},{20,28},{24,16},{28,20},{32,9... | collective-permute-start | bytes 2359304 | tf_op jit(solution)/shard_map/ppermute | solution.py:148
  35.7 21.7 %collective-permute-start.8 = (bf16[4,2,64,768]{3,2,1,0:T(8,128)(2,1)S(1)}, bf16[4,2,64,768]{3,2,1,0:T(8,128)(2,1)}, u32[]{:S(2)}, u32[]{:S(2)}) collective-permute-start(bf16[4,2,64,768]{3,2,1,0:T(8,128)(2,1)S(1)} %bitcast.44), channel_id=1, source_target_pairs={{0,96},{4,100},{8,104},{12,108},{16,28},{20,16},{24,20},{28,24},{3... | collective-permute-start | bytes 2359304 | tf_op jit(solution)/shard_map/ppermute | solution.py:148
  40.8 2.4 collective-permute-start.9
  42.4 22.4 %copy-start.38 = (f32[256,128]{1,0:T(8,128)}, f32[256,128]{1,0:T(8,128)S(1)}, u32[]{:S(2)}) copy-start(f32[256,128]{1,0:T(8,128)S(1)} %get-tuple-element.140.refs_9_.refs_11_) | copy-start | bytes 393220
  42.4 22.4 %copy-start.42 = (f32[256,128]{1,0:T(8,128)}, f32[256,128]{1,0:T(8,128)S(1)}, u32[]{:S(2)}) copy-start(f32[256,128]{1,0:T(8,128)S(1)} %get-tuple-element.139.refs_10_.refs_12_) | copy-start | bytes 393220
  64.9 50.2 %copy-start.40 = (bf16[2,256,256]{2,1,0:T(8,128)(2,1)}, bf16[2,256,256]{2,1,0:T(8,128)(2,1)S(1)}, u32[]{:S(2)}) copy-start(bf16[2,256,256]{2,1,0:T(8,128)(2,1)S(1)} %multiply_convert_fusion.refs_7_) | copy-start | bytes 786436
  66.9 309.0 %reduce-scatter.2.cloned.1.call-start = ((), (), s32[]{:S(2)}) async-start(), calls=%async_computation.3 | async-start | bytes 15597568 | tf_op jit(solution)/shard_map/reduce_scatter | solution.py:1133
  67.0 22.9 %collective-permute-start.10 = (bf16[2,256,512]{2,1,0:T(8,128)(2,1)S(1)}, bf16[2,256,512]{2,1,0:T(8,128)(2,1)S(1)}, u32[]{:S(2)}, u32[]{:S(2)}) collective-permute-start(bf16[2,256,512]{2,1,0:T(8,128)(2,1)S(1)} %convolution_convert_fusion.refs_2_), channel_id=1, source_target_pairs={{0,4},{4,8},{8,12},{1,5},{5,9},{9,13},{2,6},{6,10},{10,14},{3,7},{... | collective-permute-start | bytes 1572872 | tf_op jit(solution)/shard_map/ppermute | solution.py:28
  69.3 31.8 %collective-permute-start.11 = (bf16[2,256,512]{2,1,0:T(8,128)(2,1)S(1)}, bf16[2,256,512]{2,1,0:T(8,128)(2,1)S(1)}, u32[]{:S(2)}, u32[]{:S(2)}) collective-permute-start(bf16[2,256,512]{2,1,0:T(8,128)(2,1)S(1)} %convolution_convert_fusion.refs_2_), channel_id=1, source_target_pairs={{0,8},{4,12},{1,9},{5,13},{2,10},{6,14},{3,11},{7,15},{16,24},{20,... | collective-permute-start | bytes 1572872 | tf_op jit(solution)/shard_map/ppermute | solution.py:28
  73.5 27.8 %collective-permute-start.12 = (bf16[2,256,512]{2,1,0:T(8,128)(2,1)S(1)}, bf16[2,256,512]{2,1,0:T(8,128)(2,1)S(1)}, u32[]{:S(2)}, u32[]{:S(2)}) collective-permute-start(bf16[2,256,512]{2,1,0:T(8,128)(2,1)S(1)} %convolution_convert_fusion.refs_2_), channel_id=1, source_target_pairs={{0,12},{1,13},{2,14},{3,15},{16,28},{17,29},{18,30},{19,31},{32,44... | collective-permute-start | bytes 1572872 | tf_op jit(solution)/shard_map/ppermute | solution.py:28
  74.8 2.0 collective-permute-start
  115.1 24.3 %copy-start.5 = (bf16[256,2048]{1,0:T(8,128)(2,1)S(1)}, bf16[256,2048]{1,0:T(8,128)(2,1)}, u32[]{:S(2)}) copy-start(bf16[256,2048]{1,0:T(8,128)(2,1)} %copy-done.4) | copy-start | bytes 3145732
  115.1 24.3 %copy-start.8 = (f32[256,2048]{1,0:T(8,128)S(1)}, f32[256,2048]{1,0:T(8,128)}, u32[]{:S(2)}) copy-start(f32[256,2048]{1,0:T(8,128)} %refs_2_.3) | copy-start | bytes 6291460
  115.1 3.3 collective-permute-start.13
  119.8 13.7 %collective-permute-start.16 = (bf16[64,2048]{1,0:T(8,128)(2,1)S(1)}, bf16[64,2048]{1,0:T(8,128)(2,1)S(1)}, u32[]{:S(2)}, u32[]{:S(2)}) collective-permute-start(bf16[64,2048]{1,0:T(8,128)(2,1)S(1)} %get-tuple-element.128), channel_id=1, source_target_pairs={{0,3},{1,0},{2,1},{3,2},{4,7},{5,4},{6,5},{7,6},{8,11},{9,8},{10,9... | collective-permute-start | bytes 786440 | tf_op jit(solution)/shard_map/ppermute | solution.py:23
  122.7 10.8 %collective-permute-start.15 = (bf16[64,2048]{1,0:T(8,128)(2,1)S(1)}, bf16[64,2048]{1,0:T(8,128)(2,1)S(1)}, u32[]{:S(2)}, u32[]{:S(2)}) collective-permute-start(bf16[64,2048]{1,0:T(8,128)(2,1)S(1)} %get-tuple-element.129), channel_id=1, source_target_pairs={{0,1},{1,2},{2,3},{3,0},{4,5},{5,6},{6,7},{7,4},{8,9},{9,10},{10,1... | collective-permute-start | bytes 786440 | tf_op jit(solution)/shard_map/ppermute | solution.py:23
  122.7 13.0 %collective-permute-start.14 = (bf16[64,2048]{1,0:T(8,128)(2,1)S(1)}, bf16[64,2048]{1,0:T(8,128)(2,1)S(1)}, u32[]{:S(2)}, u32[]{:S(2)}) collective-permute-start(bf16[64,2048]{1,0:T(8,128)(2,1)S(1)} %get-tuple-element.127), channel_id=1, source_target_pairs={{0,2},{1,3},{2,0},{3,1},{4,6},{5,7},{6,4},{7,5},{8,10},{9,11},{10,... | collective-permute-start | bytes 786440 | tf_op jit(solution)/shard_map/ppermute | solution.py:23
  136.9 16.8 %copy-start.10 = (f32[256,2048]{1,0:T(8,128)S(1)}, f32[256,2048]{1,0:T(8,128)}, u32[]{:S(2)}) copy-start(f32[256,2048]{1,0:T(8,128)} %refs_1_.7) | copy-start | bytes 6291460
  136.9 16.8 %copy-start.29 = (f32[2048]{0:T(1024)S(1)}, f32[2048]{0:T(1024)}, u32[]{:S(2)}) copy-start(f32[2048]{0:T(1024)} %param.17) | copy-start | bytes 24580
  136.9 6.7 %collective-permute-start.17 = (bf16[64,2048]{1,0:T(8,128)(2,1)S(1)}, bf16[64,2048]{1,0:T(8,128)(2,1)S(1)}, u32[]{:S(2)}, u32[]{:S(2)}) collective-permute-start(bf16[64,2048]{1,0:T(8,128)(2,1)S(1)} %add_convert_fusion.6.refs_2_), channel_id=1, source_target_pairs={{0,3},{1,0},{2,1},{3,2},{4,7},{5,4},{6,5},{7,6},{8,11},{9,8},{10,9... | collective-permute-start | bytes 786440 | tf_op jit(solution)/shard_map/ppermute | solution.py:23
  138.3 7.9 %collective-permute-start.18 = (bf16[64,2048]{1,0:T(8,128)(2,1)S(1)}, bf16[64,2048]{1,0:T(8,128)(2,1)S(1)}, u32[]{:S(2)}, u32[]{:S(2)}) collective-permute-start(bf16[64,2048]{1,0:T(8,128)(2,1)S(1)} %add_convert_fusion.6.refs_2_), channel_id=1, source_target_pairs={{0,2},{1,3},{2,0},{3,1},{4,6},{5,7},{6,4},{7,5},{8,10},{9,11},{10,... | collective-permute-start | bytes 786440 | tf_op jit(solution)/shard_map/ppermute | solution.py:23
  138.7 15.1 %collective-permute-start.19 = (bf16[64,2048]{1,0:T(8,128)(2,1)S(1)}, bf16[64,2048]{1,0:T(8,128)(2,1)S(1)}, u32[]{:S(2)}, u32[]{:S(2)}) collective-permute-start(bf16[64,2048]{1,0:T(8,128)(2,1)S(1)} %add_convert_fusion.6.refs_2_), channel_id=1, source_target_pairs={{0,1},{1,2},{2,3},{3,0},{4,5},{5,6},{6,7},{7,4},{8,9},{9,10},{10,1... | collective-permute-start | bytes 786440 | tf_op jit(solution)/shard_map/ppermute | solution.py:23
  140.2 21.4 %copy-start.11 = (bf16[256,2048]{1,0:T(8,128)(2,1)}, bf16[256,2048]{1,0:T(8,128)(2,1)S(1)}, u32[]{:S(2)}) copy-start(bf16[256,2048]{1,0:T(8,128)(2,1)S(1)} %low_rows.1.refs_2_.refs_0_) | copy-start | bytes 3145732
  140.2 16.8 %collective-permute-start.21 = (bf16[256,2048]{1,0:T(8,128)(2,1)S(1)}, bf16[256,2048]{1,0:T(8,128)(2,1)S(1)}, u32[]{:S(2)}, u32[]{:S(2)}) collective-permute-start(bf16[256,2048]{1,0:T(8,128)(2,1)S(1)} %low_rows.1.refs_2_.refs_0_), channel_id=1, source_target_pairs={{0,16},{16,0},{1,17},{17,1},{2,18},{18,2},{3,19},{19,3},{4,20},{20... | collective-permute-start | bytes 3145736 | tf_op jit(solution)/shard_map/ppermute | solution.py:34
  156.5 2.8 collective-permute-start.20
  175.9 3.3 collective-permute-start.22
  180.5 13.5 %collective-permute-start.25 = (bf16[64,2048]{1,0:T(8,128)(2,1)S(1)}, bf16[64,2048]{1,0:T(8,128)(2,1)S(1)}, u32[]{:S(2)}, u32[]{:S(2)}) collective-permute-start(bf16[64,2048]{1,0:T(8,128)(2,1)S(1)} %get-tuple-element.125), channel_id=1, source_target_pairs={{0,3},{1,0},{2,1},{3,2},{4,7},{5,4},{6,5},{7,6},{8,11},{9,8},{10,9... | collective-permute-start | bytes 786440 | tf_op jit(solution)/shard_map/ppermute | solution.py:23
  183.2 10.8 %collective-permute-start.24 = (bf16[64,2048]{1,0:T(8,128)(2,1)S(1)}, bf16[64,2048]{1,0:T(8,128)(2,1)S(1)}, u32[]{:S(2)}, u32[]{:S(2)}) collective-permute-start(bf16[64,2048]{1,0:T(8,128)(2,1)S(1)} %get-tuple-element.126), channel_id=1, source_target_pairs={{0,1},{1,2},{2,3},{3,0},{4,5},{5,6},{6,7},{7,4},{8,9},{9,10},{10,1... | collective-permute-start | bytes 786440 | tf_op jit(solution)/shard_map/ppermute | solution.py:23
  183.2 13.2 %collective-permute-start.23 = (bf16[64,2048]{1,0:T(8,128)(2,1)S(1)}, bf16[64,2048]{1,0:T(8,128)(2,1)}, u32[]{:S(2)}, u32[]{:S(2)}) collective-permute-start(bf16[64,2048]{1,0:T(8,128)(2,1)S(1)} %get-tuple-element.124), channel_id=1, source_target_pairs={{0,2},{1,3},{2,0},{3,1},{4,6},{5,7},{6,4},{7,5},{8,10},{9,11},{10,... | collective-permute-start | bytes 786440 | tf_op jit(solution)/shard_map/ppermute | solution.py:23
  184.9 15.8 %copy-start.17 = (bf16[512,512]{1,0:T(8,128)(2,1)S(1)}, bf16[512,512]{1,0:T(8,128)(2,1)}, u32[]{:S(2)}) copy-start(bf16[512,512]{1,0:T(8,128)(2,1)} %get-tuple-element.82.refs_0_.refs_2_) | copy-start | bytes 1572868
  184.9 15.8 %copy-start.24 = (s32[4]{0:T(128)S(1)}, s32[4]{0:T(128)}, u32[]{:S(2)}) copy-start(s32[4]{0:T(128)} %pad_add_fusion.s_ref) | copy-start | bytes 52
  198.3 11.3 %collective-permute-start.26 = (bf16[64,2048]{1,0:T(8,128)(2,1)}, bf16[64,2048]{1,0:T(8,128)(2,1)S(1)}, u32[]{:S(2)}, u32[]{:S(2)}) collective-permute-start(bf16[64,2048]{1,0:T(8,128)(2,1)} %tie.4.refs_2_.refs_4_), channel_id=1, source_target_pairs={{0,3},{1,0},{2,1},{3,2},{4,7},{5,4},{6,5},{7,6},{8,11},{9,8},{10,9... | collective-permute-start | bytes 786440 | tf_op jit(solution)/shard_map/ppermute | solution.py:23
  199.5 10.1 %collective-permute-start.27 = (bf16[64,2048]{1,0:T(8,128)(2,1)}, bf16[64,2048]{1,0:T(8,128)(2,1)S(1)}, u32[]{:S(2)}, u32[]{:S(2)}) collective-permute-start(bf16[64,2048]{1,0:T(8,128)(2,1)} %tie.4.refs_2_.refs_4_), channel_id=1, source_target_pairs={{0,2},{1,3},{2,0},{3,1},{4,6},{5,7},{6,4},{7,5},{8,10},{9,11},{10,... | collective-permute-start | bytes 786440 | tf_op jit(solution)/shard_map/ppermute | solution.py:23
  199.9 15.2 %collective-permute-start.28 = (bf16[64,2048]{1,0:T(8,128)(2,1)}, bf16[64,2048]{1,0:T(8,128)(2,1)S(1)}, u32[]{:S(2)}, u32[]{:S(2)}) collective-permute-start(bf16[64,2048]{1,0:T(8,128)(2,1)} %tie.4.refs_2_.refs_4_), channel_id=1, source_target_pairs={{0,1},{1,2},{2,3},{3,0},{4,5},{5,6},{6,7},{7,4},{8,9},{9,10},{10,1... | collective-permute-start | bytes 786440 | tf_op jit(solution)/shard_map/ppermute | solution.py:23
  221.0 3.0 collective-permute-start.29
  234.6 28.4 %collective-permute-start.30 = (bf16[2,256,512]{2,1,0:T(8,128)(2,1)}, bf16[2,256,512]{2,1,0:T(8,128)(2,1)S(1)}, u32[]{:S(2)}, u32[]{:S(2)}) collective-permute-start(bf16[2,256,512]{2,1,0:T(8,128)(2,1)} %get-tuple-element.90.refs_7_), channel_id=1, source_target_pairs={{4,0},{8,4},{12,8},{5,1},{9,5},{13,9},{6,2},{10,6},{14,10},{7,3},{... | collective-permute-start | bytes 1572872 | tf_op jit(solution)/shard_map/ppermute | solution.py:28
  235.9 28.0 %collective-permute-start.31 = (bf16[2,256,512]{2,1,0:T(8,128)(2,1)}, bf16[2,256,512]{2,1,0:T(8,128)(2,1)}, u32[]{:S(2)}, u32[]{:S(2)}) collective-permute-start(bf16[2,256,512]{2,1,0:T(8,128)(2,1)} %get-tuple-element.90.refs_7_), channel_id=1, source_target_pairs={{8,0},{12,4},{9,1},{13,5},{10,2},{14,6},{11,3},{15,7},{24,16},{28,... | collective-permute-start | bytes 1572872 | tf_op jit(solution)/shard_map/ppermute | solution.py:28
  237.2 27.5 %collective-permute-start.32 = (bf16[2,256,512]{2,1,0:T(8,128)(2,1)}, bf16[2,256,512]{2,1,0:T(8,128)(2,1)}, u32[]{:S(2)}, u32[]{:S(2)}) collective-permute-start(bf16[2,256,512]{2,1,0:T(8,128)(2,1)} %get-tuple-element.90.refs_7_), channel_id=1, source_target_pairs={{12,0},{13,1},{14,2},{15,3},{28,16},{29,17},{30,18},{31,19},{44,32... | collective-permute-start | bytes 1572872 | tf_op jit(solution)/shard_map/ppermute | solution.py:28
  288.6 4.4 %collective-permute-start.33 = (bf16[256,2048]{1,0:T(8,128)(2,1)}, bf16[256,2048]{1,0:T(8,128)(2,1)S(1)}, u32[]{:S(2)}, u32[]{:S(2)}) collective-permute-start(bf16[256,2048]{1,0:T(8,128)(2,1)} %copy-done.32), channel_id=1, source_target_pairs={{0,16},{16,0},{1,17},{17,1},{2,18},{18,2},{3,19},{19,3},{4,20},{20... | collective-permute-start | bytes 3145736 | tf_op jit(solution)/shard_map/ppermute | solution.py:34
  289.1 4.0 %collective-permute-start.34 = (bf16[256,2048]{1,0:T(8,128)(2,1)}, bf16[256,2048]{1,0:T(8,128)(2,1)S(1)}, u32[]{:S(2)}, u32[]{:S(2)}) collective-permute-start(bf16[256,2048]{1,0:T(8,128)(2,1)} %tie.6), channel_id=1, source_target_pairs={{0,16},{16,0},{1,17},{17,1},{2,18},{18,2},{3,19},{19,3},{4,20},{20... | collective-permute-start | bytes 3145736 | tf_op jit(solution)/shard_map/ppermute | solution.py:34
  290.0 1.4 collective-permute-start.38
  291.4 10.4 %collective-permute-start.39 = (f32[2,2048]{1,0:T(2,128)S(1)}, f32[2,2048]{1,0:T(2,128)S(1)}, u32[]{:S(2)}, u32[]{:S(2)}) collective-permute-start(f32[2,2048]{1,0:T(2,128)S(1)} %fusion.11), channel_id=1, source_target_pairs={{0,4},{4,0},{8,12},{12,8},{1,5},{5,1},{9,13},{13,9},{2,6},{6,2},{1... | collective-permute-start | bytes 49160 | tf_op jit(solution)/shard_map/ppermute | solution.py:1152
  300.0 18.1 %collective-permute-start.37 = (bf16[128,2048]{1,0:T(8,128)(2,1)}, bf16[128,2048]{1,0:T(8,128)(2,1)S(1)}, u32[]{:S(2)}, u32[]{:S(2)}) collective-permute-start(bf16[128,2048]{1,0:T(8,128)(2,1)} %get-tuple-element.110), channel_id=1, source_target_pairs={{0,3},{1,0},{2,1},{3,2},{4,7},{5,4},{6,5},{7,6},{8,11},{9,8},{10,9... | collective-permute-start | bytes 1572872 | tf_op jit(solution)/shard_map/ppermute | solution.py:23
  300.3 17.8 %collective-permute-start.36 = (bf16[128,2048]{1,0:T(8,128)(2,1)}, bf16[128,2048]{1,0:T(8,128)(2,1)S(1)}, u32[]{:S(2)}, u32[]{:S(2)}) collective-permute-start(bf16[128,2048]{1,0:T(8,128)(2,1)} %get-tuple-element.109), channel_id=1, source_target_pairs={{0,1},{1,2},{2,3},{3,0},{4,5},{5,6},{6,7},{7,4},{8,9},{9,10},{10,1... | collective-permute-start | bytes 1572872 | tf_op jit(solution)/shard_map/ppermute | solution.py:23
  301.5 22.9 %collective-permute-start.35 = (bf16[128,2048]{1,0:T(8,128)(2,1)}, bf16[128,2048]{1,0:T(8,128)(2,1)S(1)}, u32[]{:S(2)}, u32[]{:S(2)}) collective-permute-start(bf16[128,2048]{1,0:T(8,128)(2,1)} %get-tuple-element.108), channel_id=1, source_target_pairs={{0,2},{1,3},{2,0},{3,1},{4,6},{5,7},{6,4},{7,5},{8,10},{9,11},{10,... | collective-permute-start | bytes 1572872 | tf_op jit(solution)/shard_map/ppermute | solution.py:23
  301.9 8.4 %collective-permute-start.40 = (f32[2,2048]{1,0:T(2,128)S(1)}, f32[2,2048]{1,0:T(2,128)S(1)}, u32[]{:S(2)}, u32[]{:S(2)}) collective-permute-start(f32[2,2048]{1,0:T(2,128)S(1)} %fusion.29), channel_id=1, source_target_pairs={{0,12},{4,8},{8,4},{12,0},{1,13},{5,9},{9,5},{13,1},{2,14},{6,10},... | collective-permute-start | bytes 49160 | tf_op jit(solution)/shard_map/ppermute | solution.py:1152
  310.3 3.6 collective-permute-start.41
  313.8 4.3 %collective-permute-start.42 = (f32[2,2048]{1,0:T(2,128)S(1)}, f32[2,2048]{1,0:T(2,128)S(1)}, u32[]{:S(2)}, u32[]{:S(2)}) collective-permute-start(f32[2,2048]{1,0:T(2,128)S(1)} %add.188), channel_id=1, source_target_pairs={{0,96},{32,64},{64,32},{96,0},{1,97},{33,65},{65,33},{97,1},{2,98}... | collective-permute-start | bytes 49160 | tf_op jit(solution)/shard_map/ppermute | solution.py:1152
  325.9 31.8 %copy-start.41 = (bf16[144,2048]{1,0:T(8,128)(2,1)}, bf16[144,2048]{1,0:T(8,128)(2,1)S(1)}, u32[]{:S(2)}) copy-start(bf16[144,2048]{1,0:T(8,128)(2,1)S(1)} %maximum_maximum_fusion.refs_4_) | copy-start | bytes 1769476
  325.9 15.5 %collective-permute-start.43 = (bf16[144,2048]{1,0:T(8,128)(2,1)S(1)}, bf16[144,2048]{1,0:T(8,128)(2,1)S(1)}, u32[]{:S(2)}, u32[]{:S(2)}) collective-permute-start(bf16[144,2048]{1,0:T(8,128)(2,1)S(1)} %maximum_maximum_fusion.refs_4_), channel_id=1, source_target_pairs={{0,3},{1,0},{2,1},{3,2},{4,7},{5,4},{6,5},{7,6},{8,11},{9,8},{10,9... | collective-permute-start | bytes 1769480 | tf_op jit(solution)/shard_map/ppermute | solution.py:23
  328.3 14.6 %collective-permute-start.44 = (bf16[144,2048]{1,0:T(8,128)(2,1)S(1)}, bf16[144,2048]{1,0:T(8,128)(2,1)S(1)}, u32[]{:S(2)}, u32[]{:S(2)}) collective-permute-start(bf16[144,2048]{1,0:T(8,128)(2,1)S(1)} %maximum_maximum_fusion.refs_4_), channel_id=1, source_target_pairs={{0,2},{1,3},{2,0},{3,1},{4,6},{5,7},{6,4},{7,5},{8,10},{9,11},{10,... | collective-permute-start | bytes 1769480 | tf_op jit(solution)/shard_map/ppermute | solution.py:23
  328.7 28.9 %collective-permute-start.45 = (bf16[144,2048]{1,0:T(8,128)(2,1)S(1)}, bf16[144,2048]{1,0:T(8,128)(2,1)S(1)}, u32[]{:S(2)}, u32[]{:S(2)}) collective-permute-start(bf16[144,2048]{1,0:T(8,128)(2,1)S(1)} %maximum_maximum_fusion.refs_4_), channel_id=1, source_target_pairs={{0,1},{1,2},{2,3},{3,0},{4,5},{5,6},{6,7},{7,4},{8,9},{9,10},{10,1... | collective-permute-start | bytes 1769480 | tf_op jit(solution)/shard_map/ppermute | solution.py:23
  341.5 16.2 %copy-start.48 = (bf16[144,2048]{1,0:T(8,128)(2,1)}, bf16[144,2048]{1,0:T(8,128)(2,1)S(1)}, u32[]{:S(2)}) copy-start(bf16[144,2048]{1,0:T(8,128)(2,1)S(1)} %collective-permute-done.43.refs_5_) | copy-start | bytes 1769476
  377.2 2.4 collective-permute-start.46
  (48 other events, 176.3 us)
Sparse Core Ops, SparseCore 0:
  16.5 77.8 all-gather.2
  96.6 64.9 all-gather.4
  272.7 103.2 reduce-scatter.1
